TPU v7x, 128 devices: a whole 4x4x4 slice. The times are simulated.
128 devices in a mesh: ctx: 4 (over z), tp: 32 (over x, y, core).
Axes of the slice: x: 4, y: 4, z: 4, core: 2. Of those that a mesh axis runs over, the one named last changes fastest.
Arguments:
- conv_out: bfloat16 [1024, 16384], P('ctx', 'tp'), may hold values from -6 to 6
- gate_in: bfloat16 [1024, 16384], P('ctx', 'tp'), may hold values from -6 to 6
- residual: bfloat16 [1024, 8192], P('ctx', 'tp')
- xproj_weight: bfloat16 [16384, 544], P('tp'), may hold values from -0.046875 to 0.046875
- dtproj_weight: bfloat16 [512, 16384], P(None, 'tp'), may hold values from -0.25 to 0.25
- dt_bias: float32 [16384], P('tp')
- a_log: float32 [16, 16384], P(None, 'tp'), may hold values from 0 to 2.77
- d_skip: float32 [16384], P('tp'), may hold values from 0.5 to 1.5
- init_state: float32 [16, 16384], P(None, 'tp'), may hold values from -2 to 2
- out_weight: bfloat16 [16384, 8192], P('tp'), may hold values from -0.09375 to 0.09375
- norm_gain: float32 [8192], P('tp'), may hold values from 0.1 to 1.9
- kv_weight: bfloat16 [8192, 2048], P('tp'), may hold values from -0.125 to 0.125
- owner: int32 [128], replicated, may hold values from 0 to 127, each once
- block_start: int32 [128], replicated, may hold values from 0 to 5, as said below
- block_count: int32 [128], replicated, may hold values from 3 to 4, as said below
Outputs:
- layer_out: bfloat16 [1024, 8192], P('ctx', 'tp')
- kv_cache: bfloat16 [128, 4, 16, 128, 128], P(('ctx', 'tp'))
Inputs may be any that keep to these rules, and one draw needn't show every extreme that they name: Each request's blocks lie in the window: block_start + block_count <= 8. `block_count`: some request has exactly 4 blocks.
All inputs are finite; a program needn't handle non-finite values.
Results may differ from a plain program's by a relative error of at most 0.033.
Values may be sent and summed in bfloat16 or wider, within the bound.
No kernel may reach another device: no remote copies, remote signals or barrier semaphores. Data moves between devices by JAX's collectives and lax.ppermute only.
A program may use at most 128 MiB of HBM per device.

v0:
```python
import jax
import jax.numpy as jnp
from jax import lax
from jax.experimental import pallas as pl
from jax.experimental.pallas import tpu as pltpu
from jax.sharding import PartitionSpec as P

D = 8192
STATE = 16
DTR = 512
KVH = 8
HEAD = 128
BLK = 128
CAP = 4
EPS = 1e-05
LOG2E = 1.4426950408889634
CHUNK = 32
BF = jnp.bfloat16
F32 = jnp.float32

VM = pl.BlockSpec(memory_space=pltpu.VMEM)
SM = pl.BlockSpec(memory_space=pltpu.SMEM)
ANY = pl.BlockSpec(memory_space=pl.ANY)


def params(mib):
    return pltpu.CompilerParams(vmem_limit_bytes=mib * 1024 * 1024)


def project_kernel(conv_ref, weight_ref, out_ref):
    out_ref[...] = lax.dot_general(
        conv_ref[...], weight_ref[...], (((1,), (1,)), ((), ())), preferred_element_type=F32
    ).astype(BF)


def advance_block(block, hidden, step_ref, drive_ref, states_ref, rates, read_out):
    states = states_ref[block]
    for group in range(CHUNK // 8):
        rows = pl.ds(pl.multiple_of(block * CHUNK + group * 8, 8), 8)
        steps, drives = step_ref[rows, :], drive_ref[rows, :]
        outs = []
        for i in range(8):
            at = group * 8 + i
            decay = jnp.exp2(steps[i : i + 1, :] * rates)
            hidden = decay * hidden + states[:STATE, at : at + 1] * drives[i : i + 1, :]
            if read_out is not None:
                outs.append(
                    jnp.sum(hidden * states[STATE:, at : at + 1], axis=0, keepdims=True)
                )
        if read_out is not None:
            read_out[rows, :] = jnp.concatenate(outs, axis=0)
    return hidden


def first_kernel(
    proj_ref, weight_ref, bias_ref, alog_ref, conv_ref,
    step_ref, states_ref, ends_ref, wide_ref, drive_ref,
):
    tokens = step_ref.shape[0]
    wide_ref[:, : 2 * STATE] = proj_ref[:, DTR:].astype(F32)
    flipped = jnp.transpose(wide_ref[...])
    for block in range(tokens // CHUNK):
        states_ref[block] = flipped[: 2 * STATE, block * CHUNK : (block + 1) * CHUNK]
    step = jax.nn.softplus(
        jnp.dot(proj_ref[:, :DTR], weight_ref[...], preferred_element_type=F32) + bias_ref[...]
    )
    step_ref[...] = step
    drive_ref[...] = step * conv_ref[...].astype(F32)
    rates = -jnp.exp(alog_ref[...]) * LOG2E
    hidden = lax.fori_loop(
        0,
        tokens // CHUNK,
        lambda k, h: advance_block(k, h, step_ref, drive_ref, states_ref, rates, None),
        jnp.zeros_like(rates),
    )
    ends_ref[:STATE, :] = hidden
    ends_ref[STATE:, :] = jnp.broadcast_to(jnp.sum(step, axis=0, keepdims=True), (8, step.shape[1]))


def second_kernel(
    place_ref, step_ref, states_ref, alog_ref, conv_ref, gate_ref, skip_ref, init_ref,
    near_ref, mid_ref, far_ref, weight_ref,
    keep_ref, give_ref, drive_ref, scan_ref, held_ref, sems,
):
    tokens = step_ref.shape[0]
    place, core = place_ref[0], place_ref[1]
    pairs = keep_ref.shape[0]
    wide = held_ref.shape[3]

    def fetch(side, pair):
        which = core if side == 1 else 1 - core
        columns = pl.ds(pl.multiple_of((2 * pair + which) * wide, wide), wide)
        return pltpu.make_async_copy(
            weight_ref.at[:, columns], held_ref.at[side, pair], sems.at[side, pair]
        )

    for side in range(2):
        for pair in range(pairs):
            fetch(side, pair).start()

    rates = -jnp.exp(alog_ref[...]) * LOG2E
    hidden = init_ref[...]
    for back, ref in ((3, far_ref), (2, mid_ref), (1, near_ref)):
        passed = jnp.exp2(ref[STATE : STATE + 1, :] * rates) * hidden + ref[:STATE, :]
        hidden = jnp.where(place >= back, passed, hidden)
    drive_ref[...] = step_ref[...] * conv_ref[...].astype(F32)
    lax.fori_loop(
        0,
        tokens // CHUNK,
        lambda k, h: advance_block(k, h, step_ref, drive_ref, states_ref, rates, scan_ref),
        hidden,
    )
    gate = gate_ref[...].astype(F32)
    gated = (
        (scan_ref[...] + skip_ref[...] * conv_ref[...].astype(F32)) * (gate / (1.0 + jnp.exp(-gate)))
    ).astype(BF)
    for side, ref in ((0, give_ref), (1, keep_ref)):
        for pair in range(pairs):
            fetch(side, pair).wait()
            ref[pair] = jnp.dot(
                gated, held_ref[side, pair], preferred_element_type=F32
            ).astype(BF)


def layer_kernel(parts_ref, residual_ref, gain_ref, weight_ref, layer_ref, out_ref):
    mixed = jnp.sum(parts_ref[...].astype(F32), axis=0)
    layer = (residual_ref[...].astype(F32) + mixed).astype(BF)
    layer_ref[...] = layer
    stream = layer.astype(F32)
    scaled = (stream * gain_ref[...]).astype(BF)
    tokens, feats = stream.shape
    squares = lax.dot_general(
        jnp.ones((16, feats), F32), stream * stream, (((1,), (1,)), ((), ())),
        preferred_element_type=F32, precision=lax.Precision.HIGHEST,
    ).astype(BF)
    term = jnp.dot(scaled, weight_ref[...], preferred_element_type=F32).astype(BF)
    for block in range(tokens // BLK):
        for j in range(2 * KVH):
            at = block * 2 * KVH + j
            out_ref[at, :BLK, :] = term[block * BLK : (block + 1) * BLK, j * HEAD : (j + 1) * HEAD]
            out_ref[at, BLK:, :] = squares[:, block * BLK : (block + 1) * BLK]


def tile_kernel(parts_ref, tile_ref):
    total = jnp.sum(parts_ref[...].astype(F32), axis=0)
    scale = lax.rsqrt(total[BLK : BLK + 1, :] / D + EPS)
    column = jnp.transpose(jnp.broadcast_to(scale, (BLK, BLK)))
    tile_ref[...] = (total[:BLK, :] * column).astype(BF)


def invert(owner_ref, start_ref, count_ref, starts, counts):
    def one(r, carry):
        starts[owner_ref[r]] = start_ref[r]
        counts[owner_ref[r]] = count_ref[r]
        return carry

    lax.fori_loop(0, owner_ref.shape[0], one, 0)


def send_kernel(
    place_ref, owner_ref, start_ref, count_ref, own_ref, near_ref, mid_ref, far_ref,
    out_ref, held_ref, starts, counts,
):
    invert(owner_ref, start_ref, count_ref, starts, counts)
    place, parity = place_ref[0], place_ref[2]
    for back, ref in enumerate((own_ref, near_ref, mid_ref, far_ref)):
        held_ref[lax.rem(place + 4 - back, 4)] = ref[...]
    targets = out_ref.shape[0]

    def one(target, carry):
        first, count = starts[place * targets + target], counts[place * targets + target]
        slot = lax.rem(parity + first, 2)
        for k in range(2):
            at = slot + 2 * k
            holder = jnp.minimum((first + at) // 2, 3)
            tile = held_ref[holder]
            out_ref[target, k] = jnp.where(at < count, tile, jnp.zeros_like(tile))
        return carry

    lax.fori_loop(0, targets, one, 0)


def cache_kernel(place_ref, owner_ref, start_ref, arrived_ref, out_ref, starts, counts, sems):
    invert(owner_ref, start_ref, start_ref, starts, counts)
    odd = lax.rem(starts[place_ref[3]], 2)
    copies = []
    for half in range(2):
        slot = jnp.where(odd == 1, 1 - half, half)
        for k in range(2):
            copies.append(
                pltpu.make_async_copy(
                    arrived_ref.at[half, :, k], out_ref.at[slot + 2 * k], sems.at[half, k]
                )
            )
    for copy in copies:
        copy.start()
    for copy in copies:
        copy.wait()


def shape(dims, kind):
    return jax.ShapeDtypeStruct(dims, kind)


def per_device(
    conv_out,
    gate_in,
    residual,
    xproj_weight,
    dtproj_weight,
    dt_bias,
    a_log,
    d_skip,
    init_state,
    out_weight,
    norm_gain,
    kv_weight,
    owner,
    block_start,
    block_count,
):
    tp_count = lax.axis_size("tp")
    ctx_count = lax.axis_size("ctx")
    tokens, chans = conv_out.shape
    feats = residual.shape[1]
    pairs = tp_count // 2
    place = lax.axis_index("ctx")
    member = lax.axis_index("tp")
    places = jnp.stack(
        [place, member % 2, member // (tp_count // 2), place * tp_count + member]
    ).astype(jnp.int32)
    columns = DTR + 2 * STATE

    part = pl.pallas_call(
        project_kernel, out_shape=shape((tokens, columns), BF), name="project"
    )(conv_out, xproj_weight.T)
    shares = lax.all_to_all(
        part.reshape(tp_count, tokens // tp_count, columns), "tp", 0, 0, tiled=True
    )
    mine = jnp.sum(shares.astype(F32), axis=0).astype(BF)
    projected = lax.all_to_all(
        jnp.broadcast_to(mine[None], (tp_count,) + mine.shape), "tp", 0, 0, tiled=True
    ).reshape(tokens, columns)

    blocks = tokens // CHUNK
    step, states, ends = pl.pallas_call(
        first_kernel,
        out_shape=(
            shape((tokens, chans), F32),
            shape((blocks, 2 * STATE, CHUNK), F32),
            shape((STATE + 8, chans), F32),
        ),
        scratch_shapes=[pltpu.VMEM((tokens, 128), F32), pltpu.VMEM((tokens, chans), F32)],
        compiler_params=params(32),
        name="first",
    )(projected, dtproj_weight, dt_bias.reshape(1, chans), a_log, conv_out)
    earlier = [
        lax.ppermute(ends, "ctx", [(z, z + s) for z in range(ctx_count - s)])
        for s in range(1, ctx_count)
    ]
    keep, give = pl.pallas_call(
        second_kernel,
        in_specs=[SM] + [VM] * 10 + [ANY],
        out_shape=(shape((pairs, tokens, feats), BF),) * 2,
        scratch_shapes=[
            pltpu.VMEM((tokens, chans), F32),
            pltpu.VMEM((tokens, chans), F32),
            pltpu.VMEM((2, pairs, chans, feats), BF),
            pltpu.SemaphoreType.DMA((2, pairs)),
        ],
        compiler_params=params(40),
        name="second",
    )(
        places, step, states, a_log, conv_out, gate_in, d_skip.reshape(1, chans), init_state,
        *earlier, out_weight,
    )
    got = lax.ppermute(give, "tp", [(i, i ^ 1) for i in range(tp_count)])
    summed = (keep.astype(F32) + got.astype(F32)).astype(BF)
    groups = [[2 * i + c for i in range(pairs)] for c in range(2)]
    parts = lax.all_to_all(summed, "tp", 0, 0, axis_index_groups=groups, tiled=True)

    layer_out, kv_terms = pl.pallas_call(
        layer_kernel,
        out_shape=(shape((tokens, feats), BF), shape((tp_count, BLK + 16, HEAD), BF)),
        compiler_params=params(32),
        name="layer",
    )(parts, residual, norm_gain.reshape(1, feats), kv_weight)
    kv_parts = lax.all_to_all(kv_terms, "tp", 0, 0, tiled=True)
    tile = pl.pallas_call(
        tile_kernel, out_shape=shape((BLK, HEAD), BF), compiler_params=params(32), name="tile"
    )(kv_parts)
    others = [
        lax.ppermute(tile, "ctx", [(z, (z + s) % ctx_count) for z in range(ctx_count)])
        for s in range(1, ctx_count)
    ]
    devices = owner.shape[0]
    outgoing = pl.pallas_call(
        send_kernel,
        in_specs=[SM] * 4 + [VM] * 4,
        out_shape=shape((tp_count, 2, BLK, HEAD), BF),
        scratch_shapes=[
            pltpu.VMEM((ctx_count, BLK, HEAD), BF),
            pltpu.SMEM((devices,), jnp.int32),
            pltpu.SMEM((devices,), jnp.int32),
        ],
        compiler_params=params(32),
        name="send",
    )(places, owner, block_start, block_count, tile, *others)
    arrived = lax.all_to_all(outgoing, "tp", 0, 0, tiled=True)
    kv_cache = pl.pallas_call(
        cache_kernel,
        in_specs=[SM] * 3 + [ANY],
        out_specs=ANY,
        out_shape=shape((CAP, 2 * KVH, BLK, HEAD), BF),
        scratch_shapes=[
            pltpu.SMEM((devices,), jnp.int32),
            pltpu.SMEM((devices,), jnp.int32),
            pltpu.SemaphoreType.DMA((2, 2)),
        ],
        compiler_params=params(32),
        name="cache",
    )(places, owner, block_start, arrived.reshape(2, 2 * KVH, 2, BLK, HEAD))
    return (layer_out, kv_cache[None])


def solution(mesh):
    placed = (
        P("ctx", "tp"),
        P("ctx", "tp"),
        P("ctx", "tp"),
        P("tp", None),
        P(None, "tp"),
        P("tp"),
        P(None, "tp"),
        P("tp"),
        P(None, "tp"),
        P("tp", None),
        P("tp"),
        P("tp", None),
        P(),
        P(),
        P(),
    )
    return jax.shard_map(
        per_device,
        mesh=mesh,
        in_specs=placed,
        out_specs=(P("ctx", "tp"), P(("ctx", "tp"), None, None, None, None)),
        check_vma=False,
    )
```

profile of v0, /device:TPU:1, one launch (start us, length us, event | category | flops | bytes accessed | tf_op | source)
XLA Modules:
  0.0 175.5 jit_solution(2880055299533999290)
XLA Ops:
  0.6 0.0 copy-start.1
  0.6 0.0 copy-start.5
  0.7 0.0 copy-start.8
  0.7 0.0 copy-start.3
  0.7 0.0 copy-start.4
  0.7 0.0 copy-start.7
  0.7 0.0 copy-start.11
  0.7 2.3 %project.1 = bf16[256,544]{1,0:T(8,128)(2,1)} custom-call(bf16[256,512]{1,0:T(8,128)(2,1)} %conv_ref.5, bf16[544,512]{1,0:T(8,128)(2,1)} %bitcast.19), custom_call_target="tpu_custom_call" | custom-call | tf_op jit(solution)/shard_map/project/pallas_call | solution.py:234
  3.0 18.2 %all_to_all.25 = bf16[32,8,544]{2,1,0:T(8,128)(2,1)S(1)} all-to-all(bf16[32,8,544]{2,1,0:T(8,128)(2,1)} %bitcast.18), channel_id=1, replica_groups=mesh['ctx'=4,'tp'=32] {'tp'}, dimensions={0} | all-to-all | bytes 557056 | tf_op jit(solution)/shard_map/all_to_all | solution.py:237
  21.3 0.1 reduce_sum.12
  21.3 0.8 broadcast_in_dim.4
  22.1 3.7 %all-to-all-start.1 = ((bf16[32,8,544]{2,1,0:T(8,128)(2,1)}), bf16[32,8,544]{2,1,0:T(8,128)(2,1)S(1)}, u32[]{:S(2)}, u32[]{:S(2)}) async-start(bf16[32,8,544]{2,1,0:T(8,128)(2,1)} %broadcast_in_dim.4), calls=%async_computation.1 | async-start | bytes 655360 | tf_op jit(solution)/shard_map/all_to_all | solution.py:241
  25.8 9.6 %all-to-all-done.1 = bf16[32,8,544]{2,1,0:T(8,128)(2,1)S(1)} async-done(((bf16[32,8,544]{2,1,0:T(8,128)(2,1)}), bf16[32,8,544]{2,1,0:T(8,128)(2,1)S(1)}, u32[]{:S(2)}, u32[]{:S(2)}) %all-to-all-start.1) | async-done | bytes 278560 | tf_op jit(solution)/shard_map/all_to_all | solution.py:241
  35.4 0.0 copy-done.1
  35.4 0.0 copy-done.5
  35.4 0.0 copy-done.3
  35.4 2.3 %first.1 = (f32[256,512]{1,0:T(8,128)S(1)}, f32[8,32,32]{2,1,0:T(8,128)S(1)}, f32[24,512]{1,0:T(8,128)S(1)}) custom-call(bf16[256,544]{1,0:T(8,128)(2,1)S(1)} %bitcast.13, bf16[512,512]{1,0:T(8,128)(2,1)S(1)} %copy-done.3, f32[1,512]{1,0:T(1,128)S(1)} %bitcast.14, f32[16,512]{1,0:T(8,128)S(1)} %copy-done.5, bf16[256,512]{1,0:T(8,128)(2,1)S(1)} %copy-done.1), custom_call_target="tpu_custom_call" | custom-call | tf_op jit(solution)/shard_map/first/pallas_call | solution.py:246
  37.7 5.7 %collective-permute-start.2 = (f32[24,512]{1,0:T(8,128)S(1)}, f32[24,512]{1,0:T(8,128)S(1)}, u32[]{:S(2)}, u32[]{:S(2)}) collective-permute-start(f32[24,512]{1,0:T(8,128)S(1)} %get-tuple-element.11), channel_id=1, source_target_pairs={{0,96},{1,97},{2,98},{3,99},{4,100},{5,101},{6,102},{7,103},{8,104... | collective-permute-start | bytes 147464 | tf_op jit(solution)/shard_map/ppermute | solution.py:258
  43.4 1.3 collective-permute-start.1
  44.7 2.5 %collective-permute-start = (f32[24,512]{1,0:T(8,128)S(1)}, f32[24,512]{1,0:T(8,128)S(1)}, u32[]{:S(2)}, u32[]{:S(2)}) collective-permute-start(f32[24,512]{1,0:T(8,128)S(1)} %get-tuple-element.11), channel_id=1, source_target_pairs={{0,32},{32,64},{64,96},{1,33},{33,65},{65,97},{2,34},{34,66},{66,9... | collective-permute-start | bytes 147464 | tf_op jit(solution)/shard_map/ppermute | solution.py:258
  47.2 0.1 pad_add_fusion.place_ref
  47.3 0.0 collective-permute-done.2.far_ref
  47.3 0.0 collective-permute-done.1.mid_ref
  47.3 1.1 collective-permute-done.near_ref
  48.3 0.0 copy-done.7
  48.3 3.4 %copy-done = bf16[512,8192]{1,0:T(8,128)(2,1)S(1)} copy-done((bf16[512,8192]{1,0:T(8,128)(2,1)S(1)}, bf16[512,8192]{1,0:T(8,128)(2,1)}, u32[]{:S(2)}) %copy-start) | copy-done | bytes 8388632
  51.7 14.7 %second.1 = (bf16[16,256,256]{2,1,0:T(8,128)(2,1)S(1)}, bf16[16,256,256]{2,1,0:T(8,128)(2,1)S(1)}) custom-call(s32[4]{0:T(128)S(1)} %pad_add_fusion.place_ref, f32[256,512]{1,0:T(8,128)S(1)} %get-tuple-element.9.step_ref, f32[8,32,32]{2,1,0:T(8,128)S(1)} %get-tuple-element.10.states_ref, f32[16,512]{1,0:T(8,128)S(1)} %copy-done.5, ...), custom_call_target="tpu_custom_call" | custom-call | tf_op jit(solution)/shard_map/second/pallas_call | solution.py:261
  66.4 1.2 collective-permute-start.3
  67.6 3.8 %collective-permute-done.3 = bf16[16,256,256]{2,1,0:T(8,128)(2,1)S(1)} collective-permute-done((bf16[16,256,256]{2,1,0:T(8,128)(2,1)S(1)}, bf16[16,256,256]{2,1,0:T(8,128)(2,1)S(1)}, u32[]{:S(2)}, u32[]{:S(2)}) %collective-permute-start.3) | collective-permute-done | bytes 2097184 | tf_op jit(solution)/shard_map/ppermute | solution.py:277
  71.4 0.7 add_convert_fusion
  72.1 0.0 copy-start.2
  72.1 0.0 copy-start.6
  72.1 0.0 copy-start.12
  72.2 30.3 %all_to_all.26.parts_ref = bf16[16,256,256]{2,1,0:T(8,128)(2,1)S(1)} all-to-all(bf16[16,256,256]{2,1,0:T(8,128)(2,1)S(1)} %add_convert_fusion), channel_id=1, replica_groups={{0,2,4,6,8,10,12,14,16,18,20,22,24,26,28,30},{1,3,5,7,9,11,13,15,17,19,..., dimensions={0} | all-to-all | bytes 4194304 | tf_op jit(solution)/shard_map/all_to_all | solution.py:280
  102.5 0.0 copy-done.6
  102.5 1.4 layer.1
  104.0 24.4 %all_to_all.27.parts_ref = bf16[32,144,128]{2,1,0:T(8,128)(2,1)S(1)} all-to-all(bf16[32,144,128]{2,1,0:T(8,128)(2,1)S(1)} %get-tuple-element.15), channel_id=1, replica_groups=mesh['ctx'=4,'tp'=32] {'tp'}, dimensions={0} | all-to-all | bytes 2359296 | tf_op jit(solution)/shard_map/all_to_all | solution.py:288
  128.4 0.2 tile.1.own_ref
  128.6 0.9 collective-permute-start.6
  129.4 3.0 %collective-permute-start.5 = (bf16[128,128]{1,0:T(8,128)(2,1)S(1)}, bf16[128,128]{1,0:T(8,128)(2,1)S(1)}, u32[]{:S(2)}, u32[]{:S(2)}) collective-permute-start(bf16[128,128]{1,0:T(8,128)(2,1)S(1)} %tile.1.own_ref), channel_id=1, source_target_pairs={{0,64},{32,96},{64,0},{96,32},{1,65},{33,97},{65,1},{97,33},{2,66}... | collective-permute-start | bytes 98312 | tf_op jit(solution)/shard_map/ppermute | solution.py:293
  132.5 0.0 collective-permute-start.4
  132.5 0.0 collective-permute-done.6.far_ref
  132.5 1.3 collective-permute-done.5.mid_ref
  133.8 2.7 %collective-permute-done.4.near_ref = bf16[128,128]{1,0:T(8,128)(2,1)S(1)} collective-permute-done((bf16[128,128]{1,0:T(8,128)(2,1)S(1)}, bf16[128,128]{1,0:T(8,128)(2,1)S(1)}, u32[]{:S(2)}, u32[]{:S(2)}) %collective-permute-start.4) | collective-permute-done | bytes 32800 | tf_op jit(solution)/shard_map/ppermute | solution.py:293
  136.5 0.0 copy-done.13
  136.5 2.7 %send.1 = bf16[32,2,128,128]{3,2,1,0:T(8,128)(2,1)S(1)} custom-call(s32[4]{0:T(128)S(1)} %pad_add_fusion.place_ref, s32[128]{0:T(128)S(1)} %copy-done.9, s32[128]{0:T(128)S(1)} %copy-done.10, s32[128]{0:T(128)S(1)} %copy-done.13, bf16[128,128]{1,0:T(8,128)(2,1)S(1)} %tile.1.own_ref, bf16[128,128]{1,0:T(8,128)(2,1)S(1)} %collective-permute-done.4.near_ref, ...), custom_call_target="tpu_custom_call" | custom-call | tf_op jit(solution)/shard_map/send/pallas_call | solution.py:297
  139.2 33.4 %all_to_all.28 = bf16[32,2,128,128]{3,2,1,0:T(8,128)(2,1)S(1)} all-to-all(bf16[32,2,128,128]{3,2,1,0:T(8,128)(2,1)S(1)} %send.1), channel_id=1, replica_groups=mesh['ctx'=4,'tp'=32] {'tp'}, dimensions={0} | all-to-all | bytes 4194304 | tf_op jit(solution)/shard_map/all_to_all | solution.py:309
  172.6 2.8 %cache.1 = bf16[4,16,128,128]{3,2,1,0:T(8,128)(2,1)} custom-call(s32[4]{0:T(128)S(1)} %pad_add_fusion.place_ref, s32[128]{0:T(128)S(1)} %copy-done.9, s32[128]{0:T(128)S(1)} %copy-done.10, bf16[2,16,2,128,128]{4,3,2,1,0:T(8,128)(2,1)S(1)} %bitcast.12), custom_call_target="tpu_custom_call" | custom-call | tf_op jit(solution)/shard_map/cache/pallas_call | solution.py:310
  (11 shorter events, 0.0 us)
Async XLA Ops:
  0.6 34.8 %copy-start.1 = (bf16[256,512]{1,0:T(8,128)(2,1)S(1)}, bf16[256,512]{1,0:T(8,128)(2,1)}, u32[]{:S(2)}) copy-start(bf16[256,512]{1,0:T(8,128)(2,1)} %conv_ref.5) | copy-start | bytes 786436
  0.6 34.8 %copy-start.5 = (f32[16,512]{1,0:T(8,128)S(1)}, f32[16,512]{1,0:T(8,128)}, u32[]{:S(2)}) copy-start(f32[16,512]{1,0:T(8,128)} %alog_ref.3) | copy-start | bytes 98308
  0.7 34.7 %copy-start.8 = (f32[512]{0:T(512)S(1)}, f32[512]{0:T(512)}, u32[]{:S(2)}) copy-start(f32[512]{0:T(512)} %param.20) | copy-start | bytes 6148
  0.7 34.7 %copy-start.3 = (bf16[512,512]{1,0:T(8,128)(2,1)S(1)}, bf16[512,512]{1,0:T(8,128)(2,1)}, u32[]{:S(2)}) copy-start(bf16[512,512]{1,0:T(8,128)(2,1)} %weight_ref.3) | copy-start | bytes 1572868
  0.7 47.7 %copy-start.4 = (bf16[256,512]{1,0:T(8,128)(2,1)S(1)}, bf16[256,512]{1,0:T(8,128)(2,1)}, u32[]{:S(2)}) copy-start(bf16[256,512]{1,0:T(8,128)(2,1)} %gate_ref.1) | copy-start | bytes 786436
  0.7 47.7 %copy-start.7 = (f32[16,512]{1,0:T(8,128)S(1)}, f32[16,512]{1,0:T(8,128)}, u32[]{:S(2)}) copy-start(f32[16,512]{1,0:T(8,128)} %init_ref.1) | copy-start | bytes 98308
  0.7 47.6 %copy-start.11 = (f32[512]{0:T(512)S(1)}, f32[512]{0:T(512)}, u32[]{:S(2)}) copy-start(f32[512]{0:T(512)} %param.22) | copy-start | bytes 6148
  22.1 13.3 %all-to-all-start.1 = ((bf16[32,8,544]{2,1,0:T(8,128)(2,1)}), bf16[32,8,544]{2,1,0:T(8,128)(2,1)S(1)}, u32[]{:S(2)}, u32[]{:S(2)}) async-start(bf16[32,8,544]{2,1,0:T(8,128)(2,1)} %broadcast_in_dim.4), calls=%async_computation.1 | async-start | bytes 655360 | tf_op jit(solution)/shard_map/all_to_all | solution.py:241
  37.7 9.5 %collective-permute-start.2 = (f32[24,512]{1,0:T(8,128)S(1)}, f32[24,512]{1,0:T(8,128)S(1)}, u32[]{:S(2)}, u32[]{:S(2)}) collective-permute-start(f32[24,512]{1,0:T(8,128)S(1)} %get-tuple-element.11), channel_id=1, source_target_pairs={{0,96},{1,97},{2,98},{3,99},{4,100},{5,101},{6,102},{7,103},{8,104... | collective-permute-start | bytes 147464 | tf_op jit(solution)/shard_map/ppermute | solution.py:258
  43.4 3.9 %collective-permute-start.1 = (f32[24,512]{1,0:T(8,128)S(1)}, f32[24,512]{1,0:T(8,128)S(1)}, u32[]{:S(2)}, u32[]{:S(2)}) collective-permute-start(f32[24,512]{1,0:T(8,128)S(1)} %get-tuple-element.11), channel_id=1, source_target_pairs={{0,64},{32,96},{1,65},{33,97},{2,66},{34,98},{3,67},{35,99},{4,68}... | collective-permute-start | bytes 147464 | tf_op jit(solution)/shard_map/ppermute | solution.py:258
  44.7 3.6 %collective-permute-start = (f32[24,512]{1,0:T(8,128)S(1)}, f32[24,512]{1,0:T(8,128)S(1)}, u32[]{:S(2)}, u32[]{:S(2)}) collective-permute-start(f32[24,512]{1,0:T(8,128)S(1)} %get-tuple-element.11), channel_id=1, source_target_pairs={{0,32},{32,64},{64,96},{1,33},{33,65},{65,97},{2,34},{34,66},{66,9... | collective-permute-start | bytes 147464 | tf_op jit(solution)/shard_map/ppermute | solution.py:258
  48.3 3.4 %copy-start = (bf16[512,8192]{1,0:T(8,128)(2,1)S(1)}, bf16[512,8192]{1,0:T(8,128)(2,1)}, u32[]{:S(2)}) copy-start(bf16[512,8192]{1,0:T(8,128)(2,1)} %weight_ref.4) | copy-start | bytes 25165828
  66.4 5.0 %collective-permute-start.3 = (bf16[16,256,256]{2,1,0:T(8,128)(2,1)S(1)}, bf16[16,256,256]{2,1,0:T(8,128)(2,1)S(1)}, u32[]{:S(2)}, u32[]{:S(2)}) collective-permute-start(bf16[16,256,256]{2,1,0:T(8,128)(2,1)S(1)} %get-tuple-element.13), channel_id=1, source_target_pairs={{0,1},{1,0},{2,3},{3,2},{4,5},{5,4},{6,7},{7,6},{8,9},{9,8},{10,11... | collective-permute-start | bytes 6291464 | tf_op jit(solution)/shard_map/ppermute | solution.py:277
  72.1 30.4 %copy-start.2 = (bf16[256,2048]{1,0:T(8,128)(2,1)S(1)}, bf16[256,2048]{1,0:T(8,128)(2,1)}, u32[]{:S(2)}) copy-start(bf16[256,2048]{1,0:T(8,128)(2,1)} %weight_ref.5) | copy-start | bytes 3145732
  72.1 30.4 %copy-start.6 = (bf16[256,256]{1,0:T(8,128)(2,1)S(1)}, bf16[256,256]{1,0:T(8,128)(2,1)}, u32[]{:S(2)}) copy-start(bf16[256,256]{1,0:T(8,128)(2,1)} %residual_ref.1) | copy-start | bytes 393220
  72.1 30.4 %copy-start.12 = (f32[256]{0:T(256)S(1)}, f32[256]{0:T(256)}, u32[]{:S(2)}) copy-start(f32[256]{0:T(256)} %param.25) | copy-start | bytes 3076
  104.0 32.5 %copy-start.9 = (s32[128]{0:T(128)S(1)}, s32[128]{0:T(128)}, u32[]{:S(2)}) copy-start(s32[128]{0:T(128)} %owner_ref.3) | copy-start | bytes 1540
  104.0 32.5 %copy-start.10 = (s32[128]{0:T(128)S(1)}, s32[128]{0:T(128)}, u32[]{:S(2)}) copy-start(s32[128]{0:T(128)} %start_ref.3) | copy-start | bytes 1540
  104.0 32.5 %copy-start.13 = (s32[128]{0:T(128)S(1)}, s32[128]{0:T(128)}, u32[]{:S(2)}) copy-start(s32[128]{0:T(128)} %count_ref.1) | copy-start | bytes 1540
  128.6 3.9 %collective-permute-start.6 = (bf16[128,128]{1,0:T(8,128)(2,1)S(1)}, bf16[128,128]{1,0:T(8,128)(2,1)S(1)}, u32[]{:S(2)}, u32[]{:S(2)}) collective-permute-start(bf16[128,128]{1,0:T(8,128)(2,1)S(1)} %tile.1.own_ref), channel_id=1, source_target_pairs={{0,96},{32,0},{64,32},{96,64},{1,97},{33,1},{65,33},{97,65},{2,98}... | collective-permute-start | bytes 98312 | tf_op jit(solution)/shard_map/ppermute | solution.py:293
  129.4 4.3 %collective-permute-start.5 = (bf16[128,128]{1,0:T(8,128)(2,1)S(1)}, bf16[128,128]{1,0:T(8,128)(2,1)S(1)}, u32[]{:S(2)}, u32[]{:S(2)}) collective-permute-start(bf16[128,128]{1,0:T(8,128)(2,1)S(1)} %tile.1.own_ref), channel_id=1, source_target_pairs={{0,64},{32,96},{64,0},{96,32},{1,65},{33,97},{65,1},{97,33},{2,66}... | collective-permute-start | bytes 98312 | tf_op jit(solution)/shard_map/ppermute | solution.py:293
  132.5 4.0 %collective-permute-start.4 = (bf16[128,128]{1,0:T(8,128)(2,1)S(1)}, bf16[128,128]{1,0:T(8,128)(2,1)S(1)}, u32[]{:S(2)}, u32[]{:S(2)}) collective-permute-start(bf16[128,128]{1,0:T(8,128)(2,1)S(1)} %tile.1.own_ref), channel_id=1, source_target_pairs={{0,32},{32,64},{64,96},{96,0},{1,33},{33,65},{65,97},{97,1},{2,34}... | collective-permute-start | bytes 98312 | tf_op jit(solution)/shard_map/ppermute | solution.py:293
where the time goes:
time: 176 us; the launch traced here: 175 us
  blocking collectives  106 us (60%)
  Pallas kernels  26.5 us (15%)
  waiting for transfers between devices  18.4 us (10%)
  starting transfers between devices  18.2 us (10%)
  local copies, waits for them, and re-layouts  4.19 us (2%)
    all_to_all x1, blocking collectives, per_device(): arrived = lax.all_to_all(outgoing, 'tp', 0, 0, tiled=True)  33.4 us
    all_to_all x1, blocking collectives, per_device(): lax.all_to_all(summed, 'tp', 0, 0, axis_index_groups=groups, tiled=True)  30.3 us
    all_to_all x1, blocking collectives, per_device(): kv_parts = lax.all_to_all(kv_terms, 'tp', 0, 0, tiled=True)  24.4 us
    all_to_all x1, blocking collectives, per_device(): lax.all_to_all(part.reshape(tp_count, tokens // tp_count, columns), 'tp',...  18.2 us
    pallas_call x1, Pallas kernels, per_device(): pl.pallas_call(second_kernel, in_specs=[SM] + [VM] * 10 + [ANY], out_shap...  14.7 us
    all_to_all x1, waiting for transfers between devices, per_device(): lax.all_to_all(jnp.broadcast_to(mine[None], (tp_count,) + mine.shape), 't...  9.61 us
    ppermute x3, starting transfers between devices, per_device(): lax.ppermute(ends, 'ctx', [(z, z + s) for z in range(ctx_count - s)])  9.44 us
    ppermute x3, waiting for transfers between devices, per_device(): lax.ppermute(tile, 'ctx', [(z, (z + s) % ctx_count) for z in range(ctx_co...  3.97 us
  transfers between devices with their start and end apart: 8, of which 5 were waited for; matrix products, arithmetic and copies ran while one was open for 0% of the time, Pallas kernels for 0%

commit v1 on v0

v1 whole, which is shorter than its diff:
```python
import jax
import jax.numpy as jnp
from jax import lax
from jax.experimental import pallas as pl
from jax.experimental.pallas import tpu as pltpu
from jax.sharding import PartitionSpec as P

D = 8192
STATE = 16
DTR = 512
KVH = 8
HEAD = 128
BLK = 128
CAP = 4
EPS = 1e-05
LOG2E = 1.4426950408889634
CHUNK = 32
PIECES = 8
BF = jnp.bfloat16
F32 = jnp.float32

VM = pl.BlockSpec(memory_space=pltpu.VMEM)
SM = pl.BlockSpec(memory_space=pltpu.SMEM)
ANY = pl.BlockSpec(memory_space=pl.ANY)


def params(mib):
    return pltpu.CompilerParams(vmem_limit_bytes=mib * 1024 * 1024)


def project_kernel(conv_ref, weight_ref, out_ref):
    out_ref[...] = lax.dot_general(
        conv_ref[...], weight_ref[...], (((1,), (1,)), ((), ())), preferred_element_type=F32
    ).astype(BF)


def advance_block(block, hidden, step_ref, drive_ref, states_ref, rates, read_out):
    states = states_ref[block]
    for group in range(CHUNK // 8):
        rows = pl.ds(pl.multiple_of(block * CHUNK + group * 8, 8), 8)
        steps, drives = step_ref[rows, :], drive_ref[rows, :]
        outs = []
        for i in range(8):
            at = group * 8 + i
            decay = jnp.exp2(steps[i : i + 1, :] * rates)
            hidden = decay * hidden + states[:STATE, at : at + 1] * drives[i : i + 1, :]
            if read_out is not None:
                outs.append(
                    jnp.sum(hidden * states[STATE:, at : at + 1], axis=0, keepdims=True)
                )
        if read_out is not None:
            read_out[rows, :] = jnp.concatenate(outs, axis=0)
    return hidden


def first_kernel(
    proj_ref, weight_ref, bias_ref, alog_ref, conv_ref,
    step_ref, states_ref, ends_ref, wide_ref, drive_ref,
):
    tokens = step_ref.shape[0]
    wide_ref[:, : 2 * STATE] = proj_ref[:, DTR:].astype(F32)
    flipped = jnp.transpose(wide_ref[...])
    for block in range(tokens // CHUNK):
        states_ref[block] = flipped[: 2 * STATE, block * CHUNK : (block + 1) * CHUNK]
    step = jax.nn.softplus(
        jnp.dot(proj_ref[:, :DTR], weight_ref[...], preferred_element_type=F32) + bias_ref[...]
    )
    step_ref[...] = step
    drive_ref[...] = step * conv_ref[...].astype(F32)
    rates = -jnp.exp(alog_ref[...]) * LOG2E
    hidden = lax.fori_loop(
        0,
        tokens // CHUNK,
        lambda k, h: advance_block(k, h, step_ref, drive_ref, states_ref, rates, None),
        jnp.zeros_like(rates),
    )
    ends_ref[:STATE, :] = hidden
    ends_ref[STATE:, :] = jnp.broadcast_to(jnp.sum(step, axis=0, keepdims=True), (8, step.shape[1]))


def give_kernel(
    place_ref, step_ref, states_ref, alog_ref, conv_ref, gate_ref, skip_ref, init_ref,
    near_ref, mid_ref, far_ref, weight_ref,
    give_ref, kept_ref, drive_ref, scan_ref, gated_ref, held_ref, sems,
):
    tokens = step_ref.shape[0]
    place, core = place_ref[0], place_ref[1]
    copies = fetch(weight_ref, held_ref, sems)
    rates = -jnp.exp(alog_ref[...]) * LOG2E
    hidden = init_ref[...]
    for back, ref in ((3, far_ref), (2, mid_ref), (1, near_ref)):
        passed = jnp.exp2(ref[STATE : STATE + 1, :] * rates) * hidden + ref[:STATE, :]
        hidden = jnp.where(place >= back, passed, hidden)
    drive_ref[...] = step_ref[...] * conv_ref[...].astype(F32)
    lax.fori_loop(
        0,
        tokens // CHUNK,
        lambda k, h: advance_block(k, h, step_ref, drive_ref, states_ref, rates, scan_ref),
        hidden,
    )
    gate = gate_ref[...].astype(F32)
    gated_ref[...] = (
        (scan_ref[...] + skip_ref[...] * conv_ref[...].astype(F32)) * (gate / (1.0 + jnp.exp(-gate)))
    ).astype(BF).reshape(gated_ref.shape)
    kept_ref[...] = gated_ref[core]
    through(gated_ref.at[1 - core], held_ref, copies, give_ref)


def fetch(weight_ref, held_ref, sems):
    wide = weight_ref.shape[1] // PIECES
    copies = [
        pltpu.make_async_copy(
            weight_ref.at[:, pl.ds(i * wide, wide)], held_ref.at[:, pl.ds(i * wide, wide)],
            sems.at[i],
        )
        for i in range(PIECES)
    ]
    for copy in copies:
        copy.start()
    return copies


def through(gated_ref, held_ref, copies, out_ref):
    chips, _, wide = out_ref.shape
    for chip in range(chips):
        if chip % (chips // PIECES) == 0:
            copies[chip // (chips // PIECES)].wait()
        out_ref[chip] = jnp.dot(
            gated_ref[...], held_ref[:, chip * wide : (chip + 1) * wide],
            preferred_element_type=F32,
        ).astype(BF)


def keep_kernel(kept_ref, weight_ref, keep_ref, held_ref, sems):
    through(kept_ref, held_ref, fetch(weight_ref, held_ref, sems), keep_ref)


def layer_kernel(
    place_ref, parts_ref, own_res_ref, got_res_ref, own_gain_ref, got_gain_ref,
    own_weight_ref, got_weight_ref, own_ref, other_ref, out_ref,
):
    mixed = jnp.sum(parts_ref[...].astype(F32), axis=0)
    half = mixed.shape[1] // 2
    first = place_ref[1] == 0
    left, right = mixed[:, :half], mixed[:, half:]
    term, squares = 0.0, 0.0
    for piece, res_ref, gain_ref, weight_ref, layer_ref in (
        (jnp.where(first, left, right), own_res_ref, own_gain_ref, own_weight_ref, own_ref),
        (jnp.where(first, right, left), got_res_ref, got_gain_ref, got_weight_ref, other_ref),
    ):
        layer = (res_ref[...].astype(F32) + piece).astype(BF)
        layer_ref[...] = layer
        stream = layer.astype(F32)
        squares = squares + lax.dot_general(
            jnp.ones((16, half), F32), stream * stream, (((1,), (1,)), ((), ())),
            preferred_element_type=F32, precision=lax.Precision.HIGHEST,
        )
        term = term + jnp.dot(
            (stream * gain_ref[...]).astype(BF), weight_ref[...], preferred_element_type=F32
        )
    term, squares = term.astype(BF), squares.astype(BF)
    for j in range(2 * KVH):
        out_ref[j, :BLK, :] = term[:, j * HEAD : (j + 1) * HEAD]
        out_ref[j, BLK:, :] = squares


def tile_kernel(parts_ref, tile_ref):
    total = jnp.sum(parts_ref[...].astype(F32), axis=0)
    scale = lax.rsqrt(total[BLK : BLK + 1, :] / D + EPS)
    column = jnp.transpose(jnp.broadcast_to(scale, (BLK, BLK)))
    tile_ref[...] = (total[:BLK, :] * column).astype(BF)


def send_kernel(
    place_ref, starts_ref, counts_ref, own_ref, near_ref, mid_ref, far_ref,
    own_layer_ref, got_layer_ref, out_ref, layer_ref, held_ref,
):
    place, core = place_ref[0], place_ref[1]
    for back, ref in enumerate((own_ref, near_ref, mid_ref, far_ref)):
        held_ref[lax.rem(place + 4 - back, 4)] = ref[...]
    for ref, half in ((own_layer_ref, core), (got_layer_ref, 1 - core)):
        rows = ref.shape[0]
        layer_ref[pl.ds(pl.multiple_of(half * rows, rows), rows), :] = ref[...]
    targets = out_ref.shape[0]

    def one(target, carry):
        first, count = starts_ref[place * targets + target], counts_ref[place * targets + target]
        slot = lax.rem(core + first, 2)
        for k in range(2):
            at = slot + 2 * k
            holder = jnp.minimum((first + at) // 2, 3)
            tile = held_ref[holder]
            out_ref[target, k] = jnp.where(at < count, tile, jnp.zeros_like(tile))
        return carry

    lax.fori_loop(0, targets, one, 0)


def cache_kernel(place_ref, starts_ref, arrived_ref, out_ref, sems):
    odd = lax.rem(starts_ref[place_ref[2]], 2)
    copies = []
    for half in range(2):
        slot = jnp.where(odd == 1, 1 - half, half)
        for k in range(2):
            copies.append(
                pltpu.make_async_copy(
                    arrived_ref.at[:, half, k], out_ref.at[slot + 2 * k], sems.at[half, k]
                )
            )
    for copy in copies:
        copy.start()
    for copy in copies:
        copy.wait()


def shape(dims, kind):
    return jax.ShapeDtypeStruct(dims, kind)


def per_device(
    conv_out,
    gate_in,
    residual,
    xproj_weight,
    dtproj_weight,
    dt_bias,
    a_log,
    d_skip,
    init_state,
    out_weight,
    norm_gain,
    kv_weight,
    owner,
    block_start,
    block_count,
):
    tp_count = lax.axis_size("tp")
    ctx_count = lax.axis_size("ctx")
    tokens, chans = conv_out.shape
    feats = residual.shape[1]
    pairs = tp_count // 2
    place = lax.axis_index("ctx")
    member = lax.axis_index("tp")
    core = member % 2
    places = jnp.stack([place, core, place * tp_count + member]).astype(jnp.int32)
    partner = [(i, i ^ 1) for i in range(tp_count)]

    def swap(value):
        return lax.ppermute(value, "tp", partner)

    halves = residual.reshape(2, tokens // 2, feats)
    own_res = lax.dynamic_index_in_dim(halves, core, 0, False)
    got_res = swap(lax.dynamic_index_in_dim(halves, 1 - core, 0, False))
    own_gain = norm_gain.reshape(1, feats)
    got_gain, got_weight = swap(own_gain), swap(kv_weight)
    devices = owner.shape[0]
    matches = owner[:, None] == jnp.arange(devices, dtype=jnp.int32)[None, :]
    starts = jnp.sum(jnp.where(matches, block_start[:, None], 0), axis=0)
    counts = jnp.sum(jnp.where(matches, block_count[:, None], 0), axis=0)
    columns = DTR + 2 * STATE

    part = pl.pallas_call(
        project_kernel, out_shape=shape((tokens, columns), BF), name="project"
    )(conv_out, xproj_weight.T)
    shares = lax.all_to_all(
        part.reshape(tp_count, tokens // tp_count, columns), "tp", 0, 0, tiled=True
    )
    shares, places, starts, counts, own_res, got_res, got_gain, got_weight = (
        lax.optimization_barrier(
            (shares, places, starts, counts, own_res, got_res, got_gain, got_weight)
        )
    )
    mine = jnp.sum(shares.astype(F32), axis=0).astype(BF)
    projected = lax.all_to_all(
        jnp.broadcast_to(mine[None], (tp_count,) + mine.shape), "tp", 0, 0, tiled=True
    ).reshape(tokens, columns)

    blocks = tokens // CHUNK
    step, states, ends = pl.pallas_call(
        first_kernel,
        out_shape=(
            shape((tokens, chans), F32),
            shape((blocks, 2 * STATE, CHUNK), F32),
            shape((STATE + 8, chans), F32),
        ),
        scratch_shapes=[pltpu.VMEM((tokens, 128), F32), pltpu.VMEM((tokens, chans), F32)],
        compiler_params=params(8),
        name="first",
    )(projected, dtproj_weight, dt_bias.reshape(1, chans), a_log, conv_out)
    def ranges_back(value):
        return [
            lax.ppermute(value, "ctx", [(z, (z + s) % ctx_count) for z in range(ctx_count)])
            for s in range(1, ctx_count)
        ]

    weight_scratch = [pltpu.VMEM(out_weight.shape, BF), pltpu.SemaphoreType.DMA((PIECES,))]
    partial = (pairs, tokens // 2, 2 * feats)
    give, kept = pl.pallas_call(
        give_kernel,
        in_specs=[SM] + [VM] * 10 + [ANY],
        out_shape=(shape(partial, BF), shape((tokens // 2, chans), BF)),
        scratch_shapes=[
            pltpu.VMEM((tokens, chans), F32),
            pltpu.VMEM((tokens, chans), F32),
            pltpu.VMEM((2, tokens // 2, chans), BF),
        ] + weight_scratch,
        compiler_params=params(46),
        name="give",
    )(
        places, step, states, a_log, conv_out, gate_in, d_skip.reshape(1, chans), init_state,
        *ranges_back(ends), out_weight,
    )
    got = swap(give)
    keep = pl.pallas_call(
        keep_kernel,
        in_specs=[VM, ANY],
        out_shape=shape(partial, BF),
        scratch_shapes=weight_scratch,
        compiler_params=params(46),
        name="keep",
    )(kept, out_weight)
    summed = (keep.astype(F32) + got.astype(F32)).astype(BF)
    groups = [[2 * i + c for i in range(pairs)] for c in range(2)]
    parts = lax.all_to_all(summed, "tp", 0, 0, axis_index_groups=groups, tiled=True)

    block_shape = shape((tokens // 2, feats), BF)
    own_layer, other_layer, kv_terms = pl.pallas_call(
        layer_kernel,
        in_specs=[SM] + [VM] * 7,
        out_shape=(block_shape, block_shape, shape((pairs, BLK + 16, HEAD), BF)),
        compiler_params=params(8),
        name="layer",
    )(places, parts, own_res, got_res, own_gain, got_gain, kv_weight, got_weight)
    got_layer = swap(other_layer)
    kv_parts = lax.all_to_all(kv_terms, "tp", 0, 0, axis_index_groups=groups, tiled=True)
    tile = pl.pallas_call(
        tile_kernel, out_shape=shape((BLK, HEAD), BF), compiler_params=params(8), name="tile"
    )(kv_parts)
    outgoing, layer_out = pl.pallas_call(
        send_kernel,
        in_specs=[SM] * 3 + [VM] * 6,
        out_shape=(shape((tp_count, 2, BLK, HEAD), BF), shape((tokens, feats), BF)),
        scratch_shapes=[pltpu.VMEM((ctx_count, BLK, HEAD), BF)],
        compiler_params=params(8),
        name="send",
    )(places, starts, counts, tile, *ranges_back(tile), own_layer, got_layer)
    arrived = lax.all_to_all(outgoing, "tp", 0, 0, tiled=True)
    kv_cache = pl.pallas_call(
        cache_kernel,
        in_specs=[SM] * 2 + [ANY],
        out_specs=ANY,
        out_shape=shape((CAP, 2 * KVH, BLK, HEAD), BF),
        scratch_shapes=[pltpu.SemaphoreType.DMA((2, 2))],
        compiler_params=params(8),
        name="cache",
    )(places, starts, arrived.reshape(2 * KVH, 2, 2, BLK, HEAD))
    return (layer_out, kv_cache[None])


def solution(mesh):
    placed = (
        P("ctx", "tp"),
        P("ctx", "tp"),
        P("ctx", "tp"),
        P("tp", None),
        P(None, "tp"),
        P("tp"),
        P(None, "tp"),
        P("tp"),
        P(None, "tp"),
        P("tp", None),
        P("tp"),
        P("tp", None),
        P(),
        P(),
        P(),
    )
    return jax.shard_map(
        per_device,
        mesh=mesh,
        in_specs=placed,
        out_specs=(P("ctx", "tp"), P(("ctx", "tp"), None, None, None, None)),
        check_vma=False,
    )
```

time: 176 us -> 152 us (0.86)
  blocking collectives: 106 us -> 80.6 us
  starting transfers between devices: 18.2 us -> 25.8 us
  Pallas kernels: 26.5 us -> 22.1 us
  local copies, waits for them, and re-layouts: 4.19 us -> 0.97 us
  waiting for transfers between devices: 18.4 us -> 20.3 us
    all_to_all x2 -> x1, blocking collectives: 42.7 us -> 13 us  [per_device(): lax.all_to_all(jnp.broadcast_to(mine[None], (tp_count,) + mine.shape), 't...]
    all_to_all x1 -> x2, starting transfers between devices: 3.66 us -> 11.2 us  [the longest x1 7.34 us: per_device(): lax.all_to_all(part.reshape(tp_count, tokens // tp_count, columns), 'tp',...]
    all_to_all x1 -> x2, waiting for transfers between devices: 9.61 us -> 14.5 us  [the longest x1 7.27 us: per_device(): lax.all_to_all(part.reshape(tp_count, tokens // tp_count, columns), 'tp',...]
    pallas_call x4 -> x5, Pallas kernels: 21.7 us -> 17.3 us  [the longest x1 6.74 us: per_device(): pl.pallas_call(give_kernel, in_specs=[SM] + [VM] * 10 + [ANY], out_shape=...]
    all_to_all x1, blocking collectives: 33.4 us -> 37.1 us  [per_device(): arrived = lax.all_to_all(outgoing, 'tp', 0, 0, tiled=True)]
    unnamed x28 -> x24, local copies, waits for them, and re-layouts: 3.44 us -> 0.05 us
    ppermute x7 -> x11, waiting for transfers between devices: 8.83 us -> 5.75 us  [the longest x6 5.1 us: ranges_back(): lax.ppermute(value, 'ctx', [(z, (z + s) % ctx_count) for z in range(ctx_c...]
    ppermute x7 -> x11, starting transfers between devices: 14.6 us -> 14.6 us  [the longest x6 9.09 us: ranges_back(): lax.ppermute(value, 'ctx', [(z, (z + s) % ctx_count) for z in range(ctx_c...]
  transfers between devices with their start and end apart: 8 -> 13, of which waited for: 5 -> 9; matrix products, arithmetic and copies ran while one was open for 0% -> 1% of each run, Pallas kernels for 0% -> 4%
where the time goes in v1:
time: 152 us
  blocking collectives  80.6 us (53%)
  starting transfers between devices  25.8 us (17%)
  Pallas kernels  22.1 us (15%)
  waiting for transfers between devices  20.3 us (13%)
    all_to_all x1, blocking collectives, per_device(): arrived = lax.all_to_all(outgoing, 'tp', 0, 0, tiled=True)  37.1 us
    all_to_all x1, blocking collectives, per_device(): lax.all_to_all(summed, 'tp', 0, 0, axis_index_groups=groups, tiled=True)  30.4 us
    all_to_all x1, blocking collectives, per_device(): lax.all_to_all(jnp.broadcast_to(mine[None], (tp_count,) + mine.shape), 't...  13 us
    ppermute x6, starting transfers between devices, ranges_back(): lax.ppermute(value, 'ctx', [(z, (z + s) % ctx_count) for z in range(ctx_c...  9.09 us
    all_to_all x1, starting transfers between devices, per_device(): lax.all_to_all(part.reshape(tp_count, tokens // tp_count, columns), 'tp',...  7.34 us
    all_to_all x1, waiting for transfers between devices, per_device(): lax.all_to_all(part.reshape(tp_count, tokens // tp_count, columns), 'tp',...  7.27 us
    all_to_all x1, waiting for transfers between devices, per_device(): lax.all_to_all(kv_terms, 'tp', 0, 0, axis_index_groups=groups, tiled=True)  7.23 us
    pallas_call x1, Pallas kernels, per_device(): pl.pallas_call(give_kernel, in_specs=[SM] + [VM] * 10 + [ANY], out_shape=...  6.74 us
  transfers between devices with their start and end apart: 13, of which 9 were waited for; matrix products, arithmetic and copies ran while one was open for 1% of the time, Pallas kernels for 4%

profile of v1, /device:TPU:1, one launch (start us, length us, event | category | flops | bytes accessed | tf_op | source)
XLA Modules:
  0.0 151.5 jit_solution(14977546347076769688)
XLA Ops:
  0.6 0.0 copy-start
  0.7 1.5 collective-permute-start.2
  2.2 2.3 %project.1 = bf16[256,544]{1,0:T(8,128)(2,1)} custom-call(bf16[256,512]{1,0:T(8,128)(2,1)} %conv_ref.5, bf16[544,512]{1,0:T(8,128)(2,1)} %bitcast.24), custom_call_target="tpu_custom_call" | custom-call | tf_op jit(solution)/shard_map/project/pallas_call | solution.py:262
  4.5 7.3 %all-to-all-start = ((bf16[32,8,544]{2,1,0:T(8,128)(2,1)}), bf16[32,8,544]{2,1,0:T(8,128)(2,1)S(1)}, u32[]{:S(2)}, u32[]{:S(2)}) async-start(bf16[32,8,544]{2,1,0:T(8,128)(2,1)} %bitcast.23), calls=%async_computation | async-start | bytes 655360 | tf_op jit(solution)/shard_map/all_to_all | solution.py:265
  11.9 0.9 dynamic-slice_bitcast_fusion
  12.8 0.3 collective-permute-start
  13.1 0.0 copy-done.8
  13.1 0.3 collective-permute-start.1
  13.4 0.0 copy-done.10
  13.4 0.1 select_reduce_fusion
  13.5 0.1 pad_add_fusion.place_ref
  13.6 0.6 collective-permute-done.1.got_gain_ref
  14.2 0.0 collective-permute-done.got_res_ref
  14.2 7.3 %all-to-all-done = bf16[32,8,544]{2,1,0:T(8,128)(2,1)S(1)} async-done(((bf16[32,8,544]{2,1,0:T(8,128)(2,1)}), bf16[32,8,544]{2,1,0:T(8,128)(2,1)S(1)}, u32[]{:S(2)}, u32[]{:S(2)}) %all-to-all-start) | async-done | bytes 278560 | tf_op jit(solution)/shard_map/all_to_all | solution.py:265
  21.5 0.0 collective-permute-done.2.got_weight_ref
  21.5 0.1 reduce_sum.32
  21.6 13.0 %all_to_all.25 = bf16[32,8,544]{2,1,0:T(8,128)(2,1)S(1)} all-to-all(bf16[32,8,544]{2,1,0:T(8,128)(2,1)S(1)} %broadcast_in_dim.34), channel_id=1, replica_groups=mesh['ctx'=4,'tp'=32] {'tp'}, dimensions={0} | all-to-all | bytes 557056 | tf_op jit(solution)/shard_map/all_to_all | solution.py:274
  34.7 0.0 copy-done.4
  34.7 2.4 %first.1 = (f32[256,512]{1,0:T(8,128)S(1)}, f32[8,32,32]{2,1,0:T(8,128)S(1)}, f32[24,512]{1,0:T(8,128)S(1)}) custom-call(bf16[256,544]{1,0:T(8,128)(2,1)S(1)} %bitcast.17, bf16[512,512]{1,0:T(8,128)(2,1)S(1)} %copy-done.2, f32[1,512]{1,0:T(1,128)S(1)} %bitcast.18, f32[16,512]{1,0:T(8,128)S(1)} %copy-done.4, bf16[256,512]{1,0:T(8,128)(2,1)S(1)} %copy-done), custom_call_target="tpu_custom_call" | custom-call | tf_op jit(solution)/shard_map/first/pallas_call | solution.py:279
  37.1 1.7 %collective-permute-start.3 = (f32[24,512]{1,0:T(8,128)S(1)}, f32[24,512]{1,0:T(8,128)S(1)}, u32[]{:S(2)}, u32[]{:S(2)}) collective-permute-start(f32[24,512]{1,0:T(8,128)S(1)} %get-tuple-element.26), channel_id=1, source_target_pairs={{0,32},{32,64},{64,96},{96,0},{1,33},{33,65},{65,97},{97,1},{2,34}... | collective-permute-start | bytes 147464 | tf_op jit(solution)/shard_map/ppermute | solution.py:292
  38.8 3.3 %collective-permute-start.4 = (f32[24,512]{1,0:T(8,128)S(1)}, f32[24,512]{1,0:T(8,128)S(1)}, u32[]{:S(2)}, u32[]{:S(2)}) collective-permute-start(f32[24,512]{1,0:T(8,128)S(1)} %get-tuple-element.26), channel_id=1, source_target_pairs={{0,64},{32,96},{64,0},{96,32},{1,65},{33,97},{65,1},{97,33},{2,66}... | collective-permute-start | bytes 147464 | tf_op jit(solution)/shard_map/ppermute | solution.py:292
  42.1 0.7 collective-permute-start.5
  42.8 0.2 collective-permute-done.3.near_ref
  43.0 2.0 %collective-permute-done.4.mid_ref = f32[24,512]{1,0:T(8,128)S(1)} collective-permute-done((f32[24,512]{1,0:T(8,128)S(1)}, f32[24,512]{1,0:T(8,128)S(1)}, u32[]{:S(2)}, u32[]{:S(2)}) %collective-permute-start.4) | collective-permute-done | bytes 49184 | tf_op jit(solution)/shard_map/ppermute | solution.py:292
  45.1 0.3 collective-permute-done.5.far_ref
  45.3 0.0 copy-done.5
  45.3 6.7 %give.1 = (bf16[16,128,512]{2,1,0:T(8,128)(2,1)S(1)}, bf16[128,512]{1,0:T(8,128)(2,1)S(1)}) custom-call(s32[3]{0:T(128)S(1)} %pad_add_fusion.place_ref, f32[256,512]{1,0:T(8,128)S(1)} %get-tuple-element.24.step_ref, f32[8,32,32]{2,1,0:T(8,128)S(1)} %get-tuple-element.25.states_ref, f32[16,512]{1,0:T(8,128)S(1)} %copy-done.4, bf16[256,512]{1,0:T(8,128)(2,1)S(1)} %copy-done, ...), custom_call_target="tpu_custom_call" | custom-call | tf_op jit(solution)/shard_map/give/pallas_call | solution.py:298
  52.1 1.5 collective-permute-start.6
  53.6 3.8 %keep.1 = bf16[16,128,512]{2,1,0:T(8,128)(2,1)S(1)} custom-call(bf16[128,512]{1,0:T(8,128)(2,1)S(1)} %get-tuple-element.27.kept_ref, bf16[512,8192]{1,0:T(8,128)(2,1)} %weight_ref.5), custom_call_target="tpu_custom_call" | custom-call | tf_op jit(solution)/shard_map/keep/pallas_call | solution.py:314
  57.4 0.0 collective-permute-done.6
  57.4 0.7 add_convert_fusion
  58.2 0.0 copy-start.1
  58.2 30.4 %all_to_all.26.parts_ref = bf16[16,128,512]{2,1,0:T(8,128)(2,1)S(1)} all-to-all(bf16[16,128,512]{2,1,0:T(8,128)(2,1)S(1)} %add_convert_fusion), channel_id=1, replica_groups={{0,2,4,6,8,10,12,14,16,18,20,22,24,26,28,30},{1,3,5,7,9,11,13,15,17,19,..., dimensions={0} | all-to-all | bytes 4194304 | tf_op jit(solution)/shard_map/all_to_all | solution.py:324
  88.6 2.4 %layer.1 = (bf16[128,256]{1,0:T(8,128)(2,1)S(1)}, bf16[128,256]{1,0:T(8,128)(2,1)S(1)}, bf16[16,144,128]{2,1,0:T(8,128)(2,1)}) custom-call(s32[3]{0:T(128)S(1)} %pad_add_fusion.place_ref, bf16[16,128,512]{2,1,0:T(8,128)(2,1)S(1)} %all_to_all.26.parts_ref, bf16[128,256]{1,0:T(8,128)(2,1)S(1)} %get-tuple-element.29.own_res_ref, ...), custom_call_target="tpu_custom_call" | custom-call | tf_op jit(solution)/shard_map/layer/pallas_call | solution.py:327
  91.0 3.8 %all-to-all-start.3 = ((bf16[16,144,128]{2,1,0:T(8,128)(2,1)}), bf16[16,144,128]{2,1,0:T(8,128)(2,1)S(1)}, u32[]{:S(2)}, u32[]{:S(2)}) async-start(bf16[16,144,128]{2,1,0:T(8,128)(2,1)} %get-tuple-element.33), calls=%async_computation.3 | async-start | bytes 1179648 | tf_op jit(solution)/shard_map/all_to_all | solution.py:335
  94.8 1.9 %collective-permute-start.10 = (bf16[128,256]{1,0:T(8,128)(2,1)S(1)}, bf16[128,256]{1,0:T(8,128)(2,1)S(1)}, u32[]{:S(2)}, u32[]{:S(2)}) collective-permute-start(bf16[128,256]{1,0:T(8,128)(2,1)S(1)} %get-tuple-element.35), channel_id=1, source_target_pairs={{0,1},{1,0},{2,3},{3,2},{4,5},{5,4},{6,7},{7,6},{8,9},{9,8},{10,11... | collective-permute-start | bytes 196616 | tf_op jit(solution)/shard_map/ppermute | solution.py:249
  96.8 7.2 %all-to-all-done.3.parts_ref = bf16[16,144,128]{2,1,0:T(8,128)(2,1)S(1)} async-done(((bf16[16,144,128]{2,1,0:T(8,128)(2,1)}), bf16[16,144,128]{2,1,0:T(8,128)(2,1)S(1)}, u32[]{:S(2)}, u32[]{:S(2)}) %all-to-all-start.3) | async-done | bytes 589856 | tf_op jit(solution)/shard_map/all_to_all | solution.py:335
  104.0 0.1 tile.1.own_ref
  104.1 0.1 collective-permute-start.7
  104.2 3.1 %collective-permute-start.8 = (bf16[128,128]{1,0:T(8,128)(2,1)S(1)}, bf16[128,128]{1,0:T(8,128)(2,1)S(1)}, u32[]{:S(2)}, u32[]{:S(2)}) collective-permute-start(bf16[128,128]{1,0:T(8,128)(2,1)S(1)} %tile.1.own_ref), channel_id=1, source_target_pairs={{0,64},{32,96},{64,0},{96,32},{1,65},{33,97},{65,1},{97,33},{2,66}... | collective-permute-start | bytes 98312 | tf_op jit(solution)/shard_map/ppermute | solution.py:292
  107.3 0.2 collective-permute-start.9
  107.5 0.0 collective-permute-done.10.got_layer_ref
  107.5 0.7 collective-permute-done.7.near_ref
  108.2 0.8 collective-permute-done.8.mid_ref
  108.9 1.1 collective-permute-done.9.far_ref
  110.1 2.4 %send.1 = (bf16[32,2,128,128]{3,2,1,0:T(8,128)(2,1)S(1)}, bf16[256,256]{1,0:T(8,128)(2,1)}) custom-call(s32[3]{0:T(128)S(1)} %pad_add_fusion.place_ref, s32[128]{0:T(128)S(1)} %get-tuple-element.21.starts_ref, s32[128]{0:T(128)S(1)} %get-tuple-element.22.counts_ref, bf16[128,128]{1,0:T(8,128)(2,1)S(1)} %tile.1.own_ref, ...), custom_call_target="tpu_custom_call" | custom-call | tf_op jit(solution)/shard_map/send/pallas_call | solution.py:339
  112.5 37.1 %all_to_all.27 = bf16[32,2,128,128]{3,2,1,0:T(8,128)(2,1)S(1)} all-to-all(bf16[32,2,128,128]{3,2,1,0:T(8,128)(2,1)S(1)} %get-tuple-element.37), channel_id=1, replica_groups=mesh['ctx'=4,'tp'=32] {'tp'}, dimensions={0} | all-to-all | bytes 4194304 | tf_op jit(solution)/shard_map/all_to_all | solution.py:347
  149.6 1.9 %cache.1 = bf16[4,16,128,128]{3,2,1,0:T(8,128)(2,1)} custom-call(s32[3]{0:T(128)S(1)} %pad_add_fusion.place_ref, s32[128]{0:T(128)S(1)} %get-tuple-element.21.starts_ref, bf16[16,2,2,128,128]{4,3,2,1,0:T(8,128)(2,1)S(1)} %bitcast.16), custom_call_target="tpu_custom_call" | custom-call | tf_op jit(solution)/shard_map/cache/pallas_call | solution.py:348
  (19 shorter events, 0.1 us)
Async XLA Ops:
  0.6 34.0 %copy-start = (bf16[256,512]{1,0:T(8,128)(2,1)S(1)}, bf16[256,512]{1,0:T(8,128)(2,1)}, u32[]{:S(2)}) copy-start(bf16[256,512]{1,0:T(8,128)(2,1)} %conv_ref.5) | copy-start | bytes 786436
  0.6 12.5 %copy-start.8 = (f32[256]{0:T(256)S(1)}, f32[256]{0:T(256)}, u32[]{:S(2)}) copy-start(f32[256]{0:T(256)} %param.25) | copy-start | bytes 3076
  0.7 12.7 %copy-start.10 = (s32[128]{0:T(128)S(1)}, s32[128]{0:T(128)}, u32[]{:S(2)}) copy-start(s32[128]{0:T(128)} %param.27) | copy-start | bytes 1540
  0.7 12.7 %copy-start.11 = (s32[128]{0:T(128)S(1)}, s32[128]{0:T(128)}, u32[]{:S(2)}) copy-start(s32[128]{0:T(128)} %param.28) | copy-start | bytes 1540
  0.7 12.7 %copy-start.9 = (s32[128]{0:T(128)S(1)}, s32[128]{0:T(128)}, u32[]{:S(2)}) copy-start(s32[128]{0:T(128)} %param.29) | copy-start | bytes 1540
  0.7 34.0 %copy-start.6 = (f32[512]{0:T(512)S(1)}, f32[512]{0:T(512)}, u32[]{:S(2)}) copy-start(f32[512]{0:T(512)} %param.20) | copy-start | bytes 6148
  0.7 34.0 %copy-start.2 = (bf16[512,512]{1,0:T(8,128)(2,1)S(1)}, bf16[512,512]{1,0:T(8,128)(2,1)}, u32[]{:S(2)}) copy-start(bf16[512,512]{1,0:T(8,128)(2,1)} %weight_ref.3) | copy-start | bytes 1572868
  0.7 34.0 %copy-start.4 = (f32[16,512]{1,0:T(8,128)S(1)}, f32[16,512]{1,0:T(8,128)}, u32[]{:S(2)}) copy-start(f32[16,512]{1,0:T(8,128)} %alog_ref.3) | copy-start | bytes 98308
  0.7 20.8 %collective-permute-start.2 = (bf16[256,2048]{1,0:T(8,128)(2,1)}, bf16[256,2048]{1,0:T(8,128)(2,1)S(1)}, u32[]{:S(2)}, u32[]{:S(2)}) collective-permute-start(bf16[256,2048]{1,0:T(8,128)(2,1)} %own_weight_ref.1), channel_id=1, source_target_pairs={{0,1},{1,0},{2,3},{3,2},{4,5},{5,4},{6,7},{7,6},{8,9},{9,8},{10,11... | collective-permute-start | bytes 3145736 | tf_op jit(solution)/shard_map/ppermute | solution.py:249
  2.2 43.1 %copy-start.3 = (bf16[256,512]{1,0:T(8,128)(2,1)S(1)}, bf16[256,512]{1,0:T(8,128)(2,1)}, u32[]{:S(2)}) copy-start(bf16[256,512]{1,0:T(8,128)(2,1)} %gate_ref.1) | copy-start | bytes 786436
  2.2 43.1 %copy-start.5 = (f32[16,512]{1,0:T(8,128)S(1)}, f32[16,512]{1,0:T(8,128)}, u32[]{:S(2)}) copy-start(f32[16,512]{1,0:T(8,128)} %init_ref.1) | copy-start | bytes 98308
  2.2 43.1 %copy-start.7 = (f32[512]{0:T(512)S(1)}, f32[512]{0:T(512)}, u32[]{:S(2)}) copy-start(f32[512]{0:T(512)} %param.22) | copy-start | bytes 6148
  4.5 17.0 %all-to-all-start = ((bf16[32,8,544]{2,1,0:T(8,128)(2,1)}), bf16[32,8,544]{2,1,0:T(8,128)(2,1)S(1)}, u32[]{:S(2)}, u32[]{:S(2)}) async-start(bf16[32,8,544]{2,1,0:T(8,128)(2,1)} %bitcast.23), calls=%async_computation | async-start | bytes 655360 | tf_op jit(solution)/shard_map/all_to_all | solution.py:265
  12.8 1.5 collective-permute-start
  13.1 1.1 collective-permute-start.1
  37.1 5.9 %collective-permute-start.3 = (f32[24,512]{1,0:T(8,128)S(1)}, f32[24,512]{1,0:T(8,128)S(1)}, u32[]{:S(2)}, u32[]{:S(2)}) collective-permute-start(f32[24,512]{1,0:T(8,128)S(1)} %get-tuple-element.26), channel_id=1, source_target_pairs={{0,32},{32,64},{64,96},{96,0},{1,33},{33,65},{65,97},{97,1},{2,34}... | collective-permute-start | bytes 147464 | tf_op jit(solution)/shard_map/ppermute | solution.py:292
  38.8 6.3 %collective-permute-start.4 = (f32[24,512]{1,0:T(8,128)S(1)}, f32[24,512]{1,0:T(8,128)S(1)}, u32[]{:S(2)}, u32[]{:S(2)}) collective-permute-start(f32[24,512]{1,0:T(8,128)S(1)} %get-tuple-element.26), channel_id=1, source_target_pairs={{0,64},{32,96},{64,0},{96,32},{1,65},{33,97},{65,1},{97,33},{2,66}... | collective-permute-start | bytes 147464 | tf_op jit(solution)/shard_map/ppermute | solution.py:292
  42.1 3.2 %collective-permute-start.5 = (f32[24,512]{1,0:T(8,128)S(1)}, f32[24,512]{1,0:T(8,128)S(1)}, u32[]{:S(2)}, u32[]{:S(2)}) collective-permute-start(f32[24,512]{1,0:T(8,128)S(1)} %get-tuple-element.26), channel_id=1, source_target_pairs={{0,96},{32,0},{64,32},{96,64},{1,97},{33,1},{65,33},{97,65},{2,98}... | collective-permute-start | bytes 147464 | tf_op jit(solution)/shard_map/ppermute | solution.py:292
  52.1 5.4 %collective-permute-start.6 = (bf16[16,128,512]{2,1,0:T(8,128)(2,1)S(1)}, bf16[16,128,512]{2,1,0:T(8,128)(2,1)S(1)}, u32[]{:S(2)}, u32[]{:S(2)}) collective-permute-start(bf16[16,128,512]{2,1,0:T(8,128)(2,1)S(1)} %get-tuple-element.28), channel_id=1, source_target_pairs={{0,1},{1,0},{2,3},{3,2},{4,5},{5,4},{6,7},{7,6},{8,9},{9,8},{10,11... | collective-permute-start | bytes 6291464 | tf_op jit(solution)/shard_map/ppermute | solution.py:249
  58.2 30.4 %copy-start.1 = (bf16[256,2048]{1,0:T(8,128)(2,1)S(1)}, bf16[256,2048]{1,0:T(8,128)(2,1)}, u32[]{:S(2)}) copy-start(bf16[256,2048]{1,0:T(8,128)(2,1)} %own_weight_ref.1) | copy-start | bytes 3145732
  91.0 13.0 %all-to-all-start.3 = ((bf16[16,144,128]{2,1,0:T(8,128)(2,1)}), bf16[16,144,128]{2,1,0:T(8,128)(2,1)S(1)}, u32[]{:S(2)}, u32[]{:S(2)}) async-start(bf16[16,144,128]{2,1,0:T(8,128)(2,1)} %get-tuple-element.33), calls=%async_computation.3 | async-start | bytes 1179648 | tf_op jit(solution)/shard_map/all_to_all | solution.py:335
  94.8 12.6 %collective-permute-start.10 = (bf16[128,256]{1,0:T(8,128)(2,1)S(1)}, bf16[128,256]{1,0:T(8,128)(2,1)S(1)}, u32[]{:S(2)}, u32[]{:S(2)}) collective-permute-start(bf16[128,256]{1,0:T(8,128)(2,1)S(1)} %get-tuple-element.35), channel_id=1, source_target_pairs={{0,1},{1,0},{2,3},{3,2},{4,5},{5,4},{6,7},{7,6},{8,9},{9,8},{10,11... | collective-permute-start | bytes 196616 | tf_op jit(solution)/shard_map/ppermute | solution.py:249
  104.1 4.0 %collective-permute-start.7 = (bf16[128,128]{1,0:T(8,128)(2,1)S(1)}, bf16[128,128]{1,0:T(8,128)(2,1)S(1)}, u32[]{:S(2)}, u32[]{:S(2)}) collective-permute-start(bf16[128,128]{1,0:T(8,128)(2,1)S(1)} %tile.1.own_ref), channel_id=1, source_target_pairs={{0,32},{32,64},{64,96},{96,0},{1,33},{33,65},{65,97},{97,1},{2,34}... | collective-permute-start | bytes 98312 | tf_op jit(solution)/shard_map/ppermute | solution.py:292
  104.2 4.8 %collective-permute-start.8 = (bf16[128,128]{1,0:T(8,128)(2,1)S(1)}, bf16[128,128]{1,0:T(8,128)(2,1)S(1)}, u32[]{:S(2)}, u32[]{:S(2)}) collective-permute-start(bf16[128,128]{1,0:T(8,128)(2,1)S(1)} %tile.1.own_ref), channel_id=1, source_target_pairs={{0,64},{32,96},{64,0},{96,32},{1,65},{33,97},{65,1},{97,33},{2,66}... | collective-permute-start | bytes 98312 | tf_op jit(solution)/shard_map/ppermute | solution.py:292
  107.3 2.8 %collective-permute-start.9 = (bf16[128,128]{1,0:T(8,128)(2,1)S(1)}, bf16[128,128]{1,0:T(8,128)(2,1)S(1)}, u32[]{:S(2)}, u32[]{:S(2)}) collective-permute-start(bf16[128,128]{1,0:T(8,128)(2,1)S(1)} %tile.1.own_ref), channel_id=1, source_target_pairs={{0,96},{32,0},{64,32},{96,64},{1,97},{33,1},{65,33},{97,65},{2,98}... | collective-permute-start | bytes 98312 | tf_op jit(solution)/shard_map/ppermute | solution.py:292

commit v2 on v1

--- a/solution.py
+++ b/solution.py
@@ -16,6 +16,7 @@
 LOG2E = 1.4426950408889634
 CHUNK = 32
 PIECES = 8
+SIDE = 4
 BF = jnp.bfloat16
 F32 = jnp.float32
 
@@ -28,10 +29,20 @@
     return pltpu.CompilerParams(vmem_limit_bytes=mib * 1024 * 1024)
 
 
-def project_kernel(conv_ref, weight_ref, out_ref):
-    out_ref[...] = lax.dot_general(
-        conv_ref[...], weight_ref[...], (((1,), (1,)), ((), ())), preferred_element_type=F32
-    ).astype(BF)
+def project_kernel(place_ref, conv_ref, weight_ref, kept_ref, give_ref):
+    rows = kept_ref.shape[0]
+    for ref, half in ((give_ref, 1 - place_ref[1]), (kept_ref, place_ref[1])):
+        ref[...] = lax.dot_general(
+            conv_ref[pl.ds(pl.multiple_of(half * rows, rows), rows), :], weight_ref[...],
+            (((1,), (1,)), ((), ())), preferred_element_type=F32,
+        ).astype(ref.dtype)
+
+
+def add_kernel(*refs):
+    total = refs[0][...].astype(F32)
+    for ref in refs[1:-1]:
+        total = total + ref[...].astype(F32)
+    refs[-1][...] = total.astype(refs[-1].dtype)
 
 
 def advance_block(block, hidden, step_ref, drive_ref, states_ref, rates, read_out):
@@ -54,9 +65,12 @@
 
 
 def first_kernel(
-    proj_ref, weight_ref, bias_ref, alog_ref, conv_ref,
-    step_ref, states_ref, ends_ref, wide_ref, drive_ref,
+    place_ref, own_proj_ref, got_proj_ref, weight_ref, bias_ref, alog_ref, conv_ref,
+    step_ref, states_ref, ends_ref, proj_ref, wide_ref, drive_ref,
 ):
+    for ref, half in ((own_proj_ref, place_ref[1]), (got_proj_ref, 1 - place_ref[1])):
+        rows = ref.shape[0]
+        proj_ref[pl.ds(pl.multiple_of(half * rows, rows), rows), :] = ref[...]
     tokens = step_ref.shape[0]
     wide_ref[:, : 2 * STATE] = proj_ref[:, DTR:].astype(F32)
     flipped = jnp.transpose(wide_ref[...])
@@ -103,7 +117,7 @@
         (scan_ref[...] + skip_ref[...] * conv_ref[...].astype(F32)) * (gate / (1.0 + jnp.exp(-gate)))
     ).astype(BF).reshape(gated_ref.shape)
     kept_ref[...] = gated_ref[core]
-    through(gated_ref.at[1 - core], held_ref, copies, give_ref)
+    through(place_ref, 1 - core, gated_ref.at[1 - core], held_ref, copies, give_ref)
 
 
 def fetch(weight_ref, held_ref, sems):
@@ -120,26 +134,51 @@
     return copies
 
 
-def through(gated_ref, held_ref, copies, out_ref):
+def chip_order(place_ref, core, chip):
+    away_x = lax.rem(chip // SIDE - place_ref[3] + SIDE, SIDE)
+    away_y = lax.rem(chip % SIDE - place_ref[4] + SIDE, SIDE)
+    return jnp.where(core == 0, away_x, away_y), jnp.where(core == 0, away_y, away_x)
+
+
+def through(place_ref, core, gated_ref, held_ref, copies, out_ref):
     chips, _, wide = out_ref.shape
     for chip in range(chips):
         if chip % (chips // PIECES) == 0:
             copies[chip // (chips // PIECES)].wait()
-        out_ref[chip] = jnp.dot(
+        product = jnp.dot(
             gated_ref[...], held_ref[:, chip * wide : (chip + 1) * wide],
             preferred_element_type=F32,
         ).astype(BF)
-
-
-def keep_kernel(kept_ref, weight_ref, keep_ref, held_ref, sems):
-    through(kept_ref, held_ref, fetch(weight_ref, held_ref, sems), keep_ref)
+        far, near = chip_order(place_ref, core, chip)
+        out_ref[far * SIDE + near] = product
+
+
+def keep_kernel(place_ref, kept_ref, weight_ref, keep_ref, held_ref, sems):
+    copies = fetch(weight_ref, held_ref, sems)
+    through(place_ref, place_ref[1], kept_ref, held_ref, copies, keep_ref)
+
+
+def pair_kernel(keep_ref, got_ref, *out_refs):
+    for shift, ref in enumerate(out_refs):
+        rows = slice(shift * SIDE, (shift + 1) * SIDE)
+        ref[...] = (keep_ref[rows].astype(F32) + got_ref[rows].astype(F32)).astype(BF)
+
+
+def line_kernel(own_ref, one_ref, two_ref, three_ref, *out_refs):
+    for shift, ref in enumerate(out_refs):
+        total = own_ref[shift].astype(F32)
+        for other in (one_ref, two_ref, three_ref):
+            total = total + other[shift].astype(F32)
+        ref[...] = total.astype(ref.dtype)
 
 
 def layer_kernel(
-    place_ref, parts_ref, own_res_ref, got_res_ref, own_gain_ref, got_gain_ref,
-    own_weight_ref, got_weight_ref, own_ref, other_ref, out_ref,
+    place_ref, own_part_ref, one_ref, two_ref, three_ref, own_res_ref, got_res_ref, own_gain_ref, got_gain_ref,
+    own_weight_ref, got_weight_ref, own_ref, other_ref, *out_refs,
 ):
-    mixed = jnp.sum(parts_ref[...].astype(F32), axis=0)
+    mixed = own_part_ref[...]
+    for ref in (one_ref, two_ref, three_ref):
+        mixed = mixed + ref[...].astype(F32)
     half = mixed.shape[1] // 2
     first = place_ref[1] == 0
     left, right = mixed[:, :half], mixed[:, half:]
@@ -160,53 +199,78 @@
         )
     term, squares = term.astype(BF), squares.astype(BF)
     for j in range(2 * KVH):
-        out_ref[j, :BLK, :] = term[:, j * HEAD : (j + 1) * HEAD]
-        out_ref[j, BLK:, :] = squares
-
-
-def tile_kernel(parts_ref, tile_ref):
-    total = jnp.sum(parts_ref[...].astype(F32), axis=0)
-    scale = lax.rsqrt(total[BLK : BLK + 1, :] / D + EPS)
-    column = jnp.transpose(jnp.broadcast_to(scale, (BLK, BLK)))
-    tile_ref[...] = (total[:BLK, :] * column).astype(BF)
-
-
-def send_kernel(
-    place_ref, starts_ref, counts_ref, own_ref, near_ref, mid_ref, far_ref,
-    own_layer_ref, got_layer_ref, out_ref, layer_ref, held_ref,
+        far, _ = chip_order(place_ref, place_ref[1], j)
+        second = jnp.where(place_ref[1] == 0, j % SIDE, j // SIDE)
+        for shift, ref in enumerate(out_refs):
+
+            @pl.when(far == shift)
+            def _(ref=ref, second=second, j=j):
+                ref[second, :BLK, :] = term[:, j * HEAD : (j + 1) * HEAD]
+                ref[second, BLK:, :] = squares
+
+
+def tile_kernel(
+    place_ref, own_part_ref, one_ref, two_ref, three_ref, own_layer_ref, got_layer_ref,
+    tile_ref, layer_ref,
 ):
-    place, core = place_ref[0], place_ref[1]
-    for back, ref in enumerate((own_ref, near_ref, mid_ref, far_ref)):
-        held_ref[lax.rem(place + 4 - back, 4)] = ref[...]
-    for ref, half in ((own_layer_ref, core), (got_layer_ref, 1 - core)):
+    for ref, half in ((own_layer_ref, place_ref[1]), (got_layer_ref, 1 - place_ref[1])):
         rows = ref.shape[0]
         layer_ref[pl.ds(pl.multiple_of(half * rows, rows), rows), :] = ref[...]
-    targets = out_ref.shape[0]
-
-    def one(target, carry):
-        first, count = starts_ref[place * targets + target], counts_ref[place * targets + target]
-        slot = lax.rem(core + first, 2)
-        for k in range(2):
-            at = slot + 2 * k
-            holder = jnp.minimum((first + at) // 2, 3)
-            tile = held_ref[holder]
-            out_ref[target, k] = jnp.where(at < count, tile, jnp.zeros_like(tile))
-        return carry
-
-    lax.fori_loop(0, targets, one, 0)
-
-
-def cache_kernel(place_ref, starts_ref, arrived_ref, out_ref, sems):
-    odd = lax.rem(starts_ref[place_ref[2]], 2)
-    copies = []
-    for half in range(2):
-        slot = jnp.where(odd == 1, 1 - half, half)
-        for k in range(2):
-            copies.append(
-                pltpu.make_async_copy(
-                    arrived_ref.at[:, half, k], out_ref.at[slot + 2 * k], sems.at[half, k]
-                )
-            )
+    total = own_part_ref[...].astype(F32)
+    for ref in (one_ref, two_ref, three_ref):
+        total = total + ref[...].astype(F32)
+    scale = lax.rsqrt(total[0, BLK : BLK + 1, :] / D + EPS)
+    column = jnp.transpose(jnp.broadcast_to(scale, (BLK, BLK)))
+    tile_ref[...] = (total[:, :BLK, :] * column[None]).astype(BF)
+
+
+def choose(place_ref, target, starts_ref, counts_ref, sources, out_ref):
+    core = place_ref[1]
+    first, count = starts_ref[target], counts_ref[target]
+    slot = lax.rem(core + first, 2)
+    for far, ref in enumerate(sources):
+        first_axis = lax.rem(jnp.where(core == 0, place_ref[3], place_ref[4]) + SIDE - far, SIDE)
+        for second in range(SIDE):
+            column = jnp.where(core == 0, first_axis * SIDE + second, second * SIDE + first_axis)
+            for k in range(2):
+                at = slot + 2 * k
+                tile = ref[jnp.minimum((first + at) // 2, SIDE - 1), second]
+                out_ref[k, column] = jnp.where(at < count, tile, jnp.zeros_like(tile))
+
+
+def stack_kernel(place_ref, own_ref, near_ref, mid_ref, far_ref, out_ref):
+    for back, ref in enumerate((own_ref, near_ref, mid_ref, far_ref)):
+        out_ref[lax.rem(place_ref[0] + SIDE - back, SIDE)] = ref[...]
+
+
+def pick_kernel(place_ref, starts_ref, counts_ref, q0, q1, q2, q3, out_ref):
+    device = place_ref[2]
+    partner = device + 1 - 2 * place_ref[1]
+    choose(place_ref, partner, starts_ref, counts_ref, (q0, q1, q2, q3), out_ref)
+
+
+def slot_copies(place_ref, starts_ref, parity, source_ref, cache_ref, sems):
+    slot = lax.rem(parity + starts_ref[place_ref[2]], 2)
+    return [
+        pltpu.make_async_copy(source_ref.at[k], cache_ref.at[slot + 2 * k], sems.at[k])
+        for k in range(2)
+    ]
+
+
+def own_kernel(
+    place_ref, starts_ref, counts_ref, q0, q1, q2, q3, cache_ref, held_ref, sems
+):
+    core = place_ref[1]
+    choose(place_ref, place_ref[2], starts_ref, counts_ref, (q0, q1, q2, q3), held_ref)
+    copies = slot_copies(place_ref, starts_ref, core, held_ref, cache_ref, sems)
+    for copy in copies:
+        copy.start()
+    for copy in copies:
+        copy.wait()
+
+
+def rest_kernel(place_ref, starts_ref, got_ref, _, cache_ref, sems):
+    copies = slot_copies(place_ref, starts_ref, 1 - place_ref[1], got_ref, cache_ref, sems)
     for copy in copies:
         copy.start()
     for copy in copies:
@@ -242,8 +306,33 @@
     place = lax.axis_index("ctx")
     member = lax.axis_index("tp")
     core = member % 2
-    places = jnp.stack([place, core, place * tp_count + member]).astype(jnp.int32)
+    places = jnp.stack(
+        [
+            place, core, place * tp_count + member,
+            member // (2 * SIDE), (member // 2) % SIDE,
+        ]
+    ).astype(jnp.int32)
     partner = [(i, i ^ 1) for i in range(tp_count)]
+
+    def line(stage, value_of):
+        return [
+            lax.ppermute(
+                value_of(shift),
+                "tp",
+                [
+                    (
+                        (x * SIDE + y) * 2 + c,
+                        ((x + shift) % SIDE * SIDE + y) * 2 + c
+                        if c == stage
+                        else (x * SIDE + (y + shift) % SIDE) * 2 + c,
+                    )
+                    for x in range(SIDE)
+                    for y in range(SIDE)
+                    for c in range(2)
+                ],
+            )
+            for shift in range(1, SIDE)
+        ]
 
     def swap(value):
         return lax.ppermute(value, "tp", partner)
@@ -259,21 +348,28 @@
     counts = jnp.sum(jnp.where(matches, block_count[:, None], 0), axis=0)
     columns = DTR + 2 * STATE
 
-    part = pl.pallas_call(
-        project_kernel, out_shape=shape((tokens, columns), BF), name="project"
-    )(conv_out, xproj_weight.T)
-    shares = lax.all_to_all(
-        part.reshape(tp_count, tokens // tp_count, columns), "tp", 0, 0, tiled=True
-    )
-    shares, places, starts, counts, own_res, got_res, got_gain, got_weight = (
-        lax.optimization_barrier(
-            (shares, places, starts, counts, own_res, got_res, got_gain, got_weight)
-        )
-    )
-    mine = jnp.sum(shares.astype(F32), axis=0).astype(BF)
-    projected = lax.all_to_all(
-        jnp.broadcast_to(mine[None], (tp_count,) + mine.shape), "tp", 0, 0, tiled=True
-    ).reshape(tokens, columns)
+    def add(name, kind, *values):
+        return pl.pallas_call(
+            add_kernel,
+            out_shape=shape(values[0].shape, kind),
+            compiler_params=params(8),
+            name=name,
+        )(*values)
+
+    rows = (tokens // 2, columns)
+    kept_share, give_share = pl.pallas_call(
+        project_kernel,
+        in_specs=[SM] + [VM] * 2,
+        out_shape=(shape(rows, F32), shape(rows, BF)),
+        compiler_params=params(8),
+        name="project",
+    )(places, conv_out, xproj_weight.T)
+    chip = add("chip", BF, kept_share, swap(give_share))
+    row = add("row", BF, chip, *line(0, lambda shift: chip))
+    row, starts, counts, own_res, got_res, got_gain, got_weight = lax.optimization_barrier(
+        (row, starts, counts, own_res, got_res, got_gain, got_weight)
+    )
+    own_proj = add("plane", BF, row, *line(1, lambda shift: row))
 
     blocks = tokens // CHUNK
     step, states, ends = pl.pallas_call(
@@ -283,10 +379,15 @@
             shape((blocks, 2 * STATE, CHUNK), F32),
             shape((STATE + 8, chans), F32),
         ),
-        scratch_shapes=[pltpu.VMEM((tokens, 128), F32), pltpu.VMEM((tokens, chans), F32)],
+        in_specs=[SM] + [VM] * 6,
+        scratch_shapes=[
+            pltpu.VMEM((tokens, columns), BF),
+            pltpu.VMEM((tokens, 128), F32),
+            pltpu.VMEM((tokens, chans), F32),
+        ],
         compiler_params=params(8),
         name="first",
-    )(projected, dtproj_weight, dt_bias.reshape(1, chans), a_log, conv_out)
+    )(places, own_proj, swap(own_proj), dtproj_weight, dt_bias.reshape(1, chans), a_log, conv_out)
     def ranges_back(value):
         return [
             lax.ppermute(value, "ctx", [(z, (z + s) % ctx_count) for z in range(ctx_count)])
@@ -313,47 +414,78 @@
     got = swap(give)
     keep = pl.pallas_call(
         keep_kernel,
-        in_specs=[VM, ANY],
+        in_specs=[SM, VM, ANY],
         out_shape=shape(partial, BF),
         scratch_shapes=weight_scratch,
         compiler_params=params(46),
         name="keep",
-    )(kept, out_weight)
-    summed = (keep.astype(F32) + got.astype(F32)).astype(BF)
-    groups = [[2 * i + c for i in range(pairs)] for c in range(2)]
-    parts = lax.all_to_all(summed, "tp", 0, 0, axis_index_groups=groups, tiled=True)
+    )(places, kept, out_weight)
+    quarter = shape((SIDE, tokens // 2, 2 * feats), BF)
+    sums = pl.pallas_call(
+        pair_kernel, out_shape=(quarter,) * SIDE, compiler_params=params(12), name="pair"
+    )(keep, got)
+    row = (tokens // 2, 2 * feats)
+    parts = pl.pallas_call(
+        line_kernel,
+        out_shape=(shape(row, F32),) + (shape(row, BF),) * (SIDE - 1),
+        compiler_params=params(12),
+        name="line",
+    )(sums[0], *line(0, lambda shift: sums[shift]))
+    parts = [parts[0]] + line(1, lambda shift: parts[shift])
 
     block_shape = shape((tokens // 2, feats), BF)
-    own_layer, other_layer, kv_terms = pl.pallas_call(
+    own_layer, other_layer, *kv_terms = pl.pallas_call(
         layer_kernel,
-        in_specs=[SM] + [VM] * 7,
-        out_shape=(block_shape, block_shape, shape((pairs, BLK + 16, HEAD), BF)),
+        in_specs=[SM] + [VM] * 10,
+        out_shape=(block_shape,) * 2 + (shape((SIDE, BLK + 16, HEAD), BF),) * SIDE,
         compiler_params=params(8),
         name="layer",
-    )(places, parts, own_res, got_res, own_gain, got_gain, kv_weight, got_weight)
+    )(places, *parts, own_res, got_res, own_gain, got_gain, kv_weight, got_weight)
     got_layer = swap(other_layer)
-    kv_parts = lax.all_to_all(kv_terms, "tp", 0, 0, axis_index_groups=groups, tiled=True)
-    tile = pl.pallas_call(
-        tile_kernel, out_shape=shape((BLK, HEAD), BF), compiler_params=params(8), name="tile"
-    )(kv_parts)
-    outgoing, layer_out = pl.pallas_call(
-        send_kernel,
-        in_specs=[SM] * 3 + [VM] * 6,
-        out_shape=(shape((tp_count, 2, BLK, HEAD), BF), shape((tokens, feats), BF)),
-        scratch_shapes=[pltpu.VMEM((ctx_count, BLK, HEAD), BF)],
+    kv_row = add("kv", BF, kv_terms[0], *line(0, lambda shift: kv_terms[shift]))
+    tile, layer_out = pl.pallas_call(
+        tile_kernel,
+        in_specs=[SM] + [VM] * 6,
+        out_shape=(shape((SIDE, BLK, HEAD), BF), shape((tokens, feats), BF)),
         compiler_params=params(8),
-        name="send",
-    )(places, starts, counts, tile, *ranges_back(tile), own_layer, got_layer)
-    arrived = lax.all_to_all(outgoing, "tp", 0, 0, tiled=True)
+        name="tile",
+    )(places, kv_row, *line(1, lambda shift: kv_row), own_layer, got_layer)
+    stacked = pl.pallas_call(
+        stack_kernel,
+        in_specs=[SM] + [VM] * 4,
+        out_shape=shape((ctx_count, SIDE, BLK, HEAD), BF),
+        compiler_params=params(4),
+        name="stack",
+    )(places, tile, *ranges_back(tile))
+    everything = [stacked] + line(0, lambda shift: stacked)
+    half_cache = shape((2, 2 * KVH, BLK, HEAD), BF)
+    give_tiles = pl.pallas_call(
+        pick_kernel,
+        in_specs=[SM] * 3 + [VM] * SIDE,
+        out_shape=half_cache,
+        compiler_params=params(8),
+        name="pick",
+    )(places, starts, counts, *everything)
+    got_tiles = swap(give_tiles)
     kv_cache = pl.pallas_call(
-        cache_kernel,
-        in_specs=[SM] * 2 + [ANY],
+        own_kernel,
+        in_specs=[SM] * 3 + [VM] * SIDE,
         out_specs=ANY,
         out_shape=shape((CAP, 2 * KVH, BLK, HEAD), BF),
-        scratch_shapes=[pltpu.SemaphoreType.DMA((2, 2))],
+        scratch_shapes=[pltpu.VMEM(half_cache.shape, BF), pltpu.SemaphoreType.DMA((2,))],
         compiler_params=params(8),
-        name="cache",
-    )(places, starts, arrived.reshape(2 * KVH, 2, 2, BLK, HEAD))
+        name="own",
+    )(places, starts, counts, *everything)
+    kv_cache = pl.pallas_call(
+        rest_kernel,
+        in_specs=[SM] * 2 + [VM, ANY],
+        out_specs=ANY,
+        out_shape=shape((CAP, 2 * KVH, BLK, HEAD), BF),
+        input_output_aliases={3: 0},
+        scratch_shapes=[pltpu.SemaphoreType.DMA((2,))],
+        compiler_params=params(4),
+        name="rest",
+    )(places, starts, got_tiles, kv_cache)
     return (layer_out, kv_cache[None])
 
 

time: 152 us -> 132 us (0.87)
  blocking collectives: 80.6 us -> 0 us
  starting transfers between devices: 25.8 us -> 58.3 us
  waiting for transfers between devices: 20.3 us -> 44.5 us
  local copies, waits for them, and re-layouts: 0.97 us -> 3.01 us
  Pallas kernels: 22.1 us -> 23.8 us
    all_to_all x3 -> x0, blocking collectives: 80.6 us -> none  [the longest x1 37.1 us: per_device(): arrived = lax.all_to_all(outgoing, 'tp', 0, 0, tiled=True)]
    ppermute x0 -> x21, waiting for transfers between devices: none -> 34.5 us  [line(): lax.ppermute(value_of(shift), 'tp', [((x * SIDE + y) * 2 + c, ((x + shift...]
    ppermute x0 -> x21, starting transfers between devices: none -> 30.7 us  [line(): lax.ppermute(value_of(shift), 'tp', [((x * SIDE + y) * 2 + c, ((x + shift...]
    all_to_all x2 -> x0, waiting for transfers between devices: 14.5 us -> none  [the longest x1 7.27 us: per_device(): lax.all_to_all(part.reshape(tp_count, tokens // tp_count, columns), 'tp',...]
    ppermute x5 -> x8, starting transfers between devices: 5.5 us -> 18.5 us  [swap(): return lax.ppermute(value, 'tp', partner)]
    all_to_all x2 -> x0, starting transfers between devices: 11.2 us -> none  [the longest x1 7.34 us: per_device(): lax.all_to_all(part.reshape(tp_count, tokens // tp_count, columns), 'tp',...]
    ppermute x5 -> x8, waiting for transfers between devices: 0.66 us -> 3.77 us  [swap(): return lax.ppermute(value, 'tp', partner)]
    unnamed x24 -> x22, local copies, waits for them, and re-layouts: 0.05 us -> 2.04 us
  transfers between devices with their start and end apart: 13 -> 35, of which waited for: 9 -> 22; matrix products, arithmetic and copies ran while one was open for 1% -> 1% of each run, Pallas kernels for 4% -> 6%
where the time goes in v2:
time: 132 us; the launch traced here: 131 us
  starting transfers between devices  58.3 us (44%)
  waiting for transfers between devices  44.5 us (34%)
  Pallas kernels  23.8 us (18%)
  local copies, waits for them, and re-layouts  3.01 us (2%)
    ppermute x21, waiting for transfers between devices, line(): lax.ppermute(value_of(shift), 'tp', [((x * SIDE + y) * 2 + c, ((x + shift...  34.5 us
    ppermute x21, starting transfers between devices, line(): lax.ppermute(value_of(shift), 'tp', [((x * SIDE + y) * 2 + c, ((x + shift...  30.7 us
    ppermute x8, starting transfers between devices, swap(): return lax.ppermute(value, 'tp', partner)  18.5 us
    ppermute x6, starting transfers between devices, ranges_back(): lax.ppermute(value, 'ctx', [(z, (z + s) % ctx_count) for z in range(ctx_c...  9.05 us
    pallas_call x1, Pallas kernels, per_device(): pl.pallas_call(give_kernel, in_specs=[SM] + [VM] * 10 + [ANY], out_shape=...  6.72 us
    ppermute x6, waiting for transfers between devices, ranges_back(): lax.ppermute(value, 'ctx', [(z, (z + s) % ctx_count) for z in range(ctx_c...  6.2 us
    pallas_call x1, Pallas kernels, per_device(): pl.pallas_call(keep_kernel, in_specs=[SM, VM, ANY], out_shape=shape(parti...  4.39 us
    ppermute x8, waiting for transfers between devices, swap(): return lax.ppermute(value, 'tp', partner)  3.77 us
  transfers between devices with their start and end apart: 35, of which 22 were waited for; matrix products, arithmetic and copies ran while one was open for 1% of the time, Pallas kernels for 6%

profile of v2, /device:TPU:1, one launch (start us, length us, event | category | flops | bytes accessed | tf_op | source)
XLA Modules:
  0.0 131.4 jit_solution(14548792243113484754)
XLA Ops:
  0.6 1.5 %collective-permute-start.6 = (bf16[256,2048]{1,0:T(8,128)(2,1)}, bf16[256,2048]{1,0:T(8,128)(2,1)S(1)}, u32[]{:S(2)}, u32[]{:S(2)}) collective-permute-start(bf16[256,2048]{1,0:T(8,128)(2,1)} %own_weight_ref.1), channel_id=1, source_target_pairs={{0,1},{1,0},{2,3},{3,2},{4,5},{5,4},{6,7},{7,6},{8,9},{9,8},{10,11... | collective-permute-start | bytes 3145736 | tf_op jit(solution)/shard_map/ppermute | solution.py:338
  2.2 0.9 copy-done
  3.2 1.1 copy-done.3
  4.3 1.1 project.1
  5.5 1.3 %collective-permute-done.refs_1_ = bf16[128,544]{1,0:T(8,128)(2,1)S(1)} collective-permute-done((bf16[128,544]{1,0:T(8,128)(2,1)S(1)}, bf16[128,544]{1,0:T(8,128)(2,1)S(1)}, u32[]{:S(2)}, u32[]{:S(2)}) %collective-permute-start) | collective-permute-done | bytes 139296 | tf_op jit(solution)/shard_map/ppermute | solution.py:338
  6.9 1.4 %collective-permute-start.1 = (bf16[128,544]{1,0:T(8,128)(2,1)S(1)}, bf16[128,544]{1,0:T(8,128)(2,1)S(1)}, u32[]{:S(2)}, u32[]{:S(2)}) collective-permute-start(bf16[128,544]{1,0:T(8,128)(2,1)S(1)} %chip.1.refs_0_), channel_id=1, source_target_pairs={{0,8},{1,3},{2,10},{3,5},{4,12},{5,7},{6,14},{7,1},{8,16},{9,11},{... | collective-permute-start | bytes 417800 | tf_op jit(solution)/shard_map/ppermute | solution.py:319
  8.3 2.6 %collective-permute-start.2 = (bf16[128,544]{1,0:T(8,128)(2,1)S(1)}, bf16[128,544]{1,0:T(8,128)(2,1)S(1)}, u32[]{:S(2)}, u32[]{:S(2)}) collective-permute-start(bf16[128,544]{1,0:T(8,128)(2,1)S(1)} %chip.1.refs_0_), channel_id=1, source_target_pairs={{0,16},{1,5},{2,18},{3,7},{4,20},{5,1},{6,22},{7,3},{8,24},{9,13},... | collective-permute-start | bytes 417800 | tf_op jit(solution)/shard_map/ppermute | solution.py:319
  10.9 1.1 collective-permute-start.3
  14.7 1.0 collective-permute-done.2.refs_2_
  15.8 1.0 collective-permute-start.7
  16.8 2.4 %collective-permute-start.8 = (bf16[128,544]{1,0:T(8,128)(2,1)S(1)}, bf16[128,544]{1,0:T(8,128)(2,1)S(1)}, u32[]{:S(2)}, u32[]{:S(2)}) collective-permute-start(bf16[128,544]{1,0:T(8,128)(2,1)S(1)} %row.1.refs_0_), channel_id=1, source_target_pairs={{0,4},{1,17},{2,6},{3,19},{4,0},{5,21},{6,2},{7,23},{8,12},{9,25},... | collective-permute-start | bytes 417800 | tf_op jit(solution)/shard_map/ppermute | solution.py:319
  19.2 1.2 collective-permute-start.9
  20.4 1.1 collective-permute-done.7.refs_1_
  21.6 2.1 %collective-permute-done.8.refs_2_ = bf16[128,544]{1,0:T(8,128)(2,1)S(1)} collective-permute-done((bf16[128,544]{1,0:T(8,128)(2,1)S(1)}, bf16[128,544]{1,0:T(8,128)(2,1)S(1)}, u32[]{:S(2)}, u32[]{:S(2)}) %collective-permute-start.8) | collective-permute-done | bytes 139296 | tf_op jit(solution)/shard_map/ppermute | solution.py:319
  23.8 3.1 %collective-permute-start.10 = (bf16[128,544]{1,0:T(8,128)(2,1)S(1)}, bf16[128,544]{1,0:T(8,128)(2,1)S(1)}, u32[]{:S(2)}, u32[]{:S(2)}) collective-permute-start(bf16[128,544]{1,0:T(8,128)(2,1)S(1)} %plane.1.own_proj_ref), channel_id=1, source_target_pairs={{0,1},{1,0},{2,3},{3,2},{4,5},{5,4},{6,7},{7,6},{8,9},{9,8},{10,11... | collective-permute-start | bytes 417800 | tf_op jit(solution)/shard_map/ppermute | solution.py:338
  26.9 1.0 collective-permute-done.10.got_proj_ref
  27.9 2.9 %first.1 = (f32[256,512]{1,0:T(8,128)S(1)}, f32[8,32,32]{2,1,0:T(8,128)S(1)}, f32[24,512]{1,0:T(8,128)S(1)}) custom-call(s32[5]{0:T(128)S(1)} %stack.24.place_ref, bf16[128,544]{1,0:T(8,128)(2,1)S(1)} %plane.1.own_proj_ref, bf16[128,544]{1,0:T(8,128)(2,1)S(1)} %collective-permute-done.10.got_proj_ref, bf16[512,512]{1,0:T(8,128)(2,1)S(1)} %copy-done.4, ...), custom_call_target="tpu_custom_call" | custom-call | tf_op jit(solution)/shard_map/first/pallas_call | solution.py:375
  30.8 1.7 %collective-permute-start.11 = (f32[24,512]{1,0:T(8,128)S(1)}, f32[24,512]{1,0:T(8,128)S(1)}, u32[]{:S(2)}, u32[]{:S(2)}) collective-permute-start(f32[24,512]{1,0:T(8,128)S(1)} %get-tuple-element.37), channel_id=1, source_target_pairs={{0,32},{32,64},{64,96},{96,0},{1,33},{33,65},{65,97},{97,1},{2,34}... | collective-permute-start | bytes 147464 | tf_op jit(solution)/shard_map/ppermute | solution.py:393
  32.5 3.3 %collective-permute-start.12 = (f32[24,512]{1,0:T(8,128)S(1)}, f32[24,512]{1,0:T(8,128)S(1)}, u32[]{:S(2)}, u32[]{:S(2)}) collective-permute-start(f32[24,512]{1,0:T(8,128)S(1)} %get-tuple-element.37), channel_id=1, source_target_pairs={{0,64},{32,96},{64,0},{96,32},{1,65},{33,97},{65,1},{97,33},{2,66}... | collective-permute-start | bytes 147464 | tf_op jit(solution)/shard_map/ppermute | solution.py:393
  36.5 1.5 %collective-permute-done.12.mid_ref = f32[24,512]{1,0:T(8,128)S(1)} collective-permute-done((f32[24,512]{1,0:T(8,128)S(1)}, f32[24,512]{1,0:T(8,128)S(1)}, u32[]{:S(2)}, u32[]{:S(2)}) %collective-permute-start.12) | collective-permute-done | bytes 49184 | tf_op jit(solution)/shard_map/ppermute | solution.py:393
  38.0 1.0 collective-permute-done.13.far_ref
  39.0 6.7 %give.1 = (bf16[16,128,512]{2,1,0:T(8,128)(2,1)S(1)}, bf16[128,512]{1,0:T(8,128)(2,1)S(1)}) custom-call(s32[5]{0:T(128)S(1)} %stack.24.place_ref, f32[256,512]{1,0:T(8,128)S(1)} %get-tuple-element.35.step_ref, f32[8,32,32]{2,1,0:T(8,128)S(1)} %get-tuple-element.36.states_ref, f32[16,512]{1,0:T(8,128)S(1)} %copy-done.6, bf16[256,512]{1,0:T(8,128)(2,1)S(1)} %copy-done.1, ...), custom_call_target="tpu_custom_call" | custom-call | tf_op jit(solution)/shard_map/give/pallas_call | solution.py:399
  45.8 1.9 %collective-permute-start.14 = (bf16[16,128,512]{2,1,0:T(8,128)(2,1)S(1)}, bf16[16,128,512]{2,1,0:T(8,128)(2,1)S(1)}, u32[]{:S(2)}, u32[]{:S(2)}) collective-permute-start(bf16[16,128,512]{2,1,0:T(8,128)(2,1)S(1)} %get-tuple-element.39), channel_id=1, source_target_pairs={{0,1},{1,0},{2,3},{3,2},{4,5},{5,4},{6,7},{7,6},{8,9},{9,8},{10,11... | collective-permute-start | bytes 6291464 | tf_op jit(solution)/shard_map/ppermute | solution.py:338
  47.6 4.4 %keep.1.keep_ref = bf16[16,128,512]{2,1,0:T(8,128)(2,1)S(1)} custom-call(s32[5]{0:T(128)S(1)} %stack.24.place_ref, bf16[128,512]{1,0:T(8,128)(2,1)S(1)} %get-tuple-element.38.kept_ref, bf16[512,8192]{1,0:T(8,128)(2,1)} %weight_ref.5), custom_call_target="tpu_custom_call" | custom-call | tf_op jit(solution)/shard_map/keep/pallas_call | solution.py:415
  52.5 1.2 collective-permute-start.15
  53.7 2.4 %collective-permute-start.16 = (bf16[4,128,512]{2,1,0:T(8,128)(2,1)S(1)}, bf16[4,128,512]{2,1,0:T(8,128)(2,1)S(1)}, u32[]{:S(2)}, u32[]{:S(2)}) collective-permute-start(bf16[4,128,512]{2,1,0:T(8,128)(2,1)S(1)} %get-tuple-element.42), channel_id=1, source_target_pairs={{0,16},{1,5},{2,18},{3,7},{4,20},{5,1},{6,22},{7,3},{8,24},{9,13},... | collective-permute-start | bytes 1572872 | tf_op jit(solution)/shard_map/ppermute | solution.py:319
  57.0 5.2 %collective-permute-done.15.one_ref = bf16[4,128,512]{2,1,0:T(8,128)(2,1)S(1)} collective-permute-done((bf16[4,128,512]{2,1,0:T(8,128)(2,1)S(1)}, bf16[4,128,512]{2,1,0:T(8,128)(2,1)S(1)}, u32[]{:S(2)}, u32[]{:S(2)}) %collective-permute-start.15) | collective-permute-done | bytes 524320 | tf_op jit(solution)/shard_map/ppermute | solution.py:319
  62.1 6.4 %collective-permute-done.16.two_ref = bf16[4,128,512]{2,1,0:T(8,128)(2,1)S(1)} collective-permute-done((bf16[4,128,512]{2,1,0:T(8,128)(2,1)S(1)}, bf16[4,128,512]{2,1,0:T(8,128)(2,1)S(1)}, u32[]{:S(2)}, u32[]{:S(2)}) %collective-permute-start.16) | collective-permute-done | bytes 524320 | tf_op jit(solution)/shard_map/ppermute | solution.py:319
  68.8 1.2 collective-permute-start.18
  70.1 2.2 %collective-permute-start.19 = (bf16[128,512]{1,0:T(8,128)(2,1)S(1)}, bf16[128,512]{1,0:T(8,128)(2,1)S(1)}, u32[]{:S(2)}, u32[]{:S(2)}) collective-permute-start(bf16[128,512]{1,0:T(8,128)(2,1)S(1)} %get-tuple-element.46), channel_id=1, source_target_pairs={{0,4},{1,17},{2,6},{3,19},{4,0},{5,21},{6,2},{7,23},{8,12},{9,25},... | collective-permute-start | bytes 393224 | tf_op jit(solution)/shard_map/ppermute | solution.py:319
  73.9 2.1 %collective-permute-done.19.two_ref = bf16[128,512]{1,0:T(8,128)(2,1)S(1)} collective-permute-done((bf16[128,512]{1,0:T(8,128)(2,1)S(1)}, bf16[128,512]{1,0:T(8,128)(2,1)S(1)}, u32[]{:S(2)}, u32[]{:S(2)}) %collective-permute-start.19) | collective-permute-done | bytes 131104 | tf_op jit(solution)/shard_map/ppermute | solution.py:319
  76.1 1.7 %layer.1 = (bf16[128,256]{1,0:T(8,128)(2,1)S(1)}, bf16[128,256]{1,0:T(8,128)(2,1)S(1)}, bf16[4,144,128]{2,1,0:T(8,128)(2,1)S(1)}, bf16[4,144,128]{2,1,0:T(8,128)...) custom-call(s32[5]{0:T(128)S(1)} %stack.24.place_ref, ...), custom_call_target="tpu_custom_call" | custom-call | tf_op jit(solution)/shard_map/layer/pallas_call | solution.py:437
  77.8 1.8 %collective-permute-start.21 = (bf16[4,144,128]{2,1,0:T(8,128)(2,1)S(1)}, bf16[4,144,128]{2,1,0:T(8,128)(2,1)S(1)}, u32[]{:S(2)}, u32[]{:S(2)}) collective-permute-start(bf16[4,144,128]{2,1,0:T(8,128)(2,1)S(1)} %get-tuple-element.53), channel_id=1, source_target_pairs={{0,8},{1,3},{2,10},{3,5},{4,12},{5,7},{6,14},{7,1},{8,16},{9,11},{... | collective-permute-start | bytes 442376 | tf_op jit(solution)/shard_map/ppermute | solution.py:319
  79.6 2.1 %collective-permute-start.22 = (bf16[4,144,128]{2,1,0:T(8,128)(2,1)S(1)}, bf16[4,144,128]{2,1,0:T(8,128)(2,1)S(1)}, u32[]{:S(2)}, u32[]{:S(2)}) collective-permute-start(bf16[4,144,128]{2,1,0:T(8,128)(2,1)S(1)} %get-tuple-element.54), channel_id=1, source_target_pairs={{0,16},{1,5},{2,18},{3,7},{4,20},{5,1},{6,22},{7,3},{8,24},{9,13},... | collective-permute-start | bytes 442376 | tf_op jit(solution)/shard_map/ppermute | solution.py:319
  83.1 2.7 %collective-permute-done.22.refs_2_ = bf16[4,144,128]{2,1,0:T(8,128)(2,1)S(1)} collective-permute-done((bf16[4,144,128]{2,1,0:T(8,128)(2,1)S(1)}, bf16[4,144,128]{2,1,0:T(8,128)(2,1)S(1)}, u32[]{:S(2)}, u32[]{:S(2)}) %collective-permute-start.22) | collective-permute-done | bytes 147488 | tf_op jit(solution)/shard_map/ppermute | solution.py:319
  86.1 1.2 collective-permute-start.24
  87.3 1.9 %collective-permute-start.25 = (bf16[4,144,128]{2,1,0:T(8,128)(2,1)S(1)}, bf16[4,144,128]{2,1,0:T(8,128)(2,1)S(1)}, u32[]{:S(2)}, u32[]{:S(2)}) collective-permute-start(bf16[4,144,128]{2,1,0:T(8,128)(2,1)S(1)} %kv.1.own_part_ref), channel_id=1, source_target_pairs={{0,4},{1,17},{2,6},{3,19},{4,0},{5,21},{6,2},{7,23},{8,12},{9,25},... | collective-permute-start | bytes 442376 | tf_op jit(solution)/shard_map/ppermute | solution.py:319
  90.0 4.7 %collective-permute-start.27 = (bf16[128,256]{1,0:T(8,128)(2,1)S(1)}, bf16[128,256]{1,0:T(8,128)(2,1)S(1)}, u32[]{:S(2)}, u32[]{:S(2)}) collective-permute-start(bf16[128,256]{1,0:T(8,128)(2,1)S(1)} %get-tuple-element.57), channel_id=1, source_target_pairs={{0,1},{1,0},{2,3},{3,2},{4,5},{5,4},{6,7},{7,6},{8,9},{9,8},{10,11... | collective-permute-start | bytes 196616 | tf_op jit(solution)/shard_map/ppermute | solution.py:338
  95.6 1.2 tile.1
  96.9 3.1 %collective-permute-start.29 = (bf16[4,128,128]{2,1,0:T(8,128)(2,1)S(1)}, bf16[4,128,128]{2,1,0:T(8,128)(2,1)S(1)}, u32[]{:S(2)}, u32[]{:S(2)}) collective-permute-start(bf16[4,128,128]{2,1,0:T(8,128)(2,1)S(1)} %get-tuple-element.61.own_ref), channel_id=1, source_target_pairs={{0,64},{32,96},{64,0},{96,32},{1,65},{33,97},{65,1},{97,33},{2,66}... | collective-permute-start | bytes 393224 | tf_op jit(solution)/shard_map/ppermute | solution.py:393
  100.2 1.7 %collective-permute-done.28.near_ref = bf16[4,128,128]{2,1,0:T(8,128)(2,1)S(1)} collective-permute-done((bf16[4,128,128]{2,1,0:T(8,128)(2,1)S(1)}, bf16[4,128,128]{2,1,0:T(8,128)(2,1)S(1)}, u32[]{:S(2)}, u32[]{:S(2)}) %collective-permute-start.28) | collective-permute-done | bytes 131104 | tf_op jit(solution)/shard_map/ppermute | solution.py:393
  101.9 1.8 %collective-permute-done.29.mid_ref = bf16[4,128,128]{2,1,0:T(8,128)(2,1)S(1)} collective-permute-done((bf16[4,128,128]{2,1,0:T(8,128)(2,1)S(1)}, bf16[4,128,128]{2,1,0:T(8,128)(2,1)S(1)}, u32[]{:S(2)}, u32[]{:S(2)}) %collective-permute-start.29) | collective-permute-done | bytes 131104 | tf_op jit(solution)/shard_map/ppermute | solution.py:393
  104.5 1.0 collective-permute-start.31
  106.3 1.7 %collective-permute-start.33 = (bf16[4,4,128,128]{3,2,1,0:T(8,128)(2,1)S(1)}, bf16[4,4,128,128]{3,2,1,0:T(8,128)(2,1)S(1)}, u32[]{:S(2)}, u32[]{:S(2)}) collective-permute-start(bf16[4,4,128,128]{3,2,1,0:T(8,128)(2,1)S(1)} %stack.25.q0), channel_id=1, source_target_pairs={{0,24},{1,7},{2,26},{3,1},{4,28},{5,3},{6,30},{7,5},{8,0},{9,15},{... | collective-permute-start | bytes 1572872 | tf_op jit(solution)/shard_map/ppermute | solution.py:319
  108.0 11.6 %collective-permute-done.31.q1 = bf16[4,4,128,128]{3,2,1,0:T(8,128)(2,1)S(1)} collective-permute-done((bf16[4,4,128,128]{3,2,1,0:T(8,128)(2,1)S(1)}, bf16[4,4,128,128]{3,2,1,0:T(8,128)(2,1)S(1)}, u32[]{:S(2)}, u32[]{:S(2)}) %collective-permute-start.31) | collective-permute-done | bytes 524320 | tf_op jit(solution)/shard_map/ppermute | solution.py:319
  121.1 6.3 %collective-permute-start.34 = (bf16[2,16,128,128]{3,2,1,0:T(8,128)(2,1)S(1)}, bf16[2,16,128,128]{3,2,1,0:T(8,128)(2,1)S(1)}, u32[]{:S(2)}, u32[]{:S(2)}) collective-permute-start(bf16[2,16,128,128]{3,2,1,0:T(8,128)(2,1)S(1)} %pick.1), channel_id=1, source_target_pairs={{0,1},{1,0},{2,3},{3,2},{4,5},{5,4},{6,7},{7,6},{8,9},{9,8},{10,11... | collective-permute-start | bytes 3145736 | tf_op jit(solution)/shard_map/ppermute | solution.py:338
  127.4 1.8 %own.1._ = bf16[4,16,128,128]{3,2,1,0:T(8,128)(2,1)} custom-call(s32[5]{0:T(128)S(1)} %stack.24.place_ref, s32[128]{0:T(128)S(1)} %get-tuple-element.59.starts_ref, s32[128]{0:T(128)S(1)} %get-tuple-element.60.counts_ref, bf16[4,4,128,128]{3,2,1,0:T(8,128)(2,1)S(1)} %stack.25.q0, bf16[4,4,128,128]{3,2,1,0:T(8,128)(2,1)S(1)} %collective-permute-done.31.q1, ...), custom_call_target="tpu_custom_call" | custom-call | tf_op jit(solution)/shard_map/own/pallas_call | solution.py:470
  129.7 1.5 %rest.1 = bf16[4,16,128,128]{3,2,1,0:T(8,128)(2,1)} custom-call(s32[5]{0:T(128)S(1)} %stack.24.place_ref, s32[128]{0:T(128)S(1)} %get-tuple-element.59.starts_ref, bf16[2,16,128,128]{3,2,1,0:T(8,128)(2,1)S(1)} %collective-permute-done.34.got_ref, bf16[4,16,128,128]{3,2,1,0:T(8,128)(2,1)} %own.1._), custom_call_target="tpu_custom_call", output_to_operand_aliasing={{}: (3, {})} | custom-call | tf_op jit(solution)/shard_map/rest/pallas_call | solution.py:479
  (63 shorter events, 14.4 us)
Async XLA Ops:
  0.6 27.3 %copy-start.8 = (f32[512]{0:T(512)S(1)}, f32[512]{0:T(512)}, u32[]{:S(2)}) copy-start(f32[512]{0:T(512)} %param.20) | copy-start | bytes 6148
  0.6 27.2 %copy-start.6 = (f32[16,512]{1,0:T(8,128)S(1)}, f32[16,512]{1,0:T(8,128)}, u32[]{:S(2)}) copy-start(f32[16,512]{1,0:T(8,128)} %alog_ref.3) | copy-start | bytes 98308
  0.6 15.2 %collective-permute-start.6 = (bf16[256,2048]{1,0:T(8,128)(2,1)}, bf16[256,2048]{1,0:T(8,128)(2,1)S(1)}, u32[]{:S(2)}, u32[]{:S(2)}) collective-permute-start(bf16[256,2048]{1,0:T(8,128)(2,1)} %own_weight_ref.1), channel_id=1, source_target_pairs={{0,1},{1,0},{2,3},{3,2},{4,5},{5,4},{6,7},{7,6},{8,9},{9,8},{10,11... | collective-permute-start | bytes 3145736 | tf_op jit(solution)/shard_map/ppermute | solution.py:338
  2.2 1.0 copy-start
  3.2 1.1 copy-start.3
  4.2 23.7 %copy-start.1 = (bf16[256,512]{1,0:T(8,128)(2,1)S(1)}, bf16[256,512]{1,0:T(8,128)(2,1)}, u32[]{:S(2)}) copy-start(bf16[256,512]{1,0:T(8,128)(2,1)} %conv_ref.5) | copy-start | bytes 786436
  4.2 23.7 %copy-start.4 = (bf16[512,512]{1,0:T(8,128)(2,1)S(1)}, bf16[512,512]{1,0:T(8,128)(2,1)}, u32[]{:S(2)}) copy-start(bf16[512,512]{1,0:T(8,128)(2,1)} %weight_ref.3) | copy-start | bytes 1572868
  4.2 34.8 %copy-start.5 = (bf16[256,512]{1,0:T(8,128)(2,1)S(1)}, bf16[256,512]{1,0:T(8,128)(2,1)}, u32[]{:S(2)}) copy-start(bf16[256,512]{1,0:T(8,128)(2,1)} %gate_ref.1) | copy-start | bytes 786436
  4.2 34.8 %copy-start.7 = (f32[16,512]{1,0:T(8,128)S(1)}, f32[16,512]{1,0:T(8,128)}, u32[]{:S(2)}) copy-start(f32[16,512]{1,0:T(8,128)} %init_ref.1) | copy-start | bytes 98308
  4.3 34.8 %copy-start.9 = (f32[512]{0:T(512)S(1)}, f32[512]{0:T(512)}, u32[]{:S(2)}) copy-start(f32[512]{0:T(512)} %param.22) | copy-start | bytes 6148
  5.3 1.5 %collective-permute-start = (bf16[128,544]{1,0:T(8,128)(2,1)S(1)}, bf16[128,544]{1,0:T(8,128)(2,1)S(1)}, u32[]{:S(2)}, u32[]{:S(2)}) collective-permute-start(bf16[128,544]{1,0:T(8,128)(2,1)S(1)} %get-tuple-element.33), channel_id=1, source_target_pairs={{0,1},{1,0},{2,3},{3,2},{4,5},{5,4},{6,7},{7,6},{8,9},{9,8},{10,11... | collective-permute-start | bytes 417800 | tf_op jit(solution)/shard_map/ppermute | solution.py:338
  6.9 6.9 %collective-permute-start.1 = (bf16[128,544]{1,0:T(8,128)(2,1)S(1)}, bf16[128,544]{1,0:T(8,128)(2,1)S(1)}, u32[]{:S(2)}, u32[]{:S(2)}) collective-permute-start(bf16[128,544]{1,0:T(8,128)(2,1)S(1)} %chip.1.refs_0_), channel_id=1, source_target_pairs={{0,8},{1,3},{2,10},{3,5},{4,12},{5,7},{6,14},{7,1},{8,16},{9,11},{... | collective-permute-start | bytes 417800 | tf_op jit(solution)/shard_map/ppermute | solution.py:319
  8.3 7.4 %collective-permute-start.2 = (bf16[128,544]{1,0:T(8,128)(2,1)S(1)}, bf16[128,544]{1,0:T(8,128)(2,1)S(1)}, u32[]{:S(2)}, u32[]{:S(2)}) collective-permute-start(bf16[128,544]{1,0:T(8,128)(2,1)S(1)} %chip.1.refs_0_), channel_id=1, source_target_pairs={{0,16},{1,5},{2,18},{3,7},{4,20},{5,1},{6,22},{7,3},{8,24},{9,13},... | collective-permute-start | bytes 417800 | tf_op jit(solution)/shard_map/ppermute | solution.py:319
  10.9 4.8 %collective-permute-start.3 = (bf16[128,544]{1,0:T(8,128)(2,1)S(1)}, bf16[128,544]{1,0:T(8,128)(2,1)S(1)}, u32[]{:S(2)}, u32[]{:S(2)}) collective-permute-start(bf16[128,544]{1,0:T(8,128)(2,1)S(1)} %chip.1.refs_0_), channel_id=1, source_target_pairs={{0,24},{1,7},{2,26},{3,1},{4,28},{5,3},{6,30},{7,5},{8,0},{9,15},{... | collective-permute-start | bytes 417800 | tf_op jit(solution)/shard_map/ppermute | solution.py:319
  12.9 2.9 %collective-permute-start.4 = (bf16[128,256]{1,0:T(8,128)(2,1)S(1)}, bf16[128,256]{1,0:T(8,128)(2,1)S(1)}, u32[]{:S(2)}, u32[]{:S(2)}) collective-permute-start(bf16[128,256]{1,0:T(8,128)(2,1)S(1)} %get-tuple-element.64), channel_id=1, source_target_pairs={{0,1},{1,0},{2,3},{3,2},{4,5},{5,4},{6,7},{7,6},{8,9},{9,8},{10,11... | collective-permute-start | bytes 196616 | tf_op jit(solution)/shard_map/ppermute | solution.py:338
  13.8 2.0 %collective-permute-start.5 = (f32[1,256]{1,0:T(1,128)}, f32[1,256]{1,0:T(1,128)S(1)}, u32[]{:S(2)}, u32[]{:S(2)}) collective-permute-start(f32[1,256]{1,0:T(1,128)} %bitcast.18), channel_id=1, source_target_pairs={{0,1},{1,0},{2,3},{3,2},{4,5},{5,4},{6,7},{7,6},{8,9},{9,8},{10,11... | collective-permute-start | bytes 3080 | tf_op jit(solution)/shard_map/ppermute | solution.py:338
  15.8 5.7 %collective-permute-start.7 = (bf16[128,544]{1,0:T(8,128)(2,1)S(1)}, bf16[128,544]{1,0:T(8,128)(2,1)S(1)}, u32[]{:S(2)}, u32[]{:S(2)}) collective-permute-start(bf16[128,544]{1,0:T(8,128)(2,1)S(1)} %row.1.refs_0_), channel_id=1, source_target_pairs={{0,2},{1,9},{2,4},{3,11},{4,6},{5,13},{6,0},{7,15},{8,10},{9,17},{... | collective-permute-start | bytes 417800 | tf_op jit(solution)/shard_map/ppermute | solution.py:319
  16.8 6.9 %collective-permute-start.8 = (bf16[128,544]{1,0:T(8,128)(2,1)S(1)}, bf16[128,544]{1,0:T(8,128)(2,1)S(1)}, u32[]{:S(2)}, u32[]{:S(2)}) collective-permute-start(bf16[128,544]{1,0:T(8,128)(2,1)S(1)} %row.1.refs_0_), channel_id=1, source_target_pairs={{0,4},{1,17},{2,6},{3,19},{4,0},{5,21},{6,2},{7,23},{8,12},{9,25},... | collective-permute-start | bytes 417800 | tf_op jit(solution)/shard_map/ppermute | solution.py:319
  19.2 4.5 %collective-permute-start.9 = (bf16[128,544]{1,0:T(8,128)(2,1)S(1)}, bf16[128,544]{1,0:T(8,128)(2,1)S(1)}, u32[]{:S(2)}, u32[]{:S(2)}) collective-permute-start(bf16[128,544]{1,0:T(8,128)(2,1)S(1)} %row.1.refs_0_), channel_id=1, source_target_pairs={{0,6},{1,25},{2,0},{3,27},{4,2},{5,29},{6,4},{7,31},{8,14},{9,1},{... | collective-permute-start | bytes 417800 | tf_op jit(solution)/shard_map/ppermute | solution.py:319
  23.8 4.1 %collective-permute-start.10 = (bf16[128,544]{1,0:T(8,128)(2,1)S(1)}, bf16[128,544]{1,0:T(8,128)(2,1)S(1)}, u32[]{:S(2)}, u32[]{:S(2)}) collective-permute-start(bf16[128,544]{1,0:T(8,128)(2,1)S(1)} %plane.1.own_proj_ref), channel_id=1, source_target_pairs={{0,1},{1,0},{2,3},{3,2},{4,5},{5,4},{6,7},{7,6},{8,9},{9,8},{10,11... | collective-permute-start | bytes 417800 | tf_op jit(solution)/shard_map/ppermute | solution.py:338
  30.8 5.7 %collective-permute-start.11 = (f32[24,512]{1,0:T(8,128)S(1)}, f32[24,512]{1,0:T(8,128)S(1)}, u32[]{:S(2)}, u32[]{:S(2)}) collective-permute-start(f32[24,512]{1,0:T(8,128)S(1)} %get-tuple-element.37), channel_id=1, source_target_pairs={{0,32},{32,64},{64,96},{96,0},{1,33},{33,65},{65,97},{97,1},{2,34}... | collective-permute-start | bytes 147464 | tf_op jit(solution)/shard_map/ppermute | solution.py:393
  32.5 5.5 %collective-permute-start.12 = (f32[24,512]{1,0:T(8,128)S(1)}, f32[24,512]{1,0:T(8,128)S(1)}, u32[]{:S(2)}, u32[]{:S(2)}) collective-permute-start(f32[24,512]{1,0:T(8,128)S(1)} %get-tuple-element.37), channel_id=1, source_target_pairs={{0,64},{32,96},{64,0},{96,32},{1,65},{33,97},{65,1},{97,33},{2,66}... | collective-permute-start | bytes 147464 | tf_op jit(solution)/shard_map/ppermute | solution.py:393
  35.8 3.2 %collective-permute-start.13 = (f32[24,512]{1,0:T(8,128)S(1)}, f32[24,512]{1,0:T(8,128)S(1)}, u32[]{:S(2)}, u32[]{:S(2)}) collective-permute-start(f32[24,512]{1,0:T(8,128)S(1)} %get-tuple-element.37), channel_id=1, source_target_pairs={{0,96},{32,0},{64,32},{96,64},{1,97},{33,1},{65,33},{97,65},{2,98}... | collective-permute-start | bytes 147464 | tf_op jit(solution)/shard_map/ppermute | solution.py:393
  45.8 6.3 %collective-permute-start.14 = (bf16[16,128,512]{2,1,0:T(8,128)(2,1)S(1)}, bf16[16,128,512]{2,1,0:T(8,128)(2,1)S(1)}, u32[]{:S(2)}, u32[]{:S(2)}) collective-permute-start(bf16[16,128,512]{2,1,0:T(8,128)(2,1)S(1)} %get-tuple-element.39), channel_id=1, source_target_pairs={{0,1},{1,0},{2,3},{3,2},{4,5},{5,4},{6,7},{7,6},{8,9},{9,8},{10,11... | collective-permute-start | bytes 6291464 | tf_op jit(solution)/shard_map/ppermute | solution.py:338
  52.5 23.6 %copy-start.2 = (bf16[256,2048]{1,0:T(8,128)(2,1)S(1)}, bf16[256,2048]{1,0:T(8,128)(2,1)}, u32[]{:S(2)}) copy-start(bf16[256,2048]{1,0:T(8,128)(2,1)} %own_weight_ref.1) | copy-start | bytes 3145732
  52.5 23.6 %copy-start.10 = (f32[256]{0:T(256)S(1)}, f32[256]{0:T(256)}, u32[]{:S(2)}) copy-start(f32[256]{0:T(256)} %param.25) | copy-start | bytes 3076
  52.5 9.6 %collective-permute-start.15 = (bf16[4,128,512]{2,1,0:T(8,128)(2,1)S(1)}, bf16[4,128,512]{2,1,0:T(8,128)(2,1)S(1)}, u32[]{:S(2)}, u32[]{:S(2)}) collective-permute-start(bf16[4,128,512]{2,1,0:T(8,128)(2,1)S(1)} %get-tuple-element.41), channel_id=1, source_target_pairs={{0,8},{1,3},{2,10},{3,5},{4,12},{5,7},{6,14},{7,1},{8,16},{9,11},{... | collective-permute-start | bytes 1572872 | tf_op jit(solution)/shard_map/ppermute | solution.py:319
  53.7 14.8 %collective-permute-start.16 = (bf16[4,128,512]{2,1,0:T(8,128)(2,1)S(1)}, bf16[4,128,512]{2,1,0:T(8,128)(2,1)S(1)}, u32[]{:S(2)}, u32[]{:S(2)}) collective-permute-start(bf16[4,128,512]{2,1,0:T(8,128)(2,1)S(1)} %get-tuple-element.42), channel_id=1, source_target_pairs={{0,16},{1,5},{2,18},{3,7},{4,20},{5,1},{6,22},{7,3},{8,24},{9,13},... | collective-permute-start | bytes 1572872 | tf_op jit(solution)/shard_map/ppermute | solution.py:319
  56.1 12.5 %collective-permute-start.17 = (bf16[4,128,512]{2,1,0:T(8,128)(2,1)S(1)}, bf16[4,128,512]{2,1,0:T(8,128)(2,1)S(1)}, u32[]{:S(2)}, u32[]{:S(2)}) collective-permute-start(bf16[4,128,512]{2,1,0:T(8,128)(2,1)S(1)} %get-tuple-element.43), channel_id=1, source_target_pairs={{0,24},{1,7},{2,26},{3,1},{4,28},{5,3},{6,30},{7,5},{8,0},{9,15},{... | collective-permute-start | bytes 1572872 | tf_op jit(solution)/shard_map/ppermute | solution.py:319
  68.8 5.1 %collective-permute-start.18 = (bf16[128,512]{1,0:T(8,128)(2,1)S(1)}, bf16[128,512]{1,0:T(8,128)(2,1)S(1)}, u32[]{:S(2)}, u32[]{:S(2)}) collective-permute-start(bf16[128,512]{1,0:T(8,128)(2,1)S(1)} %get-tuple-element.45), channel_id=1, source_target_pairs={{0,2},{1,9},{2,4},{3,11},{4,6},{5,13},{6,0},{7,15},{8,10},{9,17},{... | collective-permute-start | bytes 393224 | tf_op jit(solution)/shard_map/ppermute | solution.py:319
  70.1 6.0 %collective-permute-start.19 = (bf16[128,512]{1,0:T(8,128)(2,1)S(1)}, bf16[128,512]{1,0:T(8,128)(2,1)S(1)}, u32[]{:S(2)}, u32[]{:S(2)}) collective-permute-start(bf16[128,512]{1,0:T(8,128)(2,1)S(1)} %get-tuple-element.46), channel_id=1, source_target_pairs={{0,4},{1,17},{2,6},{3,19},{4,0},{5,21},{6,2},{7,23},{8,12},{9,25},... | collective-permute-start | bytes 393224 | tf_op jit(solution)/shard_map/ppermute | solution.py:319
  72.3 3.8 %collective-permute-start.20 = (bf16[128,512]{1,0:T(8,128)(2,1)S(1)}, bf16[128,512]{1,0:T(8,128)(2,1)S(1)}, u32[]{:S(2)}, u32[]{:S(2)}) collective-permute-start(bf16[128,512]{1,0:T(8,128)(2,1)S(1)} %get-tuple-element.47), channel_id=1, source_target_pairs={{0,6},{1,25},{2,0},{3,27},{4,2},{5,29},{6,4},{7,31},{8,14},{9,1},{... | collective-permute-start | bytes 393224 | tf_op jit(solution)/shard_map/ppermute | solution.py:319
  77.8 5.3 %collective-permute-start.21 = (bf16[4,144,128]{2,1,0:T(8,128)(2,1)S(1)}, bf16[4,144,128]{2,1,0:T(8,128)(2,1)S(1)}, u32[]{:S(2)}, u32[]{:S(2)}) collective-permute-start(bf16[4,144,128]{2,1,0:T(8,128)(2,1)S(1)} %get-tuple-element.53), channel_id=1, source_target_pairs={{0,8},{1,3},{2,10},{3,5},{4,12},{5,7},{6,14},{7,1},{8,16},{9,11},{... | collective-permute-start | bytes 442376 | tf_op jit(solution)/shard_map/ppermute | solution.py:319
  79.6 6.2 %collective-permute-start.22 = (bf16[4,144,128]{2,1,0:T(8,128)(2,1)S(1)}, bf16[4,144,128]{2,1,0:T(8,128)(2,1)S(1)}, u32[]{:S(2)}, u32[]{:S(2)}) collective-permute-start(bf16[4,144,128]{2,1,0:T(8,128)(2,1)S(1)} %get-tuple-element.54), channel_id=1, source_target_pairs={{0,16},{1,5},{2,18},{3,7},{4,20},{5,1},{6,22},{7,3},{8,24},{9,13},... | collective-permute-start | bytes 442376 | tf_op jit(solution)/shard_map/ppermute | solution.py:319
  81.7 4.3 %collective-permute-start.23 = (bf16[4,144,128]{2,1,0:T(8,128)(2,1)S(1)}, bf16[4,144,128]{2,1,0:T(8,128)(2,1)S(1)}, u32[]{:S(2)}, u32[]{:S(2)}) collective-permute-start(bf16[4,144,128]{2,1,0:T(8,128)(2,1)S(1)} %get-tuple-element.55), channel_id=1, source_target_pairs={{0,24},{1,7},{2,26},{3,1},{4,28},{5,3},{6,30},{7,5},{8,0},{9,15},{... | collective-permute-start | bytes 442376 | tf_op jit(solution)/shard_map/ppermute | solution.py:319
  86.1 9.5 %collective-permute-start.24 = (bf16[4,144,128]{2,1,0:T(8,128)(2,1)S(1)}, bf16[4,144,128]{2,1,0:T(8,128)(2,1)S(1)}, u32[]{:S(2)}, u32[]{:S(2)}) collective-permute-start(bf16[4,144,128]{2,1,0:T(8,128)(2,1)S(1)} %kv.1.own_part_ref), channel_id=1, source_target_pairs={{0,2},{1,9},{2,4},{3,11},{4,6},{5,13},{6,0},{7,15},{8,10},{9,17},{... | collective-permute-start | bytes 442376 | tf_op jit(solution)/shard_map/ppermute | solution.py:319
  87.3 8.4 %collective-permute-start.25 = (bf16[4,144,128]{2,1,0:T(8,128)(2,1)S(1)}, bf16[4,144,128]{2,1,0:T(8,128)(2,1)S(1)}, u32[]{:S(2)}, u32[]{:S(2)}) collective-permute-start(bf16[4,144,128]{2,1,0:T(8,128)(2,1)S(1)} %kv.1.own_part_ref), channel_id=1, source_target_pairs={{0,4},{1,17},{2,6},{3,19},{4,0},{5,21},{6,2},{7,23},{8,12},{9,25},... | collective-permute-start | bytes 442376 | tf_op jit(solution)/shard_map/ppermute | solution.py:319
  89.2 6.4 %collective-permute-start.26 = (bf16[4,144,128]{2,1,0:T(8,128)(2,1)S(1)}, bf16[4,144,128]{2,1,0:T(8,128)(2,1)S(1)}, u32[]{:S(2)}, u32[]{:S(2)}) collective-permute-start(bf16[4,144,128]{2,1,0:T(8,128)(2,1)S(1)} %kv.1.own_part_ref), channel_id=1, source_target_pairs={{0,6},{1,25},{2,0},{3,27},{4,2},{5,29},{6,4},{7,31},{8,14},{9,1},{... | collective-permute-start | bytes 442376 | tf_op jit(solution)/shard_map/ppermute | solution.py:319
  90.0 5.6 %collective-permute-start.27 = (bf16[128,256]{1,0:T(8,128)(2,1)S(1)}, bf16[128,256]{1,0:T(8,128)(2,1)S(1)}, u32[]{:S(2)}, u32[]{:S(2)}) collective-permute-start(bf16[128,256]{1,0:T(8,128)(2,1)S(1)} %get-tuple-element.57), channel_id=1, source_target_pairs={{0,1},{1,0},{2,3},{3,2},{4,5},{5,4},{6,7},{7,6},{8,9},{9,8},{10,11... | collective-permute-start | bytes 196616 | tf_op jit(solution)/shard_map/ppermute | solution.py:338
  96.9 5.0 %collective-permute-start.28 = (bf16[4,128,128]{2,1,0:T(8,128)(2,1)S(1)}, bf16[4,128,128]{2,1,0:T(8,128)(2,1)S(1)}, u32[]{:S(2)}, u32[]{:S(2)}) collective-permute-start(bf16[4,128,128]{2,1,0:T(8,128)(2,1)S(1)} %get-tuple-element.61.own_ref), channel_id=1, source_target_pairs={{0,32},{32,64},{64,96},{96,0},{1,33},{33,65},{65,97},{97,1},{2,34}... | collective-permute-start | bytes 393224 | tf_op jit(solution)/shard_map/ppermute | solution.py:393
  96.9 6.9 %collective-permute-start.29 = (bf16[4,128,128]{2,1,0:T(8,128)(2,1)S(1)}, bf16[4,128,128]{2,1,0:T(8,128)(2,1)S(1)}, u32[]{:S(2)}, u32[]{:S(2)}) collective-permute-start(bf16[4,128,128]{2,1,0:T(8,128)(2,1)S(1)} %get-tuple-element.61.own_ref), channel_id=1, source_target_pairs={{0,64},{32,96},{64,0},{96,32},{1,65},{33,97},{65,1},{97,33},{2,66}... | collective-permute-start | bytes 393224 | tf_op jit(solution)/shard_map/ppermute | solution.py:393
  100.0 3.9 %collective-permute-start.30 = (bf16[4,128,128]{2,1,0:T(8,128)(2,1)S(1)}, bf16[4,128,128]{2,1,0:T(8,128)(2,1)S(1)}, u32[]{:S(2)}, u32[]{:S(2)}) collective-permute-start(bf16[4,128,128]{2,1,0:T(8,128)(2,1)S(1)} %get-tuple-element.61.own_ref), channel_id=1, source_target_pairs={{0,96},{32,0},{64,32},{96,64},{1,97},{33,1},{65,33},{97,65},{2,98}... | collective-permute-start | bytes 393224 | tf_op jit(solution)/shard_map/ppermute | solution.py:393
  104.5 15.1 %collective-permute-start.31 = (bf16[4,4,128,128]{3,2,1,0:T(8,128)(2,1)S(1)}, bf16[4,4,128,128]{3,2,1,0:T(8,128)(2,1)S(1)}, u32[]{:S(2)}, u32[]{:S(2)}) collective-permute-start(bf16[4,4,128,128]{3,2,1,0:T(8,128)(2,1)S(1)} %stack.25.q0), channel_id=1, source_target_pairs={{0,8},{1,3},{2,10},{3,5},{4,12},{5,7},{6,14},{7,1},{8,16},{9,11},{... | collective-permute-start | bytes 1572872 | tf_op jit(solution)/shard_map/ppermute | solution.py:319
  105.5 14.1 %collective-permute-start.32 = (bf16[4,4,128,128]{3,2,1,0:T(8,128)(2,1)S(1)}, bf16[4,4,128,128]{3,2,1,0:T(8,128)(2,1)S(1)}, u32[]{:S(2)}, u32[]{:S(2)}) collective-permute-start(bf16[4,4,128,128]{3,2,1,0:T(8,128)(2,1)S(1)} %stack.25.q0), channel_id=1, source_target_pairs={{0,16},{1,5},{2,18},{3,7},{4,20},{5,1},{6,22},{7,3},{8,24},{9,13},... | collective-permute-start | bytes 1572872 | tf_op jit(solution)/shard_map/ppermute | solution.py:319
  106.3 14.0 %collective-permute-start.33 = (bf16[4,4,128,128]{3,2,1,0:T(8,128)(2,1)S(1)}, bf16[4,4,128,128]{3,2,1,0:T(8,128)(2,1)S(1)}, u32[]{:S(2)}, u32[]{:S(2)}) collective-permute-start(bf16[4,4,128,128]{3,2,1,0:T(8,128)(2,1)S(1)} %stack.25.q0), channel_id=1, source_target_pairs={{0,24},{1,7},{2,26},{3,1},{4,28},{5,3},{6,30},{7,5},{8,0},{9,15},{... | collective-permute-start | bytes 1572872 | tf_op jit(solution)/shard_map/ppermute | solution.py:319
  121.1 8.6 %collective-permute-start.34 = (bf16[2,16,128,128]{3,2,1,0:T(8,128)(2,1)S(1)}, bf16[2,16,128,128]{3,2,1,0:T(8,128)(2,1)S(1)}, u32[]{:S(2)}, u32[]{:S(2)}) collective-permute-start(bf16[2,16,128,128]{3,2,1,0:T(8,128)(2,1)S(1)} %pick.1), channel_id=1, source_target_pairs={{0,1},{1,0},{2,3},{3,2},{4,5},{5,4},{6,7},{7,6},{8,9},{9,8},{10,11... | collective-permute-start | bytes 3145736 | tf_op jit(solution)/shard_map/ppermute | solution.py:338

commit v3 on v2

--- a/solution.py
+++ b/solution.py
@@ -94,12 +94,11 @@
 
 def give_kernel(
     place_ref, step_ref, states_ref, alog_ref, conv_ref, gate_ref, skip_ref, init_ref,
-    near_ref, mid_ref, far_ref, weight_ref,
-    give_ref, kept_ref, drive_ref, scan_ref, gated_ref, held_ref, sems,
+    near_ref, mid_ref, far_ref, weight_ref, residual_ref,
+    give_ref, kept_ref, drive_ref, scan_ref, gated_ref,
 ):
     tokens = step_ref.shape[0]
     place, core = place_ref[0], place_ref[1]
-    copies = fetch(weight_ref, held_ref, sems)
     rates = -jnp.exp(alog_ref[...]) * LOG2E
     hidden = init_ref[...]
     for back, ref in ((3, far_ref), (2, mid_ref), (1, near_ref)):
@@ -117,10 +116,14 @@
         (scan_ref[...] + skip_ref[...] * conv_ref[...].astype(F32)) * (gate / (1.0 + jnp.exp(-gate)))
     ).astype(BF).reshape(gated_ref.shape)
     kept_ref[...] = gated_ref[core]
-    through(place_ref, 1 - core, gated_ref.at[1 - core], held_ref, copies, give_ref)
-
-
-def fetch(weight_ref, held_ref, sems):
+    through(place_ref, 1 - core, gated_ref.at[1 - core], weight_ref, give_ref)
+    rows, feats = residual_ref.shape[0] // 2, residual_ref.shape[1]
+    mine = pl.ds(pl.multiple_of(core * feats, feats), feats)
+    other = residual_ref[pl.ds(pl.multiple_of((1 - core) * rows, rows), rows), :]
+    give_ref[0, :, mine] = (give_ref[0, :, mine].astype(F32) + other.astype(F32)).astype(BF)
+
+
+def bring_kernel(weight_ref, _, held_ref, sems):
     wide = weight_ref.shape[1] // PIECES
     copies = [
         pltpu.make_async_copy(
@@ -131,7 +134,8 @@
     ]
     for copy in copies:
         copy.start()
-    return copies
+    for copy in copies:
+        copy.wait()
 
 
 def chip_order(place_ref, core, chip):
@@ -140,28 +144,25 @@
     return jnp.where(core == 0, away_x, away_y), jnp.where(core == 0, away_y, away_x)
 
 
-def through(place_ref, core, gated_ref, held_ref, copies, out_ref):
+def through(place_ref, core, gated_ref, weight_ref, out_ref):
     chips, _, wide = out_ref.shape
     for chip in range(chips):
-        if chip % (chips // PIECES) == 0:
-            copies[chip // (chips // PIECES)].wait()
         product = jnp.dot(
-            gated_ref[...], held_ref[:, chip * wide : (chip + 1) * wide],
+            gated_ref[...], weight_ref[:, chip * wide : (chip + 1) * wide],
             preferred_element_type=F32,
         ).astype(BF)
         far, near = chip_order(place_ref, core, chip)
         out_ref[far * SIDE + near] = product
 
 
-def keep_kernel(place_ref, kept_ref, weight_ref, keep_ref, held_ref, sems):
-    copies = fetch(weight_ref, held_ref, sems)
-    through(place_ref, place_ref[1], kept_ref, held_ref, copies, keep_ref)
+def keep_kernel(place_ref, kept_ref, weight_ref, keep_ref):
+    through(place_ref, place_ref[1], kept_ref, weight_ref, keep_ref)
 
 
 def pair_kernel(keep_ref, got_ref, *out_refs):
     for shift, ref in enumerate(out_refs):
         rows = slice(shift * SIDE, (shift + 1) * SIDE)
-        ref[...] = (keep_ref[rows].astype(F32) + got_ref[rows].astype(F32)).astype(BF)
+        ref[...] = (keep_ref[rows].astype(F32) + got_ref[rows].astype(F32)).astype(ref.dtype)
 
 
 def line_kernel(own_ref, one_ref, two_ref, three_ref, *out_refs):
@@ -173,8 +174,8 @@
 
 
 def layer_kernel(
-    place_ref, own_part_ref, one_ref, two_ref, three_ref, own_res_ref, got_res_ref, own_gain_ref, got_gain_ref,
-    own_weight_ref, got_weight_ref, own_ref, other_ref, *out_refs,
+    place_ref, own_part_ref, one_ref, two_ref, three_ref, residual_ref, own_gain_ref,
+    got_gain_ref, own_weight_ref, got_weight_ref, own_ref, other_ref, *out_refs,
 ):
     mixed = own_part_ref[...]
     for ref in (one_ref, two_ref, three_ref):
@@ -182,12 +183,14 @@
     half = mixed.shape[1] // 2
     first = place_ref[1] == 0
     left, right = mixed[:, :half], mixed[:, half:]
+    rows = mixed.shape[0]
+    residual = residual_ref[pl.ds(pl.multiple_of(place_ref[1] * rows, rows), rows), :].astype(F32)
     term, squares = 0.0, 0.0
-    for piece, res_ref, gain_ref, weight_ref, layer_ref in (
-        (jnp.where(first, left, right), own_res_ref, own_gain_ref, own_weight_ref, own_ref),
-        (jnp.where(first, right, left), got_res_ref, got_gain_ref, got_weight_ref, other_ref),
+    for piece, gain_ref, weight_ref, layer_ref in (
+        (jnp.where(first, left, right) + residual, own_gain_ref, own_weight_ref, own_ref),
+        (jnp.where(first, right, left), got_gain_ref, got_weight_ref, other_ref),
     ):
-        layer = (res_ref[...].astype(F32) + piece).astype(BF)
+        layer = piece.astype(BF)
         layer_ref[...] = layer
         stream = layer.astype(F32)
         squares = squares + lax.dot_general(
@@ -337,9 +340,6 @@
     def swap(value):
         return lax.ppermute(value, "tp", partner)
 
-    halves = residual.reshape(2, tokens // 2, feats)
-    own_res = lax.dynamic_index_in_dim(halves, core, 0, False)
-    got_res = swap(lax.dynamic_index_in_dim(halves, 1 - core, 0, False))
     own_gain = norm_gain.reshape(1, feats)
     got_gain, got_weight = swap(own_gain), swap(kv_weight)
     devices = owner.shape[0]
@@ -364,11 +364,9 @@
         compiler_params=params(8),
         name="project",
     )(places, conv_out, xproj_weight.T)
-    chip = add("chip", BF, kept_share, swap(give_share))
+    got_share, got_gain = lax.optimization_barrier((swap(give_share), got_gain))
+    chip = add("chip", BF, kept_share, got_share)
     row = add("row", BF, chip, *line(0, lambda shift: chip))
-    row, starts, counts, own_res, got_res, got_gain, got_weight = lax.optimization_barrier(
-        (row, starts, counts, own_res, got_res, got_gain, got_weight)
-    )
     own_proj = add("plane", BF, row, *line(1, lambda shift: row))
 
     blocks = tokens // CHUNK
@@ -394,32 +392,38 @@
             for s in range(1, ctx_count)
         ]
 
-    weight_scratch = [pltpu.VMEM(out_weight.shape, BF), pltpu.SemaphoreType.DMA((PIECES,))]
+    near_weight = pl.pallas_call(
+        bring_kernel,
+        in_specs=[ANY] * 2,
+        out_shape=shape(out_weight.shape, BF),
+        scratch_shapes=[pltpu.SemaphoreType.DMA((PIECES,))],
+        compiler_params=params(42),
+        name="bring",
+    )(out_weight, ends)
     partial = (pairs, tokens // 2, 2 * feats)
     give, kept = pl.pallas_call(
         give_kernel,
-        in_specs=[SM] + [VM] * 10 + [ANY],
+        in_specs=[SM] + [VM] * 12,
         out_shape=(shape(partial, BF), shape((tokens // 2, chans), BF)),
         scratch_shapes=[
             pltpu.VMEM((tokens, chans), F32),
             pltpu.VMEM((tokens, chans), F32),
             pltpu.VMEM((2, tokens // 2, chans), BF),
-        ] + weight_scratch,
-        compiler_params=params(46),
+        ],
+        compiler_params=params(20),
         name="give",
     )(
         places, step, states, a_log, conv_out, gate_in, d_skip.reshape(1, chans), init_state,
-        *ranges_back(ends), out_weight,
+        *ranges_back(ends), near_weight, residual,
     )
     got = swap(give)
     keep = pl.pallas_call(
         keep_kernel,
-        in_specs=[SM, VM, ANY],
+        in_specs=[SM, VM, VM],
         out_shape=shape(partial, BF),
-        scratch_shapes=weight_scratch,
-        compiler_params=params(46),
+        compiler_params=params(16),
         name="keep",
-    )(places, kept, out_weight)
+    )(places, kept, near_weight)
     quarter = shape((SIDE, tokens // 2, 2 * feats), BF)
     sums = pl.pallas_call(
         pair_kernel, out_shape=(quarter,) * SIDE, compiler_params=params(12), name="pair"
@@ -436,11 +440,11 @@
     block_shape = shape((tokens // 2, feats), BF)
     own_layer, other_layer, *kv_terms = pl.pallas_call(
         layer_kernel,
-        in_specs=[SM] + [VM] * 10,
+        in_specs=[SM] + [VM] * 9,
         out_shape=(block_shape,) * 2 + (shape((SIDE, BLK + 16, HEAD), BF),) * SIDE,
         compiler_params=params(8),
         name="layer",
-    )(places, *parts, own_res, got_res, own_gain, got_gain, kv_weight, got_weight)
+    )(places, *parts, residual, own_gain, got_gain, kv_weight, got_weight)
     got_layer = swap(other_layer)
     kv_row = add("kv", BF, kv_terms[0], *line(0, lambda shift: kv_terms[shift]))
     tile, layer_out = pl.pallas_call(

time: 132 us -> 130 us (0.985)
  waiting for transfers between devices: 44.5 us -> 46.5 us
  starting transfers between devices: 58.3 us -> 56.8 us
    ppermute x21, waiting for transfers between devices: 34.5 us -> 37.1 us  [line(): lax.ppermute(value_of(shift), 'tp', [((x * SIDE + y) * 2 + c, ((x + shift...]
    ppermute x6, waiting for transfers between devices: 6.2 us -> 3.88 us  [ranges_back(): lax.ppermute(value, 'ctx', [(z, (z + s) % ctx_count) for z in range(ctx_c...]
    ppermute x8 -> x7, waiting for transfers between devices: 3.77 us -> 5.56 us  [swap(): return lax.ppermute(value, 'tp', partner)]
    ppermute x8 -> x7, starting transfers between devices: 18.5 us -> 17.2 us  [swap(): return lax.ppermute(value, 'tp', partner)]
    pallas_call x3 -> x4, Pallas kernels: 12.8 us -> 12.3 us  [the longest x1 5.32 us: per_device(): pl.pallas_call(give_kernel, in_specs=[SM] + [VM] * 12, out_shape=(shape(p...]
  transfers between devices with their start and end apart: 35 -> 34, of which waited for: 22 -> 22; matrix products, arithmetic and copies ran while one was open for 1% -> 0% of each run, Pallas kernels for 6% -> 6%
where the time goes in v3:
time: 130 us
  starting transfers between devices  56.8 us (44%)
  waiting for transfers between devices  46.5 us (36%)
  Pallas kernels  23.2 us (18%)
  local copies, waits for them, and re-layouts  2.15 us (2%)
    ppermute x21, waiting for transfers between devices, line(): lax.ppermute(value_of(shift), 'tp', [((x * SIDE + y) * 2 + c, ((x + shift...  37.1 us
    ppermute x21, starting transfers between devices, line(): lax.ppermute(value_of(shift), 'tp', [((x * SIDE + y) * 2 + c, ((x + shift...  30.8 us
    ppermute x7, starting transfers between devices, swap(): return lax.ppermute(value, 'tp', partner)  17.2 us
    ppermute x6, starting transfers between devices, ranges_back(): lax.ppermute(value, 'ctx', [(z, (z + s) % ctx_count) for z in range(ctx_c...  8.87 us
    ppermute x7, waiting for transfers between devices, swap(): return lax.ppermute(value, 'tp', partner)  5.56 us
    pallas_call x1, Pallas kernels, per_device(): pl.pallas_call(give_kernel, in_specs=[SM] + [VM] * 12, out_shape=(shape(p...  5.32 us
    ppermute x6, waiting for transfers between devices, ranges_back(): lax.ppermute(value, 'ctx', [(z, (z + s) % ctx_count) for z in range(ctx_c...  3.88 us
    pallas_call x1, Pallas kernels, per_device(): pl.pallas_call(bring_kernel, in_specs=[ANY] * 2, out_shape=shape(out_weig...  3.5 us
  transfers between devices with their start and end apart: 34, of which 22 were waited for; matrix products, arithmetic and copies ran while one was open for 0% of the time, Pallas kernels for 6%

profile of v3, /device:TPU:1, one launch (start us, length us, event | category | flops | bytes accessed | tf_op | source)
XLA Modules:
  0.0 130.0 jit_solution(17438483116122454998)
XLA Ops:
  0.8 0.9 copy-done
  1.7 1.1 copy-done.3
  2.8 1.1 project.1
  3.9 1.5 %collective-permute-start = (bf16[128,544]{1,0:T(8,128)(2,1)S(1)}, bf16[128,544]{1,0:T(8,128)(2,1)S(1)}, u32[]{:S(2)}, u32[]{:S(2)}) collective-permute-start(bf16[128,544]{1,0:T(8,128)(2,1)S(1)} %get-tuple-element.28), channel_id=1, source_target_pairs={{0,1},{1,0},{2,3},{3,2},{4,5},{5,4},{6,7},{7,6},{8,9},{9,8},{10,11... | collective-permute-start | bytes 417800 | tf_op jit(solution)/shard_map/ppermute | solution.py:341
  5.5 1.3 collective-permute-done.1.got_gain_ref
  6.8 1.4 %collective-permute-start.2 = (bf16[128,544]{1,0:T(8,128)(2,1)S(1)}, bf16[128,544]{1,0:T(8,128)(2,1)S(1)}, u32[]{:S(2)}, u32[]{:S(2)}) collective-permute-start(bf16[128,544]{1,0:T(8,128)(2,1)S(1)} %chip.1.refs_0_), channel_id=1, source_target_pairs={{0,8},{1,3},{2,10},{3,5},{4,12},{5,7},{6,14},{7,1},{8,16},{9,11},{... | collective-permute-start | bytes 417800 | tf_op jit(solution)/shard_map/ppermute | solution.py:322
  8.2 2.6 %collective-permute-start.3 = (bf16[128,544]{1,0:T(8,128)(2,1)S(1)}, bf16[128,544]{1,0:T(8,128)(2,1)S(1)}, u32[]{:S(2)}, u32[]{:S(2)}) collective-permute-start(bf16[128,544]{1,0:T(8,128)(2,1)S(1)} %chip.1.refs_0_), channel_id=1, source_target_pairs={{0,16},{1,5},{2,18},{3,7},{4,20},{5,1},{6,22},{7,3},{8,24},{9,13},... | collective-permute-start | bytes 417800 | tf_op jit(solution)/shard_map/ppermute | solution.py:322
  10.8 1.1 collective-permute-start.4
  12.6 2.9 %collective-permute-done.3.refs_2_ = bf16[128,544]{1,0:T(8,128)(2,1)S(1)} collective-permute-done((bf16[128,544]{1,0:T(8,128)(2,1)S(1)}, bf16[128,544]{1,0:T(8,128)(2,1)S(1)}, u32[]{:S(2)}, u32[]{:S(2)}) %collective-permute-start.3) | collective-permute-done | bytes 139296 | tf_op jit(solution)/shard_map/ppermute | solution.py:322
  15.7 1.0 collective-permute-start.5
  16.7 2.4 %collective-permute-start.6 = (bf16[128,544]{1,0:T(8,128)(2,1)S(1)}, bf16[128,544]{1,0:T(8,128)(2,1)S(1)}, u32[]{:S(2)}, u32[]{:S(2)}) collective-permute-start(bf16[128,544]{1,0:T(8,128)(2,1)S(1)} %row.1.refs_0_), channel_id=1, source_target_pairs={{0,4},{1,17},{2,6},{3,19},{4,0},{5,21},{6,2},{7,23},{8,12},{9,25},... | collective-permute-start | bytes 417800 | tf_op jit(solution)/shard_map/ppermute | solution.py:322
  19.1 1.2 collective-permute-start.7
  20.3 1.1 collective-permute-done.5.refs_1_
  21.4 2.2 %collective-permute-done.6.refs_2_ = bf16[128,544]{1,0:T(8,128)(2,1)S(1)} collective-permute-done((bf16[128,544]{1,0:T(8,128)(2,1)S(1)}, bf16[128,544]{1,0:T(8,128)(2,1)S(1)}, u32[]{:S(2)}, u32[]{:S(2)}) %collective-permute-start.6) | collective-permute-done | bytes 139296 | tf_op jit(solution)/shard_map/ppermute | solution.py:322
  23.7 3.1 %collective-permute-start.8 = (bf16[128,544]{1,0:T(8,128)(2,1)S(1)}, bf16[128,544]{1,0:T(8,128)(2,1)S(1)}, u32[]{:S(2)}, u32[]{:S(2)}) collective-permute-start(bf16[128,544]{1,0:T(8,128)(2,1)S(1)} %plane.1.own_proj_ref), channel_id=1, source_target_pairs={{0,1},{1,0},{2,3},{3,2},{4,5},{5,4},{6,7},{7,6},{8,9},{9,8},{10,11... | collective-permute-start | bytes 417800 | tf_op jit(solution)/shard_map/ppermute | solution.py:341
  26.8 1.0 collective-permute-done.8.got_proj_ref
  27.8 2.8 %first.1 = (f32[256,512]{1,0:T(8,128)S(1)}, f32[8,32,32]{2,1,0:T(8,128)S(1)}, f32[24,512]{1,0:T(8,128)S(1)}) custom-call(s32[5]{0:T(128)S(1)} %stack.24.place_ref, bf16[128,544]{1,0:T(8,128)(2,1)S(1)} %plane.1.own_proj_ref, bf16[128,544]{1,0:T(8,128)(2,1)S(1)} %collective-permute-done.8.got_proj_ref, bf16[512,512]{1,0:T(8,128)(2,1)S(1)} %copy-done.5, ...), custom_call_target="tpu_custom_call" | custom-call | tf_op jit(solution)/shard_map/first/pallas_call | solution.py:373
  30.7 1.7 %collective-permute-start.9 = (f32[24,512]{1,0:T(8,128)S(1)}, f32[24,512]{1,0:T(8,128)S(1)}, u32[]{:S(2)}, u32[]{:S(2)}) collective-permute-start(f32[24,512]{1,0:T(8,128)S(1)} %get-tuple-element.32._), channel_id=1, source_target_pairs={{0,32},{32,64},{64,96},{96,0},{1,33},{33,65},{65,97},{97,1},{2,34}... | collective-permute-start | bytes 147464 | tf_op jit(solution)/shard_map/ppermute | solution.py:391
  32.5 3.3 %collective-permute-start.10 = (f32[24,512]{1,0:T(8,128)S(1)}, f32[24,512]{1,0:T(8,128)S(1)}, u32[]{:S(2)}, u32[]{:S(2)}) collective-permute-start(f32[24,512]{1,0:T(8,128)S(1)} %get-tuple-element.32._), channel_id=1, source_target_pairs={{0,64},{32,96},{64,0},{96,32},{1,65},{33,97},{65,1},{97,33},{2,66}... | collective-permute-start | bytes 147464 | tf_op jit(solution)/shard_map/ppermute | solution.py:391
  36.5 3.5 %bring.1.weight_ref = bf16[512,8192]{1,0:T(8,128)(2,1)S(1)} custom-call(bf16[512,8192]{1,0:T(8,128)(2,1)} %weight_ref.3, f32[24,512]{1,0:T(8,128)S(1)} %get-tuple-element.32._), custom_call_target="tpu_custom_call" | custom-call | tf_op jit(solution)/shard_map/bring/pallas_call | solution.py:395
  40.1 5.3 %give.1 = (bf16[16,128,512]{2,1,0:T(8,128)(2,1)S(1)}, bf16[128,512]{1,0:T(8,128)(2,1)S(1)}) custom-call(s32[5]{0:T(128)S(1)} %stack.24.place_ref, f32[256,512]{1,0:T(8,128)S(1)} %get-tuple-element.30.step_ref, f32[8,32,32]{2,1,0:T(8,128)S(1)} %get-tuple-element.31.states_ref, f32[16,512]{1,0:T(8,128)S(1)} %copy-done.7, bf16[256,512]{1,0:T(8,128)(2,1)S(1)} %copy-done.1, ...), custom_call_target="tpu_custom_call" | custom-call | tf_op jit(solution)/shard_map/give/pallas_call | solution.py:404
  45.4 1.3 collective-permute-start.12
  46.8 1.8 %keep.1.keep_ref = bf16[16,128,512]{2,1,0:T(8,128)(2,1)S(1)} custom-call(s32[5]{0:T(128)S(1)} %stack.24.place_ref, bf16[128,512]{1,0:T(8,128)(2,1)S(1)} %get-tuple-element.33.kept_ref, bf16[512,8192]{1,0:T(8,128)(2,1)S(1)} %bring.1.weight_ref), custom_call_target="tpu_custom_call" | custom-call | tf_op jit(solution)/shard_map/keep/pallas_call | solution.py:420
  48.6 1.9 %collective-permute-done.12.got_ref = bf16[16,128,512]{2,1,0:T(8,128)(2,1)S(1)} collective-permute-done((bf16[16,128,512]{2,1,0:T(8,128)(2,1)S(1)}, bf16[16,128,512]{2,1,0:T(8,128)(2,1)S(1)}, u32[]{:S(2)}, u32[]{:S(2)}) %collective-permute-start.12) | collective-permute-done | bytes 2097184 | tf_op jit(solution)/shard_map/ppermute | solution.py:341
  51.0 1.2 collective-permute-start.13
  52.1 2.4 %collective-permute-start.14 = (bf16[4,128,512]{2,1,0:T(8,128)(2,1)S(1)}, bf16[4,128,512]{2,1,0:T(8,128)(2,1)S(1)}, u32[]{:S(2)}, u32[]{:S(2)}) collective-permute-start(bf16[4,128,512]{2,1,0:T(8,128)(2,1)S(1)} %get-tuple-element.37), channel_id=1, source_target_pairs={{0,16},{1,5},{2,18},{3,7},{4,20},{5,1},{6,22},{7,3},{8,24},{9,13},... | collective-permute-start | bytes 1572872 | tf_op jit(solution)/shard_map/ppermute | solution.py:322
  55.4 5.2 %collective-permute-done.13.one_ref = bf16[4,128,512]{2,1,0:T(8,128)(2,1)S(1)} collective-permute-done((bf16[4,128,512]{2,1,0:T(8,128)(2,1)S(1)}, bf16[4,128,512]{2,1,0:T(8,128)(2,1)S(1)}, u32[]{:S(2)}, u32[]{:S(2)}) %collective-permute-start.13) | collective-permute-done | bytes 524320 | tf_op jit(solution)/shard_map/ppermute | solution.py:322
  60.6 6.4 %collective-permute-done.14.two_ref = bf16[4,128,512]{2,1,0:T(8,128)(2,1)S(1)} collective-permute-done((bf16[4,128,512]{2,1,0:T(8,128)(2,1)S(1)}, bf16[4,128,512]{2,1,0:T(8,128)(2,1)S(1)}, u32[]{:S(2)}, u32[]{:S(2)}) %collective-permute-start.14) | collective-permute-done | bytes 524320 | tf_op jit(solution)/shard_map/ppermute | solution.py:322
  67.2 1.3 collective-permute-start.16
  68.5 2.2 %collective-permute-start.17 = (bf16[128,512]{1,0:T(8,128)(2,1)S(1)}, bf16[128,512]{1,0:T(8,128)(2,1)S(1)}, u32[]{:S(2)}, u32[]{:S(2)}) collective-permute-start(bf16[128,512]{1,0:T(8,128)(2,1)S(1)} %get-tuple-element.41), channel_id=1, source_target_pairs={{0,4},{1,17},{2,6},{3,19},{4,0},{5,21},{6,2},{7,23},{8,12},{9,25},... | collective-permute-start | bytes 393224 | tf_op jit(solution)/shard_map/ppermute | solution.py:322
  72.3 2.1 %collective-permute-done.17.two_ref = bf16[128,512]{1,0:T(8,128)(2,1)S(1)} collective-permute-done((bf16[128,512]{1,0:T(8,128)(2,1)S(1)}, bf16[128,512]{1,0:T(8,128)(2,1)S(1)}, u32[]{:S(2)}, u32[]{:S(2)}) %collective-permute-start.17) | collective-permute-done | bytes 131104 | tf_op jit(solution)/shard_map/ppermute | solution.py:322
  74.5 1.7 %layer.1 = (bf16[128,256]{1,0:T(8,128)(2,1)S(1)}, bf16[128,256]{1,0:T(8,128)(2,1)S(1)}, bf16[4,144,128]{2,1,0:T(8,128)(2,1)S(1)}, bf16[4,144,128]{2,1,0:T(8,128)...) custom-call(s32[5]{0:T(128)S(1)} %stack.24.place_ref, ...), custom_call_target="tpu_custom_call" | custom-call | tf_op jit(solution)/shard_map/layer/pallas_call | solution.py:441
  76.3 1.8 %collective-permute-start.20 = (bf16[4,144,128]{2,1,0:T(8,128)(2,1)S(1)}, bf16[4,144,128]{2,1,0:T(8,128)(2,1)S(1)}, u32[]{:S(2)}, u32[]{:S(2)}) collective-permute-start(bf16[4,144,128]{2,1,0:T(8,128)(2,1)S(1)} %get-tuple-element.45), channel_id=1, source_target_pairs={{0,8},{1,3},{2,10},{3,5},{4,12},{5,7},{6,14},{7,1},{8,16},{9,11},{... | collective-permute-start | bytes 442376 | tf_op jit(solution)/shard_map/ppermute | solution.py:322
  78.0 2.1 %collective-permute-start.21 = (bf16[4,144,128]{2,1,0:T(8,128)(2,1)S(1)}, bf16[4,144,128]{2,1,0:T(8,128)(2,1)S(1)}, u32[]{:S(2)}, u32[]{:S(2)}) collective-permute-start(bf16[4,144,128]{2,1,0:T(8,128)(2,1)S(1)} %get-tuple-element.46), channel_id=1, source_target_pairs={{0,16},{1,5},{2,18},{3,7},{4,20},{5,1},{6,22},{7,3},{8,24},{9,13},... | collective-permute-start | bytes 442376 | tf_op jit(solution)/shard_map/ppermute | solution.py:322
  81.5 2.7 %collective-permute-done.21.refs_2_ = bf16[4,144,128]{2,1,0:T(8,128)(2,1)S(1)} collective-permute-done((bf16[4,144,128]{2,1,0:T(8,128)(2,1)S(1)}, bf16[4,144,128]{2,1,0:T(8,128)(2,1)S(1)}, u32[]{:S(2)}, u32[]{:S(2)}) %collective-permute-start.21) | collective-permute-done | bytes 147488 | tf_op jit(solution)/shard_map/ppermute | solution.py:322
  84.5 1.2 collective-permute-start.23
  85.7 2.1 %collective-permute-start.24 = (bf16[4,144,128]{2,1,0:T(8,128)(2,1)S(1)}, bf16[4,144,128]{2,1,0:T(8,128)(2,1)S(1)}, u32[]{:S(2)}, u32[]{:S(2)}) collective-permute-start(bf16[4,144,128]{2,1,0:T(8,128)(2,1)S(1)} %kv.1.own_part_ref), channel_id=1, source_target_pairs={{0,4},{1,17},{2,6},{3,19},{4,0},{5,21},{6,2},{7,23},{8,12},{9,25},... | collective-permute-start | bytes 442376 | tf_op jit(solution)/shard_map/ppermute | solution.py:322
  88.5 5.0 %collective-permute-start.26 = (bf16[128,256]{1,0:T(8,128)(2,1)S(1)}, bf16[128,256]{1,0:T(8,128)(2,1)S(1)}, u32[]{:S(2)}, u32[]{:S(2)}) collective-permute-start(bf16[128,256]{1,0:T(8,128)(2,1)S(1)} %get-tuple-element.49), channel_id=1, source_target_pairs={{0,1},{1,0},{2,3},{3,2},{4,5},{5,4},{6,7},{7,6},{8,9},{9,8},{10,11... | collective-permute-start | bytes 196616 | tf_op jit(solution)/shard_map/ppermute | solution.py:341
  94.4 1.2 tile.1
  96.4 1.9 %collective-permute-start.28 = (bf16[4,128,128]{2,1,0:T(8,128)(2,1)S(1)}, bf16[4,128,128]{2,1,0:T(8,128)(2,1)S(1)}, u32[]{:S(2)}, u32[]{:S(2)}) collective-permute-start(bf16[4,128,128]{2,1,0:T(8,128)(2,1)S(1)} %get-tuple-element.51.own_ref), channel_id=1, source_target_pairs={{0,64},{32,96},{64,0},{96,32},{1,65},{33,97},{65,1},{97,33},{2,66}... | collective-permute-start | bytes 393224 | tf_op jit(solution)/shard_map/ppermute | solution.py:391
  98.8 1.9 %collective-permute-done.27.near_ref = bf16[4,128,128]{2,1,0:T(8,128)(2,1)S(1)} collective-permute-done((bf16[4,128,128]{2,1,0:T(8,128)(2,1)S(1)}, bf16[4,128,128]{2,1,0:T(8,128)(2,1)S(1)}, u32[]{:S(2)}, u32[]{:S(2)}) %collective-permute-start.27) | collective-permute-done | bytes 131104 | tf_op jit(solution)/shard_map/ppermute | solution.py:391
  100.7 1.4 %collective-permute-done.28.mid_ref = bf16[4,128,128]{2,1,0:T(8,128)(2,1)S(1)} collective-permute-done((bf16[4,128,128]{2,1,0:T(8,128)(2,1)S(1)}, bf16[4,128,128]{2,1,0:T(8,128)(2,1)S(1)}, u32[]{:S(2)}, u32[]{:S(2)}) %collective-permute-start.28) | collective-permute-done | bytes 131104 | tf_op jit(solution)/shard_map/ppermute | solution.py:391
  103.3 1.0 collective-permute-start.30
  105.1 1.7 %collective-permute-start.32 = (bf16[4,4,128,128]{3,2,1,0:T(8,128)(2,1)S(1)}, bf16[4,4,128,128]{3,2,1,0:T(8,128)(2,1)S(1)}, u32[]{:S(2)}, u32[]{:S(2)}) collective-permute-start(bf16[4,4,128,128]{3,2,1,0:T(8,128)(2,1)S(1)} %stack.25.q0), channel_id=1, source_target_pairs={{0,24},{1,7},{2,26},{3,1},{4,28},{5,3},{6,30},{7,5},{8,0},{9,15},{... | collective-permute-start | bytes 1572872 | tf_op jit(solution)/shard_map/ppermute | solution.py:322
  106.9 11.3 %collective-permute-done.30.q1 = bf16[4,4,128,128]{3,2,1,0:T(8,128)(2,1)S(1)} collective-permute-done((bf16[4,4,128,128]{3,2,1,0:T(8,128)(2,1)S(1)}, bf16[4,4,128,128]{3,2,1,0:T(8,128)(2,1)S(1)}, u32[]{:S(2)}, u32[]{:S(2)}) %collective-permute-start.30) | collective-permute-done | bytes 524320 | tf_op jit(solution)/shard_map/ppermute | solution.py:322
  119.9 6.1 %collective-permute-start.33 = (bf16[2,16,128,128]{3,2,1,0:T(8,128)(2,1)S(1)}, bf16[2,16,128,128]{3,2,1,0:T(8,128)(2,1)S(1)}, u32[]{:S(2)}, u32[]{:S(2)}) collective-permute-start(bf16[2,16,128,128]{3,2,1,0:T(8,128)(2,1)S(1)} %pick.1), channel_id=1, source_target_pairs={{0,1},{1,0},{2,3},{3,2},{4,5},{5,4},{6,7},{7,6},{8,9},{9,8},{10,11... | collective-permute-start | bytes 3145736 | tf_op jit(solution)/shard_map/ppermute | solution.py:341
  126.0 1.8 %own.1._ = bf16[4,16,128,128]{3,2,1,0:T(8,128)(2,1)} custom-call(s32[5]{0:T(128)S(1)} %stack.24.place_ref, s32[128]{0:T(128)S(1)} %get-tuple-element.53.starts_ref, s32[128]{0:T(128)S(1)} %get-tuple-element.52.counts_ref, bf16[4,4,128,128]{3,2,1,0:T(8,128)(2,1)S(1)} %stack.25.q0, bf16[4,4,128,128]{3,2,1,0:T(8,128)(2,1)S(1)} %collective-permute-done.30.q1, ...), custom_call_target="tpu_custom_call" | custom-call | tf_op jit(solution)/shard_map/own/pallas_call | solution.py:474
  128.3 1.5 %rest.1 = bf16[4,16,128,128]{3,2,1,0:T(8,128)(2,1)} custom-call(s32[5]{0:T(128)S(1)} %stack.24.place_ref, s32[128]{0:T(128)S(1)} %get-tuple-element.53.starts_ref, bf16[2,16,128,128]{3,2,1,0:T(8,128)(2,1)S(1)} %collective-permute-done.33.got_ref, bf16[4,16,128,128]{3,2,1,0:T(8,128)(2,1)} %own.1._), custom_call_target="tpu_custom_call", output_to_operand_aliasing={{}: (3, {})} | custom-call | tf_op jit(solution)/shard_map/rest/pallas_call | solution.py:483
  (69 shorter events, 14.2 us)
Async XLA Ops:
  0.6 27.2 %copy-start.9 = (f32[512]{0:T(512)S(1)}, f32[512]{0:T(512)}, u32[]{:S(2)}) copy-start(f32[512]{0:T(512)} %param.20) | copy-start | bytes 6148
  0.6 27.2 %copy-start.7 = (f32[16,512]{1,0:T(8,128)S(1)}, f32[16,512]{1,0:T(8,128)}, u32[]{:S(2)}) copy-start(f32[16,512]{1,0:T(8,128)} %alog_ref.3) | copy-start | bytes 98308
  1.7 1.1 copy-start.3
  2.8 25.1 %copy-start.1 = (bf16[256,512]{1,0:T(8,128)(2,1)S(1)}, bf16[256,512]{1,0:T(8,128)(2,1)}, u32[]{:S(2)}) copy-start(bf16[256,512]{1,0:T(8,128)(2,1)} %conv_ref.5) | copy-start | bytes 786436
  2.8 25.1 %copy-start.5 = (bf16[512,512]{1,0:T(8,128)(2,1)S(1)}, bf16[512,512]{1,0:T(8,128)(2,1)}, u32[]{:S(2)}) copy-start(bf16[512,512]{1,0:T(8,128)(2,1)} %weight_ref.2) | copy-start | bytes 1572868
  3.9 2.9 %collective-permute-start = (bf16[128,544]{1,0:T(8,128)(2,1)S(1)}, bf16[128,544]{1,0:T(8,128)(2,1)S(1)}, u32[]{:S(2)}, u32[]{:S(2)}) collective-permute-start(bf16[128,544]{1,0:T(8,128)(2,1)S(1)} %get-tuple-element.28), channel_id=1, source_target_pairs={{0,1},{1,0},{2,3},{3,2},{4,5},{5,4},{6,7},{7,6},{8,9},{9,8},{10,11... | collective-permute-start | bytes 417800 | tf_op jit(solution)/shard_map/ppermute | solution.py:341
  5.4 1.4 %collective-permute-start.1 = (f32[1,256]{1,0:T(1,128)}, f32[1,256]{1,0:T(1,128)S(1)}, u32[]{:S(2)}, u32[]{:S(2)}) collective-permute-start(f32[1,256]{1,0:T(1,128)} %bitcast.13), channel_id=1, source_target_pairs={{0,1},{1,0},{2,3},{3,2},{4,5},{5,4},{6,7},{7,6},{8,9},{9,8},{10,11... | collective-permute-start | bytes 3080 | tf_op jit(solution)/shard_map/ppermute | solution.py:341
  6.8 5.9 %collective-permute-start.2 = (bf16[128,544]{1,0:T(8,128)(2,1)S(1)}, bf16[128,544]{1,0:T(8,128)(2,1)S(1)}, u32[]{:S(2)}, u32[]{:S(2)}) collective-permute-start(bf16[128,544]{1,0:T(8,128)(2,1)S(1)} %chip.1.refs_0_), channel_id=1, source_target_pairs={{0,8},{1,3},{2,10},{3,5},{4,12},{5,7},{6,14},{7,1},{8,16},{9,11},{... | collective-permute-start | bytes 417800 | tf_op jit(solution)/shard_map/ppermute | solution.py:322
  8.2 7.4 %collective-permute-start.3 = (bf16[128,544]{1,0:T(8,128)(2,1)S(1)}, bf16[128,544]{1,0:T(8,128)(2,1)S(1)}, u32[]{:S(2)}, u32[]{:S(2)}) collective-permute-start(bf16[128,544]{1,0:T(8,128)(2,1)S(1)} %chip.1.refs_0_), channel_id=1, source_target_pairs={{0,16},{1,5},{2,18},{3,7},{4,20},{5,1},{6,22},{7,3},{8,24},{9,13},... | collective-permute-start | bytes 417800 | tf_op jit(solution)/shard_map/ppermute | solution.py:322
  10.8 4.8 %collective-permute-start.4 = (bf16[128,544]{1,0:T(8,128)(2,1)S(1)}, bf16[128,544]{1,0:T(8,128)(2,1)S(1)}, u32[]{:S(2)}, u32[]{:S(2)}) collective-permute-start(bf16[128,544]{1,0:T(8,128)(2,1)S(1)} %chip.1.refs_0_), channel_id=1, source_target_pairs={{0,24},{1,7},{2,26},{3,1},{4,28},{5,3},{6,30},{7,5},{8,0},{9,15},{... | collective-permute-start | bytes 417800 | tf_op jit(solution)/shard_map/ppermute | solution.py:322
  15.7 5.7 %collective-permute-start.5 = (bf16[128,544]{1,0:T(8,128)(2,1)S(1)}, bf16[128,544]{1,0:T(8,128)(2,1)S(1)}, u32[]{:S(2)}, u32[]{:S(2)}) collective-permute-start(bf16[128,544]{1,0:T(8,128)(2,1)S(1)} %row.1.refs_0_), channel_id=1, source_target_pairs={{0,2},{1,9},{2,4},{3,11},{4,6},{5,13},{6,0},{7,15},{8,10},{9,17},{... | collective-permute-start | bytes 417800 | tf_op jit(solution)/shard_map/ppermute | solution.py:322
  16.7 6.9 %collective-permute-start.6 = (bf16[128,544]{1,0:T(8,128)(2,1)S(1)}, bf16[128,544]{1,0:T(8,128)(2,1)S(1)}, u32[]{:S(2)}, u32[]{:S(2)}) collective-permute-start(bf16[128,544]{1,0:T(8,128)(2,1)S(1)} %row.1.refs_0_), channel_id=1, source_target_pairs={{0,4},{1,17},{2,6},{3,19},{4,0},{5,21},{6,2},{7,23},{8,12},{9,25},... | collective-permute-start | bytes 417800 | tf_op jit(solution)/shard_map/ppermute | solution.py:322
  19.1 4.5 %collective-permute-start.7 = (bf16[128,544]{1,0:T(8,128)(2,1)S(1)}, bf16[128,544]{1,0:T(8,128)(2,1)S(1)}, u32[]{:S(2)}, u32[]{:S(2)}) collective-permute-start(bf16[128,544]{1,0:T(8,128)(2,1)S(1)} %row.1.refs_0_), channel_id=1, source_target_pairs={{0,6},{1,25},{2,0},{3,27},{4,2},{5,29},{6,4},{7,31},{8,14},{9,1},{... | collective-permute-start | bytes 417800 | tf_op jit(solution)/shard_map/ppermute | solution.py:322
  23.7 4.2 %collective-permute-start.8 = (bf16[128,544]{1,0:T(8,128)(2,1)S(1)}, bf16[128,544]{1,0:T(8,128)(2,1)S(1)}, u32[]{:S(2)}, u32[]{:S(2)}) collective-permute-start(bf16[128,544]{1,0:T(8,128)(2,1)S(1)} %plane.1.own_proj_ref), channel_id=1, source_target_pairs={{0,1},{1,0},{2,3},{3,2},{4,5},{5,4},{6,7},{7,6},{8,9},{9,8},{10,11... | collective-permute-start | bytes 417800 | tf_op jit(solution)/shard_map/ppermute | solution.py:341
  30.7 9.3 %copy-start.4 = (bf16[256,256]{1,0:T(8,128)(2,1)S(1)}, bf16[256,256]{1,0:T(8,128)(2,1)}, u32[]{:S(2)}) copy-start(bf16[256,256]{1,0:T(8,128)(2,1)} %residual_ref.3) | copy-start | bytes 393220
  30.7 9.3 %copy-start.6 = (bf16[256,512]{1,0:T(8,128)(2,1)S(1)}, bf16[256,512]{1,0:T(8,128)(2,1)}, u32[]{:S(2)}) copy-start(bf16[256,512]{1,0:T(8,128)(2,1)} %gate_ref.1) | copy-start | bytes 786436
  30.7 9.3 %copy-start.8 = (f32[16,512]{1,0:T(8,128)S(1)}, f32[16,512]{1,0:T(8,128)}, u32[]{:S(2)}) copy-start(f32[16,512]{1,0:T(8,128)} %init_ref.1) | copy-start | bytes 98308
  30.7 9.3 %copy-start.10 = (f32[512]{0:T(512)S(1)}, f32[512]{0:T(512)}, u32[]{:S(2)}) copy-start(f32[512]{0:T(512)} %param.22) | copy-start | bytes 6148
  30.7 9.2 %collective-permute-start.9 = (f32[24,512]{1,0:T(8,128)S(1)}, f32[24,512]{1,0:T(8,128)S(1)}, u32[]{:S(2)}, u32[]{:S(2)}) collective-permute-start(f32[24,512]{1,0:T(8,128)S(1)} %get-tuple-element.32._), channel_id=1, source_target_pairs={{0,32},{32,64},{64,96},{96,0},{1,33},{33,65},{65,97},{97,1},{2,34}... | collective-permute-start | bytes 147464 | tf_op jit(solution)/shard_map/ppermute | solution.py:391
  32.5 7.5 %collective-permute-start.10 = (f32[24,512]{1,0:T(8,128)S(1)}, f32[24,512]{1,0:T(8,128)S(1)}, u32[]{:S(2)}, u32[]{:S(2)}) collective-permute-start(f32[24,512]{1,0:T(8,128)S(1)} %get-tuple-element.32._), channel_id=1, source_target_pairs={{0,64},{32,96},{64,0},{96,32},{1,65},{33,97},{65,1},{97,33},{2,66}... | collective-permute-start | bytes 147464 | tf_op jit(solution)/shard_map/ppermute | solution.py:391
  35.8 4.3 %collective-permute-start.11 = (f32[24,512]{1,0:T(8,128)S(1)}, f32[24,512]{1,0:T(8,128)S(1)}, u32[]{:S(2)}, u32[]{:S(2)}) collective-permute-start(f32[24,512]{1,0:T(8,128)S(1)} %get-tuple-element.32._), channel_id=1, source_target_pairs={{0,96},{32,0},{64,32},{96,64},{1,97},{33,1},{65,33},{97,65},{2,98}... | collective-permute-start | bytes 147464 | tf_op jit(solution)/shard_map/ppermute | solution.py:391
  40.1 6.6 %copy-start.2 = (bf16[256,2048]{1,0:T(8,128)(2,1)S(1)}, bf16[256,2048]{1,0:T(8,128)(2,1)}, u32[]{:S(2)}) copy-start(bf16[256,2048]{1,0:T(8,128)(2,1)} %own_weight_ref.1) | copy-start | bytes 3145732
  45.4 5.1 %collective-permute-start.12 = (bf16[16,128,512]{2,1,0:T(8,128)(2,1)S(1)}, bf16[16,128,512]{2,1,0:T(8,128)(2,1)S(1)}, u32[]{:S(2)}, u32[]{:S(2)}) collective-permute-start(bf16[16,128,512]{2,1,0:T(8,128)(2,1)S(1)} %get-tuple-element.34), channel_id=1, source_target_pairs={{0,1},{1,0},{2,3},{3,2},{4,5},{5,4},{6,7},{7,6},{8,9},{9,8},{10,11... | collective-permute-start | bytes 6291464 | tf_op jit(solution)/shard_map/ppermute | solution.py:341
  46.7 24.9 %collective-permute-start.19 = (bf16[256,2048]{1,0:T(8,128)(2,1)S(1)}, bf16[256,2048]{1,0:T(8,128)(2,1)S(1)}, u32[]{:S(2)}, u32[]{:S(2)}) collective-permute-start(bf16[256,2048]{1,0:T(8,128)(2,1)S(1)} %copy-done.2), channel_id=1, source_target_pairs={{0,1},{1,0},{2,3},{3,2},{4,5},{5,4},{6,7},{7,6},{8,9},{9,8},{10,11... | collective-permute-start | bytes 3145736 | tf_op jit(solution)/shard_map/ppermute | solution.py:341
  51.0 23.6 %copy-start.11 = (f32[256]{0:T(256)S(1)}, f32[256]{0:T(256)}, u32[]{:S(2)}) copy-start(f32[256]{0:T(256)} %param.25) | copy-start | bytes 3076
  51.0 9.6 %collective-permute-start.13 = (bf16[4,128,512]{2,1,0:T(8,128)(2,1)S(1)}, bf16[4,128,512]{2,1,0:T(8,128)(2,1)S(1)}, u32[]{:S(2)}, u32[]{:S(2)}) collective-permute-start(bf16[4,128,512]{2,1,0:T(8,128)(2,1)S(1)} %get-tuple-element.36), channel_id=1, source_target_pairs={{0,8},{1,3},{2,10},{3,5},{4,12},{5,7},{6,14},{7,1},{8,16},{9,11},{... | collective-permute-start | bytes 1572872 | tf_op jit(solution)/shard_map/ppermute | solution.py:322
  52.1 14.8 %collective-permute-start.14 = (bf16[4,128,512]{2,1,0:T(8,128)(2,1)S(1)}, bf16[4,128,512]{2,1,0:T(8,128)(2,1)S(1)}, u32[]{:S(2)}, u32[]{:S(2)}) collective-permute-start(bf16[4,128,512]{2,1,0:T(8,128)(2,1)S(1)} %get-tuple-element.37), channel_id=1, source_target_pairs={{0,16},{1,5},{2,18},{3,7},{4,20},{5,1},{6,22},{7,3},{8,24},{9,13},... | collective-permute-start | bytes 1572872 | tf_op jit(solution)/shard_map/ppermute | solution.py:322
  54.5 12.5 %collective-permute-start.15 = (bf16[4,128,512]{2,1,0:T(8,128)(2,1)S(1)}, bf16[4,128,512]{2,1,0:T(8,128)(2,1)S(1)}, u32[]{:S(2)}, u32[]{:S(2)}) collective-permute-start(bf16[4,128,512]{2,1,0:T(8,128)(2,1)S(1)} %get-tuple-element.38), channel_id=1, source_target_pairs={{0,24},{1,7},{2,26},{3,1},{4,28},{5,3},{6,30},{7,5},{8,0},{9,15},{... | collective-permute-start | bytes 1572872 | tf_op jit(solution)/shard_map/ppermute | solution.py:322
  67.2 5.1 %collective-permute-start.16 = (bf16[128,512]{1,0:T(8,128)(2,1)S(1)}, bf16[128,512]{1,0:T(8,128)(2,1)S(1)}, u32[]{:S(2)}, u32[]{:S(2)}) collective-permute-start(bf16[128,512]{1,0:T(8,128)(2,1)S(1)} %get-tuple-element.40), channel_id=1, source_target_pairs={{0,2},{1,9},{2,4},{3,11},{4,6},{5,13},{6,0},{7,15},{8,10},{9,17},{... | collective-permute-start | bytes 393224 | tf_op jit(solution)/shard_map/ppermute | solution.py:322
  68.5 6.0 %collective-permute-start.17 = (bf16[128,512]{1,0:T(8,128)(2,1)S(1)}, bf16[128,512]{1,0:T(8,128)(2,1)S(1)}, u32[]{:S(2)}, u32[]{:S(2)}) collective-permute-start(bf16[128,512]{1,0:T(8,128)(2,1)S(1)} %get-tuple-element.41), channel_id=1, source_target_pairs={{0,4},{1,17},{2,6},{3,19},{4,0},{5,21},{6,2},{7,23},{8,12},{9,25},... | collective-permute-start | bytes 393224 | tf_op jit(solution)/shard_map/ppermute | solution.py:322
  70.7 3.8 %collective-permute-start.18 = (bf16[128,512]{1,0:T(8,128)(2,1)S(1)}, bf16[128,512]{1,0:T(8,128)(2,1)S(1)}, u32[]{:S(2)}, u32[]{:S(2)}) collective-permute-start(bf16[128,512]{1,0:T(8,128)(2,1)S(1)} %get-tuple-element.42), channel_id=1, source_target_pairs={{0,6},{1,25},{2,0},{3,27},{4,2},{5,29},{6,4},{7,31},{8,14},{9,1},{... | collective-permute-start | bytes 393224 | tf_op jit(solution)/shard_map/ppermute | solution.py:322
  74.5 32.2 %copy-start.12 = (s32[128]{0:T(128)S(1)}, s32[128]{0:T(128)}, u32[]{:S(2)}) copy-start(s32[128]{0:T(128)} %param.29) | copy-start | bytes 1540
  74.5 32.2 %copy-start.13 = (s32[128]{0:T(128)S(1)}, s32[128]{0:T(128)}, u32[]{:S(2)}) copy-start(s32[128]{0:T(128)} %param.27) | copy-start | bytes 1540
  74.5 32.2 %copy-start.14 = (s32[128]{0:T(128)S(1)}, s32[128]{0:T(128)}, u32[]{:S(2)}) copy-start(s32[128]{0:T(128)} %param.28) | copy-start | bytes 1540
  76.3 5.3 %collective-permute-start.20 = (bf16[4,144,128]{2,1,0:T(8,128)(2,1)S(1)}, bf16[4,144,128]{2,1,0:T(8,128)(2,1)S(1)}, u32[]{:S(2)}, u32[]{:S(2)}) collective-permute-start(bf16[4,144,128]{2,1,0:T(8,128)(2,1)S(1)} %get-tuple-element.45), channel_id=1, source_target_pairs={{0,8},{1,3},{2,10},{3,5},{4,12},{5,7},{6,14},{7,1},{8,16},{9,11},{... | collective-permute-start | bytes 442376 | tf_op jit(solution)/shard_map/ppermute | solution.py:322
  78.0 6.2 %collective-permute-start.21 = (bf16[4,144,128]{2,1,0:T(8,128)(2,1)S(1)}, bf16[4,144,128]{2,1,0:T(8,128)(2,1)S(1)}, u32[]{:S(2)}, u32[]{:S(2)}) collective-permute-start(bf16[4,144,128]{2,1,0:T(8,128)(2,1)S(1)} %get-tuple-element.46), channel_id=1, source_target_pairs={{0,16},{1,5},{2,18},{3,7},{4,20},{5,1},{6,22},{7,3},{8,24},{9,13},... | collective-permute-start | bytes 442376 | tf_op jit(solution)/shard_map/ppermute | solution.py:322
  80.1 4.3 %collective-permute-start.22 = (bf16[4,144,128]{2,1,0:T(8,128)(2,1)S(1)}, bf16[4,144,128]{2,1,0:T(8,128)(2,1)S(1)}, u32[]{:S(2)}, u32[]{:S(2)}) collective-permute-start(bf16[4,144,128]{2,1,0:T(8,128)(2,1)S(1)} %get-tuple-element.47), channel_id=1, source_target_pairs={{0,24},{1,7},{2,26},{3,1},{4,28},{5,3},{6,30},{7,5},{8,0},{9,15},{... | collective-permute-start | bytes 442376 | tf_op jit(solution)/shard_map/ppermute | solution.py:322
  84.5 9.9 %collective-permute-start.23 = (bf16[4,144,128]{2,1,0:T(8,128)(2,1)S(1)}, bf16[4,144,128]{2,1,0:T(8,128)(2,1)S(1)}, u32[]{:S(2)}, u32[]{:S(2)}) collective-permute-start(bf16[4,144,128]{2,1,0:T(8,128)(2,1)S(1)} %kv.1.own_part_ref), channel_id=1, source_target_pairs={{0,2},{1,9},{2,4},{3,11},{4,6},{5,13},{6,0},{7,15},{8,10},{9,17},{... | collective-permute-start | bytes 442376 | tf_op jit(solution)/shard_map/ppermute | solution.py:322
  85.7 8.7 %collective-permute-start.24 = (bf16[4,144,128]{2,1,0:T(8,128)(2,1)S(1)}, bf16[4,144,128]{2,1,0:T(8,128)(2,1)S(1)}, u32[]{:S(2)}, u32[]{:S(2)}) collective-permute-start(bf16[4,144,128]{2,1,0:T(8,128)(2,1)S(1)} %kv.1.own_part_ref), channel_id=1, source_target_pairs={{0,4},{1,17},{2,6},{3,19},{4,0},{5,21},{6,2},{7,23},{8,12},{9,25},... | collective-permute-start | bytes 442376 | tf_op jit(solution)/shard_map/ppermute | solution.py:322
  87.8 6.6 %collective-permute-start.25 = (bf16[4,144,128]{2,1,0:T(8,128)(2,1)S(1)}, bf16[4,144,128]{2,1,0:T(8,128)(2,1)S(1)}, u32[]{:S(2)}, u32[]{:S(2)}) collective-permute-start(bf16[4,144,128]{2,1,0:T(8,128)(2,1)S(1)} %kv.1.own_part_ref), channel_id=1, source_target_pairs={{0,6},{1,25},{2,0},{3,27},{4,2},{5,29},{6,4},{7,31},{8,14},{9,1},{... | collective-permute-start | bytes 442376 | tf_op jit(solution)/shard_map/ppermute | solution.py:322
  88.5 5.9 %collective-permute-start.26 = (bf16[128,256]{1,0:T(8,128)(2,1)S(1)}, bf16[128,256]{1,0:T(8,128)(2,1)S(1)}, u32[]{:S(2)}, u32[]{:S(2)}) collective-permute-start(bf16[128,256]{1,0:T(8,128)(2,1)S(1)} %get-tuple-element.49), channel_id=1, source_target_pairs={{0,1},{1,0},{2,3},{3,2},{4,5},{5,4},{6,7},{7,6},{8,9},{9,8},{10,11... | collective-permute-start | bytes 196616 | tf_op jit(solution)/shard_map/ppermute | solution.py:341
  95.7 5.0 %collective-permute-start.27 = (bf16[4,128,128]{2,1,0:T(8,128)(2,1)S(1)}, bf16[4,128,128]{2,1,0:T(8,128)(2,1)S(1)}, u32[]{:S(2)}, u32[]{:S(2)}) collective-permute-start(bf16[4,128,128]{2,1,0:T(8,128)(2,1)S(1)} %get-tuple-element.51.own_ref), channel_id=1, source_target_pairs={{0,32},{32,64},{64,96},{96,0},{1,33},{33,65},{65,97},{97,1},{2,34}... | collective-permute-start | bytes 393224 | tf_op jit(solution)/shard_map/ppermute | solution.py:391
  96.4 5.7 %collective-permute-start.28 = (bf16[4,128,128]{2,1,0:T(8,128)(2,1)S(1)}, bf16[4,128,128]{2,1,0:T(8,128)(2,1)S(1)}, u32[]{:S(2)}, u32[]{:S(2)}) collective-permute-start(bf16[4,128,128]{2,1,0:T(8,128)(2,1)S(1)} %get-tuple-element.51.own_ref), channel_id=1, source_target_pairs={{0,64},{32,96},{64,0},{96,32},{1,65},{33,97},{65,1},{97,33},{2,66}... | collective-permute-start | bytes 393224 | tf_op jit(solution)/shard_map/ppermute | solution.py:391
  98.3 4.4 %collective-permute-start.29 = (bf16[4,128,128]{2,1,0:T(8,128)(2,1)S(1)}, bf16[4,128,128]{2,1,0:T(8,128)(2,1)S(1)}, u32[]{:S(2)}, u32[]{:S(2)}) collective-permute-start(bf16[4,128,128]{2,1,0:T(8,128)(2,1)S(1)} %get-tuple-element.51.own_ref), channel_id=1, source_target_pairs={{0,96},{32,0},{64,32},{96,64},{1,97},{33,1},{65,33},{97,65},{2,98}... | collective-permute-start | bytes 393224 | tf_op jit(solution)/shard_map/ppermute | solution.py:391
  103.3 14.9 %collective-permute-start.30 = (bf16[4,4,128,128]{3,2,1,0:T(8,128)(2,1)S(1)}, bf16[4,4,128,128]{3,2,1,0:T(8,128)(2,1)S(1)}, u32[]{:S(2)}, u32[]{:S(2)}) collective-permute-start(bf16[4,4,128,128]{3,2,1,0:T(8,128)(2,1)S(1)} %stack.25.q0), channel_id=1, source_target_pairs={{0,8},{1,3},{2,10},{3,5},{4,12},{5,7},{6,14},{7,1},{8,16},{9,11},{... | collective-permute-start | bytes 1572872 | tf_op jit(solution)/shard_map/ppermute | solution.py:322
  104.3 13.9 %collective-permute-start.31 = (bf16[4,4,128,128]{3,2,1,0:T(8,128)(2,1)S(1)}, bf16[4,4,128,128]{3,2,1,0:T(8,128)(2,1)S(1)}, u32[]{:S(2)}, u32[]{:S(2)}) collective-permute-start(bf16[4,4,128,128]{3,2,1,0:T(8,128)(2,1)S(1)} %stack.25.q0), channel_id=1, source_target_pairs={{0,16},{1,5},{2,18},{3,7},{4,20},{5,1},{6,22},{7,3},{8,24},{9,13},... | collective-permute-start | bytes 1572872 | tf_op jit(solution)/shard_map/ppermute | solution.py:322
  105.1 14.0 %collective-permute-start.32 = (bf16[4,4,128,128]{3,2,1,0:T(8,128)(2,1)S(1)}, bf16[4,4,128,128]{3,2,1,0:T(8,128)(2,1)S(1)}, u32[]{:S(2)}, u32[]{:S(2)}) collective-permute-start(bf16[4,4,128,128]{3,2,1,0:T(8,128)(2,1)S(1)} %stack.25.q0), channel_id=1, source_target_pairs={{0,24},{1,7},{2,26},{3,1},{4,28},{5,3},{6,30},{7,5},{8,0},{9,15},{... | collective-permute-start | bytes 1572872 | tf_op jit(solution)/shard_map/ppermute | solution.py:322
  119.9 8.4 %collective-permute-start.33 = (bf16[2,16,128,128]{3,2,1,0:T(8,128)(2,1)S(1)}, bf16[2,16,128,128]{3,2,1,0:T(8,128)(2,1)S(1)}, u32[]{:S(2)}, u32[]{:S(2)}) collective-permute-start(bf16[2,16,128,128]{3,2,1,0:T(8,128)(2,1)S(1)} %pick.1), channel_id=1, source_target_pairs={{0,1},{1,0},{2,3},{3,2},{4,5},{5,4},{6,7},{7,6},{8,9},{9,8},{10,11... | collective-permute-start | bytes 3145736 | tf_op jit(solution)/shard_map/ppermute | solution.py:341
  (1 other events, 1.0 us)

commit v4 on v3

--- a/solution.py
+++ b/solution.py
@@ -1,3 +1,5 @@
+import functools
+
 import jax
 import jax.numpy as jnp
 from jax import lax
@@ -17,6 +19,7 @@
 CHUNK = 32
 PIECES = 8
 SIDE = 4
+EARLY, LATE = 1, (2, 3)
 BF = jnp.bfloat16
 F32 = jnp.float32
 
@@ -29,13 +32,17 @@
     return pltpu.CompilerParams(vmem_limit_bytes=mib * 1024 * 1024)
 
 
-def project_kernel(place_ref, conv_ref, weight_ref, kept_ref, give_ref):
-    rows = kept_ref.shape[0]
-    for ref, half in ((give_ref, 1 - place_ref[1]), (kept_ref, place_ref[1])):
-        ref[...] = lax.dot_general(
-            conv_ref[pl.ds(pl.multiple_of(half * rows, rows), rows), :], weight_ref[...],
-            (((1,), (1,)), ((), ())), preferred_element_type=F32,
-        ).astype(ref.dtype)
+def project_kernel(give, place_ref, conv_ref, weight_ref, out_ref):
+    half = 1 - place_ref[1] if give else place_ref[1]
+    conv = conv_ref[pl.ds(pl.multiple_of(half * BLK, BLK), BLK), :]
+    both = (((1,), (1,)), ((), ()))
+    out_ref[:BLK, :] = lax.dot_general(
+        conv, weight_ref[:DTR, :], both, preferred_element_type=F32
+    ).astype(out_ref.dtype)
+    states = lax.dot_general(weight_ref[DTR:, :], conv, both, preferred_element_type=F32)
+    packed = [states[i * 8 : (i + 1) * 8, :] for i in range(DTR // BLK)]
+    packed = jnp.concatenate(packed, axis=1)
+    out_ref[BLK:, :] = jnp.concatenate([packed, jnp.zeros_like(packed)], axis=0).astype(out_ref.dtype)
 
 
 def add_kernel(*refs):
@@ -66,18 +73,20 @@
 
 def first_kernel(
     place_ref, own_proj_ref, got_proj_ref, weight_ref, bias_ref, alog_ref, conv_ref,
-    step_ref, states_ref, ends_ref, proj_ref, wide_ref, drive_ref,
+    step_ref, states_ref, ends_ref, proj_ref, drive_ref,
 ):
+    tokens = step_ref.shape[0]
     for ref, half in ((own_proj_ref, place_ref[1]), (got_proj_ref, 1 - place_ref[1])):
-        rows = ref.shape[0]
-        proj_ref[pl.ds(pl.multiple_of(half * rows, rows), rows), :] = ref[...]
-    tokens = step_ref.shape[0]
-    wide_ref[:, : 2 * STATE] = proj_ref[:, DTR:].astype(F32)
-    flipped = jnp.transpose(wide_ref[...])
-    for block in range(tokens // CHUNK):
-        states_ref[block] = flipped[: 2 * STATE, block * CHUNK : (block + 1) * CHUNK]
+        proj_ref[pl.ds(pl.multiple_of(half * BLK, BLK), BLK), :] = ref[:BLK, :]
+        packed = ref[BLK:, :].astype(F32)
+        for group in range(DTR // BLK):
+            for block in range(BLK // CHUNK):
+                at = group * BLK + block * CHUNK
+                states_ref[half * (BLK // CHUNK) + block, group * 8 : (group + 1) * 8, :] = (
+                    packed[:8, at : at + CHUNK]
+                )
     step = jax.nn.softplus(
-        jnp.dot(proj_ref[:, :DTR], weight_ref[...], preferred_element_type=F32) + bias_ref[...]
+        jnp.dot(proj_ref[...], weight_ref[...], preferred_element_type=F32) + bias_ref[...]
     )
     step_ref[...] = step
     drive_ref[...] = step * conv_ref[...].astype(F32)
@@ -175,8 +184,9 @@
 
 def layer_kernel(
     place_ref, own_part_ref, one_ref, two_ref, three_ref, residual_ref, own_gain_ref,
-    got_gain_ref, own_weight_ref, got_weight_ref, own_ref, other_ref, *out_refs,
+    got_gain_ref, own_weight_ref, got_weight_ref, own_ref, other_ref, *rest,
 ):
+    *out_refs, term_ref = rest
     mixed = own_part_ref[...]
     for ref in (one_ref, two_ref, three_ref):
         mixed = mixed + ref[...].astype(F32)
@@ -193,23 +203,25 @@
         layer = piece.astype(BF)
         layer_ref[...] = layer
         stream = layer.astype(F32)
-        squares = squares + lax.dot_general(
-            jnp.ones((16, half), F32), stream * stream, (((1,), (1,)), ((), ())),
-            preferred_element_type=F32, precision=lax.Precision.HIGHEST,
-        )
+        square = stream * stream
+        upper = square.astype(BF)
+        for value in (upper, (square - upper.astype(F32)).astype(BF)):
+            squares = squares + lax.dot_general(
+                jnp.ones((16, half), BF), value, (((1,), (1,)), ((), ())),
+                preferred_element_type=F32,
+            )
         term = term + jnp.dot(
             (stream * gain_ref[...]).astype(BF), weight_ref[...], preferred_element_type=F32
         )
-    term, squares = term.astype(BF), squares.astype(BF)
-    for j in range(2 * KVH):
-        far, _ = chip_order(place_ref, place_ref[1], j)
-        second = jnp.where(place_ref[1] == 0, j % SIDE, j // SIDE)
-        for shift, ref in enumerate(out_refs):
-
-            @pl.when(far == shift)
-            def _(ref=ref, second=second, j=j):
-                ref[second, :BLK, :] = term[:, j * HEAD : (j + 1) * HEAD]
-                ref[second, BLK:, :] = squares
+    term_ref[...] = term.astype(BF)
+    squares = squares.astype(BF)
+    first_axis = jnp.where(first, place_ref[3], place_ref[4])
+    for shift, ref in enumerate(out_refs):
+        far = lax.rem(first_axis + shift, SIDE)
+        for second in range(SIDE):
+            j = jnp.where(first, far * SIDE + second, second * SIDE + far)
+            ref[second, :BLK, :] = term_ref[:, pl.ds(pl.multiple_of(j * HEAD, HEAD), HEAD)]
+            ref[second, BLK:, :] = squares
 
 
 def tile_kernel(
@@ -228,17 +240,36 @@
 
 
 def choose(place_ref, target, starts_ref, counts_ref, sources, out_ref):
-    core = place_ref[1]
     first, count = starts_ref[target], counts_ref[target]
-    slot = lax.rem(core + first, 2)
-    for far, ref in enumerate(sources):
-        first_axis = lax.rem(jnp.where(core == 0, place_ref[3], place_ref[4]) + SIDE - far, SIDE)
+    slot = lax.rem(place_ref[1] + first, 2)
+    for i, ref in enumerate(sources):
         for second in range(SIDE):
-            column = jnp.where(core == 0, first_axis * SIDE + second, second * SIDE + first_axis)
             for k in range(2):
                 at = slot + 2 * k
                 tile = ref[jnp.minimum((first + at) // 2, SIDE - 1), second]
-                out_ref[k, column] = jnp.where(at < count, tile, jnp.zeros_like(tile))
+                out_ref[k, i * SIDE + second] = jnp.where(at < count, tile, jnp.zeros_like(tile))
+
+
+def to_cache(place_ref, starts_ref, core, source_refs, cache_ref, sems):
+    slot = lax.rem(core + starts_ref[place_ref[2]], 2)
+    waits = []
+    for i, shift in enumerate((0, EARLY, *LATE)):
+        source_ref = source_refs[i // (SIDE // len(source_refs))]
+        first_axis = lax.rem(jnp.where(core == 0, place_ref[3], place_ref[4]) + SIDE - shift, SIDE)
+        at = i * SIDE % source_ref.shape[1]
+        for k in range(2):
+            part = source_ref.at[k, pl.ds(at, SIDE)]
+            along_y = pltpu.make_async_copy(
+                part, cache_ref.at[slot + 2 * k, first_axis], sems.at[k, i]
+            )
+            along_x = pltpu.make_async_copy(
+                part, cache_ref.at[slot + 2 * k, :, first_axis], sems.at[k, i]
+            )
+            pl.when(core == 0)(along_y.start)
+            pl.when(core == 1)(along_x.start)
+            waits.append(along_y)
+    for copy in waits:
+        copy.wait()
 
 
 def stack_kernel(place_ref, own_ref, near_ref, mid_ref, far_ref, out_ref):
@@ -246,38 +277,18 @@
         out_ref[lax.rem(place_ref[0] + SIDE - back, SIDE)] = ref[...]
 
 
-def pick_kernel(place_ref, starts_ref, counts_ref, q0, q1, q2, q3, out_ref):
-    device = place_ref[2]
-    partner = device + 1 - 2 * place_ref[1]
-    choose(place_ref, partner, starts_ref, counts_ref, (q0, q1, q2, q3), out_ref)
-
-
-def slot_copies(place_ref, starts_ref, parity, source_ref, cache_ref, sems):
-    slot = lax.rem(parity + starts_ref[place_ref[2]], 2)
-    return [
-        pltpu.make_async_copy(source_ref.at[k], cache_ref.at[slot + 2 * k], sems.at[k])
-        for k in range(2)
-    ]
-
-
-def own_kernel(
-    place_ref, starts_ref, counts_ref, q0, q1, q2, q3, cache_ref, held_ref, sems
-):
-    core = place_ref[1]
+def pick_kernel(place_ref, starts_ref, counts_ref, one_ref, two_ref, out_ref):
+    partner = place_ref[2] + 1 - 2 * place_ref[1]
+    choose(place_ref, partner, starts_ref, counts_ref, (one_ref, two_ref), out_ref)
+
+
+def own_kernel(place_ref, starts_ref, counts_ref, q0, q1, q2, q3, cache_ref, held_ref, sems):
     choose(place_ref, place_ref[2], starts_ref, counts_ref, (q0, q1, q2, q3), held_ref)
-    copies = slot_copies(place_ref, starts_ref, core, held_ref, cache_ref, sems)
-    for copy in copies:
-        copy.start()
-    for copy in copies:
-        copy.wait()
-
-
-def rest_kernel(place_ref, starts_ref, got_ref, _, cache_ref, sems):
-    copies = slot_copies(place_ref, starts_ref, 1 - place_ref[1], got_ref, cache_ref, sems)
-    for copy in copies:
-        copy.start()
-    for copy in copies:
-        copy.wait()
+    to_cache(place_ref, starts_ref, place_ref[1], (held_ref,), cache_ref, sems)
+
+
+def rest_kernel(place_ref, starts_ref, one_ref, two_ref, _, cache_ref, sems):
+    to_cache(place_ref, starts_ref, 1 - place_ref[1], (one_ref, two_ref), cache_ref, sems)
 
 
 def shape(dims, kind):
@@ -346,7 +357,6 @@
     matches = owner[:, None] == jnp.arange(devices, dtype=jnp.int32)[None, :]
     starts = jnp.sum(jnp.where(matches, block_start[:, None], 0), axis=0)
     counts = jnp.sum(jnp.where(matches, block_count[:, None], 0), axis=0)
-    columns = DTR + 2 * STATE
 
     def add(name, kind, *values):
         return pl.pallas_call(
@@ -356,14 +366,17 @@
             name=name,
         )(*values)
 
-    rows = (tokens // 2, columns)
-    kept_share, give_share = pl.pallas_call(
-        project_kernel,
-        in_specs=[SM] + [VM] * 2,
-        out_shape=(shape(rows, F32), shape(rows, BF)),
-        compiler_params=params(8),
-        name="project",
-    )(places, conv_out, xproj_weight.T)
+    def project(name, give, kind):
+        return pl.pallas_call(
+            functools.partial(project_kernel, give),
+            in_specs=[SM] + [VM] * 2,
+            out_shape=shape((BLK + 16, DTR), kind),
+            compiler_params=params(8),
+            name=name,
+        )(places, conv_out, xproj_weight.T)
+
+    give_share = project("project_give", True, BF)
+    kept_share = project("project_keep", False, F32)
     got_share, got_gain = lax.optimization_barrier((swap(give_share), got_gain))
     chip = add("chip", BF, kept_share, got_share)
     row = add("row", BF, chip, *line(0, lambda shift: chip))
@@ -379,8 +392,7 @@
         ),
         in_specs=[SM] + [VM] * 6,
         scratch_shapes=[
-            pltpu.VMEM((tokens, columns), BF),
-            pltpu.VMEM((tokens, 128), F32),
+            pltpu.VMEM((tokens, DTR), BF),
             pltpu.VMEM((tokens, chans), F32),
         ],
         compiler_params=params(8),
@@ -442,6 +454,7 @@
         layer_kernel,
         in_specs=[SM] + [VM] * 9,
         out_shape=(block_shape,) * 2 + (shape((SIDE, BLK + 16, HEAD), BF),) * SIDE,
+        scratch_shapes=[pltpu.VMEM((tokens // 2, 2 * KVH * HEAD), BF)],
         compiler_params=params(8),
         name="layer",
     )(places, *parts, residual, own_gain, got_gain, kv_weight, got_weight)
@@ -462,35 +475,45 @@
         name="stack",
     )(places, tile, *ranges_back(tile))
     everything = [stacked] + line(0, lambda shift: stacked)
-    half_cache = shape((2, 2 * KVH, BLK, HEAD), BF)
-    give_tiles = pl.pallas_call(
-        pick_kernel,
-        in_specs=[SM] * 3 + [VM] * SIDE,
-        out_shape=half_cache,
-        compiler_params=params(8),
-        name="pick",
-    )(places, starts, counts, *everything)
-    got_tiles = swap(give_tiles)
+    chosen = (2, 2 * SIDE, BLK, HEAD)
+    sems = pltpu.SemaphoreType.DMA((2, SIDE))
+    cache_shape = shape((CAP, SIDE, SIDE, BLK, HEAD), BF)
+
+    def for_partner(name, *sources):
+        return swap(
+            pl.pallas_call(
+                pick_kernel,
+                in_specs=[SM] * 3 + [VM] * 2,
+                out_shape=shape(chosen, BF),
+                compiler_params=params(4),
+                name=name,
+            )(places, starts, counts, *sources)
+        )
+
+    got_first = for_partner("pick0", everything[0], everything[EARLY])
+    *late, got_first = lax.optimization_barrier((*[everything[i] for i in LATE], got_first))
+    everything = [everything[0], everything[EARLY], *late]
+    got_last = for_partner("pick1", *late)
     kv_cache = pl.pallas_call(
         own_kernel,
         in_specs=[SM] * 3 + [VM] * SIDE,
         out_specs=ANY,
-        out_shape=shape((CAP, 2 * KVH, BLK, HEAD), BF),
-        scratch_shapes=[pltpu.VMEM(half_cache.shape, BF), pltpu.SemaphoreType.DMA((2,))],
+        out_shape=cache_shape,
+        scratch_shapes=[pltpu.VMEM((2, 4 * SIDE, BLK, HEAD), BF), sems],
         compiler_params=params(8),
         name="own",
     )(places, starts, counts, *everything)
     kv_cache = pl.pallas_call(
         rest_kernel,
-        in_specs=[SM] * 2 + [VM, ANY],
+        in_specs=[SM] * 2 + [VM, VM, ANY],
         out_specs=ANY,
-        out_shape=shape((CAP, 2 * KVH, BLK, HEAD), BF),
-        input_output_aliases={3: 0},
-        scratch_shapes=[pltpu.SemaphoreType.DMA((2,))],
+        out_shape=cache_shape,
+        input_output_aliases={4: 0},
+        scratch_shapes=[sems],
         compiler_params=params(4),
         name="rest",
-    )(places, starts, got_tiles, kv_cache)
-    return (layer_out, kv_cache[None])
+    )(places, starts, got_first, got_last, kv_cache)
+    return (layer_out, kv_cache.reshape(1, CAP, 2 * KVH, BLK, HEAD))
 
 
 def solution(mesh):

time: 130 us -> 129 us (level)
  starting transfers between devices: 56.8 us -> 55.2 us
    pallas_call x3 -> x5, Pallas kernels: 3.4 us -> 4.66 us  [the longest x2 1.71 us: project(): pl.pallas_call(functools.partial(project_kernel, give), in_specs=[SM] + [...]
    ppermute x7 -> x8, starting transfers between devices: 17.2 us -> 16.3 us  [swap(): return lax.ppermute(value, 'tp', partner)]
    ppermute x7 -> x8, waiting for transfers between devices: 5.56 us -> 5.72 us  [swap(): return lax.ppermute(value, 'tp', partner)]
  transfers between devices with their start and end apart: 34 -> 35, of which waited for: 22 -> 21; matrix products, arithmetic and copies ran while one was open for 0% -> 0% of each run, Pallas kernels for 6% -> 7%
where the time goes in v4:
time: 129 us; the launch traced here: 128 us
  starting transfers between devices  55.2 us (43%)
  waiting for transfers between devices  45.8 us (36%)
  Pallas kernels  24.1 us (19%)
  local copies, waits for them, and re-layouts  2.15 us (2%)
    ppermute x21, waiting for transfers between devices, line(): lax.ppermute(value_of(shift), 'tp', [((x * SIDE + y) * 2 + c, ((x + shift...  36.2 us
    ppermute x21, starting transfers between devices, line(): lax.ppermute(value_of(shift), 'tp', [((x * SIDE + y) * 2 + c, ((x + shift...  30.1 us
    ppermute x8, starting transfers between devices, swap(): return lax.ppermute(value, 'tp', partner)  16.3 us
    ppermute x6, starting transfers between devices, ranges_back(): lax.ppermute(value, 'ctx', [(z, (z + s) % ctx_count) for z in range(ctx_c...  8.86 us
    ppermute x8, waiting for transfers between devices, swap(): return lax.ppermute(value, 'tp', partner)  5.72 us
    pallas_call x1, Pallas kernels, per_device(): pl.pallas_call(give_kernel, in_specs=[SM] + [VM] * 12, out_shape=(shape(p...  5.33 us
    ppermute x6, waiting for transfers between devices, ranges_back(): lax.ppermute(value, 'ctx', [(z, (z + s) % ctx_count) for z in range(ctx_c...  3.89 us
    pallas_call x1, Pallas kernels, per_device(): pl.pallas_call(bring_kernel, in_specs=[ANY] * 2, out_shape=shape(out_weig...  3.5 us
  transfers between devices with their start and end apart: 35, of which 21 were waited for; matrix products, arithmetic and copies ran while one was open for 0% of the time, Pallas kernels for 7%

profile of v4, /device:TPU:1, one launch (start us, length us, event | category | flops | bytes accessed | tf_op | source)
XLA Modules:
  0.0 128.5 jit_solution(9928574386722707156)
XLA Ops:
  0.8 0.9 copy-done
  1.7 1.1 copy-done.2
  3.6 1.5 %collective-permute-start = (bf16[144,512]{1,0:T(8,128)(2,1)S(1)}, bf16[144,512]{1,0:T(8,128)(2,1)S(1)}, u32[]{:S(2)}, u32[]{:S(2)}) collective-permute-start(bf16[144,512]{1,0:T(8,128)(2,1)S(1)} %project_give.1), channel_id=1, source_target_pairs={{0,1},{1,0},{2,3},{3,2},{4,5},{5,4},{6,7},{7,6},{8,9},{9,8},{10,11... | collective-permute-start | bytes 442376 | tf_op jit(solution)/shard_map/ppermute | solution.py:352
  6.5 1.4 %collective-permute-start.2 = (bf16[144,512]{1,0:T(8,128)(2,1)S(1)}, bf16[144,512]{1,0:T(8,128)(2,1)S(1)}, u32[]{:S(2)}, u32[]{:S(2)}) collective-permute-start(bf16[144,512]{1,0:T(8,128)(2,1)S(1)} %chip.1.refs_0_), channel_id=1, source_target_pairs={{0,8},{1,3},{2,10},{3,5},{4,12},{5,7},{6,14},{7,1},{8,16},{9,11},{... | collective-permute-start | bytes 442376 | tf_op jit(solution)/shard_map/ppermute | solution.py:333
  8.0 2.6 %collective-permute-start.3 = (bf16[144,512]{1,0:T(8,128)(2,1)S(1)}, bf16[144,512]{1,0:T(8,128)(2,1)S(1)}, u32[]{:S(2)}, u32[]{:S(2)}) collective-permute-start(bf16[144,512]{1,0:T(8,128)(2,1)S(1)} %chip.1.refs_0_), channel_id=1, source_target_pairs={{0,16},{1,5},{2,18},{3,7},{4,20},{5,1},{6,22},{7,3},{8,24},{9,13},... | collective-permute-start | bytes 442376 | tf_op jit(solution)/shard_map/ppermute | solution.py:333
  10.6 1.1 collective-permute-start.4
  12.2 2.8 %collective-permute-done.3.refs_2_ = bf16[144,512]{1,0:T(8,128)(2,1)S(1)} collective-permute-done((bf16[144,512]{1,0:T(8,128)(2,1)S(1)}, bf16[144,512]{1,0:T(8,128)(2,1)S(1)}, u32[]{:S(2)}, u32[]{:S(2)}) %collective-permute-start.3) | collective-permute-done | bytes 147488 | tf_op jit(solution)/shard_map/ppermute | solution.py:333
  15.1 1.2 collective-permute-start.5
  16.3 2.4 %collective-permute-start.6 = (bf16[144,512]{1,0:T(8,128)(2,1)S(1)}, bf16[144,512]{1,0:T(8,128)(2,1)S(1)}, u32[]{:S(2)}, u32[]{:S(2)}) collective-permute-start(bf16[144,512]{1,0:T(8,128)(2,1)S(1)} %row.1.refs_0_), channel_id=1, source_target_pairs={{0,4},{1,17},{2,6},{3,19},{4,0},{5,21},{6,2},{7,23},{8,12},{9,25},... | collective-permute-start | bytes 442376 | tf_op jit(solution)/shard_map/ppermute | solution.py:333
  18.7 1.2 collective-permute-start.7
  20.4 2.4 %collective-permute-done.6.refs_2_ = bf16[144,512]{1,0:T(8,128)(2,1)S(1)} collective-permute-done((bf16[144,512]{1,0:T(8,128)(2,1)S(1)}, bf16[144,512]{1,0:T(8,128)(2,1)S(1)}, u32[]{:S(2)}, u32[]{:S(2)}) %collective-permute-start.6) | collective-permute-done | bytes 147488 | tf_op jit(solution)/shard_map/ppermute | solution.py:333
  22.9 3.3 %collective-permute-start.8 = (bf16[144,512]{1,0:T(8,128)(2,1)S(1)}, bf16[144,512]{1,0:T(8,128)(2,1)S(1)}, u32[]{:S(2)}, u32[]{:S(2)}) collective-permute-start(bf16[144,512]{1,0:T(8,128)(2,1)S(1)} %plane.1.own_proj_ref), channel_id=1, source_target_pairs={{0,1},{1,0},{2,3},{3,2},{4,5},{5,4},{6,7},{7,6},{8,9},{9,8},{10,11... | collective-permute-start | bytes 442376 | tf_op jit(solution)/shard_map/ppermute | solution.py:352
  26.2 1.0 collective-permute-done.8.got_proj_ref
  27.2 2.8 %first.1 = (f32[256,512]{1,0:T(8,128)S(1)}, f32[8,32,32]{2,1,0:T(8,128)S(1)}, f32[24,512]{1,0:T(8,128)S(1)}) custom-call(s32[5]{0:T(128)S(1)} %stack.24.place_ref, bf16[144,512]{1,0:T(8,128)(2,1)S(1)} %plane.1.own_proj_ref, bf16[144,512]{1,0:T(8,128)(2,1)S(1)} %collective-permute-done.8.got_proj_ref, bf16[512,512]{1,0:T(8,128)(2,1)S(1)} %copy-done.5, ...), custom_call_target="tpu_custom_call" | custom-call | tf_op jit(solution)/shard_map/first/pallas_call | solution.py:386
  30.1 1.7 %collective-permute-start.9 = (f32[24,512]{1,0:T(8,128)S(1)}, f32[24,512]{1,0:T(8,128)S(1)}, u32[]{:S(2)}, u32[]{:S(2)}) collective-permute-start(f32[24,512]{1,0:T(8,128)S(1)} %get-tuple-element.31._), channel_id=1, source_target_pairs={{0,32},{32,64},{64,96},{96,0},{1,33},{33,65},{65,97},{97,1},{2,34}... | collective-permute-start | bytes 147464 | tf_op jit(solution)/shard_map/ppermute | solution.py:403
  31.8 3.3 %collective-permute-start.10 = (f32[24,512]{1,0:T(8,128)S(1)}, f32[24,512]{1,0:T(8,128)S(1)}, u32[]{:S(2)}, u32[]{:S(2)}) collective-permute-start(f32[24,512]{1,0:T(8,128)S(1)} %get-tuple-element.31._), channel_id=1, source_target_pairs={{0,64},{32,96},{64,0},{96,32},{1,65},{33,97},{65,1},{97,33},{2,66}... | collective-permute-start | bytes 147464 | tf_op jit(solution)/shard_map/ppermute | solution.py:403
  35.8 3.5 %bring.1.weight_ref = bf16[512,8192]{1,0:T(8,128)(2,1)S(1)} custom-call(bf16[512,8192]{1,0:T(8,128)(2,1)} %weight_ref.3, f32[24,512]{1,0:T(8,128)S(1)} %get-tuple-element.31._), custom_call_target="tpu_custom_call" | custom-call | tf_op jit(solution)/shard_map/bring/pallas_call | solution.py:407
  39.4 5.3 %give.1 = (bf16[16,128,512]{2,1,0:T(8,128)(2,1)S(1)}, bf16[128,512]{1,0:T(8,128)(2,1)S(1)}) custom-call(s32[5]{0:T(128)S(1)} %stack.24.place_ref, f32[256,512]{1,0:T(8,128)S(1)} %get-tuple-element.29.step_ref, f32[8,32,32]{2,1,0:T(8,128)S(1)} %get-tuple-element.30.states_ref, f32[16,512]{1,0:T(8,128)S(1)} %copy-done.7, bf16[256,512]{1,0:T(8,128)(2,1)S(1)} %copy-done.1, ...), custom_call_target="tpu_custom_call" | custom-call | tf_op jit(solution)/shard_map/give/pallas_call | solution.py:416
  44.8 1.3 %collective-permute-start.12 = (bf16[16,128,512]{2,1,0:T(8,128)(2,1)S(1)}, bf16[16,128,512]{2,1,0:T(8,128)(2,1)S(1)}, u32[]{:S(2)}, u32[]{:S(2)}) collective-permute-start(bf16[16,128,512]{2,1,0:T(8,128)(2,1)S(1)} %get-tuple-element.33), channel_id=1, source_target_pairs={{0,1},{1,0},{2,3},{3,2},{4,5},{5,4},{6,7},{7,6},{8,9},{9,8},{10,11... | collective-permute-start | bytes 6291464 | tf_op jit(solution)/shard_map/ppermute | solution.py:352
  46.2 1.8 %keep.1.keep_ref = bf16[16,128,512]{2,1,0:T(8,128)(2,1)S(1)} custom-call(s32[5]{0:T(128)S(1)} %stack.24.place_ref, bf16[128,512]{1,0:T(8,128)(2,1)S(1)} %get-tuple-element.32.kept_ref, bf16[512,8192]{1,0:T(8,128)(2,1)S(1)} %bring.1.weight_ref), custom_call_target="tpu_custom_call" | custom-call | tf_op jit(solution)/shard_map/keep/pallas_call | solution.py:432
  48.0 1.9 %collective-permute-done.12.got_ref = bf16[16,128,512]{2,1,0:T(8,128)(2,1)S(1)} collective-permute-done((bf16[16,128,512]{2,1,0:T(8,128)(2,1)S(1)}, bf16[16,128,512]{2,1,0:T(8,128)(2,1)S(1)}, u32[]{:S(2)}, u32[]{:S(2)}) %collective-permute-start.12) | collective-permute-done | bytes 2097184 | tf_op jit(solution)/shard_map/ppermute | solution.py:352
  50.3 1.0 collective-permute-start.13
  51.3 2.5 %collective-permute-start.14 = (bf16[4,128,512]{2,1,0:T(8,128)(2,1)S(1)}, bf16[4,128,512]{2,1,0:T(8,128)(2,1)S(1)}, u32[]{:S(2)}, u32[]{:S(2)}) collective-permute-start(bf16[4,128,512]{2,1,0:T(8,128)(2,1)S(1)} %get-tuple-element.36), channel_id=1, source_target_pairs={{0,16},{1,5},{2,18},{3,7},{4,20},{5,1},{6,22},{7,3},{8,24},{9,13},... | collective-permute-start | bytes 1572872 | tf_op jit(solution)/shard_map/ppermute | solution.py:333
  54.6 5.3 %collective-permute-done.13.one_ref = bf16[4,128,512]{2,1,0:T(8,128)(2,1)S(1)} collective-permute-done((bf16[4,128,512]{2,1,0:T(8,128)(2,1)S(1)}, bf16[4,128,512]{2,1,0:T(8,128)(2,1)S(1)}, u32[]{:S(2)}, u32[]{:S(2)}) %collective-permute-start.13) | collective-permute-done | bytes 524320 | tf_op jit(solution)/shard_map/ppermute | solution.py:333
  59.9 6.4 %collective-permute-done.14.two_ref = bf16[4,128,512]{2,1,0:T(8,128)(2,1)S(1)} collective-permute-done((bf16[4,128,512]{2,1,0:T(8,128)(2,1)S(1)}, bf16[4,128,512]{2,1,0:T(8,128)(2,1)S(1)}, u32[]{:S(2)}, u32[]{:S(2)}) %collective-permute-start.14) | collective-permute-done | bytes 524320 | tf_op jit(solution)/shard_map/ppermute | solution.py:333
  66.6 1.1 collective-permute-start.16
  67.7 2.4 %collective-permute-start.17 = (bf16[128,512]{1,0:T(8,128)(2,1)S(1)}, bf16[128,512]{1,0:T(8,128)(2,1)S(1)}, u32[]{:S(2)}, u32[]{:S(2)}) collective-permute-start(bf16[128,512]{1,0:T(8,128)(2,1)S(1)} %get-tuple-element.40), channel_id=1, source_target_pairs={{0,4},{1,17},{2,6},{3,19},{4,0},{5,21},{6,2},{7,23},{8,12},{9,25},... | collective-permute-start | bytes 393224 | tf_op jit(solution)/shard_map/ppermute | solution.py:333
  71.7 2.1 %collective-permute-done.17.two_ref = bf16[128,512]{1,0:T(8,128)(2,1)S(1)} collective-permute-done((bf16[128,512]{1,0:T(8,128)(2,1)S(1)}, bf16[128,512]{1,0:T(8,128)(2,1)S(1)}, u32[]{:S(2)}, u32[]{:S(2)}) %collective-permute-start.17) | collective-permute-done | bytes 131104 | tf_op jit(solution)/shard_map/ppermute | solution.py:333
  73.9 1.3 layer.1
  75.2 1.8 %collective-permute-start.20 = (bf16[4,144,128]{2,1,0:T(8,128)(2,1)S(1)}, bf16[4,144,128]{2,1,0:T(8,128)(2,1)S(1)}, u32[]{:S(2)}, u32[]{:S(2)}) collective-permute-start(bf16[4,144,128]{2,1,0:T(8,128)(2,1)S(1)} %get-tuple-element.44), channel_id=1, source_target_pairs={{0,8},{1,3},{2,10},{3,5},{4,12},{5,7},{6,14},{7,1},{8,16},{9,11},{... | collective-permute-start | bytes 442376 | tf_op jit(solution)/shard_map/ppermute | solution.py:333
  77.0 2.1 %collective-permute-start.21 = (bf16[4,144,128]{2,1,0:T(8,128)(2,1)S(1)}, bf16[4,144,128]{2,1,0:T(8,128)(2,1)S(1)}, u32[]{:S(2)}, u32[]{:S(2)}) collective-permute-start(bf16[4,144,128]{2,1,0:T(8,128)(2,1)S(1)} %get-tuple-element.45), channel_id=1, source_target_pairs={{0,16},{1,5},{2,18},{3,7},{4,20},{5,1},{6,22},{7,3},{8,24},{9,13},... | collective-permute-start | bytes 442376 | tf_op jit(solution)/shard_map/ppermute | solution.py:333
  79.4 1.0 collective-permute-done.20.refs_1_
  80.4 2.7 %collective-permute-done.21.refs_2_ = bf16[4,144,128]{2,1,0:T(8,128)(2,1)S(1)} collective-permute-done((bf16[4,144,128]{2,1,0:T(8,128)(2,1)S(1)}, bf16[4,144,128]{2,1,0:T(8,128)(2,1)S(1)}, u32[]{:S(2)}, u32[]{:S(2)}) %collective-permute-start.21) | collective-permute-done | bytes 147488 | tf_op jit(solution)/shard_map/ppermute | solution.py:333
  83.4 1.1 collective-permute-start.23
  84.5 2.2 %collective-permute-start.24 = (bf16[4,144,128]{2,1,0:T(8,128)(2,1)S(1)}, bf16[4,144,128]{2,1,0:T(8,128)(2,1)S(1)}, u32[]{:S(2)}, u32[]{:S(2)}) collective-permute-start(bf16[4,144,128]{2,1,0:T(8,128)(2,1)S(1)} %kv.1.own_part_ref), channel_id=1, source_target_pairs={{0,4},{1,17},{2,6},{3,19},{4,0},{5,21},{6,2},{7,23},{8,12},{9,25},... | collective-permute-start | bytes 442376 | tf_op jit(solution)/shard_map/ppermute | solution.py:333
  87.3 5.0 %collective-permute-start.26 = (bf16[128,256]{1,0:T(8,128)(2,1)S(1)}, bf16[128,256]{1,0:T(8,128)(2,1)S(1)}, u32[]{:S(2)}, u32[]{:S(2)}) collective-permute-start(bf16[128,256]{1,0:T(8,128)(2,1)S(1)} %get-tuple-element.48), channel_id=1, source_target_pairs={{0,1},{1,0},{2,3},{3,2},{4,5},{5,4},{6,7},{7,6},{8,9},{9,8},{10,11... | collective-permute-start | bytes 196616 | tf_op jit(solution)/shard_map/ppermute | solution.py:352
  92.3 0.9 collective-permute-done.26.got_layer_ref
  93.2 1.2 tile.1
  95.1 1.9 %collective-permute-start.28 = (bf16[4,128,128]{2,1,0:T(8,128)(2,1)S(1)}, bf16[4,128,128]{2,1,0:T(8,128)(2,1)S(1)}, u32[]{:S(2)}, u32[]{:S(2)}) collective-permute-start(bf16[4,128,128]{2,1,0:T(8,128)(2,1)S(1)} %get-tuple-element.50.own_ref), channel_id=1, source_target_pairs={{0,64},{32,96},{64,0},{96,32},{1,65},{33,97},{65,1},{97,33},{2,66}... | collective-permute-start | bytes 393224 | tf_op jit(solution)/shard_map/ppermute | solution.py:403
  97.5 1.9 %collective-permute-done.27.near_ref = bf16[4,128,128]{2,1,0:T(8,128)(2,1)S(1)} collective-permute-done((bf16[4,128,128]{2,1,0:T(8,128)(2,1)S(1)}, bf16[4,128,128]{2,1,0:T(8,128)(2,1)S(1)}, u32[]{:S(2)}, u32[]{:S(2)}) %collective-permute-start.27) | collective-permute-done | bytes 131104 | tf_op jit(solution)/shard_map/ppermute | solution.py:403
  99.5 1.4 %collective-permute-done.28.mid_ref = bf16[4,128,128]{2,1,0:T(8,128)(2,1)S(1)} collective-permute-done((bf16[4,128,128]{2,1,0:T(8,128)(2,1)S(1)}, bf16[4,128,128]{2,1,0:T(8,128)(2,1)S(1)}, u32[]{:S(2)}, u32[]{:S(2)}) %collective-permute-start.28) | collective-permute-done | bytes 131104 | tf_op jit(solution)/shard_map/ppermute | solution.py:403
  102.0 1.0 collective-permute-start.32
  104.1 1.7 %collective-permute-start.31 = (bf16[4,4,128,128]{3,2,1,0:T(8,128)(2,1)S(1)}, bf16[4,4,128,128]{3,2,1,0:T(8,128)(2,1)S(1)}, u32[]{:S(2)}, u32[]{:S(2)}) collective-permute-start(bf16[4,4,128,128]{3,2,1,0:T(8,128)(2,1)S(1)} %stack.25.one_ref.q0), channel_id=1, source_target_pairs={{0,24},{1,7},{2,26},{3,1},{4,28},{5,3},{6,30},{7,5},{8,0},{9,15},{... | collective-permute-start | bytes 1572872 | tf_op jit(solution)/shard_map/ppermute | solution.py:333
  105.8 11.2 %collective-permute-done.32.two_ref.q1 = bf16[4,4,128,128]{3,2,1,0:T(8,128)(2,1)S(1)} collective-permute-done((bf16[4,4,128,128]{3,2,1,0:T(8,128)(2,1)S(1)}, bf16[4,4,128,128]{3,2,1,0:T(8,128)(2,1)S(1)}, u32[]{:S(2)}, u32[]{:S(2)}) %collective-permute-start.32) | collective-permute-done | bytes 524320 | tf_op jit(solution)/shard_map/ppermute | solution.py:333
  118.1 1.5 %collective-permute-done.33.one_ref = bf16[2,8,128,128]{3,2,1,0:T(8,128)(2,1)S(1)} collective-permute-done((bf16[2,8,128,128]{3,2,1,0:T(8,128)(2,1)S(1)}, bf16[2,8,128,128]{3,2,1,0:T(8,128)(2,1)S(1)}, u32[]{:S(2)}, u32[]{:S(2)}) %collective-permute-start.33) | collective-permute-done | bytes 524320 | tf_op jit(solution)/shard_map/ppermute | solution.py:352
  120.3 4.5 %collective-permute-start.34 = (bf16[2,8,128,128]{3,2,1,0:T(8,128)(2,1)S(1)}, bf16[2,8,128,128]{3,2,1,0:T(8,128)(2,1)S(1)}, u32[]{:S(2)}, u32[]{:S(2)}) collective-permute-start(bf16[2,8,128,128]{3,2,1,0:T(8,128)(2,1)S(1)} %pick1.1), channel_id=1, source_target_pairs={{0,1},{1,0},{2,3},{3,2},{4,5},{5,4},{6,7},{7,6},{8,9},{9,8},{10,11... | collective-permute-start | bytes 1572872 | tf_op jit(solution)/shard_map/ppermute | solution.py:352
  124.9 1.8 %own.1._ = bf16[4,4,4,128,128]{4,3,2,1,0:T(8,128)(2,1)} custom-call(s32[5]{0:T(128)S(1)} %stack.24.place_ref, s32[128]{0:T(128)S(1)} %get-tuple-element.55.starts_ref, s32[128]{0:T(128)S(1)} %get-tuple-element.54.counts_ref, bf16[4,4,128,128]{3,2,1,0:T(8,128)(2,1)S(1)} %stack.25.one_ref.q0, bf16[4,4,128,128]{3,2,1,0:T(8,128)(2,1)S(1)} %collective-permute-done.32.two_ref.q1, ...), custom_call_target="tpu_custom_call" | custom-call | tf_op jit(solution)/shard_map/own/pallas_call | solution.py:497
  126.7 1.6 %rest.1 = bf16[4,4,4,128,128]{4,3,2,1,0:T(8,128)(2,1)} custom-call(s32[5]{0:T(128)S(1)} %stack.24.place_ref, s32[128]{0:T(128)S(1)} %get-tuple-element.55.starts_ref, bf16[2,8,128,128]{3,2,1,0:T(8,128)(2,1)S(1)} %collective-permute-done.33.one_ref, bf16[2,8,128,128]{3,2,1,0:T(8,128)(2,1)S(1)} %collective-permute-done.34.two_ref, ...), custom_call_target="tpu_custom_call", output_to_operand_aliasing={{}: (4, {})} | custom-call | tf_op jit(solution)/shard_map/rest/pallas_call | solution.py:506
  (73 shorter events, 14.1 us)
Async XLA Ops:
  0.7 26.5 %copy-start.7 = (f32[16,512]{1,0:T(8,128)S(1)}, f32[16,512]{1,0:T(8,128)}, u32[]{:S(2)}) copy-start(f32[16,512]{1,0:T(8,128)} %alog_ref.3) | copy-start | bytes 98308
  0.7 26.5 %copy-start.9 = (f32[512]{0:T(512)S(1)}, f32[512]{0:T(512)}, u32[]{:S(2)}) copy-start(f32[512]{0:T(512)} %param.20) | copy-start | bytes 6148
  2.8 24.4 %copy-start.1 = (bf16[256,512]{1,0:T(8,128)(2,1)S(1)}, bf16[256,512]{1,0:T(8,128)(2,1)}, u32[]{:S(2)}) copy-start(bf16[256,512]{1,0:T(8,128)(2,1)} %conv_ref.7) | copy-start | bytes 786436
  2.8 24.4 %copy-start.5 = (bf16[512,512]{1,0:T(8,128)(2,1)S(1)}, bf16[512,512]{1,0:T(8,128)(2,1)}, u32[]{:S(2)}) copy-start(bf16[512,512]{1,0:T(8,128)(2,1)} %weight_ref.2) | copy-start | bytes 1572868
  3.6 2.9 %collective-permute-start = (bf16[144,512]{1,0:T(8,128)(2,1)S(1)}, bf16[144,512]{1,0:T(8,128)(2,1)S(1)}, u32[]{:S(2)}, u32[]{:S(2)}) collective-permute-start(bf16[144,512]{1,0:T(8,128)(2,1)S(1)} %project_give.1), channel_id=1, source_target_pairs={{0,1},{1,0},{2,3},{3,2},{4,5},{5,4},{6,7},{7,6},{8,9},{9,8},{10,11... | collective-permute-start | bytes 442376 | tf_op jit(solution)/shard_map/ppermute | solution.py:352
  5.1 1.4 %collective-permute-start.1 = (f32[1,256]{1,0:T(1,128)}, f32[1,256]{1,0:T(1,128)S(1)}, u32[]{:S(2)}, u32[]{:S(2)}) collective-permute-start(f32[1,256]{1,0:T(1,128)} %bitcast.14), channel_id=1, source_target_pairs={{0,1},{1,0},{2,3},{3,2},{4,5},{5,4},{6,7},{7,6},{8,9},{9,8},{10,11... | collective-permute-start | bytes 3080 | tf_op jit(solution)/shard_map/ppermute | solution.py:352
  6.5 5.7 %collective-permute-start.2 = (bf16[144,512]{1,0:T(8,128)(2,1)S(1)}, bf16[144,512]{1,0:T(8,128)(2,1)S(1)}, u32[]{:S(2)}, u32[]{:S(2)}) collective-permute-start(bf16[144,512]{1,0:T(8,128)(2,1)S(1)} %chip.1.refs_0_), channel_id=1, source_target_pairs={{0,8},{1,3},{2,10},{3,5},{4,12},{5,7},{6,14},{7,1},{8,16},{9,11},{... | collective-permute-start | bytes 442376 | tf_op jit(solution)/shard_map/ppermute | solution.py:333
  8.0 7.0 %collective-permute-start.3 = (bf16[144,512]{1,0:T(8,128)(2,1)S(1)}, bf16[144,512]{1,0:T(8,128)(2,1)S(1)}, u32[]{:S(2)}, u32[]{:S(2)}) collective-permute-start(bf16[144,512]{1,0:T(8,128)(2,1)S(1)} %chip.1.refs_0_), channel_id=1, source_target_pairs={{0,16},{1,5},{2,18},{3,7},{4,20},{5,1},{6,22},{7,3},{8,24},{9,13},... | collective-permute-start | bytes 442376 | tf_op jit(solution)/shard_map/ppermute | solution.py:333
  10.6 4.4 %collective-permute-start.4 = (bf16[144,512]{1,0:T(8,128)(2,1)S(1)}, bf16[144,512]{1,0:T(8,128)(2,1)S(1)}, u32[]{:S(2)}, u32[]{:S(2)}) collective-permute-start(bf16[144,512]{1,0:T(8,128)(2,1)S(1)} %chip.1.refs_0_), channel_id=1, source_target_pairs={{0,24},{1,7},{2,26},{3,1},{4,28},{5,3},{6,30},{7,5},{8,0},{9,15},{... | collective-permute-start | bytes 442376 | tf_op jit(solution)/shard_map/ppermute | solution.py:333
  15.1 5.3 %collective-permute-start.5 = (bf16[144,512]{1,0:T(8,128)(2,1)S(1)}, bf16[144,512]{1,0:T(8,128)(2,1)S(1)}, u32[]{:S(2)}, u32[]{:S(2)}) collective-permute-start(bf16[144,512]{1,0:T(8,128)(2,1)S(1)} %row.1.refs_0_), channel_id=1, source_target_pairs={{0,2},{1,9},{2,4},{3,11},{4,6},{5,13},{6,0},{7,15},{8,10},{9,17},{... | collective-permute-start | bytes 442376 | tf_op jit(solution)/shard_map/ppermute | solution.py:333
  16.3 6.6 %collective-permute-start.6 = (bf16[144,512]{1,0:T(8,128)(2,1)S(1)}, bf16[144,512]{1,0:T(8,128)(2,1)S(1)}, u32[]{:S(2)}, u32[]{:S(2)}) collective-permute-start(bf16[144,512]{1,0:T(8,128)(2,1)S(1)} %row.1.refs_0_), channel_id=1, source_target_pairs={{0,4},{1,17},{2,6},{3,19},{4,0},{5,21},{6,2},{7,23},{8,12},{9,25},... | collective-permute-start | bytes 442376 | tf_op jit(solution)/shard_map/ppermute | solution.py:333
  18.7 4.1 %collective-permute-start.7 = (bf16[144,512]{1,0:T(8,128)(2,1)S(1)}, bf16[144,512]{1,0:T(8,128)(2,1)S(1)}, u32[]{:S(2)}, u32[]{:S(2)}) collective-permute-start(bf16[144,512]{1,0:T(8,128)(2,1)S(1)} %row.1.refs_0_), channel_id=1, source_target_pairs={{0,6},{1,25},{2,0},{3,27},{4,2},{5,29},{6,4},{7,31},{8,14},{9,1},{... | collective-permute-start | bytes 442376 | tf_op jit(solution)/shard_map/ppermute | solution.py:333
  22.9 4.3 %collective-permute-start.8 = (bf16[144,512]{1,0:T(8,128)(2,1)S(1)}, bf16[144,512]{1,0:T(8,128)(2,1)S(1)}, u32[]{:S(2)}, u32[]{:S(2)}) collective-permute-start(bf16[144,512]{1,0:T(8,128)(2,1)S(1)} %plane.1.own_proj_ref), channel_id=1, source_target_pairs={{0,1},{1,0},{2,3},{3,2},{4,5},{5,4},{6,7},{7,6},{8,9},{9,8},{10,11... | collective-permute-start | bytes 442376 | tf_op jit(solution)/shard_map/ppermute | solution.py:352
  30.1 9.3 %copy-start.4 = (bf16[256,256]{1,0:T(8,128)(2,1)S(1)}, bf16[256,256]{1,0:T(8,128)(2,1)}, u32[]{:S(2)}) copy-start(bf16[256,256]{1,0:T(8,128)(2,1)} %residual_ref.3) | copy-start | bytes 393220
  30.1 9.3 %copy-start.6 = (bf16[256,512]{1,0:T(8,128)(2,1)S(1)}, bf16[256,512]{1,0:T(8,128)(2,1)}, u32[]{:S(2)}) copy-start(bf16[256,512]{1,0:T(8,128)(2,1)} %gate_ref.1) | copy-start | bytes 786436
  30.1 9.3 %copy-start.8 = (f32[16,512]{1,0:T(8,128)S(1)}, f32[16,512]{1,0:T(8,128)}, u32[]{:S(2)}) copy-start(f32[16,512]{1,0:T(8,128)} %init_ref.1) | copy-start | bytes 98308
  30.1 9.3 %copy-start.10 = (f32[512]{0:T(512)S(1)}, f32[512]{0:T(512)}, u32[]{:S(2)}) copy-start(f32[512]{0:T(512)} %param.22) | copy-start | bytes 6148
  30.1 9.3 %collective-permute-start.9 = (f32[24,512]{1,0:T(8,128)S(1)}, f32[24,512]{1,0:T(8,128)S(1)}, u32[]{:S(2)}, u32[]{:S(2)}) collective-permute-start(f32[24,512]{1,0:T(8,128)S(1)} %get-tuple-element.31._), channel_id=1, source_target_pairs={{0,32},{32,64},{64,96},{96,0},{1,33},{33,65},{65,97},{97,1},{2,34}... | collective-permute-start | bytes 147464 | tf_op jit(solution)/shard_map/ppermute | solution.py:403
  31.8 7.6 %collective-permute-start.10 = (f32[24,512]{1,0:T(8,128)S(1)}, f32[24,512]{1,0:T(8,128)S(1)}, u32[]{:S(2)}, u32[]{:S(2)}) collective-permute-start(f32[24,512]{1,0:T(8,128)S(1)} %get-tuple-element.31._), channel_id=1, source_target_pairs={{0,64},{32,96},{64,0},{96,32},{1,65},{33,97},{65,1},{97,33},{2,66}... | collective-permute-start | bytes 147464 | tf_op jit(solution)/shard_map/ppermute | solution.py:403
  35.1 4.3 %collective-permute-start.11 = (f32[24,512]{1,0:T(8,128)S(1)}, f32[24,512]{1,0:T(8,128)S(1)}, u32[]{:S(2)}, u32[]{:S(2)}) collective-permute-start(f32[24,512]{1,0:T(8,128)S(1)} %get-tuple-element.31._), channel_id=1, source_target_pairs={{0,96},{32,0},{64,32},{96,64},{1,97},{33,1},{65,33},{97,65},{2,98}... | collective-permute-start | bytes 147464 | tf_op jit(solution)/shard_map/ppermute | solution.py:403
  39.4 6.6 %copy-start.3 = (bf16[256,2048]{1,0:T(8,128)(2,1)S(1)}, bf16[256,2048]{1,0:T(8,128)(2,1)}, u32[]{:S(2)}) copy-start(bf16[256,2048]{1,0:T(8,128)(2,1)} %own_weight_ref.1) | copy-start | bytes 3145732
  44.8 5.1 %collective-permute-start.12 = (bf16[16,128,512]{2,1,0:T(8,128)(2,1)S(1)}, bf16[16,128,512]{2,1,0:T(8,128)(2,1)S(1)}, u32[]{:S(2)}, u32[]{:S(2)}) collective-permute-start(bf16[16,128,512]{2,1,0:T(8,128)(2,1)S(1)} %get-tuple-element.33), channel_id=1, source_target_pairs={{0,1},{1,0},{2,3},{3,2},{4,5},{5,4},{6,7},{7,6},{8,9},{9,8},{10,11... | collective-permute-start | bytes 6291464 | tf_op jit(solution)/shard_map/ppermute | solution.py:352
  46.1 24.7 %collective-permute-start.19 = (bf16[256,2048]{1,0:T(8,128)(2,1)S(1)}, bf16[256,2048]{1,0:T(8,128)(2,1)S(1)}, u32[]{:S(2)}, u32[]{:S(2)}) collective-permute-start(bf16[256,2048]{1,0:T(8,128)(2,1)S(1)} %copy-done.3), channel_id=1, source_target_pairs={{0,1},{1,0},{2,3},{3,2},{4,5},{5,4},{6,7},{7,6},{8,9},{9,8},{10,11... | collective-permute-start | bytes 3145736 | tf_op jit(solution)/shard_map/ppermute | solution.py:352
  50.3 23.6 %copy-start.11 = (f32[256]{0:T(256)S(1)}, f32[256]{0:T(256)}, u32[]{:S(2)}) copy-start(f32[256]{0:T(256)} %param.25) | copy-start | bytes 3076
  50.3 9.6 %collective-permute-start.13 = (bf16[4,128,512]{2,1,0:T(8,128)(2,1)S(1)}, bf16[4,128,512]{2,1,0:T(8,128)(2,1)S(1)}, u32[]{:S(2)}, u32[]{:S(2)}) collective-permute-start(bf16[4,128,512]{2,1,0:T(8,128)(2,1)S(1)} %get-tuple-element.35), channel_id=1, source_target_pairs={{0,8},{1,3},{2,10},{3,5},{4,12},{5,7},{6,14},{7,1},{8,16},{9,11},{... | collective-permute-start | bytes 1572872 | tf_op jit(solution)/shard_map/ppermute | solution.py:333
  51.3 15.0 %collective-permute-start.14 = (bf16[4,128,512]{2,1,0:T(8,128)(2,1)S(1)}, bf16[4,128,512]{2,1,0:T(8,128)(2,1)S(1)}, u32[]{:S(2)}, u32[]{:S(2)}) collective-permute-start(bf16[4,128,512]{2,1,0:T(8,128)(2,1)S(1)} %get-tuple-element.36), channel_id=1, source_target_pairs={{0,16},{1,5},{2,18},{3,7},{4,20},{5,1},{6,22},{7,3},{8,24},{9,13},... | collective-permute-start | bytes 1572872 | tf_op jit(solution)/shard_map/ppermute | solution.py:333
  53.9 12.5 %collective-permute-start.15 = (bf16[4,128,512]{2,1,0:T(8,128)(2,1)S(1)}, bf16[4,128,512]{2,1,0:T(8,128)(2,1)S(1)}, u32[]{:S(2)}, u32[]{:S(2)}) collective-permute-start(bf16[4,128,512]{2,1,0:T(8,128)(2,1)S(1)} %get-tuple-element.37), channel_id=1, source_target_pairs={{0,24},{1,7},{2,26},{3,1},{4,28},{5,3},{6,30},{7,5},{8,0},{9,15},{... | collective-permute-start | bytes 1572872 | tf_op jit(solution)/shard_map/ppermute | solution.py:333
  66.6 5.1 %collective-permute-start.16 = (bf16[128,512]{1,0:T(8,128)(2,1)S(1)}, bf16[128,512]{1,0:T(8,128)(2,1)S(1)}, u32[]{:S(2)}, u32[]{:S(2)}) collective-permute-start(bf16[128,512]{1,0:T(8,128)(2,1)S(1)} %get-tuple-element.39), channel_id=1, source_target_pairs={{0,2},{1,9},{2,4},{3,11},{4,6},{5,13},{6,0},{7,15},{8,10},{9,17},{... | collective-permute-start | bytes 393224 | tf_op jit(solution)/shard_map/ppermute | solution.py:333
  67.7 6.1 %collective-permute-start.17 = (bf16[128,512]{1,0:T(8,128)(2,1)S(1)}, bf16[128,512]{1,0:T(8,128)(2,1)S(1)}, u32[]{:S(2)}, u32[]{:S(2)}) collective-permute-start(bf16[128,512]{1,0:T(8,128)(2,1)S(1)} %get-tuple-element.40), channel_id=1, source_target_pairs={{0,4},{1,17},{2,6},{3,19},{4,0},{5,21},{6,2},{7,23},{8,12},{9,25},... | collective-permute-start | bytes 393224 | tf_op jit(solution)/shard_map/ppermute | solution.py:333
  70.1 3.8 %collective-permute-start.18 = (bf16[128,512]{1,0:T(8,128)(2,1)S(1)}, bf16[128,512]{1,0:T(8,128)(2,1)S(1)}, u32[]{:S(2)}, u32[]{:S(2)}) collective-permute-start(bf16[128,512]{1,0:T(8,128)(2,1)S(1)} %get-tuple-element.41), channel_id=1, source_target_pairs={{0,6},{1,25},{2,0},{3,27},{4,2},{5,29},{6,4},{7,31},{8,14},{9,1},{... | collective-permute-start | bytes 393224 | tf_op jit(solution)/shard_map/ppermute | solution.py:333
  73.9 29.2 %copy-start.12 = (s32[128]{0:T(128)S(1)}, s32[128]{0:T(128)}, u32[]{:S(2)}) copy-start(s32[128]{0:T(128)} %param.29) | copy-start | bytes 1540
  73.9 29.2 %copy-start.13 = (s32[128]{0:T(128)S(1)}, s32[128]{0:T(128)}, u32[]{:S(2)}) copy-start(s32[128]{0:T(128)} %param.27) | copy-start | bytes 1540
  73.9 29.2 %copy-start.14 = (s32[128]{0:T(128)S(1)}, s32[128]{0:T(128)}, u32[]{:S(2)}) copy-start(s32[128]{0:T(128)} %param.28) | copy-start | bytes 1540
  75.2 5.3 %collective-permute-start.20 = (bf16[4,144,128]{2,1,0:T(8,128)(2,1)S(1)}, bf16[4,144,128]{2,1,0:T(8,128)(2,1)S(1)}, u32[]{:S(2)}, u32[]{:S(2)}) collective-permute-start(bf16[4,144,128]{2,1,0:T(8,128)(2,1)S(1)} %get-tuple-element.44), channel_id=1, source_target_pairs={{0,8},{1,3},{2,10},{3,5},{4,12},{5,7},{6,14},{7,1},{8,16},{9,11},{... | collective-permute-start | bytes 442376 | tf_op jit(solution)/shard_map/ppermute | solution.py:333
  77.0 6.2 %collective-permute-start.21 = (bf16[4,144,128]{2,1,0:T(8,128)(2,1)S(1)}, bf16[4,144,128]{2,1,0:T(8,128)(2,1)S(1)}, u32[]{:S(2)}, u32[]{:S(2)}) collective-permute-start(bf16[4,144,128]{2,1,0:T(8,128)(2,1)S(1)} %get-tuple-element.45), channel_id=1, source_target_pairs={{0,16},{1,5},{2,18},{3,7},{4,20},{5,1},{6,22},{7,3},{8,24},{9,13},... | collective-permute-start | bytes 442376 | tf_op jit(solution)/shard_map/ppermute | solution.py:333
  79.1 4.3 %collective-permute-start.22 = (bf16[4,144,128]{2,1,0:T(8,128)(2,1)S(1)}, bf16[4,144,128]{2,1,0:T(8,128)(2,1)S(1)}, u32[]{:S(2)}, u32[]{:S(2)}) collective-permute-start(bf16[4,144,128]{2,1,0:T(8,128)(2,1)S(1)} %get-tuple-element.46), channel_id=1, source_target_pairs={{0,24},{1,7},{2,26},{3,1},{4,28},{5,3},{6,30},{7,5},{8,0},{9,15},{... | collective-permute-start | bytes 442376 | tf_op jit(solution)/shard_map/ppermute | solution.py:333
  83.4 9.7 %collective-permute-start.23 = (bf16[4,144,128]{2,1,0:T(8,128)(2,1)S(1)}, bf16[4,144,128]{2,1,0:T(8,128)(2,1)S(1)}, u32[]{:S(2)}, u32[]{:S(2)}) collective-permute-start(bf16[4,144,128]{2,1,0:T(8,128)(2,1)S(1)} %kv.1.own_part_ref), channel_id=1, source_target_pairs={{0,2},{1,9},{2,4},{3,11},{4,6},{5,13},{6,0},{7,15},{8,10},{9,17},{... | collective-permute-start | bytes 442376 | tf_op jit(solution)/shard_map/ppermute | solution.py:333
  84.5 8.6 %collective-permute-start.24 = (bf16[4,144,128]{2,1,0:T(8,128)(2,1)S(1)}, bf16[4,144,128]{2,1,0:T(8,128)(2,1)S(1)}, u32[]{:S(2)}, u32[]{:S(2)}) collective-permute-start(bf16[4,144,128]{2,1,0:T(8,128)(2,1)S(1)} %kv.1.own_part_ref), channel_id=1, source_target_pairs={{0,4},{1,17},{2,6},{3,19},{4,0},{5,21},{6,2},{7,23},{8,12},{9,25},... | collective-permute-start | bytes 442376 | tf_op jit(solution)/shard_map/ppermute | solution.py:333
  86.7 6.4 %collective-permute-start.25 = (bf16[4,144,128]{2,1,0:T(8,128)(2,1)S(1)}, bf16[4,144,128]{2,1,0:T(8,128)(2,1)S(1)}, u32[]{:S(2)}, u32[]{:S(2)}) collective-permute-start(bf16[4,144,128]{2,1,0:T(8,128)(2,1)S(1)} %kv.1.own_part_ref), channel_id=1, source_target_pairs={{0,6},{1,25},{2,0},{3,27},{4,2},{5,29},{6,4},{7,31},{8,14},{9,1},{... | collective-permute-start | bytes 442376 | tf_op jit(solution)/shard_map/ppermute | solution.py:333
  87.3 5.9 %collective-permute-start.26 = (bf16[128,256]{1,0:T(8,128)(2,1)S(1)}, bf16[128,256]{1,0:T(8,128)(2,1)S(1)}, u32[]{:S(2)}, u32[]{:S(2)}) collective-permute-start(bf16[128,256]{1,0:T(8,128)(2,1)S(1)} %get-tuple-element.48), channel_id=1, source_target_pairs={{0,1},{1,0},{2,3},{3,2},{4,5},{5,4},{6,7},{7,6},{8,9},{9,8},{10,11... | collective-permute-start | bytes 196616 | tf_op jit(solution)/shard_map/ppermute | solution.py:352
  94.4 5.0 %collective-permute-start.27 = (bf16[4,128,128]{2,1,0:T(8,128)(2,1)S(1)}, bf16[4,128,128]{2,1,0:T(8,128)(2,1)S(1)}, u32[]{:S(2)}, u32[]{:S(2)}) collective-permute-start(bf16[4,128,128]{2,1,0:T(8,128)(2,1)S(1)} %get-tuple-element.50.own_ref), channel_id=1, source_target_pairs={{0,32},{32,64},{64,96},{96,0},{1,33},{33,65},{65,97},{97,1},{2,34}... | collective-permute-start | bytes 393224 | tf_op jit(solution)/shard_map/ppermute | solution.py:403
  95.1 5.7 %collective-permute-start.28 = (bf16[4,128,128]{2,1,0:T(8,128)(2,1)S(1)}, bf16[4,128,128]{2,1,0:T(8,128)(2,1)S(1)}, u32[]{:S(2)}, u32[]{:S(2)}) collective-permute-start(bf16[4,128,128]{2,1,0:T(8,128)(2,1)S(1)} %get-tuple-element.50.own_ref), channel_id=1, source_target_pairs={{0,64},{32,96},{64,0},{96,32},{1,65},{33,97},{65,1},{97,33},{2,66}... | collective-permute-start | bytes 393224 | tf_op jit(solution)/shard_map/ppermute | solution.py:403
  97.1 4.4 %collective-permute-start.29 = (bf16[4,128,128]{2,1,0:T(8,128)(2,1)S(1)}, bf16[4,128,128]{2,1,0:T(8,128)(2,1)S(1)}, u32[]{:S(2)}, u32[]{:S(2)}) collective-permute-start(bf16[4,128,128]{2,1,0:T(8,128)(2,1)S(1)} %get-tuple-element.50.own_ref), channel_id=1, source_target_pairs={{0,96},{32,0},{64,32},{96,64},{1,97},{33,1},{65,33},{97,65},{2,98}... | collective-permute-start | bytes 393224 | tf_op jit(solution)/shard_map/ppermute | solution.py:403
  102.0 14.9 %collective-permute-start.32 = (bf16[4,4,128,128]{3,2,1,0:T(8,128)(2,1)S(1)}, bf16[4,4,128,128]{3,2,1,0:T(8,128)(2,1)S(1)}, u32[]{:S(2)}, u32[]{:S(2)}) collective-permute-start(bf16[4,4,128,128]{3,2,1,0:T(8,128)(2,1)S(1)} %stack.25.one_ref.q0), channel_id=1, source_target_pairs={{0,8},{1,3},{2,10},{3,5},{4,12},{5,7},{6,14},{7,1},{8,16},{9,11},{... | collective-permute-start | bytes 1572872 | tf_op jit(solution)/shard_map/ppermute | solution.py:333
  103.2 14.9 %collective-permute-start.30 = (bf16[4,4,128,128]{3,2,1,0:T(8,128)(2,1)S(1)}, bf16[4,4,128,128]{3,2,1,0:T(8,128)(2,1)S(1)}, u32[]{:S(2)}, u32[]{:S(2)}) collective-permute-start(bf16[4,4,128,128]{3,2,1,0:T(8,128)(2,1)S(1)} %stack.25.one_ref.q0), channel_id=1, source_target_pairs={{0,16},{1,5},{2,18},{3,7},{4,20},{5,1},{6,22},{7,3},{8,24},{9,13},... | collective-permute-start | bytes 1572872 | tf_op jit(solution)/shard_map/ppermute | solution.py:333
  104.1 14.0 %collective-permute-start.31 = (bf16[4,4,128,128]{3,2,1,0:T(8,128)(2,1)S(1)}, bf16[4,4,128,128]{3,2,1,0:T(8,128)(2,1)S(1)}, u32[]{:S(2)}, u32[]{:S(2)}) collective-permute-start(bf16[4,4,128,128]{3,2,1,0:T(8,128)(2,1)S(1)} %stack.25.one_ref.q0), channel_id=1, source_target_pairs={{0,24},{1,7},{2,26},{3,1},{4,28},{5,3},{6,30},{7,5},{8,0},{9,15},{... | collective-permute-start | bytes 1572872 | tf_op jit(solution)/shard_map/ppermute | solution.py:333
  117.6 2.0 %collective-permute-start.33 = (bf16[2,8,128,128]{3,2,1,0:T(8,128)(2,1)S(1)}, bf16[2,8,128,128]{3,2,1,0:T(8,128)(2,1)S(1)}, u32[]{:S(2)}, u32[]{:S(2)}) collective-permute-start(bf16[2,8,128,128]{3,2,1,0:T(8,128)(2,1)S(1)} %pick0.1), channel_id=1, source_target_pairs={{0,1},{1,0},{2,3},{3,2},{4,5},{5,4},{6,7},{7,6},{8,9},{9,8},{10,11... | collective-permute-start | bytes 1572872 | tf_op jit(solution)/shard_map/ppermute | solution.py:352
  120.3 6.4 %collective-permute-start.34 = (bf16[2,8,128,128]{3,2,1,0:T(8,128)(2,1)S(1)}, bf16[2,8,128,128]{3,2,1,0:T(8,128)(2,1)S(1)}, u32[]{:S(2)}, u32[]{:S(2)}) collective-permute-start(bf16[2,8,128,128]{3,2,1,0:T(8,128)(2,1)S(1)} %pick1.1), channel_id=1, source_target_pairs={{0,1},{1,0},{2,3},{3,2},{4,5},{5,4},{6,7},{7,6},{8,9},{9,8},{10,11... | collective-permute-start | bytes 1572872 | tf_op jit(solution)/shard_map/ppermute | solution.py:352
  (2 other events, 2.0 us)

commit v5 on v4

--- a/solution.py
+++ b/solution.py
@@ -16,7 +16,7 @@
 CAP = 4
 EPS = 1e-05
 LOG2E = 1.4426950408889634
-CHUNK = 32
+CHUNK = 64
 PIECES = 8
 SIDE = 4
 EARLY, LATE = 1, (2, 3)
@@ -52,6 +52,18 @@
     refs[-1][...] = total.astype(refs[-1].dtype)
 
 
+def fold_rows(values):
+    row = lax.broadcasted_iota(jnp.int32, values[0].shape, 0)
+    for reach in (4, 2, 1):
+        near = row % (2 * reach) < reach
+        values = [
+            jnp.where(near, a, b)
+            + jnp.where(near, pltpu.roll(a, 8 - reach, 0), pltpu.roll(b, reach, 0))
+            for a, b in zip(values[:reach], values[reach:], strict=True)
+        ]
+    return values[0]
+
+
 def advance_block(block, hidden, step_ref, drive_ref, states_ref, rates, read_out):
     states = states_ref[block]
     for group in range(CHUNK // 8):
@@ -63,11 +75,10 @@
             decay = jnp.exp2(steps[i : i + 1, :] * rates)
             hidden = decay * hidden + states[:STATE, at : at + 1] * drives[i : i + 1, :]
             if read_out is not None:
-                outs.append(
-                    jnp.sum(hidden * states[STATE:, at : at + 1], axis=0, keepdims=True)
-                )
+                terms = hidden * states[STATE:, at : at + 1]
+                outs.append(terms[:8] + terms[8:])
         if read_out is not None:
-            read_out[rows, :] = jnp.concatenate(outs, axis=0)
+            read_out[rows, :] = fold_rows(outs)
     return hidden
 
 

time: 129 us -> 128 us (level)
  no operation moved by 1% of the time
where the time goes in v5:
time: 128 us
  starting transfers between devices  55.2 us (43%)
  waiting for transfers between devices  45.8 us (36%)
  Pallas kernels  23.3 us (18%)
  local copies, waits for them, and re-layouts  2.15 us (2%)
    ppermute x21, waiting for transfers between devices, line(): lax.ppermute(value_of(shift), 'tp', [((x * SIDE + y) * 2 + c, ((x + shift...  36.2 us
    ppermute x21, starting transfers between devices, line(): lax.ppermute(value_of(shift), 'tp', [((x * SIDE + y) * 2 + c, ((x + shift...  30.1 us
    ppermute x8, starting transfers between devices, swap(): return lax.ppermute(value, 'tp', partner)  16.2 us
    ppermute x6, starting transfers between devices, ranges_back(): lax.ppermute(value, 'ctx', [(z, (z + s) % ctx_count) for z in range(ctx_c...  8.87 us
    ppermute x8, waiting for transfers between devices, swap(): return lax.ppermute(value, 'tp', partner)  5.72 us
    pallas_call x1, Pallas kernels, per_device(): pl.pallas_call(give_kernel, in_specs=[SM] + [VM] * 12, out_shape=(shape(p...  4.75 us
    ppermute x6, waiting for transfers between devices, ranges_back(): lax.ppermute(value, 'ctx', [(z, (z + s) % ctx_count) for z in range(ctx_c...  3.89 us
    pallas_call x1, Pallas kernels, per_device(): pl.pallas_call(bring_kernel, in_specs=[ANY] * 2, out_shape=shape(out_weig...  3.5 us
  transfers between devices with their start and end apart: 35, of which 21 were waited for; matrix products, arithmetic and copies ran while one was open for 0% of the time, Pallas kernels for 7%

profile of v5, /device:TPU:1, one launch (start us, length us, event | category | flops | bytes accessed | tf_op | source)
XLA Modules:
  0.0 127.7 jit_solution(2206655877738437739)
XLA Ops:
  0.8 0.9 copy-done
  1.7 1.1 copy-done.2
  3.6 1.5 %collective-permute-start = (bf16[144,512]{1,0:T(8,128)(2,1)S(1)}, bf16[144,512]{1,0:T(8,128)(2,1)S(1)}, u32[]{:S(2)}, u32[]{:S(2)}) collective-permute-start(bf16[144,512]{1,0:T(8,128)(2,1)S(1)} %project_give.1), channel_id=1, source_target_pairs={{0,1},{1,0},{2,3},{3,2},{4,5},{5,4},{6,7},{7,6},{8,9},{9,8},{10,11... | collective-permute-start | bytes 442376 | tf_op jit(solution)/shard_map/ppermute | solution.py:363
  6.5 1.4 %collective-permute-start.2 = (bf16[144,512]{1,0:T(8,128)(2,1)S(1)}, bf16[144,512]{1,0:T(8,128)(2,1)S(1)}, u32[]{:S(2)}, u32[]{:S(2)}) collective-permute-start(bf16[144,512]{1,0:T(8,128)(2,1)S(1)} %chip.1.refs_0_), channel_id=1, source_target_pairs={{0,8},{1,3},{2,10},{3,5},{4,12},{5,7},{6,14},{7,1},{8,16},{9,11},{... | collective-permute-start | bytes 442376 | tf_op jit(solution)/shard_map/ppermute | solution.py:344
  8.0 2.6 %collective-permute-start.3 = (bf16[144,512]{1,0:T(8,128)(2,1)S(1)}, bf16[144,512]{1,0:T(8,128)(2,1)S(1)}, u32[]{:S(2)}, u32[]{:S(2)}) collective-permute-start(bf16[144,512]{1,0:T(8,128)(2,1)S(1)} %chip.1.refs_0_), channel_id=1, source_target_pairs={{0,16},{1,5},{2,18},{3,7},{4,20},{5,1},{6,22},{7,3},{8,24},{9,13},... | collective-permute-start | bytes 442376 | tf_op jit(solution)/shard_map/ppermute | solution.py:344
  10.6 1.1 collective-permute-start.4
  12.2 2.8 %collective-permute-done.3.refs_2_ = bf16[144,512]{1,0:T(8,128)(2,1)S(1)} collective-permute-done((bf16[144,512]{1,0:T(8,128)(2,1)S(1)}, bf16[144,512]{1,0:T(8,128)(2,1)S(1)}, u32[]{:S(2)}, u32[]{:S(2)}) %collective-permute-start.3) | collective-permute-done | bytes 147488 | tf_op jit(solution)/shard_map/ppermute | solution.py:344
  15.1 1.2 collective-permute-start.5
  16.3 2.4 %collective-permute-start.6 = (bf16[144,512]{1,0:T(8,128)(2,1)S(1)}, bf16[144,512]{1,0:T(8,128)(2,1)S(1)}, u32[]{:S(2)}, u32[]{:S(2)}) collective-permute-start(bf16[144,512]{1,0:T(8,128)(2,1)S(1)} %row.1.refs_0_), channel_id=1, source_target_pairs={{0,4},{1,17},{2,6},{3,19},{4,0},{5,21},{6,2},{7,23},{8,12},{9,25},... | collective-permute-start | bytes 442376 | tf_op jit(solution)/shard_map/ppermute | solution.py:344
  18.7 1.2 collective-permute-start.7
  20.4 2.4 %collective-permute-done.6.refs_2_ = bf16[144,512]{1,0:T(8,128)(2,1)S(1)} collective-permute-done((bf16[144,512]{1,0:T(8,128)(2,1)S(1)}, bf16[144,512]{1,0:T(8,128)(2,1)S(1)}, u32[]{:S(2)}, u32[]{:S(2)}) %collective-permute-start.6) | collective-permute-done | bytes 147488 | tf_op jit(solution)/shard_map/ppermute | solution.py:344
  22.9 3.3 %collective-permute-start.8 = (bf16[144,512]{1,0:T(8,128)(2,1)S(1)}, bf16[144,512]{1,0:T(8,128)(2,1)S(1)}, u32[]{:S(2)}, u32[]{:S(2)}) collective-permute-start(bf16[144,512]{1,0:T(8,128)(2,1)S(1)} %plane.1.own_proj_ref), channel_id=1, source_target_pairs={{0,1},{1,0},{2,3},{3,2},{4,5},{5,4},{6,7},{7,6},{8,9},{9,8},{10,11... | collective-permute-start | bytes 442376 | tf_op jit(solution)/shard_map/ppermute | solution.py:363
  26.2 1.0 collective-permute-done.8.got_proj_ref
  27.2 2.7 %first.1 = (f32[256,512]{1,0:T(8,128)S(1)}, f32[4,32,64]{2,1,0:T(8,128)S(1)}, f32[24,512]{1,0:T(8,128)S(1)}) custom-call(s32[5]{0:T(128)S(1)} %stack.24.place_ref, bf16[144,512]{1,0:T(8,128)(2,1)S(1)} %plane.1.own_proj_ref, bf16[144,512]{1,0:T(8,128)(2,1)S(1)} %collective-permute-done.8.got_proj_ref, bf16[512,512]{1,0:T(8,128)(2,1)S(1)} %copy-done.5, ...), custom_call_target="tpu_custom_call" | custom-call | tf_op jit(solution)/shard_map/first/pallas_call | solution.py:397
  30.0 1.7 %collective-permute-start.9 = (f32[24,512]{1,0:T(8,128)S(1)}, f32[24,512]{1,0:T(8,128)S(1)}, u32[]{:S(2)}, u32[]{:S(2)}) collective-permute-start(f32[24,512]{1,0:T(8,128)S(1)} %get-tuple-element.31._), channel_id=1, source_target_pairs={{0,32},{32,64},{64,96},{96,0},{1,33},{33,65},{65,97},{97,1},{2,34}... | collective-permute-start | bytes 147464 | tf_op jit(solution)/shard_map/ppermute | solution.py:414
  31.7 3.3 %collective-permute-start.10 = (f32[24,512]{1,0:T(8,128)S(1)}, f32[24,512]{1,0:T(8,128)S(1)}, u32[]{:S(2)}, u32[]{:S(2)}) collective-permute-start(f32[24,512]{1,0:T(8,128)S(1)} %get-tuple-element.31._), channel_id=1, source_target_pairs={{0,64},{32,96},{64,0},{96,32},{1,65},{33,97},{65,1},{97,33},{2,66}... | collective-permute-start | bytes 147464 | tf_op jit(solution)/shard_map/ppermute | solution.py:414
  35.7 3.5 %bring.1.weight_ref = bf16[512,8192]{1,0:T(8,128)(2,1)S(1)} custom-call(bf16[512,8192]{1,0:T(8,128)(2,1)} %weight_ref.3, f32[24,512]{1,0:T(8,128)S(1)} %get-tuple-element.31._), custom_call_target="tpu_custom_call" | custom-call | tf_op jit(solution)/shard_map/bring/pallas_call | solution.py:418
  39.3 4.7 %give.1 = (bf16[16,128,512]{2,1,0:T(8,128)(2,1)S(1)}, bf16[128,512]{1,0:T(8,128)(2,1)S(1)}) custom-call(s32[5]{0:T(128)S(1)} %stack.24.place_ref, f32[256,512]{1,0:T(8,128)S(1)} %get-tuple-element.29.step_ref, f32[4,32,64]{2,1,0:T(8,128)S(1)} %get-tuple-element.30.states_ref, f32[16,512]{1,0:T(8,128)S(1)} %copy-done.7, bf16[256,512]{1,0:T(8,128)(2,1)S(1)} %copy-done.1, ...), custom_call_target="tpu_custom_call" | custom-call | tf_op jit(solution)/shard_map/give/pallas_call | solution.py:427
  44.0 1.3 %collective-permute-start.12 = (bf16[16,128,512]{2,1,0:T(8,128)(2,1)S(1)}, bf16[16,128,512]{2,1,0:T(8,128)(2,1)S(1)}, u32[]{:S(2)}, u32[]{:S(2)}) collective-permute-start(bf16[16,128,512]{2,1,0:T(8,128)(2,1)S(1)} %get-tuple-element.33), channel_id=1, source_target_pairs={{0,1},{1,0},{2,3},{3,2},{4,5},{5,4},{6,7},{7,6},{8,9},{9,8},{10,11... | collective-permute-start | bytes 6291464 | tf_op jit(solution)/shard_map/ppermute | solution.py:363
  45.4 1.8 %keep.1.keep_ref = bf16[16,128,512]{2,1,0:T(8,128)(2,1)S(1)} custom-call(s32[5]{0:T(128)S(1)} %stack.24.place_ref, bf16[128,512]{1,0:T(8,128)(2,1)S(1)} %get-tuple-element.32.kept_ref, bf16[512,8192]{1,0:T(8,128)(2,1)S(1)} %bring.1.weight_ref), custom_call_target="tpu_custom_call" | custom-call | tf_op jit(solution)/shard_map/keep/pallas_call | solution.py:443
  47.2 1.9 %collective-permute-done.12.got_ref = bf16[16,128,512]{2,1,0:T(8,128)(2,1)S(1)} collective-permute-done((bf16[16,128,512]{2,1,0:T(8,128)(2,1)S(1)}, bf16[16,128,512]{2,1,0:T(8,128)(2,1)S(1)}, u32[]{:S(2)}, u32[]{:S(2)}) %collective-permute-start.12) | collective-permute-done | bytes 2097184 | tf_op jit(solution)/shard_map/ppermute | solution.py:363
  49.6 1.0 collective-permute-start.13
  50.6 2.5 %collective-permute-start.14 = (bf16[4,128,512]{2,1,0:T(8,128)(2,1)S(1)}, bf16[4,128,512]{2,1,0:T(8,128)(2,1)S(1)}, u32[]{:S(2)}, u32[]{:S(2)}) collective-permute-start(bf16[4,128,512]{2,1,0:T(8,128)(2,1)S(1)} %get-tuple-element.36), channel_id=1, source_target_pairs={{0,16},{1,5},{2,18},{3,7},{4,20},{5,1},{6,22},{7,3},{8,24},{9,13},... | collective-permute-start | bytes 1572872 | tf_op jit(solution)/shard_map/ppermute | solution.py:344
  53.9 5.3 %collective-permute-done.13.one_ref = bf16[4,128,512]{2,1,0:T(8,128)(2,1)S(1)} collective-permute-done((bf16[4,128,512]{2,1,0:T(8,128)(2,1)S(1)}, bf16[4,128,512]{2,1,0:T(8,128)(2,1)S(1)}, u32[]{:S(2)}, u32[]{:S(2)}) %collective-permute-start.13) | collective-permute-done | bytes 524320 | tf_op jit(solution)/shard_map/ppermute | solution.py:344
  59.2 6.4 %collective-permute-done.14.two_ref = bf16[4,128,512]{2,1,0:T(8,128)(2,1)S(1)} collective-permute-done((bf16[4,128,512]{2,1,0:T(8,128)(2,1)S(1)}, bf16[4,128,512]{2,1,0:T(8,128)(2,1)S(1)}, u32[]{:S(2)}, u32[]{:S(2)}) %collective-permute-start.14) | collective-permute-done | bytes 524320 | tf_op jit(solution)/shard_map/ppermute | solution.py:344
  65.9 1.1 collective-permute-start.16
  67.0 2.4 %collective-permute-start.17 = (bf16[128,512]{1,0:T(8,128)(2,1)S(1)}, bf16[128,512]{1,0:T(8,128)(2,1)S(1)}, u32[]{:S(2)}, u32[]{:S(2)}) collective-permute-start(bf16[128,512]{1,0:T(8,128)(2,1)S(1)} %get-tuple-element.40), channel_id=1, source_target_pairs={{0,4},{1,17},{2,6},{3,19},{4,0},{5,21},{6,2},{7,23},{8,12},{9,25},... | collective-permute-start | bytes 393224 | tf_op jit(solution)/shard_map/ppermute | solution.py:344
  70.1 0.9 collective-permute-done.16.one_ref
  71.0 2.1 %collective-permute-done.17.two_ref = bf16[128,512]{1,0:T(8,128)(2,1)S(1)} collective-permute-done((bf16[128,512]{1,0:T(8,128)(2,1)S(1)}, bf16[128,512]{1,0:T(8,128)(2,1)S(1)}, u32[]{:S(2)}, u32[]{:S(2)}) %collective-permute-start.17) | collective-permute-done | bytes 131104 | tf_op jit(solution)/shard_map/ppermute | solution.py:344
  73.2 1.3 layer.1
  74.5 1.8 %collective-permute-start.20 = (bf16[4,144,128]{2,1,0:T(8,128)(2,1)S(1)}, bf16[4,144,128]{2,1,0:T(8,128)(2,1)S(1)}, u32[]{:S(2)}, u32[]{:S(2)}) collective-permute-start(bf16[4,144,128]{2,1,0:T(8,128)(2,1)S(1)} %get-tuple-element.44), channel_id=1, source_target_pairs={{0,8},{1,3},{2,10},{3,5},{4,12},{5,7},{6,14},{7,1},{8,16},{9,11},{... | collective-permute-start | bytes 442376 | tf_op jit(solution)/shard_map/ppermute | solution.py:344
  76.2 2.1 %collective-permute-start.21 = (bf16[4,144,128]{2,1,0:T(8,128)(2,1)S(1)}, bf16[4,144,128]{2,1,0:T(8,128)(2,1)S(1)}, u32[]{:S(2)}, u32[]{:S(2)}) collective-permute-start(bf16[4,144,128]{2,1,0:T(8,128)(2,1)S(1)} %get-tuple-element.45), channel_id=1, source_target_pairs={{0,16},{1,5},{2,18},{3,7},{4,20},{5,1},{6,22},{7,3},{8,24},{9,13},... | collective-permute-start | bytes 442376 | tf_op jit(solution)/shard_map/ppermute | solution.py:344
  78.7 1.0 collective-permute-done.20.refs_1_
  79.7 2.7 %collective-permute-done.21.refs_2_ = bf16[4,144,128]{2,1,0:T(8,128)(2,1)S(1)} collective-permute-done((bf16[4,144,128]{2,1,0:T(8,128)(2,1)S(1)}, bf16[4,144,128]{2,1,0:T(8,128)(2,1)S(1)}, u32[]{:S(2)}, u32[]{:S(2)}) %collective-permute-start.21) | collective-permute-done | bytes 147488 | tf_op jit(solution)/shard_map/ppermute | solution.py:344
  82.7 1.1 collective-permute-start.23
  83.8 2.2 %collective-permute-start.24 = (bf16[4,144,128]{2,1,0:T(8,128)(2,1)S(1)}, bf16[4,144,128]{2,1,0:T(8,128)(2,1)S(1)}, u32[]{:S(2)}, u32[]{:S(2)}) collective-permute-start(bf16[4,144,128]{2,1,0:T(8,128)(2,1)S(1)} %kv.1.own_part_ref), channel_id=1, source_target_pairs={{0,4},{1,17},{2,6},{3,19},{4,0},{5,21},{6,2},{7,23},{8,12},{9,25},... | collective-permute-start | bytes 442376 | tf_op jit(solution)/shard_map/ppermute | solution.py:344
  86.5 5.0 %collective-permute-start.26 = (bf16[128,256]{1,0:T(8,128)(2,1)S(1)}, bf16[128,256]{1,0:T(8,128)(2,1)S(1)}, u32[]{:S(2)}, u32[]{:S(2)}) collective-permute-start(bf16[128,256]{1,0:T(8,128)(2,1)S(1)} %get-tuple-element.48), channel_id=1, source_target_pairs={{0,1},{1,0},{2,3},{3,2},{4,5},{5,4},{6,7},{7,6},{8,9},{9,8},{10,11... | collective-permute-start | bytes 196616 | tf_op jit(solution)/shard_map/ppermute | solution.py:363
  92.4 1.2 tile.1
  94.4 1.9 %collective-permute-start.28 = (bf16[4,128,128]{2,1,0:T(8,128)(2,1)S(1)}, bf16[4,128,128]{2,1,0:T(8,128)(2,1)S(1)}, u32[]{:S(2)}, u32[]{:S(2)}) collective-permute-start(bf16[4,128,128]{2,1,0:T(8,128)(2,1)S(1)} %get-tuple-element.50.own_ref), channel_id=1, source_target_pairs={{0,64},{32,96},{64,0},{96,32},{1,65},{33,97},{65,1},{97,33},{2,66}... | collective-permute-start | bytes 393224 | tf_op jit(solution)/shard_map/ppermute | solution.py:414
  96.8 1.9 %collective-permute-done.27.near_ref = bf16[4,128,128]{2,1,0:T(8,128)(2,1)S(1)} collective-permute-done((bf16[4,128,128]{2,1,0:T(8,128)(2,1)S(1)}, bf16[4,128,128]{2,1,0:T(8,128)(2,1)S(1)}, u32[]{:S(2)}, u32[]{:S(2)}) %collective-permute-start.27) | collective-permute-done | bytes 131104 | tf_op jit(solution)/shard_map/ppermute | solution.py:414
  98.7 1.4 %collective-permute-done.28.mid_ref = bf16[4,128,128]{2,1,0:T(8,128)(2,1)S(1)} collective-permute-done((bf16[4,128,128]{2,1,0:T(8,128)(2,1)S(1)}, bf16[4,128,128]{2,1,0:T(8,128)(2,1)S(1)}, u32[]{:S(2)}, u32[]{:S(2)}) %collective-permute-start.28) | collective-permute-done | bytes 131104 | tf_op jit(solution)/shard_map/ppermute | solution.py:414
  101.3 1.0 collective-permute-start.32
  103.3 1.7 %collective-permute-start.31 = (bf16[4,4,128,128]{3,2,1,0:T(8,128)(2,1)S(1)}, bf16[4,4,128,128]{3,2,1,0:T(8,128)(2,1)S(1)}, u32[]{:S(2)}, u32[]{:S(2)}) collective-permute-start(bf16[4,4,128,128]{3,2,1,0:T(8,128)(2,1)S(1)} %stack.25.one_ref.q0), channel_id=1, source_target_pairs={{0,24},{1,7},{2,26},{3,1},{4,28},{5,3},{6,30},{7,5},{8,0},{9,15},{... | collective-permute-start | bytes 1572872 | tf_op jit(solution)/shard_map/ppermute | solution.py:344
  105.1 11.2 %collective-permute-done.32.two_ref.q1 = bf16[4,4,128,128]{3,2,1,0:T(8,128)(2,1)S(1)} collective-permute-done((bf16[4,4,128,128]{3,2,1,0:T(8,128)(2,1)S(1)}, bf16[4,4,128,128]{3,2,1,0:T(8,128)(2,1)S(1)}, u32[]{:S(2)}, u32[]{:S(2)}) %collective-permute-start.32) | collective-permute-done | bytes 524320 | tf_op jit(solution)/shard_map/ppermute | solution.py:344
  117.4 1.5 %collective-permute-done.33.one_ref = bf16[2,8,128,128]{3,2,1,0:T(8,128)(2,1)S(1)} collective-permute-done((bf16[2,8,128,128]{3,2,1,0:T(8,128)(2,1)S(1)}, bf16[2,8,128,128]{3,2,1,0:T(8,128)(2,1)S(1)}, u32[]{:S(2)}, u32[]{:S(2)}) %collective-permute-start.33) | collective-permute-done | bytes 524320 | tf_op jit(solution)/shard_map/ppermute | solution.py:363
  119.6 4.5 %collective-permute-start.34 = (bf16[2,8,128,128]{3,2,1,0:T(8,128)(2,1)S(1)}, bf16[2,8,128,128]{3,2,1,0:T(8,128)(2,1)S(1)}, u32[]{:S(2)}, u32[]{:S(2)}) collective-permute-start(bf16[2,8,128,128]{3,2,1,0:T(8,128)(2,1)S(1)} %pick1.1), channel_id=1, source_target_pairs={{0,1},{1,0},{2,3},{3,2},{4,5},{5,4},{6,7},{7,6},{8,9},{9,8},{10,11... | collective-permute-start | bytes 1572872 | tf_op jit(solution)/shard_map/ppermute | solution.py:363
  124.1 1.8 %own.1._ = bf16[4,4,4,128,128]{4,3,2,1,0:T(8,128)(2,1)} custom-call(s32[5]{0:T(128)S(1)} %stack.24.place_ref, s32[128]{0:T(128)S(1)} %get-tuple-element.55.starts_ref, s32[128]{0:T(128)S(1)} %get-tuple-element.54.counts_ref, bf16[4,4,128,128]{3,2,1,0:T(8,128)(2,1)S(1)} %stack.25.one_ref.q0, bf16[4,4,128,128]{3,2,1,0:T(8,128)(2,1)S(1)} %collective-permute-done.32.two_ref.q1, ...), custom_call_target="tpu_custom_call" | custom-call | tf_op jit(solution)/shard_map/own/pallas_call | solution.py:508
  126.0 1.6 %rest.1 = bf16[4,4,4,128,128]{4,3,2,1,0:T(8,128)(2,1)} custom-call(s32[5]{0:T(128)S(1)} %stack.24.place_ref, s32[128]{0:T(128)S(1)} %get-tuple-element.55.starts_ref, bf16[2,8,128,128]{3,2,1,0:T(8,128)(2,1)S(1)} %collective-permute-done.33.one_ref, bf16[2,8,128,128]{3,2,1,0:T(8,128)(2,1)S(1)} %collective-permute-done.34.two_ref, ...), custom_call_target="tpu_custom_call", output_to_operand_aliasing={{}: (4, {})} | custom-call | tf_op jit(solution)/shard_map/rest/pallas_call | solution.py:517
  (73 shorter events, 14.1 us)
Async XLA Ops:
  0.7 26.5 %copy-start.7 = (f32[16,512]{1,0:T(8,128)S(1)}, f32[16,512]{1,0:T(8,128)}, u32[]{:S(2)}) copy-start(f32[16,512]{1,0:T(8,128)} %alog_ref.3) | copy-start | bytes 98308
  0.7 26.5 %copy-start.9 = (f32[512]{0:T(512)S(1)}, f32[512]{0:T(512)}, u32[]{:S(2)}) copy-start(f32[512]{0:T(512)} %param.20) | copy-start | bytes 6148
  2.8 24.4 %copy-start.1 = (bf16[256,512]{1,0:T(8,128)(2,1)S(1)}, bf16[256,512]{1,0:T(8,128)(2,1)}, u32[]{:S(2)}) copy-start(bf16[256,512]{1,0:T(8,128)(2,1)} %conv_ref.7) | copy-start | bytes 786436
  2.8 24.4 %copy-start.5 = (bf16[512,512]{1,0:T(8,128)(2,1)S(1)}, bf16[512,512]{1,0:T(8,128)(2,1)}, u32[]{:S(2)}) copy-start(bf16[512,512]{1,0:T(8,128)(2,1)} %weight_ref.2) | copy-start | bytes 1572868
  3.6 2.9 %collective-permute-start = (bf16[144,512]{1,0:T(8,128)(2,1)S(1)}, bf16[144,512]{1,0:T(8,128)(2,1)S(1)}, u32[]{:S(2)}, u32[]{:S(2)}) collective-permute-start(bf16[144,512]{1,0:T(8,128)(2,1)S(1)} %project_give.1), channel_id=1, source_target_pairs={{0,1},{1,0},{2,3},{3,2},{4,5},{5,4},{6,7},{7,6},{8,9},{9,8},{10,11... | collective-permute-start | bytes 442376 | tf_op jit(solution)/shard_map/ppermute | solution.py:363
  5.1 1.4 %collective-permute-start.1 = (f32[1,256]{1,0:T(1,128)}, f32[1,256]{1,0:T(1,128)S(1)}, u32[]{:S(2)}, u32[]{:S(2)}) collective-permute-start(f32[1,256]{1,0:T(1,128)} %bitcast.14), channel_id=1, source_target_pairs={{0,1},{1,0},{2,3},{3,2},{4,5},{5,4},{6,7},{7,6},{8,9},{9,8},{10,11... | collective-permute-start | bytes 3080 | tf_op jit(solution)/shard_map/ppermute | solution.py:363
  6.5 5.7 %collective-permute-start.2 = (bf16[144,512]{1,0:T(8,128)(2,1)S(1)}, bf16[144,512]{1,0:T(8,128)(2,1)S(1)}, u32[]{:S(2)}, u32[]{:S(2)}) collective-permute-start(bf16[144,512]{1,0:T(8,128)(2,1)S(1)} %chip.1.refs_0_), channel_id=1, source_target_pairs={{0,8},{1,3},{2,10},{3,5},{4,12},{5,7},{6,14},{7,1},{8,16},{9,11},{... | collective-permute-start | bytes 442376 | tf_op jit(solution)/shard_map/ppermute | solution.py:344
  8.0 7.0 %collective-permute-start.3 = (bf16[144,512]{1,0:T(8,128)(2,1)S(1)}, bf16[144,512]{1,0:T(8,128)(2,1)S(1)}, u32[]{:S(2)}, u32[]{:S(2)}) collective-permute-start(bf16[144,512]{1,0:T(8,128)(2,1)S(1)} %chip.1.refs_0_), channel_id=1, source_target_pairs={{0,16},{1,5},{2,18},{3,7},{4,20},{5,1},{6,22},{7,3},{8,24},{9,13},... | collective-permute-start | bytes 442376 | tf_op jit(solution)/shard_map/ppermute | solution.py:344
  10.6 4.4 %collective-permute-start.4 = (bf16[144,512]{1,0:T(8,128)(2,1)S(1)}, bf16[144,512]{1,0:T(8,128)(2,1)S(1)}, u32[]{:S(2)}, u32[]{:S(2)}) collective-permute-start(bf16[144,512]{1,0:T(8,128)(2,1)S(1)} %chip.1.refs_0_), channel_id=1, source_target_pairs={{0,24},{1,7},{2,26},{3,1},{4,28},{5,3},{6,30},{7,5},{8,0},{9,15},{... | collective-permute-start | bytes 442376 | tf_op jit(solution)/shard_map/ppermute | solution.py:344
  15.1 5.3 %collective-permute-start.5 = (bf16[144,512]{1,0:T(8,128)(2,1)S(1)}, bf16[144,512]{1,0:T(8,128)(2,1)S(1)}, u32[]{:S(2)}, u32[]{:S(2)}) collective-permute-start(bf16[144,512]{1,0:T(8,128)(2,1)S(1)} %row.1.refs_0_), channel_id=1, source_target_pairs={{0,2},{1,9},{2,4},{3,11},{4,6},{5,13},{6,0},{7,15},{8,10},{9,17},{... | collective-permute-start | bytes 442376 | tf_op jit(solution)/shard_map/ppermute | solution.py:344
  16.3 6.6 %collective-permute-start.6 = (bf16[144,512]{1,0:T(8,128)(2,1)S(1)}, bf16[144,512]{1,0:T(8,128)(2,1)S(1)}, u32[]{:S(2)}, u32[]{:S(2)}) collective-permute-start(bf16[144,512]{1,0:T(8,128)(2,1)S(1)} %row.1.refs_0_), channel_id=1, source_target_pairs={{0,4},{1,17},{2,6},{3,19},{4,0},{5,21},{6,2},{7,23},{8,12},{9,25},... | collective-permute-start | bytes 442376 | tf_op jit(solution)/shard_map/ppermute | solution.py:344
  18.7 4.1 %collective-permute-start.7 = (bf16[144,512]{1,0:T(8,128)(2,1)S(1)}, bf16[144,512]{1,0:T(8,128)(2,1)S(1)}, u32[]{:S(2)}, u32[]{:S(2)}) collective-permute-start(bf16[144,512]{1,0:T(8,128)(2,1)S(1)} %row.1.refs_0_), channel_id=1, source_target_pairs={{0,6},{1,25},{2,0},{3,27},{4,2},{5,29},{6,4},{7,31},{8,14},{9,1},{... | collective-permute-start | bytes 442376 | tf_op jit(solution)/shard_map/ppermute | solution.py:344
  22.9 4.3 %collective-permute-start.8 = (bf16[144,512]{1,0:T(8,128)(2,1)S(1)}, bf16[144,512]{1,0:T(8,128)(2,1)S(1)}, u32[]{:S(2)}, u32[]{:S(2)}) collective-permute-start(bf16[144,512]{1,0:T(8,128)(2,1)S(1)} %plane.1.own_proj_ref), channel_id=1, source_target_pairs={{0,1},{1,0},{2,3},{3,2},{4,5},{5,4},{6,7},{7,6},{8,9},{9,8},{10,11... | collective-permute-start | bytes 442376 | tf_op jit(solution)/shard_map/ppermute | solution.py:363
  29.9 9.3 %copy-start.4 = (bf16[256,256]{1,0:T(8,128)(2,1)S(1)}, bf16[256,256]{1,0:T(8,128)(2,1)}, u32[]{:S(2)}) copy-start(bf16[256,256]{1,0:T(8,128)(2,1)} %residual_ref.3) | copy-start | bytes 393220
  29.9 9.3 %copy-start.6 = (bf16[256,512]{1,0:T(8,128)(2,1)S(1)}, bf16[256,512]{1,0:T(8,128)(2,1)}, u32[]{:S(2)}) copy-start(bf16[256,512]{1,0:T(8,128)(2,1)} %gate_ref.1) | copy-start | bytes 786436
  29.9 9.3 %copy-start.8 = (f32[16,512]{1,0:T(8,128)S(1)}, f32[16,512]{1,0:T(8,128)}, u32[]{:S(2)}) copy-start(f32[16,512]{1,0:T(8,128)} %init_ref.1) | copy-start | bytes 98308
  29.9 9.3 %copy-start.10 = (f32[512]{0:T(512)S(1)}, f32[512]{0:T(512)}, u32[]{:S(2)}) copy-start(f32[512]{0:T(512)} %param.22) | copy-start | bytes 6148
  30.0 9.3 %collective-permute-start.9 = (f32[24,512]{1,0:T(8,128)S(1)}, f32[24,512]{1,0:T(8,128)S(1)}, u32[]{:S(2)}, u32[]{:S(2)}) collective-permute-start(f32[24,512]{1,0:T(8,128)S(1)} %get-tuple-element.31._), channel_id=1, source_target_pairs={{0,32},{32,64},{64,96},{96,0},{1,33},{33,65},{65,97},{97,1},{2,34}... | collective-permute-start | bytes 147464 | tf_op jit(solution)/shard_map/ppermute | solution.py:414
  31.7 7.6 %collective-permute-start.10 = (f32[24,512]{1,0:T(8,128)S(1)}, f32[24,512]{1,0:T(8,128)S(1)}, u32[]{:S(2)}, u32[]{:S(2)}) collective-permute-start(f32[24,512]{1,0:T(8,128)S(1)} %get-tuple-element.31._), channel_id=1, source_target_pairs={{0,64},{32,96},{64,0},{96,32},{1,65},{33,97},{65,1},{97,33},{2,66}... | collective-permute-start | bytes 147464 | tf_op jit(solution)/shard_map/ppermute | solution.py:414
  35.0 4.3 %collective-permute-start.11 = (f32[24,512]{1,0:T(8,128)S(1)}, f32[24,512]{1,0:T(8,128)S(1)}, u32[]{:S(2)}, u32[]{:S(2)}) collective-permute-start(f32[24,512]{1,0:T(8,128)S(1)} %get-tuple-element.31._), channel_id=1, source_target_pairs={{0,96},{32,0},{64,32},{96,64},{1,97},{33,1},{65,33},{97,65},{2,98}... | collective-permute-start | bytes 147464 | tf_op jit(solution)/shard_map/ppermute | solution.py:414
  39.3 6.1 %copy-start.3 = (bf16[256,2048]{1,0:T(8,128)(2,1)S(1)}, bf16[256,2048]{1,0:T(8,128)(2,1)}, u32[]{:S(2)}) copy-start(bf16[256,2048]{1,0:T(8,128)(2,1)} %own_weight_ref.1) | copy-start | bytes 3145732
  44.0 5.1 %collective-permute-start.12 = (bf16[16,128,512]{2,1,0:T(8,128)(2,1)S(1)}, bf16[16,128,512]{2,1,0:T(8,128)(2,1)S(1)}, u32[]{:S(2)}, u32[]{:S(2)}) collective-permute-start(bf16[16,128,512]{2,1,0:T(8,128)(2,1)S(1)} %get-tuple-element.33), channel_id=1, source_target_pairs={{0,1},{1,0},{2,3},{3,2},{4,5},{5,4},{6,7},{7,6},{8,9},{9,8},{10,11... | collective-permute-start | bytes 6291464 | tf_op jit(solution)/shard_map/ppermute | solution.py:363
  45.3 24.7 %collective-permute-start.19 = (bf16[256,2048]{1,0:T(8,128)(2,1)S(1)}, bf16[256,2048]{1,0:T(8,128)(2,1)S(1)}, u32[]{:S(2)}, u32[]{:S(2)}) collective-permute-start(bf16[256,2048]{1,0:T(8,128)(2,1)S(1)} %copy-done.3), channel_id=1, source_target_pairs={{0,1},{1,0},{2,3},{3,2},{4,5},{5,4},{6,7},{7,6},{8,9},{9,8},{10,11... | collective-permute-start | bytes 3145736 | tf_op jit(solution)/shard_map/ppermute | solution.py:363
  49.6 23.6 %copy-start.11 = (f32[256]{0:T(256)S(1)}, f32[256]{0:T(256)}, u32[]{:S(2)}) copy-start(f32[256]{0:T(256)} %param.25) | copy-start | bytes 3076
  49.6 9.6 %collective-permute-start.13 = (bf16[4,128,512]{2,1,0:T(8,128)(2,1)S(1)}, bf16[4,128,512]{2,1,0:T(8,128)(2,1)S(1)}, u32[]{:S(2)}, u32[]{:S(2)}) collective-permute-start(bf16[4,128,512]{2,1,0:T(8,128)(2,1)S(1)} %get-tuple-element.35), channel_id=1, source_target_pairs={{0,8},{1,3},{2,10},{3,5},{4,12},{5,7},{6,14},{7,1},{8,16},{9,11},{... | collective-permute-start | bytes 1572872 | tf_op jit(solution)/shard_map/ppermute | solution.py:344
  50.6 15.0 %collective-permute-start.14 = (bf16[4,128,512]{2,1,0:T(8,128)(2,1)S(1)}, bf16[4,128,512]{2,1,0:T(8,128)(2,1)S(1)}, u32[]{:S(2)}, u32[]{:S(2)}) collective-permute-start(bf16[4,128,512]{2,1,0:T(8,128)(2,1)S(1)} %get-tuple-element.36), channel_id=1, source_target_pairs={{0,16},{1,5},{2,18},{3,7},{4,20},{5,1},{6,22},{7,3},{8,24},{9,13},... | collective-permute-start | bytes 1572872 | tf_op jit(solution)/shard_map/ppermute | solution.py:344
  53.1 12.5 %collective-permute-start.15 = (bf16[4,128,512]{2,1,0:T(8,128)(2,1)S(1)}, bf16[4,128,512]{2,1,0:T(8,128)(2,1)S(1)}, u32[]{:S(2)}, u32[]{:S(2)}) collective-permute-start(bf16[4,128,512]{2,1,0:T(8,128)(2,1)S(1)} %get-tuple-element.37), channel_id=1, source_target_pairs={{0,24},{1,7},{2,26},{3,1},{4,28},{5,3},{6,30},{7,5},{8,0},{9,15},{... | collective-permute-start | bytes 1572872 | tf_op jit(solution)/shard_map/ppermute | solution.py:344
  65.9 5.1 %collective-permute-start.16 = (bf16[128,512]{1,0:T(8,128)(2,1)S(1)}, bf16[128,512]{1,0:T(8,128)(2,1)S(1)}, u32[]{:S(2)}, u32[]{:S(2)}) collective-permute-start(bf16[128,512]{1,0:T(8,128)(2,1)S(1)} %get-tuple-element.39), channel_id=1, source_target_pairs={{0,2},{1,9},{2,4},{3,11},{4,6},{5,13},{6,0},{7,15},{8,10},{9,17},{... | collective-permute-start | bytes 393224 | tf_op jit(solution)/shard_map/ppermute | solution.py:344
  67.0 6.1 %collective-permute-start.17 = (bf16[128,512]{1,0:T(8,128)(2,1)S(1)}, bf16[128,512]{1,0:T(8,128)(2,1)S(1)}, u32[]{:S(2)}, u32[]{:S(2)}) collective-permute-start(bf16[128,512]{1,0:T(8,128)(2,1)S(1)} %get-tuple-element.40), channel_id=1, source_target_pairs={{0,4},{1,17},{2,6},{3,19},{4,0},{5,21},{6,2},{7,23},{8,12},{9,25},... | collective-permute-start | bytes 393224 | tf_op jit(solution)/shard_map/ppermute | solution.py:344
  69.3 3.8 %collective-permute-start.18 = (bf16[128,512]{1,0:T(8,128)(2,1)S(1)}, bf16[128,512]{1,0:T(8,128)(2,1)S(1)}, u32[]{:S(2)}, u32[]{:S(2)}) collective-permute-start(bf16[128,512]{1,0:T(8,128)(2,1)S(1)} %get-tuple-element.41), channel_id=1, source_target_pairs={{0,6},{1,25},{2,0},{3,27},{4,2},{5,29},{6,4},{7,31},{8,14},{9,1},{... | collective-permute-start | bytes 393224 | tf_op jit(solution)/shard_map/ppermute | solution.py:344
  73.2 29.2 %copy-start.12 = (s32[128]{0:T(128)S(1)}, s32[128]{0:T(128)}, u32[]{:S(2)}) copy-start(s32[128]{0:T(128)} %param.29) | copy-start | bytes 1540
  73.2 29.2 %copy-start.13 = (s32[128]{0:T(128)S(1)}, s32[128]{0:T(128)}, u32[]{:S(2)}) copy-start(s32[128]{0:T(128)} %param.27) | copy-start | bytes 1540
  73.2 29.2 %copy-start.14 = (s32[128]{0:T(128)S(1)}, s32[128]{0:T(128)}, u32[]{:S(2)}) copy-start(s32[128]{0:T(128)} %param.28) | copy-start | bytes 1540
  74.5 5.3 %collective-permute-start.20 = (bf16[4,144,128]{2,1,0:T(8,128)(2,1)S(1)}, bf16[4,144,128]{2,1,0:T(8,128)(2,1)S(1)}, u32[]{:S(2)}, u32[]{:S(2)}) collective-permute-start(bf16[4,144,128]{2,1,0:T(8,128)(2,1)S(1)} %get-tuple-element.44), channel_id=1, source_target_pairs={{0,8},{1,3},{2,10},{3,5},{4,12},{5,7},{6,14},{7,1},{8,16},{9,11},{... | collective-permute-start | bytes 442376 | tf_op jit(solution)/shard_map/ppermute | solution.py:344
  76.2 6.2 %collective-permute-start.21 = (bf16[4,144,128]{2,1,0:T(8,128)(2,1)S(1)}, bf16[4,144,128]{2,1,0:T(8,128)(2,1)S(1)}, u32[]{:S(2)}, u32[]{:S(2)}) collective-permute-start(bf16[4,144,128]{2,1,0:T(8,128)(2,1)S(1)} %get-tuple-element.45), channel_id=1, source_target_pairs={{0,16},{1,5},{2,18},{3,7},{4,20},{5,1},{6,22},{7,3},{8,24},{9,13},... | collective-permute-start | bytes 442376 | tf_op jit(solution)/shard_map/ppermute | solution.py:344
  78.3 4.3 %collective-permute-start.22 = (bf16[4,144,128]{2,1,0:T(8,128)(2,1)S(1)}, bf16[4,144,128]{2,1,0:T(8,128)(2,1)S(1)}, u32[]{:S(2)}, u32[]{:S(2)}) collective-permute-start(bf16[4,144,128]{2,1,0:T(8,128)(2,1)S(1)} %get-tuple-element.46), channel_id=1, source_target_pairs={{0,24},{1,7},{2,26},{3,1},{4,28},{5,3},{6,30},{7,5},{8,0},{9,15},{... | collective-permute-start | bytes 442376 | tf_op jit(solution)/shard_map/ppermute | solution.py:344
  82.7 9.7 %collective-permute-start.23 = (bf16[4,144,128]{2,1,0:T(8,128)(2,1)S(1)}, bf16[4,144,128]{2,1,0:T(8,128)(2,1)S(1)}, u32[]{:S(2)}, u32[]{:S(2)}) collective-permute-start(bf16[4,144,128]{2,1,0:T(8,128)(2,1)S(1)} %kv.1.own_part_ref), channel_id=1, source_target_pairs={{0,2},{1,9},{2,4},{3,11},{4,6},{5,13},{6,0},{7,15},{8,10},{9,17},{... | collective-permute-start | bytes 442376 | tf_op jit(solution)/shard_map/ppermute | solution.py:344
  83.8 8.6 %collective-permute-start.24 = (bf16[4,144,128]{2,1,0:T(8,128)(2,1)S(1)}, bf16[4,144,128]{2,1,0:T(8,128)(2,1)S(1)}, u32[]{:S(2)}, u32[]{:S(2)}) collective-permute-start(bf16[4,144,128]{2,1,0:T(8,128)(2,1)S(1)} %kv.1.own_part_ref), channel_id=1, source_target_pairs={{0,4},{1,17},{2,6},{3,19},{4,0},{5,21},{6,2},{7,23},{8,12},{9,25},... | collective-permute-start | bytes 442376 | tf_op jit(solution)/shard_map/ppermute | solution.py:344
  86.0 6.4 %collective-permute-start.25 = (bf16[4,144,128]{2,1,0:T(8,128)(2,1)S(1)}, bf16[4,144,128]{2,1,0:T(8,128)(2,1)S(1)}, u32[]{:S(2)}, u32[]{:S(2)}) collective-permute-start(bf16[4,144,128]{2,1,0:T(8,128)(2,1)S(1)} %kv.1.own_part_ref), channel_id=1, source_target_pairs={{0,6},{1,25},{2,0},{3,27},{4,2},{5,29},{6,4},{7,31},{8,14},{9,1},{... | collective-permute-start | bytes 442376 | tf_op jit(solution)/shard_map/ppermute | solution.py:344
  86.5 5.9 %collective-permute-start.26 = (bf16[128,256]{1,0:T(8,128)(2,1)S(1)}, bf16[128,256]{1,0:T(8,128)(2,1)S(1)}, u32[]{:S(2)}, u32[]{:S(2)}) collective-permute-start(bf16[128,256]{1,0:T(8,128)(2,1)S(1)} %get-tuple-element.48), channel_id=1, source_target_pairs={{0,1},{1,0},{2,3},{3,2},{4,5},{5,4},{6,7},{7,6},{8,9},{9,8},{10,11... | collective-permute-start | bytes 196616 | tf_op jit(solution)/shard_map/ppermute | solution.py:363
  93.7 5.0 %collective-permute-start.27 = (bf16[4,128,128]{2,1,0:T(8,128)(2,1)S(1)}, bf16[4,128,128]{2,1,0:T(8,128)(2,1)S(1)}, u32[]{:S(2)}, u32[]{:S(2)}) collective-permute-start(bf16[4,128,128]{2,1,0:T(8,128)(2,1)S(1)} %get-tuple-element.50.own_ref), channel_id=1, source_target_pairs={{0,32},{32,64},{64,96},{96,0},{1,33},{33,65},{65,97},{97,1},{2,34}... | collective-permute-start | bytes 393224 | tf_op jit(solution)/shard_map/ppermute | solution.py:414
  94.4 5.7 %collective-permute-start.28 = (bf16[4,128,128]{2,1,0:T(8,128)(2,1)S(1)}, bf16[4,128,128]{2,1,0:T(8,128)(2,1)S(1)}, u32[]{:S(2)}, u32[]{:S(2)}) collective-permute-start(bf16[4,128,128]{2,1,0:T(8,128)(2,1)S(1)} %get-tuple-element.50.own_ref), channel_id=1, source_target_pairs={{0,64},{32,96},{64,0},{96,32},{1,65},{33,97},{65,1},{97,33},{2,66}... | collective-permute-start | bytes 393224 | tf_op jit(solution)/shard_map/ppermute | solution.py:414
  96.3 4.4 %collective-permute-start.29 = (bf16[4,128,128]{2,1,0:T(8,128)(2,1)S(1)}, bf16[4,128,128]{2,1,0:T(8,128)(2,1)S(1)}, u32[]{:S(2)}, u32[]{:S(2)}) collective-permute-start(bf16[4,128,128]{2,1,0:T(8,128)(2,1)S(1)} %get-tuple-element.50.own_ref), channel_id=1, source_target_pairs={{0,96},{32,0},{64,32},{96,64},{1,97},{33,1},{65,33},{97,65},{2,98}... | collective-permute-start | bytes 393224 | tf_op jit(solution)/shard_map/ppermute | solution.py:414
  101.3 14.9 %collective-permute-start.32 = (bf16[4,4,128,128]{3,2,1,0:T(8,128)(2,1)S(1)}, bf16[4,4,128,128]{3,2,1,0:T(8,128)(2,1)S(1)}, u32[]{:S(2)}, u32[]{:S(2)}) collective-permute-start(bf16[4,4,128,128]{3,2,1,0:T(8,128)(2,1)S(1)} %stack.25.one_ref.q0), channel_id=1, source_target_pairs={{0,8},{1,3},{2,10},{3,5},{4,12},{5,7},{6,14},{7,1},{8,16},{9,11},{... | collective-permute-start | bytes 1572872 | tf_op jit(solution)/shard_map/ppermute | solution.py:344
  102.5 14.9 %collective-permute-start.30 = (bf16[4,4,128,128]{3,2,1,0:T(8,128)(2,1)S(1)}, bf16[4,4,128,128]{3,2,1,0:T(8,128)(2,1)S(1)}, u32[]{:S(2)}, u32[]{:S(2)}) collective-permute-start(bf16[4,4,128,128]{3,2,1,0:T(8,128)(2,1)S(1)} %stack.25.one_ref.q0), channel_id=1, source_target_pairs={{0,16},{1,5},{2,18},{3,7},{4,20},{5,1},{6,22},{7,3},{8,24},{9,13},... | collective-permute-start | bytes 1572872 | tf_op jit(solution)/shard_map/ppermute | solution.py:344
  103.3 14.0 %collective-permute-start.31 = (bf16[4,4,128,128]{3,2,1,0:T(8,128)(2,1)S(1)}, bf16[4,4,128,128]{3,2,1,0:T(8,128)(2,1)S(1)}, u32[]{:S(2)}, u32[]{:S(2)}) collective-permute-start(bf16[4,4,128,128]{3,2,1,0:T(8,128)(2,1)S(1)} %stack.25.one_ref.q0), channel_id=1, source_target_pairs={{0,24},{1,7},{2,26},{3,1},{4,28},{5,3},{6,30},{7,5},{8,0},{9,15},{... | collective-permute-start | bytes 1572872 | tf_op jit(solution)/shard_map/ppermute | solution.py:344
  116.9 2.0 %collective-permute-start.33 = (bf16[2,8,128,128]{3,2,1,0:T(8,128)(2,1)S(1)}, bf16[2,8,128,128]{3,2,1,0:T(8,128)(2,1)S(1)}, u32[]{:S(2)}, u32[]{:S(2)}) collective-permute-start(bf16[2,8,128,128]{3,2,1,0:T(8,128)(2,1)S(1)} %pick0.1), channel_id=1, source_target_pairs={{0,1},{1,0},{2,3},{3,2},{4,5},{5,4},{6,7},{7,6},{8,9},{9,8},{10,11... | collective-permute-start | bytes 1572872 | tf_op jit(solution)/shard_map/ppermute | solution.py:363
  119.6 6.4 %collective-permute-start.34 = (bf16[2,8,128,128]{3,2,1,0:T(8,128)(2,1)S(1)}, bf16[2,8,128,128]{3,2,1,0:T(8,128)(2,1)S(1)}, u32[]{:S(2)}, u32[]{:S(2)}) collective-permute-start(bf16[2,8,128,128]{3,2,1,0:T(8,128)(2,1)S(1)} %pick1.1), channel_id=1, source_target_pairs={{0,1},{1,0},{2,3},{3,2},{4,5},{5,4},{6,7},{7,6},{8,9},{9,8},{10,11... | collective-permute-start | bytes 1572872 | tf_op jit(solution)/shard_map/ppermute | solution.py:363
  (2 other events, 2.0 us)

commit v6 on v5

--- a/solution.py
+++ b/solution.py
@@ -19,6 +19,7 @@
 CHUNK = 64
 PIECES = 8
 SIDE = 4
+SOON, LATER = (1, 2), (0, 3)
 EARLY, LATE = 1, (2, 3)
 BF = jnp.bfloat16
 F32 = jnp.float32
@@ -115,7 +116,7 @@
 def give_kernel(
     place_ref, step_ref, states_ref, alog_ref, conv_ref, gate_ref, skip_ref, init_ref,
     near_ref, mid_ref, far_ref, weight_ref, residual_ref,
-    give_ref, kept_ref, drive_ref, scan_ref, gated_ref,
+    soon_ref, give_ref, kept_ref, drive_ref, scan_ref, gated_ref,
 ):
     tokens = step_ref.shape[0]
     place, core = place_ref[0], place_ref[1]
@@ -136,7 +137,7 @@
         (scan_ref[...] + skip_ref[...] * conv_ref[...].astype(F32)) * (gate / (1.0 + jnp.exp(-gate)))
     ).astype(BF).reshape(gated_ref.shape)
     kept_ref[...] = gated_ref[core]
-    through(place_ref, 1 - core, gated_ref.at[1 - core], weight_ref, give_ref)
+    through(place_ref, 1 - core, gated_ref.at[1 - core], weight_ref, ((SOON, soon_ref), (LATER, give_ref)))
     rows, feats = residual_ref.shape[0] // 2, residual_ref.shape[1]
     mine = pl.ds(pl.multiple_of(core * feats, feats), feats)
     other = residual_ref[pl.ds(pl.multiple_of((1 - core) * rows, rows), rows), :]
@@ -158,31 +159,28 @@
         copy.wait()
 
 
-def chip_order(place_ref, core, chip):
-    away_x = lax.rem(chip // SIDE - place_ref[3] + SIDE, SIDE)
-    away_y = lax.rem(chip % SIDE - place_ref[4] + SIDE, SIDE)
-    return jnp.where(core == 0, away_x, away_y), jnp.where(core == 0, away_y, away_x)
-
-
-def through(place_ref, core, gated_ref, weight_ref, out_ref):
-    chips, _, wide = out_ref.shape
-    for chip in range(chips):
-        product = jnp.dot(
-            gated_ref[...], weight_ref[:, chip * wide : (chip + 1) * wide],
-            preferred_element_type=F32,
-        ).astype(BF)
-        far, near = chip_order(place_ref, core, chip)
-        out_ref[far * SIDE + near] = product
+def through(place_ref, core, gated_ref, weight_ref, parts):
+    for fars, out_ref in parts:
+        wide = out_ref.shape[2]
+        for i, far in enumerate(fars):
+            for near in range(SIDE):
+                x = lax.rem(place_ref[3] + jnp.where(core == 0, far, near), SIDE)
+                y = lax.rem(place_ref[4] + jnp.where(core == 0, near, far), SIDE)
+                columns = pl.ds(pl.multiple_of((x * SIDE + y) * wide, wide), wide)
+                out_ref[i * SIDE + near] = jnp.dot(
+                    gated_ref[...], weight_ref[:, columns], preferred_element_type=F32
+                ).astype(BF)
 
 
 def keep_kernel(place_ref, kept_ref, weight_ref, keep_ref):
-    through(place_ref, place_ref[1], kept_ref, weight_ref, keep_ref)
-
-
-def pair_kernel(keep_ref, got_ref, *out_refs):
-    for shift, ref in enumerate(out_refs):
-        rows = slice(shift * SIDE, (shift + 1) * SIDE)
-        ref[...] = (keep_ref[rows].astype(F32) + got_ref[rows].astype(F32)).astype(ref.dtype)
+    through(place_ref, place_ref[1], kept_ref, weight_ref, ((range(SIDE), keep_ref),))
+
+
+def pair_kernel(fars, keep_ref, got_ref, *out_refs):
+    for i, (far, ref) in enumerate(zip(fars, out_refs, strict=True)):
+        kept = keep_ref[far * SIDE : (far + 1) * SIDE]
+        got = got_ref[i * SIDE : (i + 1) * SIDE]
+        ref[...] = (kept.astype(F32) + got.astype(F32)).astype(ref.dtype)
 
 
 def line_kernel(own_ref, one_ref, two_ref, three_ref, *out_refs):
@@ -424,10 +422,11 @@
         name="bring",
     )(out_weight, ends)
     partial = (pairs, tokens // 2, 2 * feats)
-    give, kept = pl.pallas_call(
+    half = (pairs // 2,) + partial[1:]
+    soon, give, kept = pl.pallas_call(
         give_kernel,
         in_specs=[SM] + [VM] * 12,
-        out_shape=(shape(partial, BF), shape((tokens // 2, chans), BF)),
+        out_shape=(shape(half, BF), shape(half, BF), shape((tokens // 2, chans), BF)),
         scratch_shapes=[
             pltpu.VMEM((tokens, chans), F32),
             pltpu.VMEM((tokens, chans), F32),
@@ -439,7 +438,7 @@
         places, step, states, a_log, conv_out, gate_in, d_skip.reshape(1, chans), init_state,
         *ranges_back(ends), near_weight, residual,
     )
-    got = swap(give)
+    got_soon, got = swap(soon), swap(give)
     keep = pl.pallas_call(
         keep_kernel,
         in_specs=[SM, VM, VM],
@@ -448,9 +447,16 @@
         name="keep",
     )(places, kept, near_weight)
     quarter = shape((SIDE, tokens // 2, 2 * feats), BF)
-    sums = pl.pallas_call(
-        pair_kernel, out_shape=(quarter,) * SIDE, compiler_params=params(12), name="pair"
-    )(keep, got)
+    def pair(name, fars, got):
+        return pl.pallas_call(
+            functools.partial(pair_kernel, fars),
+            out_shape=(quarter,) * 2,
+            compiler_params=params(12),
+            name=name,
+        )(keep, got)
+
+    sums = dict(zip(SOON, pair("pair_soon", SOON, got_soon), strict=True))
+    sums.update(zip(LATER, pair("pair", LATER, got), strict=True))
     row = (tokens // 2, 2 * feats)
     parts = pl.pallas_call(
         line_kernel,

time: 128 us -> 126 us (0.984)
  waiting for transfers between devices: 45.8 us -> 43.9 us
    ppermute x8 -> x9, waiting for transfers between devices: 5.72 us -> 3.87 us  [swap(): return lax.ppermute(value, 'tp', partner)]
    ppermute x8 -> x9, starting transfers between devices: 16.2 us -> 17 us  [swap(): return lax.ppermute(value, 'tp', partner)]
    pallas_call x2 -> x3, Pallas kernels: 5.22 us -> 5.24 us  [the longest x1 4.76 us: per_device(): pl.pallas_call(give_kernel, in_specs=[SM] + [VM] * 12, out_shape=(shape(h...]
  transfers between devices with their start and end apart: 35 -> 36, of which waited for: 21 -> 19; matrix products, arithmetic and copies ran while one was open for 0% -> 0% of each run, Pallas kernels for 7% -> 7%
where the time goes in v6:
time: 126 us
  starting transfers between devices  55.4 us (44%)
  waiting for transfers between devices  43.9 us (35%)
  Pallas kernels  23.4 us (19%)
  local copies, waits for them, and re-layouts  2.15 us (2%)
    ppermute x21, waiting for transfers between devices, line(): lax.ppermute(value_of(shift), 'tp', [((x * SIDE + y) * 2 + c, ((x + shift...  35.9 us
    ppermute x21, starting transfers between devices, line(): lax.ppermute(value_of(shift), 'tp', [((x * SIDE + y) * 2 + c, ((x + shift...  30.3 us
    ppermute x9, starting transfers between devices, swap(): return lax.ppermute(value, 'tp', partner)  17 us
    ppermute x6, starting transfers between devices, ranges_back(): lax.ppermute(value, 'ctx', [(z, (z + s) % ctx_count) for z in range(ctx_c...  8.09 us
    pallas_call x1, Pallas kernels, per_device(): pl.pallas_call(give_kernel, in_specs=[SM] + [VM] * 12, out_shape=(shape(h...  4.76 us
    ppermute x6, waiting for transfers between devices, ranges_back(): lax.ppermute(value, 'ctx', [(z, (z + s) % ctx_count) for z in range(ctx_c...  4.12 us
    ppermute x9, waiting for transfers between devices, swap(): return lax.ppermute(value, 'tp', partner)  3.87 us
    pallas_call x1, Pallas kernels, per_device(): pl.pallas_call(bring_kernel, in_specs=[ANY] * 2, out_shape=shape(out_weig...  3.5 us
  transfers between devices with their start and end apart: 36, of which 19 were waited for; matrix products, arithmetic and copies ran while one was open for 0% of the time, Pallas kernels for 7%

profile of v6, /device:TPU:1, one launch (start us, length us, event | category | flops | bytes accessed | tf_op | source)
XLA Modules:
  0.0 126.0 jit_solution(6789310748264201263)
XLA Ops:
  0.8 0.9 copy-done
  1.7 1.1 copy-done.2
  3.6 1.5 %collective-permute-start = (bf16[144,512]{1,0:T(8,128)(2,1)S(1)}, bf16[144,512]{1,0:T(8,128)(2,1)S(1)}, u32[]{:S(2)}, u32[]{:S(2)}) collective-permute-start(bf16[144,512]{1,0:T(8,128)(2,1)S(1)} %project_give.1), channel_id=1, source_target_pairs={{0,1},{1,0},{2,3},{3,2},{4,5},{5,4},{6,7},{7,6},{8,9},{9,8},{10,11... | collective-permute-start | bytes 442376 | tf_op jit(solution)/shard_map/ppermute | solution.py:361
  6.5 1.4 %collective-permute-start.2 = (bf16[144,512]{1,0:T(8,128)(2,1)S(1)}, bf16[144,512]{1,0:T(8,128)(2,1)S(1)}, u32[]{:S(2)}, u32[]{:S(2)}) collective-permute-start(bf16[144,512]{1,0:T(8,128)(2,1)S(1)} %chip.1.refs_0_), channel_id=1, source_target_pairs={{0,8},{1,3},{2,10},{3,5},{4,12},{5,7},{6,14},{7,1},{8,16},{9,11},{... | collective-permute-start | bytes 442376 | tf_op jit(solution)/shard_map/ppermute | solution.py:342
  8.0 2.6 %collective-permute-start.3 = (bf16[144,512]{1,0:T(8,128)(2,1)S(1)}, bf16[144,512]{1,0:T(8,128)(2,1)S(1)}, u32[]{:S(2)}, u32[]{:S(2)}) collective-permute-start(bf16[144,512]{1,0:T(8,128)(2,1)S(1)} %chip.1.refs_0_), channel_id=1, source_target_pairs={{0,16},{1,5},{2,18},{3,7},{4,20},{5,1},{6,22},{7,3},{8,24},{9,13},... | collective-permute-start | bytes 442376 | tf_op jit(solution)/shard_map/ppermute | solution.py:342
  10.6 1.1 collective-permute-start.4
  12.2 2.8 %collective-permute-done.3.refs_2_ = bf16[144,512]{1,0:T(8,128)(2,1)S(1)} collective-permute-done((bf16[144,512]{1,0:T(8,128)(2,1)S(1)}, bf16[144,512]{1,0:T(8,128)(2,1)S(1)}, u32[]{:S(2)}, u32[]{:S(2)}) %collective-permute-start.3) | collective-permute-done | bytes 147488 | tf_op jit(solution)/shard_map/ppermute | solution.py:342
  15.1 1.2 collective-permute-start.5
  16.3 2.4 %collective-permute-start.6 = (bf16[144,512]{1,0:T(8,128)(2,1)S(1)}, bf16[144,512]{1,0:T(8,128)(2,1)S(1)}, u32[]{:S(2)}, u32[]{:S(2)}) collective-permute-start(bf16[144,512]{1,0:T(8,128)(2,1)S(1)} %row.1.refs_0_), channel_id=1, source_target_pairs={{0,4},{1,17},{2,6},{3,19},{4,0},{5,21},{6,2},{7,23},{8,12},{9,25},... | collective-permute-start | bytes 442376 | tf_op jit(solution)/shard_map/ppermute | solution.py:342
  18.7 1.2 collective-permute-start.7
  20.4 2.4 %collective-permute-done.6.refs_2_ = bf16[144,512]{1,0:T(8,128)(2,1)S(1)} collective-permute-done((bf16[144,512]{1,0:T(8,128)(2,1)S(1)}, bf16[144,512]{1,0:T(8,128)(2,1)S(1)}, u32[]{:S(2)}, u32[]{:S(2)}) %collective-permute-start.6) | collective-permute-done | bytes 147488 | tf_op jit(solution)/shard_map/ppermute | solution.py:342
  22.9 3.3 %collective-permute-start.8 = (bf16[144,512]{1,0:T(8,128)(2,1)S(1)}, bf16[144,512]{1,0:T(8,128)(2,1)S(1)}, u32[]{:S(2)}, u32[]{:S(2)}) collective-permute-start(bf16[144,512]{1,0:T(8,128)(2,1)S(1)} %plane.1.own_proj_ref), channel_id=1, source_target_pairs={{0,1},{1,0},{2,3},{3,2},{4,5},{5,4},{6,7},{7,6},{8,9},{9,8},{10,11... | collective-permute-start | bytes 442376 | tf_op jit(solution)/shard_map/ppermute | solution.py:361
  26.2 1.0 collective-permute-done.8.got_proj_ref
  27.2 2.7 %first.1 = (f32[256,512]{1,0:T(8,128)S(1)}, f32[4,32,64]{2,1,0:T(8,128)S(1)}, f32[24,512]{1,0:T(8,128)S(1)}) custom-call(s32[5]{0:T(128)S(1)} %stack.24.place_ref, bf16[144,512]{1,0:T(8,128)(2,1)S(1)} %plane.1.own_proj_ref, bf16[144,512]{1,0:T(8,128)(2,1)S(1)} %collective-permute-done.8.got_proj_ref, bf16[512,512]{1,0:T(8,128)(2,1)S(1)} %copy-done.5, ...), custom_call_target="tpu_custom_call" | custom-call | tf_op jit(solution)/shard_map/first/pallas_call | solution.py:395
  30.0 3.7 %collective-permute-start.10 = (f32[24,512]{1,0:T(8,128)S(1)}, f32[24,512]{1,0:T(8,128)S(1)}, u32[]{:S(2)}, u32[]{:S(2)}) collective-permute-start(f32[24,512]{1,0:T(8,128)S(1)} %get-tuple-element.32._), channel_id=1, source_target_pairs={{0,64},{32,96},{64,0},{96,32},{1,65},{33,97},{65,1},{97,33},{2,66}... | collective-permute-start | bytes 147464 | tf_op jit(solution)/shard_map/ppermute | solution.py:412
  34.1 1.0 collective-permute-start.9
  35.1 3.5 %bring.1.weight_ref = bf16[512,8192]{1,0:T(8,128)(2,1)S(1)} custom-call(bf16[512,8192]{1,0:T(8,128)(2,1)} %weight_ref.3, f32[24,512]{1,0:T(8,128)S(1)} %get-tuple-element.32._), custom_call_target="tpu_custom_call" | custom-call | tf_op jit(solution)/shard_map/bring/pallas_call | solution.py:416
  38.7 4.8 %give.1 = (bf16[8,128,512]{2,1,0:T(8,128)(2,1)S(1)}, bf16[8,128,512]{2,1,0:T(8,128)(2,1)S(1)}, bf16[128,512]{1,0:T(8,128)(2,1)S(1)}) custom-call(s32[5]{0:T(128)S(1)} %stack.24.place_ref, f32[256,512]{1,0:T(8,128)S(1)} %get-tuple-element.30.step_ref, f32[4,32,64]{2,1,0:T(8,128)S(1)} %get-tuple-element.31.states_ref, f32[16,512]{1,0:T(8,128)S(1)} %copy-done.7, ...), custom_call_target="tpu_custom_call" | custom-call | tf_op jit(solution)/shard_map/give/pallas_call | solution.py:426
  43.5 1.7 %collective-permute-start.13 = (bf16[8,128,512]{2,1,0:T(8,128)(2,1)S(1)}, bf16[8,128,512]{2,1,0:T(8,128)(2,1)S(1)}, u32[]{:S(2)}, u32[]{:S(2)}) collective-permute-start(bf16[8,128,512]{2,1,0:T(8,128)(2,1)S(1)} %get-tuple-element.36), channel_id=1, source_target_pairs={{0,1},{1,0},{2,3},{3,2},{4,5},{5,4},{6,7},{7,6},{8,9},{9,8},{10,11... | collective-permute-start | bytes 3145736 | tf_op jit(solution)/shard_map/ppermute | solution.py:361
  45.7 1.8 %keep.1.keep_ref = bf16[16,128,512]{2,1,0:T(8,128)(2,1)S(1)} custom-call(s32[5]{0:T(128)S(1)} %stack.24.place_ref, bf16[128,512]{1,0:T(8,128)(2,1)S(1)} %get-tuple-element.33.kept_ref, bf16[512,8192]{1,0:T(8,128)(2,1)S(1)} %bring.1.weight_ref), custom_call_target="tpu_custom_call" | custom-call | tf_op jit(solution)/shard_map/keep/pallas_call | solution.py:442
  47.8 1.0 collective-permute-start.14
  48.8 2.5 %collective-permute-start.15 = (bf16[4,128,512]{2,1,0:T(8,128)(2,1)S(1)}, bf16[4,128,512]{2,1,0:T(8,128)(2,1)S(1)}, u32[]{:S(2)}, u32[]{:S(2)}) collective-permute-start(bf16[4,128,512]{2,1,0:T(8,128)(2,1)S(1)} %get-tuple-element.38), channel_id=1, source_target_pairs={{0,16},{1,5},{2,18},{3,7},{4,20},{5,1},{6,22},{7,3},{8,24},{9,13},... | collective-permute-start | bytes 1572872 | tf_op jit(solution)/shard_map/ppermute | solution.py:342
  52.4 5.0 %collective-permute-done.14.one_ref = bf16[4,128,512]{2,1,0:T(8,128)(2,1)S(1)} collective-permute-done((bf16[4,128,512]{2,1,0:T(8,128)(2,1)S(1)}, bf16[4,128,512]{2,1,0:T(8,128)(2,1)S(1)}, u32[]{:S(2)}, u32[]{:S(2)}) %collective-permute-start.14) | collective-permute-done | bytes 524320 | tf_op jit(solution)/shard_map/ppermute | solution.py:342
  57.4 6.4 %collective-permute-done.15.two_ref = bf16[4,128,512]{2,1,0:T(8,128)(2,1)S(1)} collective-permute-done((bf16[4,128,512]{2,1,0:T(8,128)(2,1)S(1)}, bf16[4,128,512]{2,1,0:T(8,128)(2,1)S(1)}, u32[]{:S(2)}, u32[]{:S(2)}) %collective-permute-start.15) | collective-permute-done | bytes 524320 | tf_op jit(solution)/shard_map/ppermute | solution.py:342
  64.1 1.3 collective-permute-start.17
  65.3 2.4 %collective-permute-start.18 = (bf16[128,512]{1,0:T(8,128)(2,1)S(1)}, bf16[128,512]{1,0:T(8,128)(2,1)S(1)}, u32[]{:S(2)}, u32[]{:S(2)}) collective-permute-start(bf16[128,512]{1,0:T(8,128)(2,1)S(1)} %get-tuple-element.42), channel_id=1, source_target_pairs={{0,4},{1,17},{2,6},{3,19},{4,0},{5,21},{6,2},{7,23},{8,12},{9,25},... | collective-permute-start | bytes 393224 | tf_op jit(solution)/shard_map/ppermute | solution.py:342
  68.4 0.9 collective-permute-done.17.one_ref
  69.3 2.1 %collective-permute-done.18.two_ref = bf16[128,512]{1,0:T(8,128)(2,1)S(1)} collective-permute-done((bf16[128,512]{1,0:T(8,128)(2,1)S(1)}, bf16[128,512]{1,0:T(8,128)(2,1)S(1)}, u32[]{:S(2)}, u32[]{:S(2)}) %collective-permute-start.18) | collective-permute-done | bytes 131104 | tf_op jit(solution)/shard_map/ppermute | solution.py:342
  71.5 1.3 %layer.1 = (bf16[128,256]{1,0:T(8,128)(2,1)S(1)}, bf16[128,256]{1,0:T(8,128)(2,1)S(1)}, bf16[4,144,128]{2,1,0:T(8,128)(2,1)S(1)}, bf16[4,144,128]{2,1,0:T(8,128)...) custom-call(s32[5]{0:T(128)S(1)} %stack.24.place_ref, ...), custom_call_target="tpu_custom_call" | custom-call | tf_op jit(solution)/shard_map/layer/pallas_call | solution.py:470
  72.8 1.8 %collective-permute-start.21 = (bf16[4,144,128]{2,1,0:T(8,128)(2,1)S(1)}, bf16[4,144,128]{2,1,0:T(8,128)(2,1)S(1)}, u32[]{:S(2)}, u32[]{:S(2)}) collective-permute-start(bf16[4,144,128]{2,1,0:T(8,128)(2,1)S(1)} %get-tuple-element.46), channel_id=1, source_target_pairs={{0,8},{1,3},{2,10},{3,5},{4,12},{5,7},{6,14},{7,1},{8,16},{9,11},{... | collective-permute-start | bytes 442376 | tf_op jit(solution)/shard_map/ppermute | solution.py:342
  74.6 2.1 %collective-permute-start.22 = (bf16[4,144,128]{2,1,0:T(8,128)(2,1)S(1)}, bf16[4,144,128]{2,1,0:T(8,128)(2,1)S(1)}, u32[]{:S(2)}, u32[]{:S(2)}) collective-permute-start(bf16[4,144,128]{2,1,0:T(8,128)(2,1)S(1)} %get-tuple-element.47), channel_id=1, source_target_pairs={{0,16},{1,5},{2,18},{3,7},{4,20},{5,1},{6,22},{7,3},{8,24},{9,13},... | collective-permute-start | bytes 442376 | tf_op jit(solution)/shard_map/ppermute | solution.py:342
  77.1 1.0 collective-permute-done.21.refs_1_
  78.1 2.7 %collective-permute-done.22.refs_2_ = bf16[4,144,128]{2,1,0:T(8,128)(2,1)S(1)} collective-permute-done((bf16[4,144,128]{2,1,0:T(8,128)(2,1)S(1)}, bf16[4,144,128]{2,1,0:T(8,128)(2,1)S(1)}, u32[]{:S(2)}, u32[]{:S(2)}) %collective-permute-start.22) | collective-permute-done | bytes 147488 | tf_op jit(solution)/shard_map/ppermute | solution.py:342
  81.1 1.0 collective-permute-start.24
  82.1 2.3 %collective-permute-start.25 = (bf16[4,144,128]{2,1,0:T(8,128)(2,1)S(1)}, bf16[4,144,128]{2,1,0:T(8,128)(2,1)S(1)}, u32[]{:S(2)}, u32[]{:S(2)}) collective-permute-start(bf16[4,144,128]{2,1,0:T(8,128)(2,1)S(1)} %kv.1.own_part_ref), channel_id=1, source_target_pairs={{0,4},{1,17},{2,6},{3,19},{4,0},{5,21},{6,2},{7,23},{8,12},{9,25},... | collective-permute-start | bytes 442376 | tf_op jit(solution)/shard_map/ppermute | solution.py:342
  84.8 5.0 %collective-permute-start.27 = (bf16[128,256]{1,0:T(8,128)(2,1)S(1)}, bf16[128,256]{1,0:T(8,128)(2,1)S(1)}, u32[]{:S(2)}, u32[]{:S(2)}) collective-permute-start(bf16[128,256]{1,0:T(8,128)(2,1)S(1)} %get-tuple-element.50), channel_id=1, source_target_pairs={{0,1},{1,0},{2,3},{3,2},{4,5},{5,4},{6,7},{7,6},{8,9},{9,8},{10,11... | collective-permute-start | bytes 196616 | tf_op jit(solution)/shard_map/ppermute | solution.py:361
  89.8 0.9 collective-permute-done.27.got_layer_ref
  90.8 1.2 tile.1
  92.3 2.1 %collective-permute-start.29 = (bf16[4,128,128]{2,1,0:T(8,128)(2,1)S(1)}, bf16[4,128,128]{2,1,0:T(8,128)(2,1)S(1)}, u32[]{:S(2)}, u32[]{:S(2)}) collective-permute-start(bf16[4,128,128]{2,1,0:T(8,128)(2,1)S(1)} %get-tuple-element.52.own_ref), channel_id=1, source_target_pairs={{0,64},{32,96},{64,0},{96,32},{1,65},{33,97},{65,1},{97,33},{2,66}... | collective-permute-start | bytes 393224 | tf_op jit(solution)/shard_map/ppermute | solution.py:412
  94.9 3.5 %collective-permute-done.28.near_ref = bf16[4,128,128]{2,1,0:T(8,128)(2,1)S(1)} collective-permute-done((bf16[4,128,128]{2,1,0:T(8,128)(2,1)S(1)}, bf16[4,128,128]{2,1,0:T(8,128)(2,1)S(1)}, u32[]{:S(2)}, u32[]{:S(2)}) %collective-permute-start.28) | collective-permute-done | bytes 131104 | tf_op jit(solution)/shard_map/ppermute | solution.py:412
  99.6 1.0 collective-permute-start.33
  100.8 0.9 collective-permute-start.31
  101.7 1.7 %collective-permute-start.32 = (bf16[4,4,128,128]{3,2,1,0:T(8,128)(2,1)S(1)}, bf16[4,4,128,128]{3,2,1,0:T(8,128)(2,1)S(1)}, u32[]{:S(2)}, u32[]{:S(2)}) collective-permute-start(bf16[4,4,128,128]{3,2,1,0:T(8,128)(2,1)S(1)} %stack.25.one_ref.q0), channel_id=1, source_target_pairs={{0,24},{1,7},{2,26},{3,1},{4,28},{5,3},{6,30},{7,5},{8,0},{9,15},{... | collective-permute-start | bytes 1572872 | tf_op jit(solution)/shard_map/ppermute | solution.py:342
  103.4 11.2 %collective-permute-done.33.two_ref.q1 = bf16[4,4,128,128]{3,2,1,0:T(8,128)(2,1)S(1)} collective-permute-done((bf16[4,4,128,128]{3,2,1,0:T(8,128)(2,1)S(1)}, bf16[4,4,128,128]{3,2,1,0:T(8,128)(2,1)S(1)}, u32[]{:S(2)}, u32[]{:S(2)}) %collective-permute-start.33) | collective-permute-done | bytes 524320 | tf_op jit(solution)/shard_map/ppermute | solution.py:342
  115.7 1.5 %collective-permute-done.34.one_ref = bf16[2,8,128,128]{3,2,1,0:T(8,128)(2,1)S(1)} collective-permute-done((bf16[2,8,128,128]{3,2,1,0:T(8,128)(2,1)S(1)}, bf16[2,8,128,128]{3,2,1,0:T(8,128)(2,1)S(1)}, u32[]{:S(2)}, u32[]{:S(2)}) %collective-permute-start.34) | collective-permute-done | bytes 524320 | tf_op jit(solution)/shard_map/ppermute | solution.py:361
  118.0 4.5 %collective-permute-start.35 = (bf16[2,8,128,128]{3,2,1,0:T(8,128)(2,1)S(1)}, bf16[2,8,128,128]{3,2,1,0:T(8,128)(2,1)S(1)}, u32[]{:S(2)}, u32[]{:S(2)}) collective-permute-start(bf16[2,8,128,128]{3,2,1,0:T(8,128)(2,1)S(1)} %pick1.1), channel_id=1, source_target_pairs={{0,1},{1,0},{2,3},{3,2},{4,5},{5,4},{6,7},{7,6},{8,9},{9,8},{10,11... | collective-permute-start | bytes 1572872 | tf_op jit(solution)/shard_map/ppermute | solution.py:361
  122.4 1.8 %own.1._ = bf16[4,4,4,128,128]{4,3,2,1,0:T(8,128)(2,1)} custom-call(s32[5]{0:T(128)S(1)} %stack.24.place_ref, s32[128]{0:T(128)S(1)} %get-tuple-element.57.starts_ref, s32[128]{0:T(128)S(1)} %get-tuple-element.56.counts_ref, bf16[4,4,128,128]{3,2,1,0:T(8,128)(2,1)S(1)} %stack.25.one_ref.q0, bf16[4,4,128,128]{3,2,1,0:T(8,128)(2,1)S(1)} %collective-permute-done.33.two_ref.q1, ...), custom_call_target="tpu_custom_call" | custom-call | tf_op jit(solution)/shard_map/own/pallas_call | solution.py:514
  124.3 1.6 %rest.1 = bf16[4,4,4,128,128]{4,3,2,1,0:T(8,128)(2,1)} custom-call(s32[5]{0:T(128)S(1)} %stack.24.place_ref, s32[128]{0:T(128)S(1)} %get-tuple-element.57.starts_ref, bf16[2,8,128,128]{3,2,1,0:T(8,128)(2,1)S(1)} %collective-permute-done.34.one_ref, bf16[2,8,128,128]{3,2,1,0:T(8,128)(2,1)S(1)} %collective-permute-done.35.two_ref, ...), custom_call_target="tpu_custom_call", output_to_operand_aliasing={{}: (4, {})} | custom-call | tf_op jit(solution)/shard_map/rest/pallas_call | solution.py:523
  (76 shorter events, 12.1 us)
Async XLA Ops:
  0.7 26.5 %copy-start.7 = (f32[16,512]{1,0:T(8,128)S(1)}, f32[16,512]{1,0:T(8,128)}, u32[]{:S(2)}) copy-start(f32[16,512]{1,0:T(8,128)} %alog_ref.3) | copy-start | bytes 98308
  0.7 26.5 %copy-start.9 = (f32[512]{0:T(512)S(1)}, f32[512]{0:T(512)}, u32[]{:S(2)}) copy-start(f32[512]{0:T(512)} %param.20) | copy-start | bytes 6148
  2.8 24.4 %copy-start.1 = (bf16[256,512]{1,0:T(8,128)(2,1)S(1)}, bf16[256,512]{1,0:T(8,128)(2,1)}, u32[]{:S(2)}) copy-start(bf16[256,512]{1,0:T(8,128)(2,1)} %conv_ref.7) | copy-start | bytes 786436
  2.8 24.4 %copy-start.5 = (bf16[512,512]{1,0:T(8,128)(2,1)S(1)}, bf16[512,512]{1,0:T(8,128)(2,1)}, u32[]{:S(2)}) copy-start(bf16[512,512]{1,0:T(8,128)(2,1)} %weight_ref.2) | copy-start | bytes 1572868
  3.6 2.9 %collective-permute-start = (bf16[144,512]{1,0:T(8,128)(2,1)S(1)}, bf16[144,512]{1,0:T(8,128)(2,1)S(1)}, u32[]{:S(2)}, u32[]{:S(2)}) collective-permute-start(bf16[144,512]{1,0:T(8,128)(2,1)S(1)} %project_give.1), channel_id=1, source_target_pairs={{0,1},{1,0},{2,3},{3,2},{4,5},{5,4},{6,7},{7,6},{8,9},{9,8},{10,11... | collective-permute-start | bytes 442376 | tf_op jit(solution)/shard_map/ppermute | solution.py:361
  5.1 1.4 %collective-permute-start.1 = (f32[1,256]{1,0:T(1,128)}, f32[1,256]{1,0:T(1,128)S(1)}, u32[]{:S(2)}, u32[]{:S(2)}) collective-permute-start(f32[1,256]{1,0:T(1,128)} %bitcast.14), channel_id=1, source_target_pairs={{0,1},{1,0},{2,3},{3,2},{4,5},{5,4},{6,7},{7,6},{8,9},{9,8},{10,11... | collective-permute-start | bytes 3080 | tf_op jit(solution)/shard_map/ppermute | solution.py:361
  6.5 5.7 %collective-permute-start.2 = (bf16[144,512]{1,0:T(8,128)(2,1)S(1)}, bf16[144,512]{1,0:T(8,128)(2,1)S(1)}, u32[]{:S(2)}, u32[]{:S(2)}) collective-permute-start(bf16[144,512]{1,0:T(8,128)(2,1)S(1)} %chip.1.refs_0_), channel_id=1, source_target_pairs={{0,8},{1,3},{2,10},{3,5},{4,12},{5,7},{6,14},{7,1},{8,16},{9,11},{... | collective-permute-start | bytes 442376 | tf_op jit(solution)/shard_map/ppermute | solution.py:342
  8.0 7.0 %collective-permute-start.3 = (bf16[144,512]{1,0:T(8,128)(2,1)S(1)}, bf16[144,512]{1,0:T(8,128)(2,1)S(1)}, u32[]{:S(2)}, u32[]{:S(2)}) collective-permute-start(bf16[144,512]{1,0:T(8,128)(2,1)S(1)} %chip.1.refs_0_), channel_id=1, source_target_pairs={{0,16},{1,5},{2,18},{3,7},{4,20},{5,1},{6,22},{7,3},{8,24},{9,13},... | collective-permute-start | bytes 442376 | tf_op jit(solution)/shard_map/ppermute | solution.py:342
  10.6 4.4 %collective-permute-start.4 = (bf16[144,512]{1,0:T(8,128)(2,1)S(1)}, bf16[144,512]{1,0:T(8,128)(2,1)S(1)}, u32[]{:S(2)}, u32[]{:S(2)}) collective-permute-start(bf16[144,512]{1,0:T(8,128)(2,1)S(1)} %chip.1.refs_0_), channel_id=1, source_target_pairs={{0,24},{1,7},{2,26},{3,1},{4,28},{5,3},{6,30},{7,5},{8,0},{9,15},{... | collective-permute-start | bytes 442376 | tf_op jit(solution)/shard_map/ppermute | solution.py:342
  15.1 5.3 %collective-permute-start.5 = (bf16[144,512]{1,0:T(8,128)(2,1)S(1)}, bf16[144,512]{1,0:T(8,128)(2,1)S(1)}, u32[]{:S(2)}, u32[]{:S(2)}) collective-permute-start(bf16[144,512]{1,0:T(8,128)(2,1)S(1)} %row.1.refs_0_), channel_id=1, source_target_pairs={{0,2},{1,9},{2,4},{3,11},{4,6},{5,13},{6,0},{7,15},{8,10},{9,17},{... | collective-permute-start | bytes 442376 | tf_op jit(solution)/shard_map/ppermute | solution.py:342
  16.3 6.6 %collective-permute-start.6 = (bf16[144,512]{1,0:T(8,128)(2,1)S(1)}, bf16[144,512]{1,0:T(8,128)(2,1)S(1)}, u32[]{:S(2)}, u32[]{:S(2)}) collective-permute-start(bf16[144,512]{1,0:T(8,128)(2,1)S(1)} %row.1.refs_0_), channel_id=1, source_target_pairs={{0,4},{1,17},{2,6},{3,19},{4,0},{5,21},{6,2},{7,23},{8,12},{9,25},... | collective-permute-start | bytes 442376 | tf_op jit(solution)/shard_map/ppermute | solution.py:342
  18.7 4.1 %collective-permute-start.7 = (bf16[144,512]{1,0:T(8,128)(2,1)S(1)}, bf16[144,512]{1,0:T(8,128)(2,1)S(1)}, u32[]{:S(2)}, u32[]{:S(2)}) collective-permute-start(bf16[144,512]{1,0:T(8,128)(2,1)S(1)} %row.1.refs_0_), channel_id=1, source_target_pairs={{0,6},{1,25},{2,0},{3,27},{4,2},{5,29},{6,4},{7,31},{8,14},{9,1},{... | collective-permute-start | bytes 442376 | tf_op jit(solution)/shard_map/ppermute | solution.py:342
  22.9 4.3 %collective-permute-start.8 = (bf16[144,512]{1,0:T(8,128)(2,1)S(1)}, bf16[144,512]{1,0:T(8,128)(2,1)S(1)}, u32[]{:S(2)}, u32[]{:S(2)}) collective-permute-start(bf16[144,512]{1,0:T(8,128)(2,1)S(1)} %plane.1.own_proj_ref), channel_id=1, source_target_pairs={{0,1},{1,0},{2,3},{3,2},{4,5},{5,4},{6,7},{7,6},{8,9},{9,8},{10,11... | collective-permute-start | bytes 442376 | tf_op jit(solution)/shard_map/ppermute | solution.py:361
  29.9 8.7 %copy-start.4 = (bf16[256,256]{1,0:T(8,128)(2,1)S(1)}, bf16[256,256]{1,0:T(8,128)(2,1)}, u32[]{:S(2)}) copy-start(bf16[256,256]{1,0:T(8,128)(2,1)} %residual_ref.3) | copy-start | bytes 393220
  29.9 8.7 %copy-start.6 = (bf16[256,512]{1,0:T(8,128)(2,1)S(1)}, bf16[256,512]{1,0:T(8,128)(2,1)}, u32[]{:S(2)}) copy-start(bf16[256,512]{1,0:T(8,128)(2,1)} %gate_ref.1) | copy-start | bytes 786436
  29.9 8.7 %copy-start.8 = (f32[16,512]{1,0:T(8,128)S(1)}, f32[16,512]{1,0:T(8,128)}, u32[]{:S(2)}) copy-start(f32[16,512]{1,0:T(8,128)} %init_ref.1) | copy-start | bytes 98308
  29.9 8.7 %copy-start.10 = (f32[512]{0:T(512)S(1)}, f32[512]{0:T(512)}, u32[]{:S(2)}) copy-start(f32[512]{0:T(512)} %param.22) | copy-start | bytes 6148
  30.0 8.7 %collective-permute-start.10 = (f32[24,512]{1,0:T(8,128)S(1)}, f32[24,512]{1,0:T(8,128)S(1)}, u32[]{:S(2)}, u32[]{:S(2)}) collective-permute-start(f32[24,512]{1,0:T(8,128)S(1)} %get-tuple-element.32._), channel_id=1, source_target_pairs={{0,64},{32,96},{64,0},{96,32},{1,65},{33,97},{65,1},{97,33},{2,66}... | collective-permute-start | bytes 147464 | tf_op jit(solution)/shard_map/ppermute | solution.py:412
  33.6 5.0 %collective-permute-start.11 = (f32[24,512]{1,0:T(8,128)S(1)}, f32[24,512]{1,0:T(8,128)S(1)}, u32[]{:S(2)}, u32[]{:S(2)}) collective-permute-start(f32[24,512]{1,0:T(8,128)S(1)} %get-tuple-element.32._), channel_id=1, source_target_pairs={{0,96},{32,0},{64,32},{96,64},{1,97},{33,1},{65,33},{97,65},{2,98}... | collective-permute-start | bytes 147464 | tf_op jit(solution)/shard_map/ppermute | solution.py:412
  34.1 4.6 %collective-permute-start.9 = (f32[24,512]{1,0:T(8,128)S(1)}, f32[24,512]{1,0:T(8,128)S(1)}, u32[]{:S(2)}, u32[]{:S(2)}) collective-permute-start(f32[24,512]{1,0:T(8,128)S(1)} %get-tuple-element.32._), channel_id=1, source_target_pairs={{0,32},{32,64},{64,96},{96,0},{1,33},{33,65},{65,97},{97,1},{2,34}... | collective-permute-start | bytes 147464 | tf_op jit(solution)/shard_map/ppermute | solution.py:412
  43.5 4.1 %collective-permute-start.13 = (bf16[8,128,512]{2,1,0:T(8,128)(2,1)S(1)}, bf16[8,128,512]{2,1,0:T(8,128)(2,1)S(1)}, u32[]{:S(2)}, u32[]{:S(2)}) collective-permute-start(bf16[8,128,512]{2,1,0:T(8,128)(2,1)S(1)} %get-tuple-element.36), channel_id=1, source_target_pairs={{0,1},{1,0},{2,3},{3,2},{4,5},{5,4},{6,7},{7,6},{8,9},{9,8},{10,11... | collective-permute-start | bytes 3145736 | tf_op jit(solution)/shard_map/ppermute | solution.py:361
  45.2 6.1 %collective-permute-start.12 = (bf16[8,128,512]{2,1,0:T(8,128)(2,1)S(1)}, bf16[8,128,512]{2,1,0:T(8,128)(2,1)S(1)}, u32[]{:S(2)}, u32[]{:S(2)}) collective-permute-start(bf16[8,128,512]{2,1,0:T(8,128)(2,1)S(1)} %get-tuple-element.34), channel_id=1, source_target_pairs={{0,1},{1,0},{2,3},{3,2},{4,5},{5,4},{6,7},{7,6},{8,9},{9,8},{10,11... | collective-permute-start | bytes 3145736 | tf_op jit(solution)/shard_map/ppermute | solution.py:361
  45.3 23.1 %collective-permute-start.20 = (bf16[256,2048]{1,0:T(8,128)(2,1)S(1)}, bf16[256,2048]{1,0:T(8,128)(2,1)S(1)}, u32[]{:S(2)}, u32[]{:S(2)}) collective-permute-start(bf16[256,2048]{1,0:T(8,128)(2,1)S(1)} %copy-done.3), channel_id=1, source_target_pairs={{0,1},{1,0},{2,3},{3,2},{4,5},{5,4},{6,7},{7,6},{8,9},{9,8},{10,11... | collective-permute-start | bytes 3145736 | tf_op jit(solution)/shard_map/ppermute | solution.py:361
  47.8 9.6 %collective-permute-start.14 = (bf16[4,128,512]{2,1,0:T(8,128)(2,1)S(1)}, bf16[4,128,512]{2,1,0:T(8,128)(2,1)S(1)}, u32[]{:S(2)}, u32[]{:S(2)}) collective-permute-start(bf16[4,128,512]{2,1,0:T(8,128)(2,1)S(1)} %get-tuple-element.37), channel_id=1, source_target_pairs={{0,8},{1,3},{2,10},{3,5},{4,12},{5,7},{6,14},{7,1},{8,16},{9,11},{... | collective-permute-start | bytes 1572872 | tf_op jit(solution)/shard_map/ppermute | solution.py:342
  48.8 22.7 %copy-start.11 = (f32[256]{0:T(256)S(1)}, f32[256]{0:T(256)}, u32[]{:S(2)}) copy-start(f32[256]{0:T(256)} %param.25) | copy-start | bytes 3076
  48.8 15.0 %collective-permute-start.15 = (bf16[4,128,512]{2,1,0:T(8,128)(2,1)S(1)}, bf16[4,128,512]{2,1,0:T(8,128)(2,1)S(1)}, u32[]{:S(2)}, u32[]{:S(2)}) collective-permute-start(bf16[4,128,512]{2,1,0:T(8,128)(2,1)S(1)} %get-tuple-element.38), channel_id=1, source_target_pairs={{0,16},{1,5},{2,18},{3,7},{4,20},{5,1},{6,22},{7,3},{8,24},{9,13},... | collective-permute-start | bytes 1572872 | tf_op jit(solution)/shard_map/ppermute | solution.py:342
  51.6 12.2 %collective-permute-start.16 = (bf16[4,128,512]{2,1,0:T(8,128)(2,1)S(1)}, bf16[4,128,512]{2,1,0:T(8,128)(2,1)S(1)}, u32[]{:S(2)}, u32[]{:S(2)}) collective-permute-start(bf16[4,128,512]{2,1,0:T(8,128)(2,1)S(1)} %get-tuple-element.39), channel_id=1, source_target_pairs={{0,24},{1,7},{2,26},{3,1},{4,28},{5,3},{6,30},{7,5},{8,0},{9,15},{... | collective-permute-start | bytes 1572872 | tf_op jit(solution)/shard_map/ppermute | solution.py:342
  64.1 5.3 %collective-permute-start.17 = (bf16[128,512]{1,0:T(8,128)(2,1)S(1)}, bf16[128,512]{1,0:T(8,128)(2,1)S(1)}, u32[]{:S(2)}, u32[]{:S(2)}) collective-permute-start(bf16[128,512]{1,0:T(8,128)(2,1)S(1)} %get-tuple-element.41), channel_id=1, source_target_pairs={{0,2},{1,9},{2,4},{3,11},{4,6},{5,13},{6,0},{7,15},{8,10},{9,17},{... | collective-permute-start | bytes 393224 | tf_op jit(solution)/shard_map/ppermute | solution.py:342
  65.3 6.2 %collective-permute-start.18 = (bf16[128,512]{1,0:T(8,128)(2,1)S(1)}, bf16[128,512]{1,0:T(8,128)(2,1)S(1)}, u32[]{:S(2)}, u32[]{:S(2)}) collective-permute-start(bf16[128,512]{1,0:T(8,128)(2,1)S(1)} %get-tuple-element.42), channel_id=1, source_target_pairs={{0,4},{1,17},{2,6},{3,19},{4,0},{5,21},{6,2},{7,23},{8,12},{9,25},... | collective-permute-start | bytes 393224 | tf_op jit(solution)/shard_map/ppermute | solution.py:342
  67.7 3.8 %collective-permute-start.19 = (bf16[128,512]{1,0:T(8,128)(2,1)S(1)}, bf16[128,512]{1,0:T(8,128)(2,1)S(1)}, u32[]{:S(2)}, u32[]{:S(2)}) collective-permute-start(bf16[128,512]{1,0:T(8,128)(2,1)S(1)} %get-tuple-element.43), channel_id=1, source_target_pairs={{0,6},{1,25},{2,0},{3,27},{4,2},{5,29},{6,4},{7,31},{8,14},{9,1},{... | collective-permute-start | bytes 393224 | tf_op jit(solution)/shard_map/ppermute | solution.py:342
  71.5 29.1 %copy-start.12 = (s32[128]{0:T(128)S(1)}, s32[128]{0:T(128)}, u32[]{:S(2)}) copy-start(s32[128]{0:T(128)} %param.29) | copy-start | bytes 1540
  71.5 29.1 %copy-start.13 = (s32[128]{0:T(128)S(1)}, s32[128]{0:T(128)}, u32[]{:S(2)}) copy-start(s32[128]{0:T(128)} %param.27) | copy-start | bytes 1540
  71.5 29.1 %copy-start.14 = (s32[128]{0:T(128)S(1)}, s32[128]{0:T(128)}, u32[]{:S(2)}) copy-start(s32[128]{0:T(128)} %param.28) | copy-start | bytes 1540
  72.8 5.3 %collective-permute-start.21 = (bf16[4,144,128]{2,1,0:T(8,128)(2,1)S(1)}, bf16[4,144,128]{2,1,0:T(8,128)(2,1)S(1)}, u32[]{:S(2)}, u32[]{:S(2)}) collective-permute-start(bf16[4,144,128]{2,1,0:T(8,128)(2,1)S(1)} %get-tuple-element.46), channel_id=1, source_target_pairs={{0,8},{1,3},{2,10},{3,5},{4,12},{5,7},{6,14},{7,1},{8,16},{9,11},{... | collective-permute-start | bytes 442376 | tf_op jit(solution)/shard_map/ppermute | solution.py:342
  74.6 6.2 %collective-permute-start.22 = (bf16[4,144,128]{2,1,0:T(8,128)(2,1)S(1)}, bf16[4,144,128]{2,1,0:T(8,128)(2,1)S(1)}, u32[]{:S(2)}, u32[]{:S(2)}) collective-permute-start(bf16[4,144,128]{2,1,0:T(8,128)(2,1)S(1)} %get-tuple-element.47), channel_id=1, source_target_pairs={{0,16},{1,5},{2,18},{3,7},{4,20},{5,1},{6,22},{7,3},{8,24},{9,13},... | collective-permute-start | bytes 442376 | tf_op jit(solution)/shard_map/ppermute | solution.py:342
  76.7 4.3 %collective-permute-start.23 = (bf16[4,144,128]{2,1,0:T(8,128)(2,1)S(1)}, bf16[4,144,128]{2,1,0:T(8,128)(2,1)S(1)}, u32[]{:S(2)}, u32[]{:S(2)}) collective-permute-start(bf16[4,144,128]{2,1,0:T(8,128)(2,1)S(1)} %get-tuple-element.48), channel_id=1, source_target_pairs={{0,24},{1,7},{2,26},{3,1},{4,28},{5,3},{6,30},{7,5},{8,0},{9,15},{... | collective-permute-start | bytes 442376 | tf_op jit(solution)/shard_map/ppermute | solution.py:342
  81.1 9.6 %collective-permute-start.24 = (bf16[4,144,128]{2,1,0:T(8,128)(2,1)S(1)}, bf16[4,144,128]{2,1,0:T(8,128)(2,1)S(1)}, u32[]{:S(2)}, u32[]{:S(2)}) collective-permute-start(bf16[4,144,128]{2,1,0:T(8,128)(2,1)S(1)} %kv.1.own_part_ref), channel_id=1, source_target_pairs={{0,2},{1,9},{2,4},{3,11},{4,6},{5,13},{6,0},{7,15},{8,10},{9,17},{... | collective-permute-start | bytes 442376 | tf_op jit(solution)/shard_map/ppermute | solution.py:342
  82.1 8.6 %collective-permute-start.25 = (bf16[4,144,128]{2,1,0:T(8,128)(2,1)S(1)}, bf16[4,144,128]{2,1,0:T(8,128)(2,1)S(1)}, u32[]{:S(2)}, u32[]{:S(2)}) collective-permute-start(bf16[4,144,128]{2,1,0:T(8,128)(2,1)S(1)} %kv.1.own_part_ref), channel_id=1, source_target_pairs={{0,4},{1,17},{2,6},{3,19},{4,0},{5,21},{6,2},{7,23},{8,12},{9,25},... | collective-permute-start | bytes 442376 | tf_op jit(solution)/shard_map/ppermute | solution.py:342
  84.4 6.4 %collective-permute-start.26 = (bf16[4,144,128]{2,1,0:T(8,128)(2,1)S(1)}, bf16[4,144,128]{2,1,0:T(8,128)(2,1)S(1)}, u32[]{:S(2)}, u32[]{:S(2)}) collective-permute-start(bf16[4,144,128]{2,1,0:T(8,128)(2,1)S(1)} %kv.1.own_part_ref), channel_id=1, source_target_pairs={{0,6},{1,25},{2,0},{3,27},{4,2},{5,29},{6,4},{7,31},{8,14},{9,1},{... | collective-permute-start | bytes 442376 | tf_op jit(solution)/shard_map/ppermute | solution.py:342
  84.8 5.9 %collective-permute-start.27 = (bf16[128,256]{1,0:T(8,128)(2,1)S(1)}, bf16[128,256]{1,0:T(8,128)(2,1)S(1)}, u32[]{:S(2)}, u32[]{:S(2)}) collective-permute-start(bf16[128,256]{1,0:T(8,128)(2,1)S(1)} %get-tuple-element.50), channel_id=1, source_target_pairs={{0,1},{1,0},{2,3},{3,2},{4,5},{5,4},{6,7},{7,6},{8,9},{9,8},{10,11... | collective-permute-start | bytes 196616 | tf_op jit(solution)/shard_map/ppermute | solution.py:361
  92.0 6.4 %collective-permute-start.28 = (bf16[4,128,128]{2,1,0:T(8,128)(2,1)S(1)}, bf16[4,128,128]{2,1,0:T(8,128)(2,1)S(1)}, u32[]{:S(2)}, u32[]{:S(2)}) collective-permute-start(bf16[4,128,128]{2,1,0:T(8,128)(2,1)S(1)} %get-tuple-element.52.own_ref), channel_id=1, source_target_pairs={{0,32},{32,64},{64,96},{96,0},{1,33},{33,65},{65,97},{97,1},{2,34}... | collective-permute-start | bytes 393224 | tf_op jit(solution)/shard_map/ppermute | solution.py:412
  92.3 6.1 %collective-permute-start.29 = (bf16[4,128,128]{2,1,0:T(8,128)(2,1)S(1)}, bf16[4,128,128]{2,1,0:T(8,128)(2,1)S(1)}, u32[]{:S(2)}, u32[]{:S(2)}) collective-permute-start(bf16[4,128,128]{2,1,0:T(8,128)(2,1)S(1)} %get-tuple-element.52.own_ref), channel_id=1, source_target_pairs={{0,64},{32,96},{64,0},{96,32},{1,65},{33,97},{65,1},{97,33},{2,66}... | collective-permute-start | bytes 393224 | tf_op jit(solution)/shard_map/ppermute | solution.py:412
  94.4 4.7 %collective-permute-start.30 = (bf16[4,128,128]{2,1,0:T(8,128)(2,1)S(1)}, bf16[4,128,128]{2,1,0:T(8,128)(2,1)S(1)}, u32[]{:S(2)}, u32[]{:S(2)}) collective-permute-start(bf16[4,128,128]{2,1,0:T(8,128)(2,1)S(1)} %get-tuple-element.52.own_ref), channel_id=1, source_target_pairs={{0,96},{32,0},{64,32},{96,64},{1,97},{33,1},{65,33},{97,65},{2,98}... | collective-permute-start | bytes 393224 | tf_op jit(solution)/shard_map/ppermute | solution.py:412
  99.6 14.9 %collective-permute-start.33 = (bf16[4,4,128,128]{3,2,1,0:T(8,128)(2,1)S(1)}, bf16[4,4,128,128]{3,2,1,0:T(8,128)(2,1)S(1)}, u32[]{:S(2)}, u32[]{:S(2)}) collective-permute-start(bf16[4,4,128,128]{3,2,1,0:T(8,128)(2,1)S(1)} %stack.25.one_ref.q0), channel_id=1, source_target_pairs={{0,8},{1,3},{2,10},{3,5},{4,12},{5,7},{6,14},{7,1},{8,16},{9,11},{... | collective-permute-start | bytes 1572872 | tf_op jit(solution)/shard_map/ppermute | solution.py:342
  100.8 14.9 %collective-permute-start.31 = (bf16[4,4,128,128]{3,2,1,0:T(8,128)(2,1)S(1)}, bf16[4,4,128,128]{3,2,1,0:T(8,128)(2,1)S(1)}, u32[]{:S(2)}, u32[]{:S(2)}) collective-permute-start(bf16[4,4,128,128]{3,2,1,0:T(8,128)(2,1)S(1)} %stack.25.one_ref.q0), channel_id=1, source_target_pairs={{0,16},{1,5},{2,18},{3,7},{4,20},{5,1},{6,22},{7,3},{8,24},{9,13},... | collective-permute-start | bytes 1572872 | tf_op jit(solution)/shard_map/ppermute | solution.py:342
  101.7 14.0 %collective-permute-start.32 = (bf16[4,4,128,128]{3,2,1,0:T(8,128)(2,1)S(1)}, bf16[4,4,128,128]{3,2,1,0:T(8,128)(2,1)S(1)}, u32[]{:S(2)}, u32[]{:S(2)}) collective-permute-start(bf16[4,4,128,128]{3,2,1,0:T(8,128)(2,1)S(1)} %stack.25.one_ref.q0), channel_id=1, source_target_pairs={{0,24},{1,7},{2,26},{3,1},{4,28},{5,3},{6,30},{7,5},{8,0},{9,15},{... | collective-permute-start | bytes 1572872 | tf_op jit(solution)/shard_map/ppermute | solution.py:342
  115.3 2.0 %collective-permute-start.34 = (bf16[2,8,128,128]{3,2,1,0:T(8,128)(2,1)S(1)}, bf16[2,8,128,128]{3,2,1,0:T(8,128)(2,1)S(1)}, u32[]{:S(2)}, u32[]{:S(2)}) collective-permute-start(bf16[2,8,128,128]{3,2,1,0:T(8,128)(2,1)S(1)} %pick0.1), channel_id=1, source_target_pairs={{0,1},{1,0},{2,3},{3,2},{4,5},{5,4},{6,7},{7,6},{8,9},{9,8},{10,11... | collective-permute-start | bytes 1572872 | tf_op jit(solution)/shard_map/ppermute | solution.py:361
  118.0 6.3 %collective-permute-start.35 = (bf16[2,8,128,128]{3,2,1,0:T(8,128)(2,1)S(1)}, bf16[2,8,128,128]{3,2,1,0:T(8,128)(2,1)S(1)}, u32[]{:S(2)}, u32[]{:S(2)}) collective-permute-start(bf16[2,8,128,128]{3,2,1,0:T(8,128)(2,1)S(1)} %pick1.1), channel_id=1, source_target_pairs={{0,1},{1,0},{2,3},{3,2},{4,5},{5,4},{6,7},{7,6},{8,9},{9,8},{10,11... | collective-permute-start | bytes 1572872 | tf_op jit(solution)/shard_map/ppermute | solution.py:361
  (3 other events, 8.6 us)

commit v7 on v6

--- a/solution.py
+++ b/solution.py
@@ -19,7 +19,7 @@
 CHUNK = 64
 PIECES = 8
 SIDE = 4
-SOON, LATER = (1, 2), (0, 3)
+SOON, LATER = (2, 3), (0, 1)
 EARLY, LATE = 1, (2, 3)
 BF = jnp.bfloat16
 F32 = jnp.float32

time: 126 us -> 126 us (level)
  transfers between devices with their start and end apart: 36 -> 36, of which waited for: 19 -> 20; matrix products, arithmetic and copies ran while one was open for 0% -> 0% of each run, Pallas kernels for 7% -> 8%
where the time goes in v7:
time: 126 us; the launch traced here: 125 us
  starting transfers between devices  55 us (44%)
  waiting for transfers between devices  43.7 us (35%)
  Pallas kernels  23.4 us (19%)
  local copies, waits for them, and re-layouts  2.15 us (2%)
    ppermute x21, waiting for transfers between devices, line(): lax.ppermute(value_of(shift), 'tp', [((x * SIDE + y) * 2 + c, ((x + shift...  35.7 us
    ppermute x21, starting transfers between devices, line(): lax.ppermute(value_of(shift), 'tp', [((x * SIDE + y) * 2 + c, ((x + shift...  30 us
    ppermute x9, starting transfers between devices, swap(): return lax.ppermute(value, 'tp', partner)  16.9 us
    ppermute x6, starting transfers between devices, ranges_back(): lax.ppermute(value, 'ctx', [(z, (z + s) % ctx_count) for z in range(ctx_c...  8.1 us
    pallas_call x1, Pallas kernels, per_device(): pl.pallas_call(give_kernel, in_specs=[SM] + [VM] * 12, out_shape=(shape(h...  4.76 us
    ppermute x6, waiting for transfers between devices, ranges_back(): lax.ppermute(value, 'ctx', [(z, (z + s) % ctx_count) for z in range(ctx_c...  4.11 us
    ppermute x9, waiting for transfers between devices, swap(): return lax.ppermute(value, 'tp', partner)  3.87 us
    pallas_call x1, Pallas kernels, per_device(): pl.pallas_call(bring_kernel, in_specs=[ANY] * 2, out_shape=shape(out_weig...  3.5 us
  transfers between devices with their start and end apart: 36, of which 20 were waited for; matrix products, arithmetic and copies ran while one was open for 0% of the time, Pallas kernels for 8%

profile of v7, /device:TPU:1, one launch (start us, length us, event | category | flops | bytes accessed | tf_op | source)
XLA Modules:
  0.0 125.4 jit_solution(9445970322858451968)
XLA Ops:
  0.8 0.9 copy-done
  1.7 1.1 copy-done.2
  2.8 0.9 project_give.1
  3.6 1.5 %collective-permute-start = (bf16[144,512]{1,0:T(8,128)(2,1)S(1)}, bf16[144,512]{1,0:T(8,128)(2,1)S(1)}, u32[]{:S(2)}, u32[]{:S(2)}) collective-permute-start(bf16[144,512]{1,0:T(8,128)(2,1)S(1)} %project_give.1), channel_id=1, source_target_pairs={{0,1},{1,0},{2,3},{3,2},{4,5},{5,4},{6,7},{7,6},{8,9},{9,8},{10,11... | collective-permute-start | bytes 442376 | tf_op jit(solution)/shard_map/ppermute | solution.py:361
  5.2 0.8 project_keep.1.refs_0_
  6.5 1.4 %collective-permute-start.2 = (bf16[144,512]{1,0:T(8,128)(2,1)S(1)}, bf16[144,512]{1,0:T(8,128)(2,1)S(1)}, u32[]{:S(2)}, u32[]{:S(2)}) collective-permute-start(bf16[144,512]{1,0:T(8,128)(2,1)S(1)} %chip.1.refs_0_), channel_id=1, source_target_pairs={{0,8},{1,3},{2,10},{3,5},{4,12},{5,7},{6,14},{7,1},{8,16},{9,11},{... | collective-permute-start | bytes 442376 | tf_op jit(solution)/shard_map/ppermute | solution.py:342
  8.0 2.6 %collective-permute-start.3 = (bf16[144,512]{1,0:T(8,128)(2,1)S(1)}, bf16[144,512]{1,0:T(8,128)(2,1)S(1)}, u32[]{:S(2)}, u32[]{:S(2)}) collective-permute-start(bf16[144,512]{1,0:T(8,128)(2,1)S(1)} %chip.1.refs_0_), channel_id=1, source_target_pairs={{0,16},{1,5},{2,18},{3,7},{4,20},{5,1},{6,22},{7,3},{8,24},{9,13},... | collective-permute-start | bytes 442376 | tf_op jit(solution)/shard_map/ppermute | solution.py:342
  10.6 1.1 collective-permute-start.4
  12.2 2.8 %collective-permute-done.3.refs_2_ = bf16[144,512]{1,0:T(8,128)(2,1)S(1)} collective-permute-done((bf16[144,512]{1,0:T(8,128)(2,1)S(1)}, bf16[144,512]{1,0:T(8,128)(2,1)S(1)}, u32[]{:S(2)}, u32[]{:S(2)}) %collective-permute-start.3) | collective-permute-done | bytes 147488 | tf_op jit(solution)/shard_map/ppermute | solution.py:342
  15.1 1.2 collective-permute-start.5
  16.3 2.4 %collective-permute-start.6 = (bf16[144,512]{1,0:T(8,128)(2,1)S(1)}, bf16[144,512]{1,0:T(8,128)(2,1)S(1)}, u32[]{:S(2)}, u32[]{:S(2)}) collective-permute-start(bf16[144,512]{1,0:T(8,128)(2,1)S(1)} %row.1.refs_0_), channel_id=1, source_target_pairs={{0,4},{1,17},{2,6},{3,19},{4,0},{5,21},{6,2},{7,23},{8,12},{9,25},... | collective-permute-start | bytes 442376 | tf_op jit(solution)/shard_map/ppermute | solution.py:342
  18.7 1.2 collective-permute-start.7
  20.4 2.4 %collective-permute-done.6.refs_2_ = bf16[144,512]{1,0:T(8,128)(2,1)S(1)} collective-permute-done((bf16[144,512]{1,0:T(8,128)(2,1)S(1)}, bf16[144,512]{1,0:T(8,128)(2,1)S(1)}, u32[]{:S(2)}, u32[]{:S(2)}) %collective-permute-start.6) | collective-permute-done | bytes 147488 | tf_op jit(solution)/shard_map/ppermute | solution.py:342
  22.9 3.3 %collective-permute-start.8 = (bf16[144,512]{1,0:T(8,128)(2,1)S(1)}, bf16[144,512]{1,0:T(8,128)(2,1)S(1)}, u32[]{:S(2)}, u32[]{:S(2)}) collective-permute-start(bf16[144,512]{1,0:T(8,128)(2,1)S(1)} %plane.1.own_proj_ref), channel_id=1, source_target_pairs={{0,1},{1,0},{2,3},{3,2},{4,5},{5,4},{6,7},{7,6},{8,9},{9,8},{10,11... | collective-permute-start | bytes 442376 | tf_op jit(solution)/shard_map/ppermute | solution.py:361
  26.2 1.0 collective-permute-done.8.got_proj_ref
  27.2 2.7 %first.1 = (f32[256,512]{1,0:T(8,128)S(1)}, f32[4,32,64]{2,1,0:T(8,128)S(1)}, f32[24,512]{1,0:T(8,128)S(1)}) custom-call(s32[5]{0:T(128)S(1)} %stack.24.place_ref, bf16[144,512]{1,0:T(8,128)(2,1)S(1)} %plane.1.own_proj_ref, bf16[144,512]{1,0:T(8,128)(2,1)S(1)} %collective-permute-done.8.got_proj_ref, bf16[512,512]{1,0:T(8,128)(2,1)S(1)} %copy-done.5, ...), custom_call_target="tpu_custom_call" | custom-call | tf_op jit(solution)/shard_map/first/pallas_call | solution.py:395
  30.0 3.7 %collective-permute-start.10 = (f32[24,512]{1,0:T(8,128)S(1)}, f32[24,512]{1,0:T(8,128)S(1)}, u32[]{:S(2)}, u32[]{:S(2)}) collective-permute-start(f32[24,512]{1,0:T(8,128)S(1)} %get-tuple-element.32._), channel_id=1, source_target_pairs={{0,64},{32,96},{64,0},{96,32},{1,65},{33,97},{65,1},{97,33},{2,66}... | collective-permute-start | bytes 147464 | tf_op jit(solution)/shard_map/ppermute | solution.py:412
  34.1 1.0 collective-permute-start.9
  35.1 3.5 %bring.1.weight_ref = bf16[512,8192]{1,0:T(8,128)(2,1)S(1)} custom-call(bf16[512,8192]{1,0:T(8,128)(2,1)} %weight_ref.3, f32[24,512]{1,0:T(8,128)S(1)} %get-tuple-element.32._), custom_call_target="tpu_custom_call" | custom-call | tf_op jit(solution)/shard_map/bring/pallas_call | solution.py:416
  38.7 4.8 %give.1 = (bf16[8,128,512]{2,1,0:T(8,128)(2,1)S(1)}, bf16[8,128,512]{2,1,0:T(8,128)(2,1)S(1)}, bf16[128,512]{1,0:T(8,128)(2,1)S(1)}) custom-call(s32[5]{0:T(128)S(1)} %stack.24.place_ref, f32[256,512]{1,0:T(8,128)S(1)} %get-tuple-element.30.step_ref, f32[4,32,64]{2,1,0:T(8,128)S(1)} %get-tuple-element.31.states_ref, f32[16,512]{1,0:T(8,128)S(1)} %copy-done.7, ...), custom_call_target="tpu_custom_call" | custom-call | tf_op jit(solution)/shard_map/give/pallas_call | solution.py:426
  43.5 1.7 %collective-permute-start.14 = (bf16[8,128,512]{2,1,0:T(8,128)(2,1)S(1)}, bf16[8,128,512]{2,1,0:T(8,128)(2,1)S(1)}, u32[]{:S(2)}, u32[]{:S(2)}) collective-permute-start(bf16[8,128,512]{2,1,0:T(8,128)(2,1)S(1)} %get-tuple-element.37), channel_id=1, source_target_pairs={{0,1},{1,0},{2,3},{3,2},{4,5},{5,4},{6,7},{7,6},{8,9},{9,8},{10,11... | collective-permute-start | bytes 3145736 | tf_op jit(solution)/shard_map/ppermute | solution.py:361
  45.7 1.8 %keep.1.keep_ref = bf16[16,128,512]{2,1,0:T(8,128)(2,1)S(1)} custom-call(s32[5]{0:T(128)S(1)} %stack.24.place_ref, bf16[128,512]{1,0:T(8,128)(2,1)S(1)} %get-tuple-element.33.kept_ref, bf16[512,8192]{1,0:T(8,128)(2,1)S(1)} %bring.1.weight_ref), custom_call_target="tpu_custom_call" | custom-call | tf_op jit(solution)/shard_map/keep/pallas_call | solution.py:442
  47.8 2.2 %collective-permute-start.15 = (bf16[4,128,512]{2,1,0:T(8,128)(2,1)S(1)}, bf16[4,128,512]{2,1,0:T(8,128)(2,1)S(1)}, u32[]{:S(2)}, u32[]{:S(2)}) collective-permute-start(bf16[4,128,512]{2,1,0:T(8,128)(2,1)S(1)} %get-tuple-element.38), channel_id=1, source_target_pairs={{0,16},{1,5},{2,18},{3,7},{4,20},{5,1},{6,22},{7,3},{8,24},{9,13},... | collective-permute-start | bytes 1572872 | tf_op jit(solution)/shard_map/ppermute | solution.py:342
  50.0 1.2 collective-permute-start.16
  51.8 6.0 %collective-permute-done.15.two_ref = bf16[4,128,512]{2,1,0:T(8,128)(2,1)S(1)} collective-permute-done((bf16[4,128,512]{2,1,0:T(8,128)(2,1)S(1)}, bf16[4,128,512]{2,1,0:T(8,128)(2,1)S(1)}, u32[]{:S(2)}, u32[]{:S(2)}) %collective-permute-start.15) | collective-permute-done | bytes 524320 | tf_op jit(solution)/shard_map/ppermute | solution.py:342
  57.7 5.5 %collective-permute-done.16.three_ref = bf16[4,128,512]{2,1,0:T(8,128)(2,1)S(1)} collective-permute-done((bf16[4,128,512]{2,1,0:T(8,128)(2,1)S(1)}, bf16[4,128,512]{2,1,0:T(8,128)(2,1)S(1)}, u32[]{:S(2)}, u32[]{:S(2)}) %collective-permute-start.16) | collective-permute-done | bytes 524320 | tf_op jit(solution)/shard_map/ppermute | solution.py:342
  63.6 1.4 %collective-permute-start.17 = (bf16[128,512]{1,0:T(8,128)(2,1)S(1)}, bf16[128,512]{1,0:T(8,128)(2,1)S(1)}, u32[]{:S(2)}, u32[]{:S(2)}) collective-permute-start(bf16[128,512]{1,0:T(8,128)(2,1)S(1)} %get-tuple-element.41), channel_id=1, source_target_pairs={{0,2},{1,9},{2,4},{3,11},{4,6},{5,13},{6,0},{7,15},{8,10},{9,17},{... | collective-permute-start | bytes 393224 | tf_op jit(solution)/shard_map/ppermute | solution.py:342
  64.9 2.4 %collective-permute-start.18 = (bf16[128,512]{1,0:T(8,128)(2,1)S(1)}, bf16[128,512]{1,0:T(8,128)(2,1)S(1)}, u32[]{:S(2)}, u32[]{:S(2)}) collective-permute-start(bf16[128,512]{1,0:T(8,128)(2,1)S(1)} %get-tuple-element.42), channel_id=1, source_target_pairs={{0,4},{1,17},{2,6},{3,19},{4,0},{5,21},{6,2},{7,23},{8,12},{9,25},... | collective-permute-start | bytes 393224 | tf_op jit(solution)/shard_map/ppermute | solution.py:342
  68.8 2.3 %collective-permute-done.18.two_ref = bf16[128,512]{1,0:T(8,128)(2,1)S(1)} collective-permute-done((bf16[128,512]{1,0:T(8,128)(2,1)S(1)}, bf16[128,512]{1,0:T(8,128)(2,1)S(1)}, u32[]{:S(2)}, u32[]{:S(2)}) %collective-permute-start.18) | collective-permute-done | bytes 131104 | tf_op jit(solution)/shard_map/ppermute | solution.py:342
  71.2 1.3 %layer.1 = (bf16[128,256]{1,0:T(8,128)(2,1)S(1)}, bf16[128,256]{1,0:T(8,128)(2,1)S(1)}, bf16[4,144,128]{2,1,0:T(8,128)(2,1)S(1)}, bf16[4,144,128]{2,1,0:T(8,128)...) custom-call(s32[5]{0:T(128)S(1)} %stack.24.place_ref, ...), custom_call_target="tpu_custom_call" | custom-call | tf_op jit(solution)/shard_map/layer/pallas_call | solution.py:470
  72.5 1.3 %collective-permute-start.21 = (bf16[4,144,128]{2,1,0:T(8,128)(2,1)S(1)}, bf16[4,144,128]{2,1,0:T(8,128)(2,1)S(1)}, u32[]{:S(2)}, u32[]{:S(2)}) collective-permute-start(bf16[4,144,128]{2,1,0:T(8,128)(2,1)S(1)} %get-tuple-element.46), channel_id=1, source_target_pairs={{0,8},{1,3},{2,10},{3,5},{4,12},{5,7},{6,14},{7,1},{8,16},{9,11},{... | collective-permute-start | bytes 442376 | tf_op jit(solution)/shard_map/ppermute | solution.py:342
  73.8 2.5 %collective-permute-start.22 = (bf16[4,144,128]{2,1,0:T(8,128)(2,1)S(1)}, bf16[4,144,128]{2,1,0:T(8,128)(2,1)S(1)}, u32[]{:S(2)}, u32[]{:S(2)}) collective-permute-start(bf16[4,144,128]{2,1,0:T(8,128)(2,1)S(1)} %get-tuple-element.47), channel_id=1, source_target_pairs={{0,16},{1,5},{2,18},{3,7},{4,20},{5,1},{6,22},{7,3},{8,24},{9,13},... | collective-permute-start | bytes 442376 | tf_op jit(solution)/shard_map/ppermute | solution.py:342
  77.8 2.7 %collective-permute-done.22.refs_2_ = bf16[4,144,128]{2,1,0:T(8,128)(2,1)S(1)} collective-permute-done((bf16[4,144,128]{2,1,0:T(8,128)(2,1)S(1)}, bf16[4,144,128]{2,1,0:T(8,128)(2,1)S(1)}, u32[]{:S(2)}, u32[]{:S(2)}) %collective-permute-start.22) | collective-permute-done | bytes 147488 | tf_op jit(solution)/shard_map/ppermute | solution.py:342
  80.7 0.9 collective-permute-start.24
  81.5 2.3 %collective-permute-start.25 = (bf16[4,144,128]{2,1,0:T(8,128)(2,1)S(1)}, bf16[4,144,128]{2,1,0:T(8,128)(2,1)S(1)}, u32[]{:S(2)}, u32[]{:S(2)}) collective-permute-start(bf16[4,144,128]{2,1,0:T(8,128)(2,1)S(1)} %kv.1.own_part_ref), channel_id=1, source_target_pairs={{0,4},{1,17},{2,6},{3,19},{4,0},{5,21},{6,2},{7,23},{8,12},{9,25},... | collective-permute-start | bytes 442376 | tf_op jit(solution)/shard_map/ppermute | solution.py:342
  84.4 4.8 %collective-permute-start.27 = (bf16[128,256]{1,0:T(8,128)(2,1)S(1)}, bf16[128,256]{1,0:T(8,128)(2,1)S(1)}, u32[]{:S(2)}, u32[]{:S(2)}) collective-permute-start(bf16[128,256]{1,0:T(8,128)(2,1)S(1)} %get-tuple-element.50), channel_id=1, source_target_pairs={{0,1},{1,0},{2,3},{3,2},{4,5},{5,4},{6,7},{7,6},{8,9},{9,8},{10,11... | collective-permute-start | bytes 196616 | tf_op jit(solution)/shard_map/ppermute | solution.py:361
  89.2 0.9 collective-permute-done.27.got_layer_ref
  90.2 1.2 tile.1
  91.7 2.1 %collective-permute-start.29 = (bf16[4,128,128]{2,1,0:T(8,128)(2,1)S(1)}, bf16[4,128,128]{2,1,0:T(8,128)(2,1)S(1)}, u32[]{:S(2)}, u32[]{:S(2)}) collective-permute-start(bf16[4,128,128]{2,1,0:T(8,128)(2,1)S(1)} %get-tuple-element.52.own_ref), channel_id=1, source_target_pairs={{0,64},{32,96},{64,0},{96,32},{1,65},{33,97},{65,1},{97,33},{2,66}... | collective-permute-start | bytes 393224 | tf_op jit(solution)/shard_map/ppermute | solution.py:412
  94.4 3.5 %collective-permute-done.28.near_ref = bf16[4,128,128]{2,1,0:T(8,128)(2,1)S(1)} collective-permute-done((bf16[4,128,128]{2,1,0:T(8,128)(2,1)S(1)}, bf16[4,128,128]{2,1,0:T(8,128)(2,1)S(1)}, u32[]{:S(2)}, u32[]{:S(2)}) %collective-permute-start.28) | collective-permute-done | bytes 131104 | tf_op jit(solution)/shard_map/ppermute | solution.py:412
  99.1 1.0 collective-permute-start.33
  100.2 0.9 collective-permute-start.31
  101.1 1.7 %collective-permute-start.32 = (bf16[4,4,128,128]{3,2,1,0:T(8,128)(2,1)S(1)}, bf16[4,4,128,128]{3,2,1,0:T(8,128)(2,1)S(1)}, u32[]{:S(2)}, u32[]{:S(2)}) collective-permute-start(bf16[4,4,128,128]{3,2,1,0:T(8,128)(2,1)S(1)} %stack.25.one_ref.q0), channel_id=1, source_target_pairs={{0,24},{1,7},{2,26},{3,1},{4,28},{5,3},{6,30},{7,5},{8,0},{9,15},{... | collective-permute-start | bytes 1572872 | tf_op jit(solution)/shard_map/ppermute | solution.py:342
  102.8 11.2 %collective-permute-done.33.two_ref.q1 = bf16[4,4,128,128]{3,2,1,0:T(8,128)(2,1)S(1)} collective-permute-done((bf16[4,4,128,128]{3,2,1,0:T(8,128)(2,1)S(1)}, bf16[4,4,128,128]{3,2,1,0:T(8,128)(2,1)S(1)}, u32[]{:S(2)}, u32[]{:S(2)}) %collective-permute-start.33) | collective-permute-done | bytes 524320 | tf_op jit(solution)/shard_map/ppermute | solution.py:342
  115.1 1.5 %collective-permute-done.34.one_ref = bf16[2,8,128,128]{3,2,1,0:T(8,128)(2,1)S(1)} collective-permute-done((bf16[2,8,128,128]{3,2,1,0:T(8,128)(2,1)S(1)}, bf16[2,8,128,128]{3,2,1,0:T(8,128)(2,1)S(1)}, u32[]{:S(2)}, u32[]{:S(2)}) %collective-permute-start.34) | collective-permute-done | bytes 524320 | tf_op jit(solution)/shard_map/ppermute | solution.py:361
  117.4 4.5 %collective-permute-start.35 = (bf16[2,8,128,128]{3,2,1,0:T(8,128)(2,1)S(1)}, bf16[2,8,128,128]{3,2,1,0:T(8,128)(2,1)S(1)}, u32[]{:S(2)}, u32[]{:S(2)}) collective-permute-start(bf16[2,8,128,128]{3,2,1,0:T(8,128)(2,1)S(1)} %pick1.1), channel_id=1, source_target_pairs={{0,1},{1,0},{2,3},{3,2},{4,5},{5,4},{6,7},{7,6},{8,9},{9,8},{10,11... | collective-permute-start | bytes 1572872 | tf_op jit(solution)/shard_map/ppermute | solution.py:361
  121.8 1.8 %own.1._ = bf16[4,4,4,128,128]{4,3,2,1,0:T(8,128)(2,1)} custom-call(s32[5]{0:T(128)S(1)} %stack.24.place_ref, s32[128]{0:T(128)S(1)} %get-tuple-element.57.starts_ref, s32[128]{0:T(128)S(1)} %get-tuple-element.56.counts_ref, bf16[4,4,128,128]{3,2,1,0:T(8,128)(2,1)S(1)} %stack.25.one_ref.q0, bf16[4,4,128,128]{3,2,1,0:T(8,128)(2,1)S(1)} %collective-permute-done.33.two_ref.q1, ...), custom_call_target="tpu_custom_call" | custom-call | tf_op jit(solution)/shard_map/own/pallas_call | solution.py:514
  123.7 1.6 %rest.1 = bf16[4,4,4,128,128]{4,3,2,1,0:T(8,128)(2,1)} custom-call(s32[5]{0:T(128)S(1)} %stack.24.place_ref, s32[128]{0:T(128)S(1)} %get-tuple-element.57.starts_ref, bf16[2,8,128,128]{3,2,1,0:T(8,128)(2,1)S(1)} %collective-permute-done.34.one_ref, bf16[2,8,128,128]{3,2,1,0:T(8,128)(2,1)S(1)} %collective-permute-done.35.two_ref, ...), custom_call_target="tpu_custom_call", output_to_operand_aliasing={{}: (4, {})} | custom-call | tf_op jit(solution)/shard_map/rest/pallas_call | solution.py:523
  (76 shorter events, 11.9 us)
Async XLA Ops:
  0.7 26.5 %copy-start.7 = (f32[16,512]{1,0:T(8,128)S(1)}, f32[16,512]{1,0:T(8,128)}, u32[]{:S(2)}) copy-start(f32[16,512]{1,0:T(8,128)} %alog_ref.3) | copy-start | bytes 98308
  0.7 26.5 %copy-start.9 = (f32[512]{0:T(512)S(1)}, f32[512]{0:T(512)}, u32[]{:S(2)}) copy-start(f32[512]{0:T(512)} %param.20) | copy-start | bytes 6148
  2.8 24.4 %copy-start.1 = (bf16[256,512]{1,0:T(8,128)(2,1)S(1)}, bf16[256,512]{1,0:T(8,128)(2,1)}, u32[]{:S(2)}) copy-start(bf16[256,512]{1,0:T(8,128)(2,1)} %conv_ref.7) | copy-start | bytes 786436
  2.8 24.4 %copy-start.5 = (bf16[512,512]{1,0:T(8,128)(2,1)S(1)}, bf16[512,512]{1,0:T(8,128)(2,1)}, u32[]{:S(2)}) copy-start(bf16[512,512]{1,0:T(8,128)(2,1)} %weight_ref.2) | copy-start | bytes 1572868
  3.6 2.9 %collective-permute-start = (bf16[144,512]{1,0:T(8,128)(2,1)S(1)}, bf16[144,512]{1,0:T(8,128)(2,1)S(1)}, u32[]{:S(2)}, u32[]{:S(2)}) collective-permute-start(bf16[144,512]{1,0:T(8,128)(2,1)S(1)} %project_give.1), channel_id=1, source_target_pairs={{0,1},{1,0},{2,3},{3,2},{4,5},{5,4},{6,7},{7,6},{8,9},{9,8},{10,11... | collective-permute-start | bytes 442376 | tf_op jit(solution)/shard_map/ppermute | solution.py:361
  5.1 1.4 %collective-permute-start.1 = (f32[1,256]{1,0:T(1,128)}, f32[1,256]{1,0:T(1,128)S(1)}, u32[]{:S(2)}, u32[]{:S(2)}) collective-permute-start(f32[1,256]{1,0:T(1,128)} %bitcast.14), channel_id=1, source_target_pairs={{0,1},{1,0},{2,3},{3,2},{4,5},{5,4},{6,7},{7,6},{8,9},{9,8},{10,11... | collective-permute-start | bytes 3080 | tf_op jit(solution)/shard_map/ppermute | solution.py:361
  6.5 5.7 %collective-permute-start.2 = (bf16[144,512]{1,0:T(8,128)(2,1)S(1)}, bf16[144,512]{1,0:T(8,128)(2,1)S(1)}, u32[]{:S(2)}, u32[]{:S(2)}) collective-permute-start(bf16[144,512]{1,0:T(8,128)(2,1)S(1)} %chip.1.refs_0_), channel_id=1, source_target_pairs={{0,8},{1,3},{2,10},{3,5},{4,12},{5,7},{6,14},{7,1},{8,16},{9,11},{... | collective-permute-start | bytes 442376 | tf_op jit(solution)/shard_map/ppermute | solution.py:342
  8.0 7.0 %collective-permute-start.3 = (bf16[144,512]{1,0:T(8,128)(2,1)S(1)}, bf16[144,512]{1,0:T(8,128)(2,1)S(1)}, u32[]{:S(2)}, u32[]{:S(2)}) collective-permute-start(bf16[144,512]{1,0:T(8,128)(2,1)S(1)} %chip.1.refs_0_), channel_id=1, source_target_pairs={{0,16},{1,5},{2,18},{3,7},{4,20},{5,1},{6,22},{7,3},{8,24},{9,13},... | collective-permute-start | bytes 442376 | tf_op jit(solution)/shard_map/ppermute | solution.py:342
  10.6 4.4 %collective-permute-start.4 = (bf16[144,512]{1,0:T(8,128)(2,1)S(1)}, bf16[144,512]{1,0:T(8,128)(2,1)S(1)}, u32[]{:S(2)}, u32[]{:S(2)}) collective-permute-start(bf16[144,512]{1,0:T(8,128)(2,1)S(1)} %chip.1.refs_0_), channel_id=1, source_target_pairs={{0,24},{1,7},{2,26},{3,1},{4,28},{5,3},{6,30},{7,5},{8,0},{9,15},{... | collective-permute-start | bytes 442376 | tf_op jit(solution)/shard_map/ppermute | solution.py:342
  15.1 5.3 %collective-permute-start.5 = (bf16[144,512]{1,0:T(8,128)(2,1)S(1)}, bf16[144,512]{1,0:T(8,128)(2,1)S(1)}, u32[]{:S(2)}, u32[]{:S(2)}) collective-permute-start(bf16[144,512]{1,0:T(8,128)(2,1)S(1)} %row.1.refs_0_), channel_id=1, source_target_pairs={{0,2},{1,9},{2,4},{3,11},{4,6},{5,13},{6,0},{7,15},{8,10},{9,17},{... | collective-permute-start | bytes 442376 | tf_op jit(solution)/shard_map/ppermute | solution.py:342
  16.3 6.6 %collective-permute-start.6 = (bf16[144,512]{1,0:T(8,128)(2,1)S(1)}, bf16[144,512]{1,0:T(8,128)(2,1)S(1)}, u32[]{:S(2)}, u32[]{:S(2)}) collective-permute-start(bf16[144,512]{1,0:T(8,128)(2,1)S(1)} %row.1.refs_0_), channel_id=1, source_target_pairs={{0,4},{1,17},{2,6},{3,19},{4,0},{5,21},{6,2},{7,23},{8,12},{9,25},... | collective-permute-start | bytes 442376 | tf_op jit(solution)/shard_map/ppermute | solution.py:342
  18.7 4.1 %collective-permute-start.7 = (bf16[144,512]{1,0:T(8,128)(2,1)S(1)}, bf16[144,512]{1,0:T(8,128)(2,1)S(1)}, u32[]{:S(2)}, u32[]{:S(2)}) collective-permute-start(bf16[144,512]{1,0:T(8,128)(2,1)S(1)} %row.1.refs_0_), channel_id=1, source_target_pairs={{0,6},{1,25},{2,0},{3,27},{4,2},{5,29},{6,4},{7,31},{8,14},{9,1},{... | collective-permute-start | bytes 442376 | tf_op jit(solution)/shard_map/ppermute | solution.py:342
  22.9 4.3 %collective-permute-start.8 = (bf16[144,512]{1,0:T(8,128)(2,1)S(1)}, bf16[144,512]{1,0:T(8,128)(2,1)S(1)}, u32[]{:S(2)}, u32[]{:S(2)}) collective-permute-start(bf16[144,512]{1,0:T(8,128)(2,1)S(1)} %plane.1.own_proj_ref), channel_id=1, source_target_pairs={{0,1},{1,0},{2,3},{3,2},{4,5},{5,4},{6,7},{7,6},{8,9},{9,8},{10,11... | collective-permute-start | bytes 442376 | tf_op jit(solution)/shard_map/ppermute | solution.py:361
  29.9 8.7 %copy-start.4 = (bf16[256,256]{1,0:T(8,128)(2,1)S(1)}, bf16[256,256]{1,0:T(8,128)(2,1)}, u32[]{:S(2)}) copy-start(bf16[256,256]{1,0:T(8,128)(2,1)} %residual_ref.3) | copy-start | bytes 393220
  29.9 8.7 %copy-start.6 = (bf16[256,512]{1,0:T(8,128)(2,1)S(1)}, bf16[256,512]{1,0:T(8,128)(2,1)}, u32[]{:S(2)}) copy-start(bf16[256,512]{1,0:T(8,128)(2,1)} %gate_ref.1) | copy-start | bytes 786436
  29.9 8.7 %copy-start.8 = (f32[16,512]{1,0:T(8,128)S(1)}, f32[16,512]{1,0:T(8,128)}, u32[]{:S(2)}) copy-start(f32[16,512]{1,0:T(8,128)} %init_ref.1) | copy-start | bytes 98308
  29.9 8.7 %copy-start.10 = (f32[512]{0:T(512)S(1)}, f32[512]{0:T(512)}, u32[]{:S(2)}) copy-start(f32[512]{0:T(512)} %param.22) | copy-start | bytes 6148
  30.0 8.7 %collective-permute-start.10 = (f32[24,512]{1,0:T(8,128)S(1)}, f32[24,512]{1,0:T(8,128)S(1)}, u32[]{:S(2)}, u32[]{:S(2)}) collective-permute-start(f32[24,512]{1,0:T(8,128)S(1)} %get-tuple-element.32._), channel_id=1, source_target_pairs={{0,64},{32,96},{64,0},{96,32},{1,65},{33,97},{65,1},{97,33},{2,66}... | collective-permute-start | bytes 147464 | tf_op jit(solution)/shard_map/ppermute | solution.py:412
  33.6 5.0 %collective-permute-start.11 = (f32[24,512]{1,0:T(8,128)S(1)}, f32[24,512]{1,0:T(8,128)S(1)}, u32[]{:S(2)}, u32[]{:S(2)}) collective-permute-start(f32[24,512]{1,0:T(8,128)S(1)} %get-tuple-element.32._), channel_id=1, source_target_pairs={{0,96},{32,0},{64,32},{96,64},{1,97},{33,1},{65,33},{97,65},{2,98}... | collective-permute-start | bytes 147464 | tf_op jit(solution)/shard_map/ppermute | solution.py:412
  34.1 4.6 %collective-permute-start.9 = (f32[24,512]{1,0:T(8,128)S(1)}, f32[24,512]{1,0:T(8,128)S(1)}, u32[]{:S(2)}, u32[]{:S(2)}) collective-permute-start(f32[24,512]{1,0:T(8,128)S(1)} %get-tuple-element.32._), channel_id=1, source_target_pairs={{0,32},{32,64},{64,96},{96,0},{1,33},{33,65},{65,97},{97,1},{2,34}... | collective-permute-start | bytes 147464 | tf_op jit(solution)/shard_map/ppermute | solution.py:412
  43.5 4.1 %collective-permute-start.14 = (bf16[8,128,512]{2,1,0:T(8,128)(2,1)S(1)}, bf16[8,128,512]{2,1,0:T(8,128)(2,1)S(1)}, u32[]{:S(2)}, u32[]{:S(2)}) collective-permute-start(bf16[8,128,512]{2,1,0:T(8,128)(2,1)S(1)} %get-tuple-element.37), channel_id=1, source_target_pairs={{0,1},{1,0},{2,3},{3,2},{4,5},{5,4},{6,7},{7,6},{8,9},{9,8},{10,11... | collective-permute-start | bytes 3145736 | tf_op jit(solution)/shard_map/ppermute | solution.py:361
  45.2 6.0 %collective-permute-start.12 = (bf16[8,128,512]{2,1,0:T(8,128)(2,1)S(1)}, bf16[8,128,512]{2,1,0:T(8,128)(2,1)S(1)}, u32[]{:S(2)}, u32[]{:S(2)}) collective-permute-start(bf16[8,128,512]{2,1,0:T(8,128)(2,1)S(1)} %get-tuple-element.34), channel_id=1, source_target_pairs={{0,1},{1,0},{2,3},{3,2},{4,5},{5,4},{6,7},{7,6},{8,9},{9,8},{10,11... | collective-permute-start | bytes 3145736 | tf_op jit(solution)/shard_map/ppermute | solution.py:361
  45.3 22.8 %collective-permute-start.20 = (bf16[256,2048]{1,0:T(8,128)(2,1)S(1)}, bf16[256,2048]{1,0:T(8,128)(2,1)S(1)}, u32[]{:S(2)}, u32[]{:S(2)}) collective-permute-start(bf16[256,2048]{1,0:T(8,128)(2,1)S(1)} %copy-done.3), channel_id=1, source_target_pairs={{0,1},{1,0},{2,3},{3,2},{4,5},{5,4},{6,7},{7,6},{8,9},{9,8},{10,11... | collective-permute-start | bytes 3145736 | tf_op jit(solution)/shard_map/ppermute | solution.py:361
  47.8 10.0 %collective-permute-start.15 = (bf16[4,128,512]{2,1,0:T(8,128)(2,1)S(1)}, bf16[4,128,512]{2,1,0:T(8,128)(2,1)S(1)}, u32[]{:S(2)}, u32[]{:S(2)}) collective-permute-start(bf16[4,128,512]{2,1,0:T(8,128)(2,1)S(1)} %get-tuple-element.38), channel_id=1, source_target_pairs={{0,16},{1,5},{2,18},{3,7},{4,20},{5,1},{6,22},{7,3},{8,24},{9,13},... | collective-permute-start | bytes 1572872 | tf_op jit(solution)/shard_map/ppermute | solution.py:342
  50.0 21.2 %copy-start.11 = (f32[256]{0:T(256)S(1)}, f32[256]{0:T(256)}, u32[]{:S(2)}) copy-start(f32[256]{0:T(256)} %param.25) | copy-start | bytes 3076
  50.0 13.2 %collective-permute-start.16 = (bf16[4,128,512]{2,1,0:T(8,128)(2,1)S(1)}, bf16[4,128,512]{2,1,0:T(8,128)(2,1)S(1)}, u32[]{:S(2)}, u32[]{:S(2)}) collective-permute-start(bf16[4,128,512]{2,1,0:T(8,128)(2,1)S(1)} %get-tuple-element.39), channel_id=1, source_target_pairs={{0,24},{1,7},{2,26},{3,1},{4,28},{5,3},{6,30},{7,5},{8,0},{9,15},{... | collective-permute-start | bytes 1572872 | tf_op jit(solution)/shard_map/ppermute | solution.py:342
  51.4 11.9 %collective-permute-start.13 = (bf16[4,128,512]{2,1,0:T(8,128)(2,1)S(1)}, bf16[4,128,512]{2,1,0:T(8,128)(2,1)S(1)}, u32[]{:S(2)}, u32[]{:S(2)}) collective-permute-start(bf16[4,128,512]{2,1,0:T(8,128)(2,1)S(1)} %get-tuple-element.36), channel_id=1, source_target_pairs={{0,8},{1,3},{2,10},{3,5},{4,12},{5,7},{6,14},{7,1},{8,16},{9,11},{... | collective-permute-start | bytes 1572872 | tf_op jit(solution)/shard_map/ppermute | solution.py:342
  63.6 5.3 %collective-permute-start.17 = (bf16[128,512]{1,0:T(8,128)(2,1)S(1)}, bf16[128,512]{1,0:T(8,128)(2,1)S(1)}, u32[]{:S(2)}, u32[]{:S(2)}) collective-permute-start(bf16[128,512]{1,0:T(8,128)(2,1)S(1)} %get-tuple-element.41), channel_id=1, source_target_pairs={{0,2},{1,9},{2,4},{3,11},{4,6},{5,13},{6,0},{7,15},{8,10},{9,17},{... | collective-permute-start | bytes 393224 | tf_op jit(solution)/shard_map/ppermute | solution.py:342
  64.9 6.2 %collective-permute-start.18 = (bf16[128,512]{1,0:T(8,128)(2,1)S(1)}, bf16[128,512]{1,0:T(8,128)(2,1)S(1)}, u32[]{:S(2)}, u32[]{:S(2)}) collective-permute-start(bf16[128,512]{1,0:T(8,128)(2,1)S(1)} %get-tuple-element.42), channel_id=1, source_target_pairs={{0,4},{1,17},{2,6},{3,19},{4,0},{5,21},{6,2},{7,23},{8,12},{9,25},... | collective-permute-start | bytes 393224 | tf_op jit(solution)/shard_map/ppermute | solution.py:342
  67.4 3.8 %collective-permute-start.19 = (bf16[128,512]{1,0:T(8,128)(2,1)S(1)}, bf16[128,512]{1,0:T(8,128)(2,1)S(1)}, u32[]{:S(2)}, u32[]{:S(2)}) collective-permute-start(bf16[128,512]{1,0:T(8,128)(2,1)S(1)} %get-tuple-element.43), channel_id=1, source_target_pairs={{0,6},{1,25},{2,0},{3,27},{4,2},{5,29},{6,4},{7,31},{8,14},{9,1},{... | collective-permute-start | bytes 393224 | tf_op jit(solution)/shard_map/ppermute | solution.py:342
  71.2 28.9 %copy-start.12 = (s32[128]{0:T(128)S(1)}, s32[128]{0:T(128)}, u32[]{:S(2)}) copy-start(s32[128]{0:T(128)} %param.29) | copy-start | bytes 1540
  71.2 28.9 %copy-start.13 = (s32[128]{0:T(128)S(1)}, s32[128]{0:T(128)}, u32[]{:S(2)}) copy-start(s32[128]{0:T(128)} %param.27) | copy-start | bytes 1540
  71.2 28.9 %copy-start.14 = (s32[128]{0:T(128)S(1)}, s32[128]{0:T(128)}, u32[]{:S(2)}) copy-start(s32[128]{0:T(128)} %param.28) | copy-start | bytes 1540
  72.5 5.3 %collective-permute-start.21 = (bf16[4,144,128]{2,1,0:T(8,128)(2,1)S(1)}, bf16[4,144,128]{2,1,0:T(8,128)(2,1)S(1)}, u32[]{:S(2)}, u32[]{:S(2)}) collective-permute-start(bf16[4,144,128]{2,1,0:T(8,128)(2,1)S(1)} %get-tuple-element.46), channel_id=1, source_target_pairs={{0,8},{1,3},{2,10},{3,5},{4,12},{5,7},{6,14},{7,1},{8,16},{9,11},{... | collective-permute-start | bytes 442376 | tf_op jit(solution)/shard_map/ppermute | solution.py:342
  73.8 6.7 %collective-permute-start.22 = (bf16[4,144,128]{2,1,0:T(8,128)(2,1)S(1)}, bf16[4,144,128]{2,1,0:T(8,128)(2,1)S(1)}, u32[]{:S(2)}, u32[]{:S(2)}) collective-permute-start(bf16[4,144,128]{2,1,0:T(8,128)(2,1)S(1)} %get-tuple-element.47), channel_id=1, source_target_pairs={{0,16},{1,5},{2,18},{3,7},{4,20},{5,1},{6,22},{7,3},{8,24},{9,13},... | collective-permute-start | bytes 442376 | tf_op jit(solution)/shard_map/ppermute | solution.py:342
  76.3 4.3 %collective-permute-start.23 = (bf16[4,144,128]{2,1,0:T(8,128)(2,1)S(1)}, bf16[4,144,128]{2,1,0:T(8,128)(2,1)S(1)}, u32[]{:S(2)}, u32[]{:S(2)}) collective-permute-start(bf16[4,144,128]{2,1,0:T(8,128)(2,1)S(1)} %get-tuple-element.48), channel_id=1, source_target_pairs={{0,24},{1,7},{2,26},{3,1},{4,28},{5,3},{6,30},{7,5},{8,0},{9,15},{... | collective-permute-start | bytes 442376 | tf_op jit(solution)/shard_map/ppermute | solution.py:342
  80.7 9.5 %collective-permute-start.24 = (bf16[4,144,128]{2,1,0:T(8,128)(2,1)S(1)}, bf16[4,144,128]{2,1,0:T(8,128)(2,1)S(1)}, u32[]{:S(2)}, u32[]{:S(2)}) collective-permute-start(bf16[4,144,128]{2,1,0:T(8,128)(2,1)S(1)} %kv.1.own_part_ref), channel_id=1, source_target_pairs={{0,2},{1,9},{2,4},{3,11},{4,6},{5,13},{6,0},{7,15},{8,10},{9,17},{... | collective-permute-start | bytes 442376 | tf_op jit(solution)/shard_map/ppermute | solution.py:342
  81.5 8.6 %collective-permute-start.25 = (bf16[4,144,128]{2,1,0:T(8,128)(2,1)S(1)}, bf16[4,144,128]{2,1,0:T(8,128)(2,1)S(1)}, u32[]{:S(2)}, u32[]{:S(2)}) collective-permute-start(bf16[4,144,128]{2,1,0:T(8,128)(2,1)S(1)} %kv.1.own_part_ref), channel_id=1, source_target_pairs={{0,4},{1,17},{2,6},{3,19},{4,0},{5,21},{6,2},{7,23},{8,12},{9,25},... | collective-permute-start | bytes 442376 | tf_op jit(solution)/shard_map/ppermute | solution.py:342
  83.8 6.4 %collective-permute-start.26 = (bf16[4,144,128]{2,1,0:T(8,128)(2,1)S(1)}, bf16[4,144,128]{2,1,0:T(8,128)(2,1)S(1)}, u32[]{:S(2)}, u32[]{:S(2)}) collective-permute-start(bf16[4,144,128]{2,1,0:T(8,128)(2,1)S(1)} %kv.1.own_part_ref), channel_id=1, source_target_pairs={{0,6},{1,25},{2,0},{3,27},{4,2},{5,29},{6,4},{7,31},{8,14},{9,1},{... | collective-permute-start | bytes 442376 | tf_op jit(solution)/shard_map/ppermute | solution.py:342
  84.4 5.7 %collective-permute-start.27 = (bf16[128,256]{1,0:T(8,128)(2,1)S(1)}, bf16[128,256]{1,0:T(8,128)(2,1)S(1)}, u32[]{:S(2)}, u32[]{:S(2)}) collective-permute-start(bf16[128,256]{1,0:T(8,128)(2,1)S(1)} %get-tuple-element.50), channel_id=1, source_target_pairs={{0,1},{1,0},{2,3},{3,2},{4,5},{5,4},{6,7},{7,6},{8,9},{9,8},{10,11... | collective-permute-start | bytes 196616 | tf_op jit(solution)/shard_map/ppermute | solution.py:361
  91.4 6.4 %collective-permute-start.28 = (bf16[4,128,128]{2,1,0:T(8,128)(2,1)S(1)}, bf16[4,128,128]{2,1,0:T(8,128)(2,1)S(1)}, u32[]{:S(2)}, u32[]{:S(2)}) collective-permute-start(bf16[4,128,128]{2,1,0:T(8,128)(2,1)S(1)} %get-tuple-element.52.own_ref), channel_id=1, source_target_pairs={{0,32},{32,64},{64,96},{96,0},{1,33},{33,65},{65,97},{97,1},{2,34}... | collective-permute-start | bytes 393224 | tf_op jit(solution)/shard_map/ppermute | solution.py:412
  91.7 6.1 %collective-permute-start.29 = (bf16[4,128,128]{2,1,0:T(8,128)(2,1)S(1)}, bf16[4,128,128]{2,1,0:T(8,128)(2,1)S(1)}, u32[]{:S(2)}, u32[]{:S(2)}) collective-permute-start(bf16[4,128,128]{2,1,0:T(8,128)(2,1)S(1)} %get-tuple-element.52.own_ref), channel_id=1, source_target_pairs={{0,64},{32,96},{64,0},{96,32},{1,65},{33,97},{65,1},{97,33},{2,66}... | collective-permute-start | bytes 393224 | tf_op jit(solution)/shard_map/ppermute | solution.py:412
  93.8 4.7 %collective-permute-start.30 = (bf16[4,128,128]{2,1,0:T(8,128)(2,1)S(1)}, bf16[4,128,128]{2,1,0:T(8,128)(2,1)S(1)}, u32[]{:S(2)}, u32[]{:S(2)}) collective-permute-start(bf16[4,128,128]{2,1,0:T(8,128)(2,1)S(1)} %get-tuple-element.52.own_ref), channel_id=1, source_target_pairs={{0,96},{32,0},{64,32},{96,64},{1,97},{33,1},{65,33},{97,65},{2,98}... | collective-permute-start | bytes 393224 | tf_op jit(solution)/shard_map/ppermute | solution.py:412
  99.1 14.9 %collective-permute-start.33 = (bf16[4,4,128,128]{3,2,1,0:T(8,128)(2,1)S(1)}, bf16[4,4,128,128]{3,2,1,0:T(8,128)(2,1)S(1)}, u32[]{:S(2)}, u32[]{:S(2)}) collective-permute-start(bf16[4,4,128,128]{3,2,1,0:T(8,128)(2,1)S(1)} %stack.25.one_ref.q0), channel_id=1, source_target_pairs={{0,8},{1,3},{2,10},{3,5},{4,12},{5,7},{6,14},{7,1},{8,16},{9,11},{... | collective-permute-start | bytes 1572872 | tf_op jit(solution)/shard_map/ppermute | solution.py:342
  100.2 14.9 %collective-permute-start.31 = (bf16[4,4,128,128]{3,2,1,0:T(8,128)(2,1)S(1)}, bf16[4,4,128,128]{3,2,1,0:T(8,128)(2,1)S(1)}, u32[]{:S(2)}, u32[]{:S(2)}) collective-permute-start(bf16[4,4,128,128]{3,2,1,0:T(8,128)(2,1)S(1)} %stack.25.one_ref.q0), channel_id=1, source_target_pairs={{0,16},{1,5},{2,18},{3,7},{4,20},{5,1},{6,22},{7,3},{8,24},{9,13},... | collective-permute-start | bytes 1572872 | tf_op jit(solution)/shard_map/ppermute | solution.py:342
  101.1 14.0 %collective-permute-start.32 = (bf16[4,4,128,128]{3,2,1,0:T(8,128)(2,1)S(1)}, bf16[4,4,128,128]{3,2,1,0:T(8,128)(2,1)S(1)}, u32[]{:S(2)}, u32[]{:S(2)}) collective-permute-start(bf16[4,4,128,128]{3,2,1,0:T(8,128)(2,1)S(1)} %stack.25.one_ref.q0), channel_id=1, source_target_pairs={{0,24},{1,7},{2,26},{3,1},{4,28},{5,3},{6,30},{7,5},{8,0},{9,15},{... | collective-permute-start | bytes 1572872 | tf_op jit(solution)/shard_map/ppermute | solution.py:342
  114.7 2.0 %collective-permute-start.34 = (bf16[2,8,128,128]{3,2,1,0:T(8,128)(2,1)S(1)}, bf16[2,8,128,128]{3,2,1,0:T(8,128)(2,1)S(1)}, u32[]{:S(2)}, u32[]{:S(2)}) collective-permute-start(bf16[2,8,128,128]{3,2,1,0:T(8,128)(2,1)S(1)} %pick0.1), channel_id=1, source_target_pairs={{0,1},{1,0},{2,3},{3,2},{4,5},{5,4},{6,7},{7,6},{8,9},{9,8},{10,11... | collective-permute-start | bytes 1572872 | tf_op jit(solution)/shard_map/ppermute | solution.py:361
  117.4 6.3 %collective-permute-start.35 = (bf16[2,8,128,128]{3,2,1,0:T(8,128)(2,1)S(1)}, bf16[2,8,128,128]{3,2,1,0:T(8,128)(2,1)S(1)}, u32[]{:S(2)}, u32[]{:S(2)}) collective-permute-start(bf16[2,8,128,128]{3,2,1,0:T(8,128)(2,1)S(1)} %pick1.1), channel_id=1, source_target_pairs={{0,1},{1,0},{2,3},{3,2},{4,5},{5,4},{6,7},{7,6},{8,9},{9,8},{10,11... | collective-permute-start | bytes 1572872 | tf_op jit(solution)/shard_map/ppermute | solution.py:361
  (3 other events, 8.6 us)

commit v8 on v7

--- a/solution.py
+++ b/solution.py
@@ -20,7 +20,7 @@
 PIECES = 8
 SIDE = 4
 SOON, LATER = (2, 3), (0, 1)
-EARLY, LATE = 1, (2, 3)
+EARLY, LATE = 3, (1, 2)
 BF = jnp.bfloat16
 F32 = jnp.float32
 

time: 126 us -> 127 us (level)
  starting transfers between devices: 55 us -> 62.2 us
  waiting for transfers between devices: 43.7 us -> 37.7 us
    ppermute x9, starting transfers between devices: 16.9 us -> 24.7 us  [swap(): return lax.ppermute(value, 'tp', partner)]
    ppermute x21, waiting for transfers between devices: 35.7 us -> 29.8 us  [line(): lax.ppermute(value_of(shift), 'tp', [((x * SIDE + y) * 2 + c, ((x + shift...]
  transfers between devices with their start and end apart: 36 -> 36, of which waited for: 20 -> 20; matrix products, arithmetic and copies ran while one was open for 0% -> 0% of each run, Pallas kernels for 8% -> 7%
where the time goes in v8:
time: 127 us
  starting transfers between devices  62.2 us (49%)
  waiting for transfers between devices  37.7 us (30%)
  Pallas kernels  23.4 us (18%)
  local copies, waits for them, and re-layouts  2.15 us (2%)
    ppermute x21, waiting for transfers between devices, line(): lax.ppermute(value_of(shift), 'tp', [((x * SIDE + y) * 2 + c, ((x + shift...  29.8 us
    ppermute x21, starting transfers between devices, line(): lax.ppermute(value_of(shift), 'tp', [((x * SIDE + y) * 2 + c, ((x + shift...  29.4 us
    ppermute x9, starting transfers between devices, swap(): return lax.ppermute(value, 'tp', partner)  24.7 us
    ppermute x6, starting transfers between devices, ranges_back(): lax.ppermute(value, 'ctx', [(z, (z + s) % ctx_count) for z in range(ctx_c...  8.1 us
    pallas_call x1, Pallas kernels, per_device(): pl.pallas_call(give_kernel, in_specs=[SM] + [VM] * 12, out_shape=(shape(h...  4.76 us
    ppermute x6, waiting for transfers between devices, ranges_back(): lax.ppermute(value, 'ctx', [(z, (z + s) % ctx_count) for z in range(ctx_c...  4.11 us
    ppermute x9, waiting for transfers between devices, swap(): return lax.ppermute(value, 'tp', partner)  3.85 us
    pallas_call x1, Pallas kernels, per_device(): pl.pallas_call(bring_kernel, in_specs=[ANY] * 2, out_shape=shape(out_weig...  3.5 us
  transfers between devices with their start and end apart: 36, of which 20 were waited for; matrix products, arithmetic and copies ran while one was open for 0% of the time, Pallas kernels for 7%

profile of v8, /device:TPU:1, one launch (start us, length us, event | category | flops | bytes accessed | tf_op | source)
XLA Modules:
  0.0 126.8 jit_solution(1577343171668103661)
XLA Ops:
  0.8 0.9 copy-done
  1.7 1.1 copy-done.2
  2.8 0.9 project_give.1
  3.6 1.5 %collective-permute-start = (bf16[144,512]{1,0:T(8,128)(2,1)S(1)}, bf16[144,512]{1,0:T(8,128)(2,1)S(1)}, u32[]{:S(2)}, u32[]{:S(2)}) collective-permute-start(bf16[144,512]{1,0:T(8,128)(2,1)S(1)} %project_give.1), channel_id=1, source_target_pairs={{0,1},{1,0},{2,3},{3,2},{4,5},{5,4},{6,7},{7,6},{8,9},{9,8},{10,11... | collective-permute-start | bytes 442376 | tf_op jit(solution)/shard_map/ppermute | solution.py:361
  5.2 0.8 project_keep.1.refs_0_
  6.5 1.4 %collective-permute-start.2 = (bf16[144,512]{1,0:T(8,128)(2,1)S(1)}, bf16[144,512]{1,0:T(8,128)(2,1)S(1)}, u32[]{:S(2)}, u32[]{:S(2)}) collective-permute-start(bf16[144,512]{1,0:T(8,128)(2,1)S(1)} %chip.1.refs_0_), channel_id=1, source_target_pairs={{0,8},{1,3},{2,10},{3,5},{4,12},{5,7},{6,14},{7,1},{8,16},{9,11},{... | collective-permute-start | bytes 442376 | tf_op jit(solution)/shard_map/ppermute | solution.py:342
  8.0 2.6 %collective-permute-start.3 = (bf16[144,512]{1,0:T(8,128)(2,1)S(1)}, bf16[144,512]{1,0:T(8,128)(2,1)S(1)}, u32[]{:S(2)}, u32[]{:S(2)}) collective-permute-start(bf16[144,512]{1,0:T(8,128)(2,1)S(1)} %chip.1.refs_0_), channel_id=1, source_target_pairs={{0,16},{1,5},{2,18},{3,7},{4,20},{5,1},{6,22},{7,3},{8,24},{9,13},... | collective-permute-start | bytes 442376 | tf_op jit(solution)/shard_map/ppermute | solution.py:342
  10.6 1.1 collective-permute-start.4
  12.2 2.8 %collective-permute-done.3.refs_2_ = bf16[144,512]{1,0:T(8,128)(2,1)S(1)} collective-permute-done((bf16[144,512]{1,0:T(8,128)(2,1)S(1)}, bf16[144,512]{1,0:T(8,128)(2,1)S(1)}, u32[]{:S(2)}, u32[]{:S(2)}) %collective-permute-start.3) | collective-permute-done | bytes 147488 | tf_op jit(solution)/shard_map/ppermute | solution.py:342
  15.1 1.2 collective-permute-start.5
  16.3 2.4 %collective-permute-start.6 = (bf16[144,512]{1,0:T(8,128)(2,1)S(1)}, bf16[144,512]{1,0:T(8,128)(2,1)S(1)}, u32[]{:S(2)}, u32[]{:S(2)}) collective-permute-start(bf16[144,512]{1,0:T(8,128)(2,1)S(1)} %row.1.refs_0_), channel_id=1, source_target_pairs={{0,4},{1,17},{2,6},{3,19},{4,0},{5,21},{6,2},{7,23},{8,12},{9,25},... | collective-permute-start | bytes 442376 | tf_op jit(solution)/shard_map/ppermute | solution.py:342
  18.7 1.2 collective-permute-start.7
  20.4 2.4 %collective-permute-done.6.refs_2_ = bf16[144,512]{1,0:T(8,128)(2,1)S(1)} collective-permute-done((bf16[144,512]{1,0:T(8,128)(2,1)S(1)}, bf16[144,512]{1,0:T(8,128)(2,1)S(1)}, u32[]{:S(2)}, u32[]{:S(2)}) %collective-permute-start.6) | collective-permute-done | bytes 147488 | tf_op jit(solution)/shard_map/ppermute | solution.py:342
  22.9 3.3 %collective-permute-start.8 = (bf16[144,512]{1,0:T(8,128)(2,1)S(1)}, bf16[144,512]{1,0:T(8,128)(2,1)S(1)}, u32[]{:S(2)}, u32[]{:S(2)}) collective-permute-start(bf16[144,512]{1,0:T(8,128)(2,1)S(1)} %plane.1.own_proj_ref), channel_id=1, source_target_pairs={{0,1},{1,0},{2,3},{3,2},{4,5},{5,4},{6,7},{7,6},{8,9},{9,8},{10,11... | collective-permute-start | bytes 442376 | tf_op jit(solution)/shard_map/ppermute | solution.py:361
  26.2 1.0 collective-permute-done.8.got_proj_ref
  27.2 2.7 %first.1 = (f32[256,512]{1,0:T(8,128)S(1)}, f32[4,32,64]{2,1,0:T(8,128)S(1)}, f32[24,512]{1,0:T(8,128)S(1)}) custom-call(s32[5]{0:T(128)S(1)} %stack.24.place_ref, bf16[144,512]{1,0:T(8,128)(2,1)S(1)} %plane.1.own_proj_ref, bf16[144,512]{1,0:T(8,128)(2,1)S(1)} %collective-permute-done.8.got_proj_ref, bf16[512,512]{1,0:T(8,128)(2,1)S(1)} %copy-done.5, ...), custom_call_target="tpu_custom_call" | custom-call | tf_op jit(solution)/shard_map/first/pallas_call | solution.py:395
  30.0 3.7 %collective-permute-start.10 = (f32[24,512]{1,0:T(8,128)S(1)}, f32[24,512]{1,0:T(8,128)S(1)}, u32[]{:S(2)}, u32[]{:S(2)}) collective-permute-start(f32[24,512]{1,0:T(8,128)S(1)} %get-tuple-element.32._), channel_id=1, source_target_pairs={{0,64},{32,96},{64,0},{96,32},{1,65},{33,97},{65,1},{97,33},{2,66}... | collective-permute-start | bytes 147464 | tf_op jit(solution)/shard_map/ppermute | solution.py:412
  34.1 1.0 collective-permute-start.9
  35.1 3.5 %bring.1.weight_ref = bf16[512,8192]{1,0:T(8,128)(2,1)S(1)} custom-call(bf16[512,8192]{1,0:T(8,128)(2,1)} %weight_ref.3, f32[24,512]{1,0:T(8,128)S(1)} %get-tuple-element.32._), custom_call_target="tpu_custom_call" | custom-call | tf_op jit(solution)/shard_map/bring/pallas_call | solution.py:416
  38.7 4.8 %give.1 = (bf16[8,128,512]{2,1,0:T(8,128)(2,1)S(1)}, bf16[8,128,512]{2,1,0:T(8,128)(2,1)S(1)}, bf16[128,512]{1,0:T(8,128)(2,1)S(1)}) custom-call(s32[5]{0:T(128)S(1)} %stack.24.place_ref, f32[256,512]{1,0:T(8,128)S(1)} %get-tuple-element.30.step_ref, f32[4,32,64]{2,1,0:T(8,128)S(1)} %get-tuple-element.31.states_ref, f32[16,512]{1,0:T(8,128)S(1)} %copy-done.7, ...), custom_call_target="tpu_custom_call" | custom-call | tf_op jit(solution)/shard_map/give/pallas_call | solution.py:426
  43.5 1.7 %collective-permute-start.14 = (bf16[8,128,512]{2,1,0:T(8,128)(2,1)S(1)}, bf16[8,128,512]{2,1,0:T(8,128)(2,1)S(1)}, u32[]{:S(2)}, u32[]{:S(2)}) collective-permute-start(bf16[8,128,512]{2,1,0:T(8,128)(2,1)S(1)} %get-tuple-element.37), channel_id=1, source_target_pairs={{0,1},{1,0},{2,3},{3,2},{4,5},{5,4},{6,7},{7,6},{8,9},{9,8},{10,11... | collective-permute-start | bytes 3145736 | tf_op jit(solution)/shard_map/ppermute | solution.py:361
  45.7 1.8 %keep.1.keep_ref = bf16[16,128,512]{2,1,0:T(8,128)(2,1)S(1)} custom-call(s32[5]{0:T(128)S(1)} %stack.24.place_ref, bf16[128,512]{1,0:T(8,128)(2,1)S(1)} %get-tuple-element.33.kept_ref, bf16[512,8192]{1,0:T(8,128)(2,1)S(1)} %bring.1.weight_ref), custom_call_target="tpu_custom_call" | custom-call | tf_op jit(solution)/shard_map/keep/pallas_call | solution.py:442
  47.8 2.2 %collective-permute-start.15 = (bf16[4,128,512]{2,1,0:T(8,128)(2,1)S(1)}, bf16[4,128,512]{2,1,0:T(8,128)(2,1)S(1)}, u32[]{:S(2)}, u32[]{:S(2)}) collective-permute-start(bf16[4,128,512]{2,1,0:T(8,128)(2,1)S(1)} %get-tuple-element.38), channel_id=1, source_target_pairs={{0,16},{1,5},{2,18},{3,7},{4,20},{5,1},{6,22},{7,3},{8,24},{9,13},... | collective-permute-start | bytes 1572872 | tf_op jit(solution)/shard_map/ppermute | solution.py:342
  50.0 1.2 collective-permute-start.16
  51.8 6.0 %collective-permute-done.15.two_ref = bf16[4,128,512]{2,1,0:T(8,128)(2,1)S(1)} collective-permute-done((bf16[4,128,512]{2,1,0:T(8,128)(2,1)S(1)}, bf16[4,128,512]{2,1,0:T(8,128)(2,1)S(1)}, u32[]{:S(2)}, u32[]{:S(2)}) %collective-permute-start.15) | collective-permute-done | bytes 524320 | tf_op jit(solution)/shard_map/ppermute | solution.py:342
  57.7 5.5 %collective-permute-done.16.three_ref = bf16[4,128,512]{2,1,0:T(8,128)(2,1)S(1)} collective-permute-done((bf16[4,128,512]{2,1,0:T(8,128)(2,1)S(1)}, bf16[4,128,512]{2,1,0:T(8,128)(2,1)S(1)}, u32[]{:S(2)}, u32[]{:S(2)}) %collective-permute-start.16) | collective-permute-done | bytes 524320 | tf_op jit(solution)/shard_map/ppermute | solution.py:342
  63.6 1.4 %collective-permute-start.17 = (bf16[128,512]{1,0:T(8,128)(2,1)S(1)}, bf16[128,512]{1,0:T(8,128)(2,1)S(1)}, u32[]{:S(2)}, u32[]{:S(2)}) collective-permute-start(bf16[128,512]{1,0:T(8,128)(2,1)S(1)} %get-tuple-element.41), channel_id=1, source_target_pairs={{0,2},{1,9},{2,4},{3,11},{4,6},{5,13},{6,0},{7,15},{8,10},{9,17},{... | collective-permute-start | bytes 393224 | tf_op jit(solution)/shard_map/ppermute | solution.py:342
  64.9 2.4 %collective-permute-start.18 = (bf16[128,512]{1,0:T(8,128)(2,1)S(1)}, bf16[128,512]{1,0:T(8,128)(2,1)S(1)}, u32[]{:S(2)}, u32[]{:S(2)}) collective-permute-start(bf16[128,512]{1,0:T(8,128)(2,1)S(1)} %get-tuple-element.42), channel_id=1, source_target_pairs={{0,4},{1,17},{2,6},{3,19},{4,0},{5,21},{6,2},{7,23},{8,12},{9,25},... | collective-permute-start | bytes 393224 | tf_op jit(solution)/shard_map/ppermute | solution.py:342
  68.8 2.3 %collective-permute-done.18.two_ref = bf16[128,512]{1,0:T(8,128)(2,1)S(1)} collective-permute-done((bf16[128,512]{1,0:T(8,128)(2,1)S(1)}, bf16[128,512]{1,0:T(8,128)(2,1)S(1)}, u32[]{:S(2)}, u32[]{:S(2)}) %collective-permute-start.18) | collective-permute-done | bytes 131104 | tf_op jit(solution)/shard_map/ppermute | solution.py:342
  71.2 1.3 %layer.1 = (bf16[128,256]{1,0:T(8,128)(2,1)S(1)}, bf16[128,256]{1,0:T(8,128)(2,1)S(1)}, bf16[4,144,128]{2,1,0:T(8,128)(2,1)S(1)}, bf16[4,144,128]{2,1,0:T(8,128)...) custom-call(s32[5]{0:T(128)S(1)} %stack.24.place_ref, ...), custom_call_target="tpu_custom_call" | custom-call | tf_op jit(solution)/shard_map/layer/pallas_call | solution.py:470
  72.5 1.3 %collective-permute-start.21 = (bf16[4,144,128]{2,1,0:T(8,128)(2,1)S(1)}, bf16[4,144,128]{2,1,0:T(8,128)(2,1)S(1)}, u32[]{:S(2)}, u32[]{:S(2)}) collective-permute-start(bf16[4,144,128]{2,1,0:T(8,128)(2,1)S(1)} %get-tuple-element.46), channel_id=1, source_target_pairs={{0,8},{1,3},{2,10},{3,5},{4,12},{5,7},{6,14},{7,1},{8,16},{9,11},{... | collective-permute-start | bytes 442376 | tf_op jit(solution)/shard_map/ppermute | solution.py:342
  73.8 2.5 %collective-permute-start.22 = (bf16[4,144,128]{2,1,0:T(8,128)(2,1)S(1)}, bf16[4,144,128]{2,1,0:T(8,128)(2,1)S(1)}, u32[]{:S(2)}, u32[]{:S(2)}) collective-permute-start(bf16[4,144,128]{2,1,0:T(8,128)(2,1)S(1)} %get-tuple-element.47), channel_id=1, source_target_pairs={{0,16},{1,5},{2,18},{3,7},{4,20},{5,1},{6,22},{7,3},{8,24},{9,13},... | collective-permute-start | bytes 442376 | tf_op jit(solution)/shard_map/ppermute | solution.py:342
  77.8 2.7 %collective-permute-done.22.refs_2_ = bf16[4,144,128]{2,1,0:T(8,128)(2,1)S(1)} collective-permute-done((bf16[4,144,128]{2,1,0:T(8,128)(2,1)S(1)}, bf16[4,144,128]{2,1,0:T(8,128)(2,1)S(1)}, u32[]{:S(2)}, u32[]{:S(2)}) %collective-permute-start.22) | collective-permute-done | bytes 147488 | tf_op jit(solution)/shard_map/ppermute | solution.py:342
  80.7 0.9 collective-permute-start.24
  81.5 2.3 %collective-permute-start.25 = (bf16[4,144,128]{2,1,0:T(8,128)(2,1)S(1)}, bf16[4,144,128]{2,1,0:T(8,128)(2,1)S(1)}, u32[]{:S(2)}, u32[]{:S(2)}) collective-permute-start(bf16[4,144,128]{2,1,0:T(8,128)(2,1)S(1)} %kv.1.own_part_ref), channel_id=1, source_target_pairs={{0,4},{1,17},{2,6},{3,19},{4,0},{5,21},{6,2},{7,23},{8,12},{9,25},... | collective-permute-start | bytes 442376 | tf_op jit(solution)/shard_map/ppermute | solution.py:342
  84.4 4.8 %collective-permute-start.27 = (bf16[128,256]{1,0:T(8,128)(2,1)S(1)}, bf16[128,256]{1,0:T(8,128)(2,1)S(1)}, u32[]{:S(2)}, u32[]{:S(2)}) collective-permute-start(bf16[128,256]{1,0:T(8,128)(2,1)S(1)} %get-tuple-element.50), channel_id=1, source_target_pairs={{0,1},{1,0},{2,3},{3,2},{4,5},{5,4},{6,7},{7,6},{8,9},{9,8},{10,11... | collective-permute-start | bytes 196616 | tf_op jit(solution)/shard_map/ppermute | solution.py:361
  89.2 0.9 collective-permute-done.27.got_layer_ref
  90.2 1.2 tile.1
  91.7 2.1 %collective-permute-start.29 = (bf16[4,128,128]{2,1,0:T(8,128)(2,1)S(1)}, bf16[4,128,128]{2,1,0:T(8,128)(2,1)S(1)}, u32[]{:S(2)}, u32[]{:S(2)}) collective-permute-start(bf16[4,128,128]{2,1,0:T(8,128)(2,1)S(1)} %get-tuple-element.52.own_ref), channel_id=1, source_target_pairs={{0,64},{32,96},{64,0},{96,32},{1,65},{33,97},{65,1},{97,33},{2,66}... | collective-permute-start | bytes 393224 | tf_op jit(solution)/shard_map/ppermute | solution.py:412
  94.4 3.5 %collective-permute-done.28.near_ref = bf16[4,128,128]{2,1,0:T(8,128)(2,1)S(1)} collective-permute-done((bf16[4,128,128]{2,1,0:T(8,128)(2,1)S(1)}, bf16[4,128,128]{2,1,0:T(8,128)(2,1)S(1)}, u32[]{:S(2)}, u32[]{:S(2)}) %collective-permute-start.28) | collective-permute-done | bytes 131104 | tf_op jit(solution)/shard_map/ppermute | solution.py:412
  99.8 1.0 collective-permute-start.31
  100.8 1.4 %collective-permute-start.32 = (bf16[4,4,128,128]{3,2,1,0:T(8,128)(2,1)S(1)}, bf16[4,4,128,128]{3,2,1,0:T(8,128)(2,1)S(1)}, u32[]{:S(2)}, u32[]{:S(2)}) collective-permute-start(bf16[4,4,128,128]{3,2,1,0:T(8,128)(2,1)S(1)} %stack.25.one_ref.q0), channel_id=1, source_target_pairs={{0,16},{1,5},{2,18},{3,7},{4,20},{5,1},{6,22},{7,3},{8,24},{9,13},... | collective-permute-start | bytes 1572872 | tf_op jit(solution)/shard_map/ppermute | solution.py:342
  102.2 5.3 %collective-permute-done.33.two_ref.q1 = bf16[4,4,128,128]{3,2,1,0:T(8,128)(2,1)S(1)} collective-permute-done((bf16[4,4,128,128]{3,2,1,0:T(8,128)(2,1)S(1)}, bf16[4,4,128,128]{3,2,1,0:T(8,128)(2,1)S(1)}, u32[]{:S(2)}, u32[]{:S(2)}) %collective-permute-start.33) | collective-permute-done | bytes 524320 | tf_op jit(solution)/shard_map/ppermute | solution.py:342
  108.1 11.1 %collective-permute-start.34 = (bf16[2,8,128,128]{3,2,1,0:T(8,128)(2,1)S(1)}, bf16[2,8,128,128]{3,2,1,0:T(8,128)(2,1)S(1)}, u32[]{:S(2)}, u32[]{:S(2)}) collective-permute-start(bf16[2,8,128,128]{3,2,1,0:T(8,128)(2,1)S(1)} %pick0.1), channel_id=1, source_target_pairs={{0,1},{1,0},{2,3},{3,2},{4,5},{5,4},{6,7},{7,6},{8,9},{9,8},{10,11... | collective-permute-start | bytes 1572872 | tf_op jit(solution)/shard_map/ppermute | solution.py:361
  119.3 1.5 %collective-permute-done.34.one_ref = bf16[2,8,128,128]{3,2,1,0:T(8,128)(2,1)S(1)} collective-permute-done((bf16[2,8,128,128]{3,2,1,0:T(8,128)(2,1)S(1)}, bf16[2,8,128,128]{3,2,1,0:T(8,128)(2,1)S(1)}, u32[]{:S(2)}, u32[]{:S(2)}) %collective-permute-start.34) | collective-permute-done | bytes 524320 | tf_op jit(solution)/shard_map/ppermute | solution.py:361
  121.5 1.6 %collective-permute-start.35 = (bf16[2,8,128,128]{3,2,1,0:T(8,128)(2,1)S(1)}, bf16[2,8,128,128]{3,2,1,0:T(8,128)(2,1)S(1)}, u32[]{:S(2)}, u32[]{:S(2)}) collective-permute-start(bf16[2,8,128,128]{3,2,1,0:T(8,128)(2,1)S(1)} %pick1.1), channel_id=1, source_target_pairs={{0,1},{1,0},{2,3},{3,2},{4,5},{5,4},{6,7},{7,6},{8,9},{9,8},{10,11... | collective-permute-start | bytes 1572872 | tf_op jit(solution)/shard_map/ppermute | solution.py:361
  123.2 1.8 %own.1._ = bf16[4,4,4,128,128]{4,3,2,1,0:T(8,128)(2,1)} custom-call(s32[5]{0:T(128)S(1)} %stack.24.place_ref, s32[128]{0:T(128)S(1)} %get-tuple-element.57.starts_ref, s32[128]{0:T(128)S(1)} %get-tuple-element.56.counts_ref, bf16[4,4,128,128]{3,2,1,0:T(8,128)(2,1)S(1)} %stack.25.one_ref.q0, bf16[4,4,128,128]{3,2,1,0:T(8,128)(2,1)S(1)} %collective-permute-done.33.two_ref.q1, ...), custom_call_target="tpu_custom_call" | custom-call | tf_op jit(solution)/shard_map/own/pallas_call | solution.py:514
  125.0 1.6 %rest.1 = bf16[4,4,4,128,128]{4,3,2,1,0:T(8,128)(2,1)} custom-call(s32[5]{0:T(128)S(1)} %stack.24.place_ref, s32[128]{0:T(128)S(1)} %get-tuple-element.57.starts_ref, bf16[2,8,128,128]{3,2,1,0:T(8,128)(2,1)S(1)} %collective-permute-done.34.one_ref, bf16[2,8,128,128]{3,2,1,0:T(8,128)(2,1)S(1)} %collective-permute-done.35.two_ref, ...), custom_call_target="tpu_custom_call", output_to_operand_aliasing={{}: (4, {})} | custom-call | tf_op jit(solution)/shard_map/rest/pallas_call | solution.py:523
  (76 shorter events, 12.1 us)
Async XLA Ops:
  0.7 26.5 %copy-start.7 = (f32[16,512]{1,0:T(8,128)S(1)}, f32[16,512]{1,0:T(8,128)}, u32[]{:S(2)}) copy-start(f32[16,512]{1,0:T(8,128)} %alog_ref.3) | copy-start | bytes 98308
  0.7 26.5 %copy-start.9 = (f32[512]{0:T(512)S(1)}, f32[512]{0:T(512)}, u32[]{:S(2)}) copy-start(f32[512]{0:T(512)} %param.20) | copy-start | bytes 6148
  2.8 24.4 %copy-start.1 = (bf16[256,512]{1,0:T(8,128)(2,1)S(1)}, bf16[256,512]{1,0:T(8,128)(2,1)}, u32[]{:S(2)}) copy-start(bf16[256,512]{1,0:T(8,128)(2,1)} %conv_ref.7) | copy-start | bytes 786436
  2.8 24.4 %copy-start.5 = (bf16[512,512]{1,0:T(8,128)(2,1)S(1)}, bf16[512,512]{1,0:T(8,128)(2,1)}, u32[]{:S(2)}) copy-start(bf16[512,512]{1,0:T(8,128)(2,1)} %weight_ref.2) | copy-start | bytes 1572868
  3.6 2.9 %collective-permute-start = (bf16[144,512]{1,0:T(8,128)(2,1)S(1)}, bf16[144,512]{1,0:T(8,128)(2,1)S(1)}, u32[]{:S(2)}, u32[]{:S(2)}) collective-permute-start(bf16[144,512]{1,0:T(8,128)(2,1)S(1)} %project_give.1), channel_id=1, source_target_pairs={{0,1},{1,0},{2,3},{3,2},{4,5},{5,4},{6,7},{7,6},{8,9},{9,8},{10,11... | collective-permute-start | bytes 442376 | tf_op jit(solution)/shard_map/ppermute | solution.py:361
  5.1 1.4 %collective-permute-start.1 = (f32[1,256]{1,0:T(1,128)}, f32[1,256]{1,0:T(1,128)S(1)}, u32[]{:S(2)}, u32[]{:S(2)}) collective-permute-start(f32[1,256]{1,0:T(1,128)} %bitcast.14), channel_id=1, source_target_pairs={{0,1},{1,0},{2,3},{3,2},{4,5},{5,4},{6,7},{7,6},{8,9},{9,8},{10,11... | collective-permute-start | bytes 3080 | tf_op jit(solution)/shard_map/ppermute | solution.py:361
  6.5 5.7 %collective-permute-start.2 = (bf16[144,512]{1,0:T(8,128)(2,1)S(1)}, bf16[144,512]{1,0:T(8,128)(2,1)S(1)}, u32[]{:S(2)}, u32[]{:S(2)}) collective-permute-start(bf16[144,512]{1,0:T(8,128)(2,1)S(1)} %chip.1.refs_0_), channel_id=1, source_target_pairs={{0,8},{1,3},{2,10},{3,5},{4,12},{5,7},{6,14},{7,1},{8,16},{9,11},{... | collective-permute-start | bytes 442376 | tf_op jit(solution)/shard_map/ppermute | solution.py:342
  8.0 7.0 %collective-permute-start.3 = (bf16[144,512]{1,0:T(8,128)(2,1)S(1)}, bf16[144,512]{1,0:T(8,128)(2,1)S(1)}, u32[]{:S(2)}, u32[]{:S(2)}) collective-permute-start(bf16[144,512]{1,0:T(8,128)(2,1)S(1)} %chip.1.refs_0_), channel_id=1, source_target_pairs={{0,16},{1,5},{2,18},{3,7},{4,20},{5,1},{6,22},{7,3},{8,24},{9,13},... | collective-permute-start | bytes 442376 | tf_op jit(solution)/shard_map/ppermute | solution.py:342
  10.6 4.4 %collective-permute-start.4 = (bf16[144,512]{1,0:T(8,128)(2,1)S(1)}, bf16[144,512]{1,0:T(8,128)(2,1)S(1)}, u32[]{:S(2)}, u32[]{:S(2)}) collective-permute-start(bf16[144,512]{1,0:T(8,128)(2,1)S(1)} %chip.1.refs_0_), channel_id=1, source_target_pairs={{0,24},{1,7},{2,26},{3,1},{4,28},{5,3},{6,30},{7,5},{8,0},{9,15},{... | collective-permute-start | bytes 442376 | tf_op jit(solution)/shard_map/ppermute | solution.py:342
  15.1 5.3 %collective-permute-start.5 = (bf16[144,512]{1,0:T(8,128)(2,1)S(1)}, bf16[144,512]{1,0:T(8,128)(2,1)S(1)}, u32[]{:S(2)}, u32[]{:S(2)}) collective-permute-start(bf16[144,512]{1,0:T(8,128)(2,1)S(1)} %row.1.refs_0_), channel_id=1, source_target_pairs={{0,2},{1,9},{2,4},{3,11},{4,6},{5,13},{6,0},{7,15},{8,10},{9,17},{... | collective-permute-start | bytes 442376 | tf_op jit(solution)/shard_map/ppermute | solution.py:342
  16.3 6.6 %collective-permute-start.6 = (bf16[144,512]{1,0:T(8,128)(2,1)S(1)}, bf16[144,512]{1,0:T(8,128)(2,1)S(1)}, u32[]{:S(2)}, u32[]{:S(2)}) collective-permute-start(bf16[144,512]{1,0:T(8,128)(2,1)S(1)} %row.1.refs_0_), channel_id=1, source_target_pairs={{0,4},{1,17},{2,6},{3,19},{4,0},{5,21},{6,2},{7,23},{8,12},{9,25},... | collective-permute-start | bytes 442376 | tf_op jit(solution)/shard_map/ppermute | solution.py:342
  18.7 4.1 %collective-permute-start.7 = (bf16[144,512]{1,0:T(8,128)(2,1)S(1)}, bf16[144,512]{1,0:T(8,128)(2,1)S(1)}, u32[]{:S(2)}, u32[]{:S(2)}) collective-permute-start(bf16[144,512]{1,0:T(8,128)(2,1)S(1)} %row.1.refs_0_), channel_id=1, source_target_pairs={{0,6},{1,25},{2,0},{3,27},{4,2},{5,29},{6,4},{7,31},{8,14},{9,1},{... | collective-permute-start | bytes 442376 | tf_op jit(solution)/shard_map/ppermute | solution.py:342
  22.9 4.3 %collective-permute-start.8 = (bf16[144,512]{1,0:T(8,128)(2,1)S(1)}, bf16[144,512]{1,0:T(8,128)(2,1)S(1)}, u32[]{:S(2)}, u32[]{:S(2)}) collective-permute-start(bf16[144,512]{1,0:T(8,128)(2,1)S(1)} %plane.1.own_proj_ref), channel_id=1, source_target_pairs={{0,1},{1,0},{2,3},{3,2},{4,5},{5,4},{6,7},{7,6},{8,9},{9,8},{10,11... | collective-permute-start | bytes 442376 | tf_op jit(solution)/shard_map/ppermute | solution.py:361
  29.9 8.7 %copy-start.4 = (bf16[256,256]{1,0:T(8,128)(2,1)S(1)}, bf16[256,256]{1,0:T(8,128)(2,1)}, u32[]{:S(2)}) copy-start(bf16[256,256]{1,0:T(8,128)(2,1)} %residual_ref.3) | copy-start | bytes 393220
  29.9 8.7 %copy-start.6 = (bf16[256,512]{1,0:T(8,128)(2,1)S(1)}, bf16[256,512]{1,0:T(8,128)(2,1)}, u32[]{:S(2)}) copy-start(bf16[256,512]{1,0:T(8,128)(2,1)} %gate_ref.1) | copy-start | bytes 786436
  29.9 8.7 %copy-start.8 = (f32[16,512]{1,0:T(8,128)S(1)}, f32[16,512]{1,0:T(8,128)}, u32[]{:S(2)}) copy-start(f32[16,512]{1,0:T(8,128)} %init_ref.1) | copy-start | bytes 98308
  29.9 8.7 %copy-start.10 = (f32[512]{0:T(512)S(1)}, f32[512]{0:T(512)}, u32[]{:S(2)}) copy-start(f32[512]{0:T(512)} %param.22) | copy-start | bytes 6148
  30.0 8.7 %collective-permute-start.10 = (f32[24,512]{1,0:T(8,128)S(1)}, f32[24,512]{1,0:T(8,128)S(1)}, u32[]{:S(2)}, u32[]{:S(2)}) collective-permute-start(f32[24,512]{1,0:T(8,128)S(1)} %get-tuple-element.32._), channel_id=1, source_target_pairs={{0,64},{32,96},{64,0},{96,32},{1,65},{33,97},{65,1},{97,33},{2,66}... | collective-permute-start | bytes 147464 | tf_op jit(solution)/shard_map/ppermute | solution.py:412
  33.6 5.0 %collective-permute-start.11 = (f32[24,512]{1,0:T(8,128)S(1)}, f32[24,512]{1,0:T(8,128)S(1)}, u32[]{:S(2)}, u32[]{:S(2)}) collective-permute-start(f32[24,512]{1,0:T(8,128)S(1)} %get-tuple-element.32._), channel_id=1, source_target_pairs={{0,96},{32,0},{64,32},{96,64},{1,97},{33,1},{65,33},{97,65},{2,98}... | collective-permute-start | bytes 147464 | tf_op jit(solution)/shard_map/ppermute | solution.py:412
  34.1 4.6 %collective-permute-start.9 = (f32[24,512]{1,0:T(8,128)S(1)}, f32[24,512]{1,0:T(8,128)S(1)}, u32[]{:S(2)}, u32[]{:S(2)}) collective-permute-start(f32[24,512]{1,0:T(8,128)S(1)} %get-tuple-element.32._), channel_id=1, source_target_pairs={{0,32},{32,64},{64,96},{96,0},{1,33},{33,65},{65,97},{97,1},{2,34}... | collective-permute-start | bytes 147464 | tf_op jit(solution)/shard_map/ppermute | solution.py:412
  43.5 4.1 %collective-permute-start.14 = (bf16[8,128,512]{2,1,0:T(8,128)(2,1)S(1)}, bf16[8,128,512]{2,1,0:T(8,128)(2,1)S(1)}, u32[]{:S(2)}, u32[]{:S(2)}) collective-permute-start(bf16[8,128,512]{2,1,0:T(8,128)(2,1)S(1)} %get-tuple-element.37), channel_id=1, source_target_pairs={{0,1},{1,0},{2,3},{3,2},{4,5},{5,4},{6,7},{7,6},{8,9},{9,8},{10,11... | collective-permute-start | bytes 3145736 | tf_op jit(solution)/shard_map/ppermute | solution.py:361
  45.2 6.0 %collective-permute-start.12 = (bf16[8,128,512]{2,1,0:T(8,128)(2,1)S(1)}, bf16[8,128,512]{2,1,0:T(8,128)(2,1)S(1)}, u32[]{:S(2)}, u32[]{:S(2)}) collective-permute-start(bf16[8,128,512]{2,1,0:T(8,128)(2,1)S(1)} %get-tuple-element.34), channel_id=1, source_target_pairs={{0,1},{1,0},{2,3},{3,2},{4,5},{5,4},{6,7},{7,6},{8,9},{9,8},{10,11... | collective-permute-start | bytes 3145736 | tf_op jit(solution)/shard_map/ppermute | solution.py:361
  45.3 22.8 %collective-permute-start.20 = (bf16[256,2048]{1,0:T(8,128)(2,1)S(1)}, bf16[256,2048]{1,0:T(8,128)(2,1)S(1)}, u32[]{:S(2)}, u32[]{:S(2)}) collective-permute-start(bf16[256,2048]{1,0:T(8,128)(2,1)S(1)} %copy-done.3), channel_id=1, source_target_pairs={{0,1},{1,0},{2,3},{3,2},{4,5},{5,4},{6,7},{7,6},{8,9},{9,8},{10,11... | collective-permute-start | bytes 3145736 | tf_op jit(solution)/shard_map/ppermute | solution.py:361
  47.8 10.0 %collective-permute-start.15 = (bf16[4,128,512]{2,1,0:T(8,128)(2,1)S(1)}, bf16[4,128,512]{2,1,0:T(8,128)(2,1)S(1)}, u32[]{:S(2)}, u32[]{:S(2)}) collective-permute-start(bf16[4,128,512]{2,1,0:T(8,128)(2,1)S(1)} %get-tuple-element.38), channel_id=1, source_target_pairs={{0,16},{1,5},{2,18},{3,7},{4,20},{5,1},{6,22},{7,3},{8,24},{9,13},... | collective-permute-start | bytes 1572872 | tf_op jit(solution)/shard_map/ppermute | solution.py:342
  50.0 21.2 %copy-start.11 = (f32[256]{0:T(256)S(1)}, f32[256]{0:T(256)}, u32[]{:S(2)}) copy-start(f32[256]{0:T(256)} %param.25) | copy-start | bytes 3076
  50.0 13.2 %collective-permute-start.16 = (bf16[4,128,512]{2,1,0:T(8,128)(2,1)S(1)}, bf16[4,128,512]{2,1,0:T(8,128)(2,1)S(1)}, u32[]{:S(2)}, u32[]{:S(2)}) collective-permute-start(bf16[4,128,512]{2,1,0:T(8,128)(2,1)S(1)} %get-tuple-element.39), channel_id=1, source_target_pairs={{0,24},{1,7},{2,26},{3,1},{4,28},{5,3},{6,30},{7,5},{8,0},{9,15},{... | collective-permute-start | bytes 1572872 | tf_op jit(solution)/shard_map/ppermute | solution.py:342
  51.4 11.9 %collective-permute-start.13 = (bf16[4,128,512]{2,1,0:T(8,128)(2,1)S(1)}, bf16[4,128,512]{2,1,0:T(8,128)(2,1)S(1)}, u32[]{:S(2)}, u32[]{:S(2)}) collective-permute-start(bf16[4,128,512]{2,1,0:T(8,128)(2,1)S(1)} %get-tuple-element.36), channel_id=1, source_target_pairs={{0,8},{1,3},{2,10},{3,5},{4,12},{5,7},{6,14},{7,1},{8,16},{9,11},{... | collective-permute-start | bytes 1572872 | tf_op jit(solution)/shard_map/ppermute | solution.py:342
  63.6 5.3 %collective-permute-start.17 = (bf16[128,512]{1,0:T(8,128)(2,1)S(1)}, bf16[128,512]{1,0:T(8,128)(2,1)S(1)}, u32[]{:S(2)}, u32[]{:S(2)}) collective-permute-start(bf16[128,512]{1,0:T(8,128)(2,1)S(1)} %get-tuple-element.41), channel_id=1, source_target_pairs={{0,2},{1,9},{2,4},{3,11},{4,6},{5,13},{6,0},{7,15},{8,10},{9,17},{... | collective-permute-start | bytes 393224 | tf_op jit(solution)/shard_map/ppermute | solution.py:342
  64.9 6.2 %collective-permute-start.18 = (bf16[128,512]{1,0:T(8,128)(2,1)S(1)}, bf16[128,512]{1,0:T(8,128)(2,1)S(1)}, u32[]{:S(2)}, u32[]{:S(2)}) collective-permute-start(bf16[128,512]{1,0:T(8,128)(2,1)S(1)} %get-tuple-element.42), channel_id=1, source_target_pairs={{0,4},{1,17},{2,6},{3,19},{4,0},{5,21},{6,2},{7,23},{8,12},{9,25},... | collective-permute-start | bytes 393224 | tf_op jit(solution)/shard_map/ppermute | solution.py:342
  67.4 3.8 %collective-permute-start.19 = (bf16[128,512]{1,0:T(8,128)(2,1)S(1)}, bf16[128,512]{1,0:T(8,128)(2,1)S(1)}, u32[]{:S(2)}, u32[]{:S(2)}) collective-permute-start(bf16[128,512]{1,0:T(8,128)(2,1)S(1)} %get-tuple-element.43), channel_id=1, source_target_pairs={{0,6},{1,25},{2,0},{3,27},{4,2},{5,29},{6,4},{7,31},{8,14},{9,1},{... | collective-permute-start | bytes 393224 | tf_op jit(solution)/shard_map/ppermute | solution.py:342
  71.2 28.5 %copy-start.12 = (s32[128]{0:T(128)S(1)}, s32[128]{0:T(128)}, u32[]{:S(2)}) copy-start(s32[128]{0:T(128)} %param.29) | copy-start | bytes 1540
  71.2 28.5 %copy-start.13 = (s32[128]{0:T(128)S(1)}, s32[128]{0:T(128)}, u32[]{:S(2)}) copy-start(s32[128]{0:T(128)} %param.27) | copy-start | bytes 1540
  71.2 28.5 %copy-start.14 = (s32[128]{0:T(128)S(1)}, s32[128]{0:T(128)}, u32[]{:S(2)}) copy-start(s32[128]{0:T(128)} %param.28) | copy-start | bytes 1540
  72.5 5.3 %collective-permute-start.21 = (bf16[4,144,128]{2,1,0:T(8,128)(2,1)S(1)}, bf16[4,144,128]{2,1,0:T(8,128)(2,1)S(1)}, u32[]{:S(2)}, u32[]{:S(2)}) collective-permute-start(bf16[4,144,128]{2,1,0:T(8,128)(2,1)S(1)} %get-tuple-element.46), channel_id=1, source_target_pairs={{0,8},{1,3},{2,10},{3,5},{4,12},{5,7},{6,14},{7,1},{8,16},{9,11},{... | collective-permute-start | bytes 442376 | tf_op jit(solution)/shard_map/ppermute | solution.py:342
  73.8 6.7 %collective-permute-start.22 = (bf16[4,144,128]{2,1,0:T(8,128)(2,1)S(1)}, bf16[4,144,128]{2,1,0:T(8,128)(2,1)S(1)}, u32[]{:S(2)}, u32[]{:S(2)}) collective-permute-start(bf16[4,144,128]{2,1,0:T(8,128)(2,1)S(1)} %get-tuple-element.47), channel_id=1, source_target_pairs={{0,16},{1,5},{2,18},{3,7},{4,20},{5,1},{6,22},{7,3},{8,24},{9,13},... | collective-permute-start | bytes 442376 | tf_op jit(solution)/shard_map/ppermute | solution.py:342
  76.3 4.3 %collective-permute-start.23 = (bf16[4,144,128]{2,1,0:T(8,128)(2,1)S(1)}, bf16[4,144,128]{2,1,0:T(8,128)(2,1)S(1)}, u32[]{:S(2)}, u32[]{:S(2)}) collective-permute-start(bf16[4,144,128]{2,1,0:T(8,128)(2,1)S(1)} %get-tuple-element.48), channel_id=1, source_target_pairs={{0,24},{1,7},{2,26},{3,1},{4,28},{5,3},{6,30},{7,5},{8,0},{9,15},{... | collective-permute-start | bytes 442376 | tf_op jit(solution)/shard_map/ppermute | solution.py:342
  80.7 9.5 %collective-permute-start.24 = (bf16[4,144,128]{2,1,0:T(8,128)(2,1)S(1)}, bf16[4,144,128]{2,1,0:T(8,128)(2,1)S(1)}, u32[]{:S(2)}, u32[]{:S(2)}) collective-permute-start(bf16[4,144,128]{2,1,0:T(8,128)(2,1)S(1)} %kv.1.own_part_ref), channel_id=1, source_target_pairs={{0,2},{1,9},{2,4},{3,11},{4,6},{5,13},{6,0},{7,15},{8,10},{9,17},{... | collective-permute-start | bytes 442376 | tf_op jit(solution)/shard_map/ppermute | solution.py:342
  81.5 8.6 %collective-permute-start.25 = (bf16[4,144,128]{2,1,0:T(8,128)(2,1)S(1)}, bf16[4,144,128]{2,1,0:T(8,128)(2,1)S(1)}, u32[]{:S(2)}, u32[]{:S(2)}) collective-permute-start(bf16[4,144,128]{2,1,0:T(8,128)(2,1)S(1)} %kv.1.own_part_ref), channel_id=1, source_target_pairs={{0,4},{1,17},{2,6},{3,19},{4,0},{5,21},{6,2},{7,23},{8,12},{9,25},... | collective-permute-start | bytes 442376 | tf_op jit(solution)/shard_map/ppermute | solution.py:342
  83.8 6.4 %collective-permute-start.26 = (bf16[4,144,128]{2,1,0:T(8,128)(2,1)S(1)}, bf16[4,144,128]{2,1,0:T(8,128)(2,1)S(1)}, u32[]{:S(2)}, u32[]{:S(2)}) collective-permute-start(bf16[4,144,128]{2,1,0:T(8,128)(2,1)S(1)} %kv.1.own_part_ref), channel_id=1, source_target_pairs={{0,6},{1,25},{2,0},{3,27},{4,2},{5,29},{6,4},{7,31},{8,14},{9,1},{... | collective-permute-start | bytes 442376 | tf_op jit(solution)/shard_map/ppermute | solution.py:342
  84.4 5.7 %collective-permute-start.27 = (bf16[128,256]{1,0:T(8,128)(2,1)S(1)}, bf16[128,256]{1,0:T(8,128)(2,1)S(1)}, u32[]{:S(2)}, u32[]{:S(2)}) collective-permute-start(bf16[128,256]{1,0:T(8,128)(2,1)S(1)} %get-tuple-element.50), channel_id=1, source_target_pairs={{0,1},{1,0},{2,3},{3,2},{4,5},{5,4},{6,7},{7,6},{8,9},{9,8},{10,11... | collective-permute-start | bytes 196616 | tf_op jit(solution)/shard_map/ppermute | solution.py:361
  91.4 6.4 %collective-permute-start.28 = (bf16[4,128,128]{2,1,0:T(8,128)(2,1)S(1)}, bf16[4,128,128]{2,1,0:T(8,128)(2,1)S(1)}, u32[]{:S(2)}, u32[]{:S(2)}) collective-permute-start(bf16[4,128,128]{2,1,0:T(8,128)(2,1)S(1)} %get-tuple-element.52.own_ref), channel_id=1, source_target_pairs={{0,32},{32,64},{64,96},{96,0},{1,33},{33,65},{65,97},{97,1},{2,34}... | collective-permute-start | bytes 393224 | tf_op jit(solution)/shard_map/ppermute | solution.py:412
  91.7 6.1 %collective-permute-start.29 = (bf16[4,128,128]{2,1,0:T(8,128)(2,1)S(1)}, bf16[4,128,128]{2,1,0:T(8,128)(2,1)S(1)}, u32[]{:S(2)}, u32[]{:S(2)}) collective-permute-start(bf16[4,128,128]{2,1,0:T(8,128)(2,1)S(1)} %get-tuple-element.52.own_ref), channel_id=1, source_target_pairs={{0,64},{32,96},{64,0},{96,32},{1,65},{33,97},{65,1},{97,33},{2,66}... | collective-permute-start | bytes 393224 | tf_op jit(solution)/shard_map/ppermute | solution.py:412
  93.8 4.7 %collective-permute-start.30 = (bf16[4,128,128]{2,1,0:T(8,128)(2,1)S(1)}, bf16[4,128,128]{2,1,0:T(8,128)(2,1)S(1)}, u32[]{:S(2)}, u32[]{:S(2)}) collective-permute-start(bf16[4,128,128]{2,1,0:T(8,128)(2,1)S(1)} %get-tuple-element.52.own_ref), channel_id=1, source_target_pairs={{0,96},{32,0},{64,32},{96,64},{1,97},{33,1},{65,33},{97,65},{2,98}... | collective-permute-start | bytes 393224 | tf_op jit(solution)/shard_map/ppermute | solution.py:412
  99.1 8.4 %collective-permute-start.33 = (bf16[4,4,128,128]{3,2,1,0:T(8,128)(2,1)S(1)}, bf16[4,4,128,128]{3,2,1,0:T(8,128)(2,1)S(1)}, u32[]{:S(2)}, u32[]{:S(2)}) collective-permute-start(bf16[4,4,128,128]{3,2,1,0:T(8,128)(2,1)S(1)} %stack.25.one_ref.q0), channel_id=1, source_target_pairs={{0,24},{1,7},{2,26},{3,1},{4,28},{5,3},{6,30},{7,5},{8,0},{9,15},{... | collective-permute-start | bytes 1572872 | tf_op jit(solution)/shard_map/ppermute | solution.py:342
  99.8 19.4 %collective-permute-start.31 = (bf16[4,4,128,128]{3,2,1,0:T(8,128)(2,1)S(1)}, bf16[4,4,128,128]{3,2,1,0:T(8,128)(2,1)S(1)}, u32[]{:S(2)}, u32[]{:S(2)}) collective-permute-start(bf16[4,4,128,128]{3,2,1,0:T(8,128)(2,1)S(1)} %stack.25.one_ref.q0), channel_id=1, source_target_pairs={{0,8},{1,3},{2,10},{3,5},{4,12},{5,7},{6,14},{7,1},{8,16},{9,11},{... | collective-permute-start | bytes 1572872 | tf_op jit(solution)/shard_map/ppermute | solution.py:342
  100.8 18.5 %collective-permute-start.32 = (bf16[4,4,128,128]{3,2,1,0:T(8,128)(2,1)S(1)}, bf16[4,4,128,128]{3,2,1,0:T(8,128)(2,1)S(1)}, u32[]{:S(2)}, u32[]{:S(2)}) collective-permute-start(bf16[4,4,128,128]{3,2,1,0:T(8,128)(2,1)S(1)} %stack.25.one_ref.q0), channel_id=1, source_target_pairs={{0,16},{1,5},{2,18},{3,7},{4,20},{5,1},{6,22},{7,3},{8,24},{9,13},... | collective-permute-start | bytes 1572872 | tf_op jit(solution)/shard_map/ppermute | solution.py:342
  108.1 12.7 %collective-permute-start.34 = (bf16[2,8,128,128]{3,2,1,0:T(8,128)(2,1)S(1)}, bf16[2,8,128,128]{3,2,1,0:T(8,128)(2,1)S(1)}, u32[]{:S(2)}, u32[]{:S(2)}) collective-permute-start(bf16[2,8,128,128]{3,2,1,0:T(8,128)(2,1)S(1)} %pick0.1), channel_id=1, source_target_pairs={{0,1},{1,0},{2,3},{3,2},{4,5},{5,4},{6,7},{7,6},{8,9},{9,8},{10,11... | collective-permute-start | bytes 1572872 | tf_op jit(solution)/shard_map/ppermute | solution.py:361
  121.5 3.5 %collective-permute-start.35 = (bf16[2,8,128,128]{3,2,1,0:T(8,128)(2,1)S(1)}, bf16[2,8,128,128]{3,2,1,0:T(8,128)(2,1)S(1)}, u32[]{:S(2)}, u32[]{:S(2)}) collective-permute-start(bf16[2,8,128,128]{3,2,1,0:T(8,128)(2,1)S(1)} %pick1.1), channel_id=1, source_target_pairs={{0,1},{1,0},{2,3},{3,2},{4,5},{5,4},{6,7},{7,6},{8,9},{9,8},{10,11... | collective-permute-start | bytes 1572872 | tf_op jit(solution)/shard_map/ppermute | solution.py:361
  (3 other events, 8.6 us)
